TPU v7x, 32 devices: a whole 2x2x4 slice. The times are simulated.
32 devices in a mesh: sub: 8 (over z, y), blk: 4 (over x, core).
Axes of the slice: x: 2, y: 2, z: 4, core: 2. Of those that a mesh axis runs over, the one named last changes fastest.
Arguments:
- right_side: float32 [8, 4, 96, 32], P('sub', 'blk')
- stiffness: bfloat16 [8, 4, 48, 9216], P('sub', 'blk'), may hold values from -1 to 7, as said below
- block_pairs: int32 [8, 4, 2, 16], P('sub', 'blk'), may hold values from 0 to 31, as said below
- trace_rows: int32 [8, 4, 128, 128], P('sub', 'blk'), may hold values from 0 to 3071
- partner_face: int32 [8, 4, 64], P('sub', 'blk'), may hold values from 0 to 63, each once within a row
- owner_list: int32 [8, 4, 4], P('sub', 'blk'), may hold values from 0 to 3, as said below
- mortar_weight: float32 [8, 4, 4, 16, 128], P('sub', 'blk'), may hold values from 0.1 to 1
Outputs:
- solution_field: float32 [8, 4, 96, 32], P('sub', 'blk')
- residual: float32 [8, 4, 96, 32], P('sub', 'blk')
Inputs may be any that keep to these rules, and one draw needn't show every extreme that they name: `block_pairs`: on each subdomain every block row 0 to 31 appears exactly once among the 2 rows. `owner_list`: for each subdomain the 4 face groups go to distinct owners, and within a group every owner receives exactly one face group from each subdomain slot. The assembled stiffness K is symmetric positive definite.
All inputs are finite; a program needn't handle non-finite values.
Results may differ from a plain program's by a relative error of at most 0.005.
Values sent between devices are 32-bit elements; how exact they have to be, the bound alone decides.
No kernel may reach another device: no remote copies, remote signals or barrier semaphores. Data moves between devices by JAX's collectives and lax.ppermute only.
A program may use at most 64 MiB of HBM per device.

v0:
```python
import jax
import jax.numpy as jnp
from jax import lax
from jax.sharding import PartitionSpec as P

ITERS = 2


HIGH = lax.Precision.HIGHEST


def from_behind(value, axis, steps):
    count = lax.axis_size(axis)
    pairs = [(source, (source + steps) % count) for source in range(count)]
    return lax.ppermute(value, axis, pairs)


def local_stiffness(vector, widened, pair_rows):
    width = vector.shape[1]
    first_end = pair_rows[0]
    other_end = pair_rows[1]
    result = jnp.einsum("iab,bi->ai", widened[:width], vector, precision=HIGH)
    to_first = jnp.einsum("pab,bp->ap", widened[width:], vector[:, other_end], precision=HIGH)
    to_other = jnp.einsum("pab,ap->bp", widened[width:], vector[:, first_end], precision=HIGH)
    return result.at[:, first_end].add(to_first).at[:, other_end].add(to_other)


def inverse_order(order):
    count = order.shape[0]
    return jnp.zeros_like(order).at[order].set(jnp.arange(count, dtype=jnp.int32))


def squares(residual):
    return lax.psum(jnp.sum(residual * residual), ("sub", "blk"))


def on_device(
    right_side, stiffness, block_pairs, trace_rows, partner_face, owner_list, mortar_weight
):
    source = right_side[0, 0]
    block_size = source.shape[0]
    stored = stiffness[0, 0]
    widened = stored.reshape(stored.shape[0], block_size, block_size).astype(jnp.float32)
    pair_rows = block_pairs[0, 0]
    face_rows = trace_rows[0, 0]
    partner = partner_face[0, 0]
    owners = owner_list[0, 0]
    weights = mortar_weight[0, 0]
    faces = partner.shape[0]
    groups = owners.shape[0]
    face_dofs = face_rows.shape[1]
    partner_inverse = inverse_order(partner)
    owner_inverse = inverse_order(owners)
    flat_rows = face_rows.reshape(-1)
    solution_field = jnp.zeros_like(source)
    residual = source
    direction = source
    norm_now = squares(residual)
    for iteration in range(ITERS):
        traces = direction.reshape(-1)[face_rows]
        east = traces[:faces]
        west = traces[faces:]
        beyond = from_behind(west, "sub", -1)
        jump = (east - beyond[partner]).reshape(groups, faces // groups, face_dofs)
        outgoing = jump[owner_inverse]
        arrived = lax.all_to_all(outgoing, "blk", split_axis=0, concat_axis=0, tiled=True)
        answered = lax.all_to_all(weights * arrived, "blk", split_axis=0, concat_axis=0, tiled=True)
        scaled = answered[owners]
        scaled = scaled.reshape(faces, face_dofs)
        handed = from_behind(scaled[partner_inverse], "sub", 1)
        values = jnp.concatenate([scaled, -handed], axis=0)
        coupled = (
            jnp.zeros((direction.size,), jnp.float32)
            .at[flat_rows]
            .add(values.reshape(-1))
            .reshape(direction.shape)
        )
        image = local_stiffness(direction, widened, pair_rows) + coupled
        alpha = norm_now / lax.psum(jnp.sum(direction * image), ("sub", "blk"))
        solution_field = solution_field + alpha * direction
        residual = residual - alpha * image
        if iteration + 1 < ITERS:
            norm_next = squares(residual)
            direction = residual + norm_next / norm_now * direction
            norm_now = norm_next
    return (solution_field[None, None], residual[None, None])


def solution(mesh):
    in_specs = (
        P("sub", "blk", None, None),
        P("sub", "blk", None, None),
        P("sub", "blk", None, None),
        P("sub", "blk", None, None),
        P("sub", "blk", None),
        P("sub", "blk", None),
        P("sub", "blk", None, None, None),
    )
    out_specs = (P("sub", "blk", None, None), P("sub", "blk", None, None))
    return jax.shard_map(
        on_device, mesh=mesh, in_specs=in_specs, out_specs=out_specs, check_vma=False
    )
```

profile of v0, /device:TPU:0, one launch (start us, length us, event | category | flops | bytes accessed | tf_op | source)
XLA Modules:
  0.0 547.2 jit_solution(7953476866970553838)
XLA Ops:
  1.7 90.5 %gather_fusion = f32[16384]{0:T(1024)S(1)} fusion(f32[3072]{0:T(1024)S(1)} %reshape_squeeze.8, s32[16384]{0:T(1024)S(1)} %fusion.1), kind=kCustom, calls=%fused_computation | custom fusion | bytes 196608 | tf_op jit(solution)/shard_map/gather | solution.py:60
  92.2 6.1 %collective-permute-start = (f32[64,128]{1,0:T(8,128)S(1)}, f32[64,128]{1,0:T(8,128)S(1)}, u32[]{:S(2)}, u32[]{:S(2)}) collective-permute-start(f32[64,128]{1,0:T(8,128)S(1)} %slice_bitcast_fusion.2), channel_id=1, source_target_pairs={{0,28},{4,0},{8,4},{12,8},{16,12},{20,16},{24,20},{28,24},{1,29},{... | collective-permute-start | bytes 98312 | tf_op jit(solution)/shard_map/ppermute | solution.py:15
  102.5 1.3 fusion.16
  105.7 1.1 gather_fusion.2
  106.9 3.4 all-to-all-start
  110.3 3.9 all-to-all-done
  114.8 3.3 all-to-all-start.1
  118.6 3.3 all-to-all-done.1
  123.6 6.2 %collective-permute-done.1 = f32[64,128]{1,0:T(8,128)S(1)} collective-permute-done((f32[64,128]{1,0:T(8,128)S(1)}, f32[64,128]{1,0:T(8,128)S(1)}, u32[]{:S(2)}, u32[]{:S(2)}) %collective-permute-start.1) | collective-permute-done | bytes 32800 | tf_op jit(solution)/shard_map/ppermute | solution.py:15
  129.8 85.8 %scatter_custom_fusion.2 = f32[3072]{0:T(1024)S(1)} fusion(s32[16384]{0:T(1024)S(1)} %bitcast.136, f32[16384]{0:T(1024)S(1)} %maximum_bitcast_fusion, f32[]{:T(128)} %constant.6.clone.1), kind=kCustom, calls=%fused_computation.46 | custom fusion | flops 16384 | bytes 12292 | tf_op jit(solution)/shard_map/scatter-add | solution.py:75
  217.8 37.1 %all-reduce = (f32[]{:T(128)}, f32[]{:T(128)}) all-reduce(f32[]{:T(128)} %get-tuple-element.3, f32[]{:T(128)} %get-tuple-element.2), channel_id=1, replica_groups=mesh['sub'=8,'blk'=4] {'sub','blk'}, use_global_device_ids=true, to_apply=%region_1.0 | all-reduce | flops 2 | bytes 16 | tf_op jit(solution)/shard_map/psum | solution.py:34
  256.8 41.3 %psum.30 = f32[]{:T(128)} all-reduce(f32[]{:T(128)} %multiply_reduce_fusion.1), channel_id=1, replica_groups=mesh['sub'=8,'blk'=4] {'sub','blk'}, use_global_device_ids=true, to_apply=%region_10.0 | all-reduce | flops 1 | bytes 8 | tf_op jit(solution)/shard_map/psum | solution.py:34
  299.7 90.5 %gather_fusion.7 = f32[16384]{0:T(1024)S(1)} fusion(f32[3072]{0:T(1024)S(1)} %reshape.209, s32[16384]{0:T(1024)S(1)} %fusion.1), kind=kCustom, calls=%fused_computation.7 | custom fusion | bytes 196608 | tf_op jit(solution)/shard_map/gather | solution.py:60
  390.2 3.6 collective-permute-start.2
  393.8 1.6 collective-permute-done.2
  397.2 3.3 all-to-all-start.2
  400.4 1.3 fusion.19
  402.3 2.0 all-to-all-done.2
  405.0 3.3 all-to-all-start.3
  409.2 2.9 all-to-all-done.3
  413.3 2.2 collective-permute-start.3
  416.2 4.1 collective-permute-done.3
  420.3 85.8 %scatter_custom_fusion.5 = f32[3072]{0:T(1024)S(1)} fusion(s32[16384]{0:T(1024)S(1)} %bitcast.137, f32[16384]{0:T(1024)S(1)} %maximum_bitcast_fusion.1, f32[]{:T(128)} %constant.6.clone.1), kind=kCustom, calls=%fused_computation.44 | custom fusion | flops 16384 | bytes 12292 | tf_op jit(solution)/shard_map/scatter-add | solution.py:75
  508.2 37.1 %psum.31 = f32[]{:T(128)} all-reduce(f32[]{:T(128)} %multiply_reduce_fusion), channel_id=1, replica_groups=mesh['sub'=8,'blk'=4] {'sub','blk'}, use_global_device_ids=true, to_apply=%region_15.0 | all-reduce | flops 1 | bytes 8 | tf_op jit(solution)/shard_map/psum | solution.py:79
  (80 shorter events, 21.2 us)
Async XLA Ops:
  0.6 0.9 copy-start
  92.2 12.9 %collective-permute-start = (f32[64,128]{1,0:T(8,128)S(1)}, f32[64,128]{1,0:T(8,128)S(1)}, u32[]{:S(2)}, u32[]{:S(2)}) collective-permute-start(f32[64,128]{1,0:T(8,128)S(1)} %slice_bitcast_fusion.2), channel_id=1, source_target_pairs={{0,28},{4,0},{8,4},{12,8},{16,12},{20,16},{24,20},{28,24},{1,29},{... | collective-permute-start | bytes 98312 | tf_op jit(solution)/shard_map/ppermute | solution.py:15
  98.3 0.7 copy-start.4
  98.3 2.7 copy-start.1
  98.3 2.8 slice-start
  99.0 0.7 copy-start.5
  101.1 0.8 copy-start.3
  101.1 1.0 slice-start.1
  106.9 7.3 %copy-start.2 = (f32[1,1,4,16,128]{4,3,2,1,0:T(8,128)S(1)}, f32[1,1,4,16,128]{4,3,2,1,0:T(8,128)}, u32[]{:S(2)}) copy-start(f32[1,1,4,16,128]{4,3,2,1,0:T(8,128)} %param.13) | copy-start | bytes 98308
  106.9 7.3 %all-to-all-start = ((f32[4,16,128]{2,1,0:T(8,128)}), f32[4,16,128]{2,1,0:T(8,128)S(1)}, u32[]{:S(2)}, u32[]{:S(2)}) async-start(f32[4,16,128]{2,1,0:T(8,128)} %gather_fusion.2), calls=%async_computation | async-start | bytes 65536 | tf_op jit(solution)/shard_map/all_to_all | solution.py:66
  114.8 7.2 %all-to-all-start.1 = ((f32[4,16,128]{2,1,0:T(8,128)}), f32[4,16,128]{2,1,0:T(8,128)S(1)}, u32[]{:S(2)}, u32[]{:S(2)}) async-start(f32[4,16,128]{2,1,0:T(8,128)} %bitcast_multiply_fusion.1), calls=%async_computation.1 | async-start | bytes 65536 | tf_op jit(solution)/shard_map/all_to_all | solution.py:67
  123.1 6.7 %collective-permute-start.1 = (f32[64,128]{1,0:T(8,128)S(1)}, f32[64,128]{1,0:T(8,128)S(1)}, u32[]{:S(2)}, u32[]{:S(2)}) collective-permute-start(f32[64,128]{1,0:T(8,128)S(1)} %gather_fusion.4), channel_id=1, source_target_pairs={{0,4},{4,8},{8,12},{12,16},{16,20},{20,24},{24,28},{28,0},{1,5},{5... | collective-permute-start | bytes 98312 | tf_op jit(solution)/shard_map/ppermute | solution.py:15
  390.2 5.2 collective-permute-start.2
  397.2 7.2 %all-to-all-start.2 = ((f32[4,16,128]{2,1,0:T(8,128)}), f32[4,16,128]{2,1,0:T(8,128)S(1)}, u32[]{:S(2)}, u32[]{:S(2)}) async-start(f32[4,16,128]{2,1,0:T(8,128)} %gather_fusion.9), calls=%async_computation.2 | async-start | bytes 65536 | tf_op jit(solution)/shard_map/all_to_all | solution.py:66
  405.0 7.2 %all-to-all-start.3 = ((f32[4,16,128]{2,1,0:T(8,128)}), f32[4,16,128]{2,1,0:T(8,128)S(1)}, u32[]{:S(2)}, u32[]{:S(2)}) async-start(f32[4,16,128]{2,1,0:T(8,128)} %bitcast_multiply_fusion), calls=%async_computation.3 | async-start | bytes 65536 | tf_op jit(solution)/shard_map/all_to_all | solution.py:67
  413.3 7.0 %collective-permute-start.3 = (f32[64,128]{1,0:T(8,128)S(1)}, f32[64,128]{1,0:T(8,128)S(1)}, u32[]{:S(2)}, u32[]{:S(2)}) collective-permute-start(f32[64,128]{1,0:T(8,128)S(1)} %gather_fusion.11), channel_id=1, source_target_pairs={{0,4},{4,8},{8,12},{12,16},{16,20},{20,24},{24,28},{28,0},{1,5},{5... | collective-permute-start | bytes 98312 | tf_op jit(solution)/shard_map/ppermute | solution.py:15
where the time goes:
time: 549 us; the launch traced here: 547 us
  local copies, waits for them, and re-layouts  194 us (35%)
  other arithmetic  179 us (33%)
  blocking collectives  115 us (21%)
  starting transfers between devices  25.1 us (5%)
  waiting for transfers between devices  24 us (4%)
    gather x2, local copies, waits for them, and re-layouts, on_device(): traces = direction.reshape(-1)[face_rows]  181 us
    scatter-add x2, other arithmetic, on_device(): coupled = jnp.zeros((direction.size,), jnp.float32).at[flat_rows].add(val...  172 us
    psum x2, blocking collectives, squares(): return lax.psum(jnp.sum(residual * residual), ('sub', 'blk'))  78.4 us
    psum x1, blocking collectives, on_device(): alpha = norm_now / lax.psum(jnp.sum(direction * image), ('sub', 'blk'))  37.1 us
    ppermute x4, starting transfers between devices, from_behind(): return lax.ppermute(value, axis, pairs)  11.9 us
    ppermute x4, waiting for transfers between devices, from_behind(): return lax.ppermute(value, axis, pairs)  11.9 us
  transfers between devices with their start and end apart: 8, of which 7 were waited for; matrix products, arithmetic and copies ran while one was open for 2% of the time, Pallas kernels for 0%

commit v1 on v0

v1 whole, which is shorter than its diff:
```python
import functools

import jax
import jax.numpy as jnp
from jax import lax
from jax.experimental import pallas as pl
from jax.experimental.pallas import tpu as pltpu
from jax.sharding import PartitionSpec as P

LANES = 128
SUBLANES = 8
VMEM = pl.BlockSpec(memory_space=pltpu.VMEM)
SMEM = pl.BlockSpec(memory_space=pltpu.SMEM)
PARAMS = pltpu.CompilerParams(vmem_limit_bytes=32 * 1024 * 1024)
F32 = jnp.float32
BF16 = jnp.bfloat16


def call(body, outs, inputs, scratch=(), flops=1_000_000):
    return pl.pallas_call(
        body,
        out_shape=outs,
        in_specs=[spec for _, spec in inputs],
        out_specs=[VMEM] * len(outs),
        scratch_shapes=list(scratch),
        compiler_params=PARAMS,
        cost_estimate=pl.CostEstimate(
            flops=flops, bytes_accessed=1_000_000, transcendentals=0
        ),
    )(*[value for value, _ in inputs])


def shape(rows, dtype=F32):
    return jax.ShapeDtypeStruct((rows, LANES), dtype)


def halves(value):
    high = value.astype(BF16).astype(F32)
    return high, value - high


def gather_traces(field, rows_ref, east_ref, west_ref):
    block_rows = field.shape[0]
    faces = east_ref.shape[0]
    spread = [
        jnp.broadcast_to(field[i : i + 1, :], (SUBLANES, LANES)) for i in range(block_rows)
    ]

    def step(target, base, k):
        index = rows_ref[pl.ds(pl.multiple_of(base + k * SUBLANES, SUBLANES), SUBLANES), :]
        dof = index // block_rows
        row = index % block_rows
        taken = jnp.zeros((SUBLANES, LANES), F32)
        for i in range(block_rows):
            here = jnp.take_along_axis(spread[i], dof, axis=1, mode="promise_in_bounds")
            taken = jnp.where(row == i, here, taken)
        target[pl.ds(pl.multiple_of(k * SUBLANES, SUBLANES), SUBLANES), :] = taken

    for target, base in ((east_ref, 0), (west_ref, faces)):

        def body(k, _, target=target, base=base):
            step(target, base, k)
            return 0

        lax.fori_loop(0, faces // SUBLANES, body, 0)


def first_kernel(partner_ref, field_ref, rows_ref, aligned_ref, padded_ref, east_ref, west_ref):
    faces = east_ref.shape[0]
    size = field_ref.shape[1]
    aligned_ref[faces:, :] = rows_ref[faces:, :]

    def move(f, _):
        aligned_ref[pl.ds(partner_ref[f], 1), :] = rows_ref[pl.ds(f, 1), :]
        return 0

    lax.fori_loop(0, faces, move, 0, unroll=8)
    padded_ref[...] = jnp.zeros_like(padded_ref)
    padded_ref[:, :size] = field_ref[...]
    gather_traces(padded_ref[...], aligned_ref, east_ref, west_ref)


def weight_kernel(partner_ref, owner_ref, arrived_ref, out_ref):
    groups, per_group, _ = arrived_ref.shape
    for g in range(groups):
        owner = owner_ref[g]
        for k in range(per_group):
            out_ref[pl.ds(partner_ref[g * per_group + k], 1), :] = arrived_ref[
                owner, pl.ds(k, 1), :
            ]


def stiffness_kernel(pairs_ref, blocks_ref, field_ref, out_ref, pieces, sums):
    block_rows = field_ref.shape[0]
    size = blocks_ref.shape[1]
    count = pairs_ref.shape[1]
    high, low = halves(field_ref[...])
    pieces[...] = jnp.zeros_like(pieces)
    pieces[pl.ds(0, block_rows, stride=SUBLANES), :] = high
    pieces[pl.ds(1, block_rows, stride=SUBLANES), :] = low

    def times(row, block, contract):
        left = pieces[pl.ds(pl.multiple_of(row * SUBLANES, SUBLANES), SUBLANES), :]
        return lax.dot_general(
            left[:, :size].astype(BF16),
            block,
            (((1,), (contract,)), ((), ())),
            preferred_element_type=F32,
        )

    def add(row, value):
        place = pl.ds(pl.multiple_of(row * SUBLANES, SUBLANES), SUBLANES)
        sums[place, :size] = sums[place, :size] + value

    sums[...] = jnp.zeros_like(sums)
    for i in range(block_rows):
        sums[i * SUBLANES : (i + 1) * SUBLANES, :size] = times(i, blocks_ref[i], 1)
    for p in range(count):
        first = pairs_ref[0, p]
        other = pairs_ref[1, p]
        block = blocks_ref[block_rows + p]
        add(first, times(other, block, 1))
        add(other, times(first, block, 0))
    out_ref[...] = (
        sums[pl.ds(0, block_rows, stride=SUBLANES), :]
        + sums[pl.ds(1, block_rows, stride=SUBLANES), :]
    )


def spread_jumps(block_rows, size, aligned_ref, weights, own, arrived):
    faces = own[0].shape[0]
    dof_of = lax.broadcasted_iota(jnp.int32, (size, LANES), 0)
    row_of = lax.broadcasted_iota(jnp.int32, (block_rows, LANES), 0)

    def step(k, total, side):
        place = pl.ds(pl.multiple_of(k * SUBLANES, SUBLANES), SUBLANES)
        lam = weights[side][place, :] * (own[side][place, :] - arrived[side][place, :])
        high, low = halves(lam)
        index = aligned_ref[pl.ds(pl.multiple_of(side * faces + k * SUBLANES, SUBLANES), SUBLANES), :]
        dof = index // block_rows
        row = index % block_rows
        left = []
        right = []
        for f in range(SUBLANES):
            here = row_of == row[f : f + 1, :]
            left.append(
                jnp.concatenate(
                    [
                        jnp.where(here, high[f : f + 1, :], 0.0),
                        jnp.where(here, low[f : f + 1, :], 0.0),
                    ],
                    axis=0,
                ).astype(BF16)
            )
            right.append(jnp.where(dof_of == dof[f : f + 1, :], 1.0, 0.0).astype(BF16))
        return total + lax.dot_general(
            jnp.concatenate(left, axis=1),
            jnp.concatenate(right, axis=1),
            (((1,), (1,)), ((), ())),
            preferred_element_type=F32,
        )

    total = jnp.zeros((2 * block_rows, size), F32)
    for side in (0, 1):
        total = lax.fori_loop(
            0, faces // SUBLANES, functools.partial(step, side=side), total
        )
    return total[:block_rows] + total[block_rows:]


def middle_kernel(
    size,
    aligned_ref,
    product_ref,
    weight_east_ref,
    weight_west_ref,
    east_ref,
    west_ref,
    from_next_ref,
    from_last_ref,
    image_ref,
    next_east_ref,
    next_west_ref,
):
    block_rows = product_ref.shape[0]
    coupled = spread_jumps(
        block_rows,
        size,
        aligned_ref,
        (weight_east_ref, weight_west_ref),
        (east_ref, west_ref),
        (from_next_ref, from_last_ref),
    )
    image_ref[...] = product_ref[...]
    image_ref[:, :size] = image_ref[:, :size] + coupled
    gather_traces(image_ref[...], aligned_ref, next_east_ref, next_west_ref)


def total_of(value):
    return jnp.sum(jnp.sum(value, axis=0, keepdims=True), axis=1, keepdims=True)


def last_kernel(
    size,
    aligned_ref,
    product_ref,
    weight_east_ref,
    weight_west_ref,
    east_ref,
    west_ref,
    from_next_ref,
    from_last_ref,
    field_ref,
    image_ref,
    second_ref,
    sums_ref,
):
    block_rows = product_ref.shape[0]
    coupled = spread_jumps(
        block_rows,
        size,
        aligned_ref,
        (weight_east_ref, weight_west_ref),
        (east_ref, west_ref),
        (from_next_ref, from_last_ref),
    )
    second_ref[...] = product_ref[...]
    second_ref[:, :size] = second_ref[:, :size] + coupled
    field = field_ref[...]
    image = image_ref[...]
    second = second_ref[...]
    lane = lax.broadcasted_iota(jnp.int32, (1, LANES), 1)
    row = jnp.zeros((1, LANES), F32)
    for k, product in enumerate(
        (field * field, field * image, image * image, field * second, image * second)
    ):
        row = jnp.where(lane == k, total_of(product), row)
    sums_ref[...] = jnp.broadcast_to(row[None], sums_ref.shape)


def final_kernel(field_ref, image_ref, second_ref, sums_ref, solution_ref, residual_ref):
    size = solution_ref.shape[1]
    row = jnp.sum(sums_ref[...], axis=0)
    lane = lax.broadcasted_iota(jnp.int32, (1, LANES), 1)

    def entry(k):
        return jnp.sum(jnp.where(lane == k, row, 0.0), axis=1, keepdims=True)

    bb, bq, qq, bw, qw = (entry(k) for k in range(5))
    field = field_ref[:, :size]
    image = image_ref[:, :size]
    second = second_ref[:, :size]
    alpha = bb / bq
    norm = bb - alpha * (2.0 * bq - alpha * qq)
    beta = norm / bb
    grown = 1.0 + beta
    energy = grown * (grown * bq - alpha * (bw + qq)) + alpha * alpha * qw
    alpha_next = norm / energy
    residual = field - alpha * image
    direction = residual + beta * field
    moved = (image - alpha * second) + beta * image
    solution_ref[...] = alpha * field + alpha_next * direction
    residual_ref[...] = residual - alpha_next * moved


def from_behind(value, axis, steps):
    count = lax.axis_size(axis)
    pairs = [(source, (source + steps) % count) for source in range(count)]
    return lax.ppermute(value, axis, pairs)


def on_device(
    right_side, stiffness, block_pairs, trace_rows, partner_face, owner_list, mortar_weight
):
    field = right_side[0, 0].T
    block_rows, size = field.shape
    stored = stiffness[0, 0]
    blocks = stored.reshape(stored.shape[0], size, size)
    pairs = block_pairs[0, 0]
    rows = trace_rows[0, 0]
    partner = partner_face[0, 0]
    owners = owner_list[0, 0]
    faces = partner.shape[0]
    groups = owners.shape[0]
    devices = lax.axis_size("sub") * lax.axis_size("blk")

    held = lax.all_to_all(mortar_weight[0, 0], "blk", split_axis=0, concat_axis=0, tiled=True)
    aligned, padded, east, west = call(
        first_kernel,
        [shape(2 * faces, jnp.int32), shape(block_rows), shape(faces), shape(faces)],
        [(partner, SMEM), (field, VMEM), (rows, VMEM)],
    )
    from_last = from_behind(east, "sub", 1)
    from_next = from_behind(west, "sub", -1)
    (weight_east,) = call(
        weight_kernel,
        [shape(faces)],
        [(partner, SMEM), (owners, SMEM), (held, VMEM)],
    )
    weight_west = from_behind(weight_east, "sub", 1)

    def stiff(vector):
        (product,) = call(
            stiffness_kernel,
            [shape(block_rows)],
            [(pairs, SMEM), (blocks, VMEM), (vector, VMEM)],
            scratch=[pltpu.VMEM((block_rows * SUBLANES, LANES), F32)] * 2,
        )
        return product

    product = stiff(padded)
    image, next_east, next_west = call(
        functools.partial(middle_kernel, size),
        [shape(block_rows), shape(faces), shape(faces)],
        [
            (value, VMEM)
            for value in (
                aligned, product, weight_east, weight_west, east, west, from_next, from_last
            )
        ],
    )
    second_last = from_behind(next_east, "sub", 1)
    second_next = from_behind(next_west, "sub", -1)
    product = stiff(image)
    second, sums = call(
        functools.partial(last_kernel, size),
        [shape(block_rows), jax.ShapeDtypeStruct((devices, 1, LANES), F32)],
        [
            (value, VMEM)
            for value in (
                aligned,
                product,
                weight_east,
                weight_west,
                next_east,
                next_west,
                second_next,
                second_last,
                padded,
                image,
            )
        ],
    )
    sums = lax.all_to_all(sums, ("sub", "blk"), split_axis=0, concat_axis=0, tiled=True)
    solution_field, residual = call(
        final_kernel,
        [jax.ShapeDtypeStruct((block_rows, size), F32)] * 2,
        [(padded, VMEM), (image, VMEM), (second, VMEM), (sums, VMEM)],
    )
    return (solution_field.T[None, None], residual.T[None, None])


def solution(mesh):
    in_specs = (
        P("sub", "blk", None, None),
        P("sub", "blk", None, None),
        P("sub", "blk", None, None),
        P("sub", "blk", None, None),
        P("sub", "blk", None),
        P("sub", "blk", None),
        P("sub", "blk", None, None, None),
    )
    out_specs = (P("sub", "blk", None, None), P("sub", "blk", None, None))
    return jax.shard_map(
        on_device, mesh=mesh, in_specs=in_specs, out_specs=out_specs, check_vma=False
    )
```

time: 549 us -> 53 us (0.10)
  local copies, waits for them, and re-layouts: 194 us -> 5.82 us
  other arithmetic: 179 us -> 0 us
  blocking collectives: 115 us -> 13.5 us
  waiting for transfers between devices: 24 us -> 3.33 us
  Pallas kernels: 0 us -> 15 us
  starting transfers between devices: 25.1 us -> 14.2 us
    gather x14 -> x0, local copies, waits for them, and re-layouts: 189 us -> none  [the longest x2 181 us: on_device(): traces = direction.reshape(-1)[face_rows]]
    scatter-add x6 -> x0, other arithmetic: 174 us -> none  [the longest x2 172 us: on_device(): coupled = jnp.zeros((direction.size,), jnp.float32).at[flat_rows].add(val...]
    psum x3 -> x0, blocking collectives: 115 us -> none  [the longest x2 78.4 us: squares(): return lax.psum(jnp.sum(residual * residual), ('sub', 'blk'))]
    pallas_call x0 -> x7, Pallas kernels: none -> 15 us  [call(): pl.pallas_call(body, out_shape=outs, in_specs=[spec for _, spec in inputs...]
    all_to_all x0 -> x1, blocking collectives: none -> 13.5 us  [on_device(): lax.all_to_all(sums, ('sub', 'blk'), split_axis=0, concat_axis=0, tiled=T...]
    all_to_all x4 -> x1, waiting for transfers between devices: 12.2 us -> 0.01 us  [on_device(): lax.all_to_all(mortar_weight[0, 0], 'blk', split_axis=0, concat_axis=0, t...]
    all_to_all x4 -> x1, starting transfers between devices: 13.2 us -> 4.22 us  [on_device(): lax.all_to_all(mortar_weight[0, 0], 'blk', split_axis=0, concat_axis=0, t...]
    ppermute x4 -> x5, waiting for transfers between devices: 11.9 us -> 3.33 us  [from_behind(): return lax.ppermute(value, axis, pairs)]
  transfers between devices with their start and end apart: 8 -> 6, of which waited for: 7 -> 2; matrix products, arithmetic and copies ran while one was open for 2% -> 4% of each run, Pallas kernels for 0% -> 11%
where the time goes in v1:
time: 53 us; the launch traced here: 52.6 us
  Pallas kernels  15 us (28%)
  starting transfers between devices  14.2 us (27%)
  blocking collectives  13.5 us (25%)
  local copies, waits for them, and re-layouts  5.82 us (11%)
  waiting for transfers between devices  3.33 us (6%)
  between operations  0.74 us (1%)
    pallas_call x7, Pallas kernels, call(): pl.pallas_call(body, out_shape=outs, in_specs=[spec for _, spec in inputs...  15 us
    all_to_all x1, blocking collectives, on_device(): lax.all_to_all(sums, ('sub', 'blk'), split_axis=0, concat_axis=0, tiled=T...  13.5 us
    ppermute x5, starting transfers between devices, from_behind(): return lax.ppermute(value, axis, pairs)  10 us
    all_to_all x1, starting transfers between devices, on_device(): lax.all_to_all(mortar_weight[0, 0], 'blk', split_axis=0, concat_axis=0, t...  4.22 us
    unnamed x12, local copies, waits for them, and re-layouts  3.53 us
    ppermute x5, waiting for transfers between devices, from_behind(): return lax.ppermute(value, axis, pairs)  3.33 us
    another operation x1, local copies, waits for them, and re-layouts, on_device(): blocks = stored.reshape(stored.shape[0], size, size)  2.3 us
  transfers between devices with their start and end apart: 6, of which 2 were waited for; matrix products, arithmetic and copies ran while one was open for 4% of the time, Pallas kernels for 11%

profile of v1, /device:TPU:0, one launch (start us, length us, event | category | flops | bytes accessed | tf_op | source)
XLA Modules:
  0.0 52.6 jit_solution(3878385502746641637)
XLA Ops:
  0.6 4.2 %all-to-all-start = ((f32[4,16,128]{2,1,0:T(8,128)}), f32[4,16,128]{2,1,0:T(8,128)S(1)}, u32[]{:S(2)}, u32[]{:S(2)}) async-start(f32[4,16,128]{2,1,0:T(8,128)} %bitcast.23), calls=%async_computation | async-start | bytes 65536 | tf_op jit(solution)/shard_map/all_to_all | solution.py:287
  4.9 0.8 %copy-done = s32[1,1,128,128]{3,2,1,0:T(8,128)S(1)} copy-done((s32[1,1,128,128]{3,2,1,0:T(8,128)S(1)}, s32[1,1,128,128]{3,2,1,0:T(8,128)}, u32[]{:S(2)}) %copy-start) | copy-done | bytes 65560
  5.7 0.7 %copy-done.1 = f32[1,1,96,32]{2,3,1,0:T(8,128)S(1)} copy-done((f32[1,1,96,32]{2,3,1,0:T(8,128)S(1)}, f32[1,1,96,32]{2,3,1,0:T(8,128)}, u32[]{:S(2)}) %copy-start.1) | copy-done | bytes 12312
  6.4 0.7 %copy-done.3 = s32[1,1,64]{2,1,0:T(1,128)S(1)} copy-done((s32[1,1,64]{2,1,0:T(1,128)S(1)}, s32[1,1,64]{2,1,0:T(1,128)}, u32[]{:S(2)}) %copy-start.3) | copy-done | bytes 280
  7.1 2.4 %shard_map.86 = (s32[128,128]{1,0:T(8,128)S(1)}, f32[32,128]{1,0:T(8,128)S(1)}, f32[64,128]{1,0:T(8,128)S(1)}, f32[64,128]{1,0:T(8,128)S(1)}) custom-call(s32[64]{0:T(128)S(1)} %bitcast.20, f32[32,96]{1,0:T(8,128)S(1)} %bitcast.17, s32[128,128]{1,0:T(8,128)S(1)} %bitcast.16), custom_call_target="tpu_custom_call" | custom-call | flops 1000000 | bytes 1000000 | tf_op jit(solution)/shard_map/pallas_call | solution.py:20
  9.5 2.1 %collective-permute-start.2 = (f32[64,128]{1,0:T(8,128)S(1)}, f32[64,128]{1,0:T(8,128)S(1)}, u32[]{:S(2)}, u32[]{:S(2)}) collective-permute-start(f32[64,128]{1,0:T(8,128)S(1)} %get-tuple-element.15.east_ref), channel_id=1, source_target_pairs={{0,4},{4,8},{8,12},{12,16},{16,20},{20,24},{24,28},{28,0},{1,5},{5... | collective-permute-start | bytes 98312 | tf_op jit(solution)/shard_map/ppermute | solution.py:269
  11.6 3.1 %collective-permute-start.1 = (f32[64,128]{1,0:T(8,128)S(1)}, f32[64,128]{1,0:T(8,128)S(1)}, u32[]{:S(2)}, u32[]{:S(2)}) collective-permute-start(f32[64,128]{1,0:T(8,128)S(1)} %get-tuple-element.16.west_ref), channel_id=1, source_target_pairs={{0,28},{4,0},{8,4},{12,8},{16,12},{20,16},{24,20},{28,24},{1,29},{... | collective-permute-start | bytes 98312 | tf_op jit(solution)/shard_map/ppermute | solution.py:269
  14.7 0.0 all-to-all-done.arrived_ref
  14.7 0.7 %copy-done.4 = s32[1,1,64]{2,1,0:T(1,128)S(1)} copy-done((s32[1,1,64]{2,1,0:T(1,128)S(1)}, s32[1,1,64]{2,1,0:T(1,128)}, u32[]{:S(2)}) %copy-start.4) | copy-done | bytes 280
  15.3 0.7 %copy-done.5 = s32[1,1,4]{2,1,0:T(1,128)S(1)} copy-done((s32[1,1,4]{2,1,0:T(1,128)S(1)}, s32[1,1,4]{2,1,0:T(1,128)}, u32[]{:S(2)}) %copy-start.5) | copy-done | bytes 40
  16.0 0.6 %shard_map.88.weight_east_ref = f32[64,128]{1,0:T(8,128)S(1)} custom-call(s32[64]{0:T(128)S(1)} %bitcast.21, s32[4]{0:T(128)S(1)} %bitcast.22, f32[4,16,128]{2,1,0:T(8,128)S(1)} %all-to-all-done.arrived_ref), custom_call_target="tpu_custom_call" | custom-call | flops 1000000 | bytes 1000000 | tf_op jit(solution)/shard_map/pallas_call | solution.py:20
  16.6 0.1 collective-permute-start
  16.7 2.3 %reshape_squeeze.3.blocks_ref = bf16[48,96,96]{2,1,0:T(8,128)(2,1)S(1)} reshape(bf16[1,1,48,9216]{3,2,1,0:T(8,128)(2,1)} %param.8) | data formatting | bytes 1769472 | tf_op jit(solution)/shard_map/reshape;squeeze | solution.py:278
  19.0 1.4 %shard_map.87.product_ref = f32[32,128]{1,0:T(8,128)S(1)} custom-call(s32[2,16]{1,0:T(2,128)S(1)} %bitcast.18, bf16[48,96,96]{2,1,0:T(8,128)(2,1)S(1)} %reshape_squeeze.3.blocks_ref, f32[32,128]{1,0:T(8,128)S(1)} %get-tuple-element.13.field_ref), custom_call_target="tpu_custom_call" | custom-call | flops 1000000 | bytes 1000000 | tf_op jit(solution)/shard_map/pallas_call | solution.py:20
  20.4 0.0 collective-permute-done.2.from_last_ref
  20.4 2.8 %collective-permute-done.weight_west_ref = f32[64,128]{1,0:T(8,128)S(1)} collective-permute-done((f32[64,128]{1,0:T(8,128)S(1)}, f32[64,128]{1,0:T(8,128)S(1)}, u32[]{:S(2)}, u32[]{:S(2)}) %collective-permute-start) | collective-permute-done | bytes 32800 | tf_op jit(solution)/shard_map/ppermute | solution.py:269
  23.3 5.1 %shard_map.89 = (f32[32,128]{1,0:T(8,128)S(1)}, f32[64,128]{1,0:T(8,128)S(1)}, f32[64,128]{1,0:T(8,128)S(1)}) custom-call(s32[128,128]{1,0:T(8,128)S(1)} %get-tuple-element.14.aligned_ref, f32[32,128]{1,0:T(8,128)S(1)} %shard_map.87.product_ref, f32[64,128]{1,0:T(8,128)S(1)} %shard_map.88.weight_east_ref, ...), custom_call_target="tpu_custom_call" | custom-call | flops 1000000 | bytes 1000000 | tf_op jit(solution)/shard_map/pallas_call | solution.py:20
  28.3 0.1 collective-permute-start.4
  28.4 4.7 %collective-permute-start.3 = (f32[64,128]{1,0:T(8,128)S(1)}, f32[64,128]{1,0:T(8,128)S(1)}, u32[]{:S(2)}, u32[]{:S(2)}) collective-permute-start(f32[64,128]{1,0:T(8,128)S(1)} %get-tuple-element.19.west_ref), channel_id=1, source_target_pairs={{0,28},{4,0},{8,4},{12,8},{16,12},{20,16},{24,20},{28,24},{1,29},{... | collective-permute-start | bytes 98312 | tf_op jit(solution)/shard_map/ppermute | solution.py:269
  33.1 1.4 %shard_map.90.product_ref = f32[32,128]{1,0:T(8,128)S(1)} custom-call(s32[2,16]{1,0:T(2,128)S(1)} %bitcast.19, bf16[48,96,96]{2,1,0:T(8,128)(2,1)S(1)} %reshape_squeeze.3.blocks_ref, f32[32,128]{1,0:T(8,128)S(1)} %get-tuple-element.17.field_ref.image_ref), custom_call_target="tpu_custom_call" | custom-call | flops 1000000 | bytes 1000000 | tf_op jit(solution)/shard_map/pallas_call | solution.py:20
  34.5 0.5 collective-permute-done.4.from_last_ref
  35.0 3.4 %shard_map.91 = (f32[32,128]{1,0:T(8,128)S(1)}, f32[32,1,128]{2,1,0:T(1,128)S(1)}) custom-call(s32[128,128]{1,0:T(8,128)S(1)} %get-tuple-element.14.aligned_ref, f32[32,128]{1,0:T(8,128)S(1)} %shard_map.90.product_ref, f32[64,128]{1,0:T(8,128)S(1)} %shard_map.88.weight_east_ref, f32[64,128]{1,0:T(8,128)S(1)} %collective-permute-done.weight_west_ref, ...), custom_call_target="tpu_custom_call" | custom-call | flops 1000000 | bytes 1000000 | tf_op jit(solution)/shard_map/pallas_call | solution.py:20
  38.4 13.5 %all_to_all.10.sums_ref = f32[32,1,128]{2,1,0:T(1,128)S(1)} all-to-all(f32[32,1,128]{2,1,0:T(1,128)S(1)} %get-tuple-element.21), channel_id=1, replica_groups=mesh['sub'=8,'blk'=4] {'sub','blk'}, dimensions={0} | all-to-all | bytes 32768 | tf_op jit(solution)/shard_map/all_to_all | solution.py:344
  51.9 0.7 %shard_map.92 = (f32[32,96]{1,0:T(8,128)}, f32[32,96]{1,0:T(8,128)}) custom-call(f32[32,128]{1,0:T(8,128)S(1)} %get-tuple-element.13.field_ref, f32[32,128]{1,0:T(8,128)S(1)} %get-tuple-element.17.field_ref.image_ref, f32[32,128]{1,0:T(8,128)S(1)} %get-tuple-element.20.second_ref, f32[32,1,128]{2,1,0:T(1,128)S(1)} %all_to_all.10.sums_ref), custom_call_target="tpu_custom_call" | custom-call | flops 1000000 | bytes 1000000 | tf_op jit(solution)/shard_map/pallas_call | solution.py:20
  (9 shorter events, 0.0 us)
Async XLA Ops:
  0.6 18.3 %copy-start.2 = (s32[1,1,2,16]{3,2,1,0:T(2,128)S(1)}, s32[1,1,2,16]{3,2,1,0:T(2,128)}, u32[]{:S(2)}) copy-start(s32[1,1,2,16]{3,2,1,0:T(2,128)} %param.9) | copy-start | bytes 388
  0.6 14.0 %all-to-all-start = ((f32[4,16,128]{2,1,0:T(8,128)}), f32[4,16,128]{2,1,0:T(8,128)S(1)}, u32[]{:S(2)}, u32[]{:S(2)}) async-start(f32[4,16,128]{2,1,0:T(8,128)} %bitcast.23), calls=%async_computation | async-start | bytes 65536 | tf_op jit(solution)/shard_map/all_to_all | solution.py:287
  4.9 0.8 %copy-start = (s32[1,1,128,128]{3,2,1,0:T(8,128)S(1)}, s32[1,1,128,128]{3,2,1,0:T(8,128)}, u32[]{:S(2)}) copy-start(s32[1,1,128,128]{3,2,1,0:T(8,128)} %param.10) | copy-start | bytes 196612
  5.7 0.7 %copy-start.1 = (f32[1,1,96,32]{2,3,1,0:T(8,128)S(1)}, f32[1,1,96,32]{2,3,1,0:T(8,128)}, u32[]{:S(2)}) copy-start(f32[1,1,96,32]{2,3,1,0:T(8,128)} %param.7) | copy-start | bytes 36868
  6.4 0.7 %copy-start.3 = (s32[1,1,64]{2,1,0:T(1,128)S(1)}, s32[1,1,64]{2,1,0:T(1,128)}, u32[]{:S(2)}) copy-start(s32[1,1,64]{2,1,0:T(1,128)} %param.11) | copy-start | bytes 772
  9.5 10.9 %collective-permute-start.2 = (f32[64,128]{1,0:T(8,128)S(1)}, f32[64,128]{1,0:T(8,128)S(1)}, u32[]{:S(2)}, u32[]{:S(2)}) collective-permute-start(f32[64,128]{1,0:T(8,128)S(1)} %get-tuple-element.15.east_ref), channel_id=1, source_target_pairs={{0,4},{4,8},{8,12},{12,16},{16,20},{20,24},{24,28},{28,0},{1,5},{5... | collective-permute-start | bytes 98312 | tf_op jit(solution)/shard_map/ppermute | solution.py:269
  11.6 8.8 %collective-permute-start.1 = (f32[64,128]{1,0:T(8,128)S(1)}, f32[64,128]{1,0:T(8,128)S(1)}, u32[]{:S(2)}, u32[]{:S(2)}) collective-permute-start(f32[64,128]{1,0:T(8,128)S(1)} %get-tuple-element.16.west_ref), channel_id=1, source_target_pairs={{0,28},{4,0},{8,4},{12,8},{16,12},{20,16},{24,20},{28,24},{1,29},{... | collective-permute-start | bytes 98312 | tf_op jit(solution)/shard_map/ppermute | solution.py:269
  14.7 0.7 %copy-start.4 = (s32[1,1,64]{2,1,0:T(1,128)S(1)}, s32[1,1,64]{2,1,0:T(1,128)}, u32[]{:S(2)}) copy-start(s32[1,1,64]{2,1,0:T(1,128)} %param.11) | copy-start | bytes 772
  15.3 0.7 %copy-start.5 = (s32[1,1,4]{2,1,0:T(1,128)S(1)}, s32[1,1,4]{2,1,0:T(1,128)}, u32[]{:S(2)}) copy-start(s32[1,1,4]{2,1,0:T(1,128)} %param.12) | copy-start | bytes 52
  16.6 6.7 %collective-permute-start = (f32[64,128]{1,0:T(8,128)S(1)}, f32[64,128]{1,0:T(8,128)S(1)}, u32[]{:S(2)}, u32[]{:S(2)}) collective-permute-start(f32[64,128]{1,0:T(8,128)S(1)} %shard_map.88.weight_east_ref), channel_id=1, source_target_pairs={{0,4},{4,8},{8,12},{12,16},{16,20},{20,24},{24,28},{28,0},{1,5},{5... | collective-permute-start | bytes 98312 | tf_op jit(solution)/shard_map/ppermute | solution.py:269
  28.3 6.7 %collective-permute-start.4 = (f32[64,128]{1,0:T(8,128)S(1)}, f32[64,128]{1,0:T(8,128)S(1)}, u32[]{:S(2)}, u32[]{:S(2)}) collective-permute-start(f32[64,128]{1,0:T(8,128)S(1)} %get-tuple-element.18.east_ref), channel_id=1, source_target_pairs={{0,4},{4,8},{8,12},{12,16},{16,20},{20,24},{24,28},{28,0},{1,5},{5... | collective-permute-start | bytes 98312 | tf_op jit(solution)/shard_map/ppermute | solution.py:269
  28.4 6.6 %collective-permute-start.3 = (f32[64,128]{1,0:T(8,128)S(1)}, f32[64,128]{1,0:T(8,128)S(1)}, u32[]{:S(2)}, u32[]{:S(2)}) collective-permute-start(f32[64,128]{1,0:T(8,128)S(1)} %get-tuple-element.19.west_ref), channel_id=1, source_target_pairs={{0,28},{4,0},{8,4},{12,8},{16,12},{20,16},{24,20},{28,24},{1,29},{... | collective-permute-start | bytes 98312 | tf_op jit(solution)/shard_map/ppermute | solution.py:269

commit v2 on v1

--- a/solution.py
+++ b/solution.py
@@ -62,7 +62,7 @@
             step(target, base, k)
             return 0
 
-        lax.fori_loop(0, faces // SUBLANES, body, 0)
+        lax.fori_loop(0, faces // SUBLANES, body, 0, unroll=4)
 
 
 def first_kernel(partner_ref, field_ref, rows_ref, aligned_ref, padded_ref, east_ref, west_ref):
@@ -80,13 +80,14 @@
     gather_traces(padded_ref[...], aligned_ref, east_ref, west_ref)
 
 
-def weight_kernel(partner_ref, owner_ref, arrived_ref, out_ref):
-    groups, per_group, _ = arrived_ref.shape
+def weight_kernel(partner_ref, owner_ref, place_ref, arrived_ref, out_ref):
+    _, groups, per_group, _ = arrived_ref.shape
+    place = place_ref[0]
     for g in range(groups):
         owner = owner_ref[g]
         for k in range(per_group):
             out_ref[pl.ds(partner_ref[g * per_group + k], 1), :] = arrived_ref[
-                owner, pl.ds(k, 1), :
+                owner, place, pl.ds(k, 1), :
             ]
 
 
@@ -163,7 +164,7 @@
     total = jnp.zeros((2 * block_rows, size), F32)
     for side in (0, 1):
         total = lax.fori_loop(
-            0, faces // SUBLANES, functools.partial(step, side=side), total
+            0, faces // SUBLANES, functools.partial(step, side=side), total, unroll=2
         )
     return total[:block_rows] + total[block_rows:]
 
@@ -235,7 +236,7 @@
         (field * field, field * image, image * image, field * second, image * second)
     ):
         row = jnp.where(lane == k, total_of(product), row)
-    sums_ref[...] = jnp.broadcast_to(row[None], sums_ref.shape)
+    sums_ref[...] = row
 
 
 def final_kernel(field_ref, image_ref, second_ref, sums_ref, solution_ref, residual_ref):
@@ -282,9 +283,9 @@
     owners = owner_list[0, 0]
     faces = partner.shape[0]
     groups = owners.shape[0]
-    devices = lax.axis_size("sub") * lax.axis_size("blk")
-
-    held = lax.all_to_all(mortar_weight[0, 0], "blk", split_axis=0, concat_axis=0, tiled=True)
+
+    held = lax.all_gather(mortar_weight[0, 0], "blk")
+    place = lax.axis_index("blk").astype(jnp.int32).reshape(1)
     aligned, padded, east, west = call(
         first_kernel,
         [shape(2 * faces, jnp.int32), shape(block_rows), shape(faces), shape(faces)],
@@ -295,7 +296,7 @@
     (weight_east,) = call(
         weight_kernel,
         [shape(faces)],
-        [(partner, SMEM), (owners, SMEM), (held, VMEM)],
+        [(partner, SMEM), (owners, SMEM), (place, SMEM), (held, VMEM)],
     )
     weight_west = from_behind(weight_east, "sub", 1)
 
@@ -324,7 +325,7 @@
     product = stiff(image)
     second, sums = call(
         functools.partial(last_kernel, size),
-        [shape(block_rows), jax.ShapeDtypeStruct((devices, 1, LANES), F32)],
+        [shape(block_rows), shape(1)],
         [
             (value, VMEM)
             for value in (
@@ -341,7 +342,7 @@
             )
         ],
     )
-    sums = lax.all_to_all(sums, ("sub", "blk"), split_axis=0, concat_axis=0, tiled=True)
+    sums = lax.all_gather(sums, ("sub", "blk"))
     solution_field, residual = call(
         final_kernel,
         [jax.ShapeDtypeStruct((block_rows, size), F32)] * 2,

time: 53 us -> 77.6 us (1.46)
  blocking collectives: 13.5 us -> 48.4 us
  Pallas kernels: 15 us -> 11 us
  waiting for transfers between devices: 3.33 us -> 0.49 us
  starting transfers between devices: 14.2 us -> 11.5 us
    all_gather x0 -> x2, blocking collectives: none -> 48.4 us  [the longest x1 41.7 us: on_device(): sums = lax.all_gather(sums, ('sub', 'blk'))]
    all_to_all x1 -> x0, blocking collectives: 13.5 us -> none  [on_device(): lax.all_to_all(sums, ('sub', 'blk'), split_axis=0, concat_axis=0, tiled=T...]
    all_to_all x1 -> x0, starting transfers between devices: 4.22 us -> none  [on_device(): lax.all_to_all(mortar_weight[0, 0], 'blk', split_axis=0, concat_axis=0, t...]
    pallas_call x7, Pallas kernels: 15 us -> 11 us  [call(): pl.pallas_call(body, out_shape=outs, in_specs=[spec for _, spec in inputs...]
    ppermute x5, waiting for transfers between devices: 3.33 us -> 0.49 us  [from_behind(): return lax.ppermute(value, axis, pairs)]
    ppermute x5, starting transfers between devices: 10 us -> 11.5 us  [from_behind(): return lax.ppermute(value, axis, pairs)]
    unnamed x12 -> x10, local copies, waits for them, and re-layouts: 3.53 us -> 2.88 us
  transfers between devices with their start and end apart: 6 -> 5, of which waited for: 2 -> 1; matrix products, arithmetic and copies ran while one was open for 4% -> 3% of each run, Pallas kernels for 11% -> 6%
where the time goes in v2:
time: 77.6 us; the launch traced here: 77.4 us
  blocking collectives  48.4 us (62%)
  starting transfers between devices  11.5 us (15%)
  Pallas kernels  11 us (14%)
  local copies, waits for them, and re-layouts  5.17 us (7%)
    all_gather x1, blocking collectives, on_device(): sums = lax.all_gather(sums, ('sub', 'blk'))  41.7 us
    ppermute x5, starting transfers between devices, from_behind(): return lax.ppermute(value, axis, pairs)  11.5 us
    pallas_call x7, Pallas kernels, call(): pl.pallas_call(body, out_shape=outs, in_specs=[spec for _, spec in inputs...  11 us
    all_gather x1, blocking collectives, on_device(): held = lax.all_gather(mortar_weight[0, 0], 'blk')  6.69 us
    unnamed x10, local copies, waits for them, and re-layouts  2.88 us
    another operation x1, local copies, waits for them, and re-layouts, on_device(): blocks = stored.reshape(stored.shape[0], size, size)  2.29 us
  transfers between devices with their start and end apart: 5, of which 1 were waited for; matrix products, arithmetic and copies ran while one was open for 3% of the time, Pallas kernels for 6%

profile of v2, /device:TPU:0, one launch (start us, length us, event | category | flops | bytes accessed | tf_op | source)
XLA Modules:
  0.0 77.4 jit_solution(13954706765532704555)
XLA Ops:
  0.6 6.7 %all-gather = f32[4,1,4,16,128]{4,3,2,1,0:T(8,128)S(1)} all-gather(f32[1,1,4,16,128]{4,3,2,1,0:T(8,128)} %param.13), channel_id=2, replica_groups=mesh['sub'=8,'blk'=4] {'blk'}, dimensions={0}, use_global_device_ids=true | all-gather | bytes 163840 | tf_op jit(solution)/shard_map/all_gather | solution.py:287
  7.3 0.7 copy-done.3
  8.0 0.7 copy-done.4
  8.7 0.6 shard_map.88.weight_east_ref
  9.2 2.0 %collective-permute-start = (f32[64,128]{1,0:T(8,128)S(1)}, f32[64,128]{1,0:T(8,128)S(1)}, u32[]{:S(2)}, u32[]{:S(2)}) collective-permute-start(f32[64,128]{1,0:T(8,128)S(1)} %shard_map.88.weight_east_ref), channel_id=1, source_target_pairs={{0,4},{4,8},{8,12},{12,16},{16,20},{20,24},{24,28},{28,0},{1,5},{5... | collective-permute-start | bytes 98312 | tf_op jit(solution)/shard_map/ppermute | solution.py:270
  11.2 0.8 %copy-done = s32[1,1,128,128]{3,2,1,0:T(8,128)S(1)} copy-done((s32[1,1,128,128]{3,2,1,0:T(8,128)S(1)}, s32[1,1,128,128]{3,2,1,0:T(8,128)}, u32[]{:S(2)}) %copy-start) | copy-done | bytes 65560
  12.1 0.7 copy-done.1
  12.8 1.5 %shard_map.86 = (s32[128,128]{1,0:T(8,128)S(1)}, f32[32,128]{1,0:T(8,128)S(1)}, f32[64,128]{1,0:T(8,128)S(1)}, f32[64,128]{1,0:T(8,128)S(1)}) custom-call(s32[64]{0:T(128)S(1)} %bitcast.24, f32[32,96]{1,0:T(8,128)S(1)} %bitcast.20, s32[128,128]{1,0:T(8,128)S(1)} %bitcast.19), custom_call_target="tpu_custom_call" | custom-call | flops 1000000 | bytes 1000000 | tf_op jit(solution)/shard_map/pallas_call | solution.py:20
  14.3 1.6 %collective-permute-start.2 = (f32[64,128]{1,0:T(8,128)S(1)}, f32[64,128]{1,0:T(8,128)S(1)}, u32[]{:S(2)}, u32[]{:S(2)}) collective-permute-start(f32[64,128]{1,0:T(8,128)S(1)} %get-tuple-element.15.east_ref), channel_id=1, source_target_pairs={{0,4},{4,8},{8,12},{12,16},{16,20},{20,24},{24,28},{28,0},{1,5},{5... | collective-permute-start | bytes 98312 | tf_op jit(solution)/shard_map/ppermute | solution.py:270
  15.9 3.2 %collective-permute-start.1 = (f32[64,128]{1,0:T(8,128)S(1)}, f32[64,128]{1,0:T(8,128)S(1)}, u32[]{:S(2)}, u32[]{:S(2)}) collective-permute-start(f32[64,128]{1,0:T(8,128)S(1)} %get-tuple-element.16.west_ref), channel_id=1, source_target_pairs={{0,28},{4,0},{8,4},{12,8},{16,12},{20,16},{24,20},{28,24},{1,29},{... | collective-permute-start | bytes 98312 | tf_op jit(solution)/shard_map/ppermute | solution.py:270
  19.1 2.3 %reshape_squeeze.3.blocks_ref = bf16[48,96,96]{2,1,0:T(8,128)(2,1)S(1)} reshape(bf16[1,1,48,9216]{3,2,1,0:T(8,128)(2,1)} %param.8) | data formatting | bytes 1769472 | tf_op jit(solution)/shard_map/reshape;squeeze | solution.py:279
  21.4 1.4 %shard_map.87.product_ref = f32[32,128]{1,0:T(8,128)S(1)} custom-call(s32[2,16]{1,0:T(2,128)S(1)} %bitcast.21, bf16[48,96,96]{2,1,0:T(8,128)(2,1)S(1)} %reshape_squeeze.3.blocks_ref, f32[32,128]{1,0:T(8,128)S(1)} %get-tuple-element.13.field_ref), custom_call_target="tpu_custom_call" | custom-call | flops 1000000 | bytes 1000000 | tf_op jit(solution)/shard_map/pallas_call | solution.py:20
  22.8 0.0 collective-permute-done.weight_west_ref
  22.8 0.0 collective-permute-done.2.from_last_ref
  22.8 0.0 collective-permute-done.1.from_next_ref
  22.8 3.1 %shard_map.89 = (f32[32,128]{1,0:T(8,128)S(1)}, f32[64,128]{1,0:T(8,128)S(1)}, f32[64,128]{1,0:T(8,128)S(1)}) custom-call(s32[128,128]{1,0:T(8,128)S(1)} %get-tuple-element.14.aligned_ref, f32[32,128]{1,0:T(8,128)S(1)} %shard_map.87.product_ref, f32[64,128]{1,0:T(8,128)S(1)} %shard_map.88.weight_east_ref, ...), custom_call_target="tpu_custom_call" | custom-call | flops 1000000 | bytes 1000000 | tf_op jit(solution)/shard_map/pallas_call | solution.py:20
  25.9 0.1 collective-permute-start.4
  26.0 4.7 %collective-permute-start.3 = (f32[64,128]{1,0:T(8,128)S(1)}, f32[64,128]{1,0:T(8,128)S(1)}, u32[]{:S(2)}, u32[]{:S(2)}) collective-permute-start(f32[64,128]{1,0:T(8,128)S(1)} %get-tuple-element.19.west_ref), channel_id=1, source_target_pairs={{0,28},{4,0},{8,4},{12,8},{16,12},{20,16},{24,20},{28,24},{1,29},{... | collective-permute-start | bytes 98312 | tf_op jit(solution)/shard_map/ppermute | solution.py:270
  30.7 1.4 %shard_map.90.product_ref = f32[32,128]{1,0:T(8,128)S(1)} custom-call(s32[2,16]{1,0:T(2,128)S(1)} %bitcast.22, bf16[48,96,96]{2,1,0:T(8,128)(2,1)S(1)} %reshape_squeeze.3.blocks_ref, f32[32,128]{1,0:T(8,128)S(1)} %get-tuple-element.17.field_ref.image_ref), custom_call_target="tpu_custom_call" | custom-call | flops 1000000 | bytes 1000000 | tf_op jit(solution)/shard_map/pallas_call | solution.py:20
  32.1 0.5 collective-permute-done.4.from_last_ref
  32.6 0.0 collective-permute-done.3.from_next_ref
  32.6 2.3 %shard_map.91 = (f32[32,128]{1,0:T(8,128)S(1)}, f32[1,128]{1,0:T(1,128)S(1)}) custom-call(s32[128,128]{1,0:T(8,128)S(1)} %get-tuple-element.14.aligned_ref, f32[32,128]{1,0:T(8,128)S(1)} %shard_map.90.product_ref, f32[64,128]{1,0:T(8,128)S(1)} %shard_map.88.weight_east_ref, f32[64,128]{1,0:T(8,128)S(1)} %collective-permute-done.weight_west_ref, ...), custom_call_target="tpu_custom_call" | custom-call | flops 1000000 | bytes 1000000 | tf_op jit(solution)/shard_map/pallas_call | solution.py:20
  34.9 41.7 %all-gather.2.sums_ref = f32[32,1,128]{2,1,0:T(1,128)S(1)} all-gather(f32[1,1,128]{2,1,0:T(1,128)S(1)} %bitcast.26), channel_id=3, replica_groups=mesh['sub'=8,'blk'=4] {'sub','blk'}, dimensions={0}, use_global_device_ids=true | all-gather | bytes 16896 | tf_op jit(solution)/shard_map/all_gather | solution.py:345
  76.6 0.7 shard_map.92
  (6 shorter events, 0.0 us)
Async XLA Ops:
  7.3 14.0 %copy-start.2 = (s32[1,1,2,16]{3,2,1,0:T(2,128)S(1)}, s32[1,1,2,16]{3,2,1,0:T(2,128)}, u32[]{:S(2)}) copy-start(s32[1,1,2,16]{3,2,1,0:T(2,128)} %param.9) | copy-start | bytes 388
  7.3 0.7 copy-start.3
  8.0 0.7 copy-start.4
  9.2 13.5 %collective-permute-start = (f32[64,128]{1,0:T(8,128)S(1)}, f32[64,128]{1,0:T(8,128)S(1)}, u32[]{:S(2)}, u32[]{:S(2)}) collective-permute-start(f32[64,128]{1,0:T(8,128)S(1)} %shard_map.88.weight_east_ref), channel_id=1, source_target_pairs={{0,4},{4,8},{8,12},{12,16},{16,20},{20,24},{24,28},{28,0},{1,5},{5... | collective-permute-start | bytes 98312 | tf_op jit(solution)/shard_map/ppermute | solution.py:270
  11.2 0.8 %copy-start = (s32[1,1,128,128]{3,2,1,0:T(8,128)S(1)}, s32[1,1,128,128]{3,2,1,0:T(8,128)}, u32[]{:S(2)}) copy-start(s32[1,1,128,128]{3,2,1,0:T(8,128)} %param.10) | copy-start | bytes 196612
  12.1 0.7 copy-start.1
  14.3 8.5 %collective-permute-start.2 = (f32[64,128]{1,0:T(8,128)S(1)}, f32[64,128]{1,0:T(8,128)S(1)}, u32[]{:S(2)}, u32[]{:S(2)}) collective-permute-start(f32[64,128]{1,0:T(8,128)S(1)} %get-tuple-element.15.east_ref), channel_id=1, source_target_pairs={{0,4},{4,8},{8,12},{12,16},{16,20},{20,24},{24,28},{28,0},{1,5},{5... | collective-permute-start | bytes 98312 | tf_op jit(solution)/shard_map/ppermute | solution.py:270
  15.9 7.0 %collective-permute-start.1 = (f32[64,128]{1,0:T(8,128)S(1)}, f32[64,128]{1,0:T(8,128)S(1)}, u32[]{:S(2)}, u32[]{:S(2)}) collective-permute-start(f32[64,128]{1,0:T(8,128)S(1)} %get-tuple-element.16.west_ref), channel_id=1, source_target_pairs={{0,28},{4,0},{8,4},{12,8},{16,12},{20,16},{24,20},{28,24},{1,29},{... | collective-permute-start | bytes 98312 | tf_op jit(solution)/shard_map/ppermute | solution.py:270
  25.9 6.7 %collective-permute-start.4 = (f32[64,128]{1,0:T(8,128)S(1)}, f32[64,128]{1,0:T(8,128)S(1)}, u32[]{:S(2)}, u32[]{:S(2)}) collective-permute-start(f32[64,128]{1,0:T(8,128)S(1)} %get-tuple-element.18.east_ref), channel_id=1, source_target_pairs={{0,4},{4,8},{8,12},{12,16},{16,20},{20,24},{24,28},{28,0},{1,5},{5... | collective-permute-start | bytes 98312 | tf_op jit(solution)/shard_map/ppermute | solution.py:270
  26.0 6.6 %collective-permute-start.3 = (f32[64,128]{1,0:T(8,128)S(1)}, f32[64,128]{1,0:T(8,128)S(1)}, u32[]{:S(2)}, u32[]{:S(2)}) collective-permute-start(f32[64,128]{1,0:T(8,128)S(1)} %get-tuple-element.19.west_ref), channel_id=1, source_target_pairs={{0,28},{4,0},{8,4},{12,8},{16,12},{20,16},{24,20},{28,24},{1,29},{... | collective-permute-start | bytes 98312 | tf_op jit(solution)/shard_map/ppermute | solution.py:270

commit v3 on v1

--- a/solution.py
+++ b/solution.py
@@ -10,6 +10,7 @@
 LANES = 128
 SUBLANES = 8
 VMEM = pl.BlockSpec(memory_space=pltpu.VMEM)
+HBM = pl.BlockSpec(memory_space=pltpu.HBM)
 SMEM = pl.BlockSpec(memory_space=pltpu.SMEM)
 PARAMS = pltpu.CompilerParams(vmem_limit_bytes=32 * 1024 * 1024)
 F32 = jnp.float32
@@ -39,55 +40,98 @@
     return high, value - high
 
 
-def gather_traces(field, rows_ref, east_ref, west_ref):
+def gather_traces(field, rows_ref, traces_refs):
     block_rows = field.shape[0]
-    faces = east_ref.shape[0]
     spread = [
         jnp.broadcast_to(field[i : i + 1, :], (SUBLANES, LANES)) for i in range(block_rows)
     ]
-
-    def step(target, base, k):
-        index = rows_ref[pl.ds(pl.multiple_of(base + k * SUBLANES, SUBLANES), SUBLANES), :]
-        dof = index // block_rows
-        row = index % block_rows
-        taken = jnp.zeros((SUBLANES, LANES), F32)
-        for i in range(block_rows):
-            here = jnp.take_along_axis(spread[i], dof, axis=1, mode="promise_in_bounds")
-            taken = jnp.where(row == i, here, taken)
-        target[pl.ds(pl.multiple_of(k * SUBLANES, SUBLANES), SUBLANES), :] = taken
-
-    for target, base in ((east_ref, 0), (west_ref, faces)):
-
-        def body(k, _, target=target, base=base):
-            step(target, base, k)
+    faces = rows_ref.shape[0] // len(traces_refs)
+    for side, target in enumerate(traces_refs):
+
+        def step(k, _, target=target, side=side):
+            index = rows_ref[tile(side * faces // SUBLANES + k), :]
+            dof, row = split(index, block_rows)
+            taken = jnp.zeros((SUBLANES, LANES), F32)
+            for i in range(block_rows):
+                here = jnp.take_along_axis(spread[i], dof, axis=1, mode="promise_in_bounds")
+                taken = jnp.where(row == i, here, taken)
+            target[tile(k), :] = taken
             return 0
 
-        lax.fori_loop(0, faces // SUBLANES, body, 0)
-
-
-def first_kernel(partner_ref, field_ref, rows_ref, aligned_ref, padded_ref, east_ref, west_ref):
-    faces = east_ref.shape[0]
+        lax.fori_loop(0, faces // SUBLANES, step, 0, unroll=4)
+
+
+def tile(k):
+    return pl.ds(pl.multiple_of(k * SUBLANES, SUBLANES), SUBLANES)
+
+
+def split(index, block_rows):
+    if block_rows & (block_rows - 1) == 0:
+        shift = block_rows.bit_length() - 1
+        return index >> shift, index & (block_rows - 1)
+    return lax.div(index, block_rows), lax.rem(index, block_rows)
+
+
+def first_kernel(
+    partner_hbm,
+    owner_hbm,
+    rows_hbm,
+    field_hbm,
+    aligned_ref,
+    padded_ref,
+    chosen_ref,
+    side_a_ref,
+    side_b_ref,
+    partner_ref,
+    owner_ref,
+    rows_ref,
+    field_ref,
+    sems,
+):
+    copies = [
+        pltpu.make_async_copy(source, target, sems.at[k])
+        for k, (source, target) in enumerate(
+            (
+                (partner_hbm, partner_ref),
+                (owner_hbm, owner_ref),
+                (rows_hbm, rows_ref),
+                (field_hbm, field_ref),
+            )
+        )
+    ]
+    for copy in copies:
+        copy.start()
+    faces = side_a_ref.shape[0]
+    per_group = faces // owner_ref.shape[0]
     size = field_ref.shape[1]
-    aligned_ref[faces:, :] = rows_ref[faces:, :]
-
-    def move(f, _):
-        aligned_ref[pl.ds(partner_ref[f], 1), :] = rows_ref[pl.ds(f, 1), :]
-        return 0
-
-    lax.fori_loop(0, faces, move, 0, unroll=8)
+    parity = lax.rem(lax.axis_index("sub"), 2)
+    east = pl.multiple_of((1 - parity) * faces, faces)
+    west = pl.multiple_of(parity * faces, faces)
     padded_ref[...] = jnp.zeros_like(padded_ref)
+    lane = lax.broadcasted_iota(jnp.int32, (1, chosen_ref.shape[1]), 1)
+    for copy in copies:
+        copy.wait()
+    aligned_ref[pl.ds(west, faces), :] = rows_ref[faces:, :]
+    for f in range(faces):
+        place = partner_ref[f]
+        source = owner_ref[f // per_group] * per_group + f % per_group
+        aligned_ref[pl.ds(east + place, 1), :] = rows_ref[f : f + 1, :]
+        chosen_ref[pl.ds(place, 1), :] = jnp.where(lane == source, 1.0, 0.0)
     padded_ref[:, :size] = field_ref[...]
-    gather_traces(padded_ref[...], aligned_ref, east_ref, west_ref)
-
-
-def weight_kernel(partner_ref, owner_ref, arrived_ref, out_ref):
-    groups, per_group, _ = arrived_ref.shape
-    for g in range(groups):
-        owner = owner_ref[g]
-        for k in range(per_group):
-            out_ref[pl.ds(partner_ref[g * per_group + k], 1), :] = arrived_ref[
-                owner, pl.ds(k, 1), :
-            ]
+    gather_traces(padded_ref[...], aligned_ref, (side_a_ref, side_b_ref))
+
+
+def message_kernel(held_ref, chosen_ref, side_a_ref, side_b_ref, to_a_ref, to_b_ref):
+    faces = side_a_ref.shape[0]
+    own = jnp.dot(
+        chosen_ref[...],
+        held_ref[...],
+        precision=lax.Precision.HIGHEST,
+        preferred_element_type=F32,
+    )
+    for side, target in ((side_a_ref, to_a_ref), (side_b_ref, to_b_ref)):
+        target[:faces, :] = side[...]
+        target[faces:, :] = own
 
 
 def stiffness_kernel(pairs_ref, blocks_ref, field_ref, out_ref, pieces, sums):
@@ -127,18 +171,16 @@
     )
 
 
-def spread_jumps(block_rows, size, aligned_ref, weights, own, arrived):
-    faces = own[0].shape[0]
+def spread_jumps(block_rows, size, aligned_ref, weights_ref, own, arrived):
+    faces = weights_ref.shape[0] // 2
     dof_of = lax.broadcasted_iota(jnp.int32, (size, LANES), 0)
     row_of = lax.broadcasted_iota(jnp.int32, (block_rows, LANES), 0)
 
     def step(k, total, side):
-        place = pl.ds(pl.multiple_of(k * SUBLANES, SUBLANES), SUBLANES)
-        lam = weights[side][place, :] * (own[side][place, :] - arrived[side][place, :])
+        place = tile(side * faces // SUBLANES + k)
+        lam = weights_ref[place, :] * (own[side][tile(k), :] - arrived[side][tile(k), :])
         high, low = halves(lam)
-        index = aligned_ref[pl.ds(pl.multiple_of(side * faces + k * SUBLANES, SUBLANES), SUBLANES), :]
-        dof = index // block_rows
-        row = index % block_rows
+        dof, row = split(aligned_ref[place, :], block_rows)
         left = []
         right = []
         for f in range(SUBLANES):
@@ -163,7 +205,7 @@
     total = jnp.zeros((2 * block_rows, size), F32)
     for side in (0, 1):
         total = lax.fori_loop(
-            0, faces // SUBLANES, functools.partial(step, side=side), total
+            0, faces // SUBLANES, functools.partial(step, side=side), total, unroll=2
         )
     return total[:block_rows] + total[block_rows:]
 
@@ -172,28 +214,31 @@
     size,
     aligned_ref,
     product_ref,
-    weight_east_ref,
-    weight_west_ref,
-    east_ref,
-    west_ref,
-    from_next_ref,
-    from_last_ref,
+    to_a_ref,
+    to_b_ref,
+    from_a_ref,
+    from_b_ref,
     image_ref,
-    next_east_ref,
-    next_west_ref,
+    weights_ref,
+    side_a_ref,
+    side_b_ref,
 ):
     block_rows = product_ref.shape[0]
+    faces = side_a_ref.shape[0]
+    odd = lax.rem(lax.axis_index("sub"), 2) == 1
+    weights_ref[:faces, :] = jnp.where(odd, to_a_ref[faces:, :], from_a_ref[faces:, :])
+    weights_ref[faces:, :] = jnp.where(odd, from_b_ref[faces:, :], to_a_ref[faces:, :])
     coupled = spread_jumps(
         block_rows,
         size,
         aligned_ref,
-        (weight_east_ref, weight_west_ref),
-        (east_ref, west_ref),
-        (from_next_ref, from_last_ref),
+        weights_ref,
+        (to_a_ref, to_b_ref),
+        (from_a_ref, from_b_ref),
     )
     image_ref[...] = product_ref[...]
     image_ref[:, :size] = image_ref[:, :size] + coupled
-    gather_traces(image_ref[...], aligned_ref, next_east_ref, next_west_ref)
+    gather_traces(image_ref[...], aligned_ref, (side_a_ref, side_b_ref))
 
 
 def total_of(value):
@@ -204,12 +249,11 @@
     size,
     aligned_ref,
     product_ref,
-    weight_east_ref,
-    weight_west_ref,
-    east_ref,
-    west_ref,
-    from_next_ref,
-    from_last_ref,
+    weights_ref,
+    side_a_ref,
+    side_b_ref,
+    from_a_ref,
+    from_b_ref,
     field_ref,
     image_ref,
     second_ref,
@@ -220,9 +264,9 @@
         block_rows,
         size,
         aligned_ref,
-        (weight_east_ref, weight_west_ref),
-        (east_ref, west_ref),
-        (from_next_ref, from_last_ref),
+        weights_ref,
+        (side_a_ref, side_b_ref),
+        (from_a_ref, from_b_ref),
     )
     second_ref[...] = product_ref[...]
     second_ref[:, :size] = second_ref[:, :size] + coupled
@@ -263,10 +307,13 @@
     residual_ref[...] = residual - alpha_next * moved
 
 
-def from_behind(value, axis, steps):
-    count = lax.axis_size(axis)
-    pairs = [(source, (source + steps) % count) for source in range(count)]
-    return lax.ppermute(value, axis, pairs)
+def swap(value, odd):
+    count = lax.axis_size("sub")
+    pairs = []
+    for first in range(odd, count, 2):
+        second = (first + 1) % count
+        pairs += [(first, second), (second, first)]
+    return lax.ppermute(value, "sub", pairs)
 
 
 def on_device(
@@ -281,23 +328,34 @@
     partner = partner_face[0, 0]
     owners = owner_list[0, 0]
     faces = partner.shape[0]
-    groups = owners.shape[0]
     devices = lax.axis_size("sub") * lax.axis_size("blk")
 
     held = lax.all_to_all(mortar_weight[0, 0], "blk", split_axis=0, concat_axis=0, tiled=True)
-    aligned, padded, east, west = call(
+    aligned, padded, chosen, side_a, side_b = call(
         first_kernel,
-        [shape(2 * faces, jnp.int32), shape(block_rows), shape(faces), shape(faces)],
-        [(partner, SMEM), (field, VMEM), (rows, VMEM)],
-    )
-    from_last = from_behind(east, "sub", 1)
-    from_next = from_behind(west, "sub", -1)
-    (weight_east,) = call(
-        weight_kernel,
-        [shape(faces)],
-        [(partner, SMEM), (owners, SMEM), (held, VMEM)],
-    )
-    weight_west = from_behind(weight_east, "sub", 1)
+        [
+            shape(2 * faces, jnp.int32),
+            shape(block_rows),
+            jax.ShapeDtypeStruct((faces, faces), F32),
+            shape(faces),
+            shape(faces),
+        ],
+        [(partner, HBM), (owners, HBM), (rows, HBM), (field, HBM)],
+        scratch=[
+            pltpu.SMEM(partner.shape, jnp.int32),
+            pltpu.SMEM(owners.shape, jnp.int32),
+            pltpu.VMEM(rows.shape, jnp.int32),
+            pltpu.VMEM(field.shape, F32),
+            pltpu.SemaphoreType.DMA((4,)),
+        ],
+    )
+    to_a, to_b = call(
+        message_kernel,
+        [shape(2 * faces)] * 2,
+        [(value, VMEM) for value in (held.reshape(faces, LANES), chosen, side_a, side_b)],
+    )
+    from_a = swap(to_a, 1)
+    from_b = swap(to_b, 0)
 
     def stiff(vector):
         (product,) = call(
@@ -308,36 +366,20 @@
         )
         return product
 
-    product = stiff(padded)
-    image, next_east, next_west = call(
+    image, weights, side_a, side_b = call(
         functools.partial(middle_kernel, size),
-        [shape(block_rows), shape(faces), shape(faces)],
-        [
-            (value, VMEM)
-            for value in (
-                aligned, product, weight_east, weight_west, east, west, from_next, from_last
-            )
-        ],
-    )
-    second_last = from_behind(next_east, "sub", 1)
-    second_next = from_behind(next_west, "sub", -1)
-    product = stiff(image)
+        [shape(block_rows), shape(2 * faces), shape(faces), shape(faces)],
+        [(value, VMEM) for value in (aligned, stiff(padded), to_a, to_b, from_a, from_b)],
+    )
+    from_a = swap(side_a, 1)
+    from_b = swap(side_b, 0)
     second, sums = call(
         functools.partial(last_kernel, size),
         [shape(block_rows), jax.ShapeDtypeStruct((devices, 1, LANES), F32)],
         [
             (value, VMEM)
             for value in (
-                aligned,
-                product,
-                weight_east,
-                weight_west,
-                next_east,
-                next_west,
-                second_next,
-                second_last,
-                padded,
-                image,
+                aligned, stiff(image), weights, side_a, side_b, from_a, from_b, padded, image
             )
         ],
     )

time: 53 us -> 43.4 us (0.82)
  Pallas kernels: 15 us -> 10.5 us
  blocking collectives: 13.5 us -> 11.1 us
  starting transfers between devices: 14.2 us -> 12.3 us
  local copies, waits for them, and re-layouts: 5.82 us -> 5.16 us
    pallas_call x7, Pallas kernels: 15 us -> 10.5 us  [call(): pl.pallas_call(body, out_shape=outs, in_specs=[spec for _, spec in inputs...]
    all_to_all x1, blocking collectives: 13.5 us -> 11.1 us  [on_device(): lax.all_to_all(sums, ('sub', 'blk'), split_axis=0, concat_axis=0, tiled=T...]
    ppermute x5 -> x4, starting transfers between devices: 10 us -> 8.09 us  [swap(): return lax.ppermute(value, 'sub', pairs)]
    unnamed x12 -> x10, local copies, waits for them, and re-layouts: 3.53 us -> 2.87 us
    ppermute x5 -> x4, waiting for transfers between devices: 3.33 us -> 3.17 us  [swap(): return lax.ppermute(value, 'sub', pairs)]
  transfers between devices with their start and end apart: 6 -> 5, of which waited for: 2 -> 3; matrix products, arithmetic and copies ran while one was open for 4% -> 5% of each run, Pallas kernels for 11% -> 10%
where the time goes in v3:
time: 43.4 us; the launch traced here: 43 us
  starting transfers between devices  12.3 us (28%)
  blocking collectives  11.1 us (26%)
  Pallas kernels  10.5 us (24%)
  local copies, waits for them, and re-layouts  5.16 us (12%)
  waiting for transfers between devices  3.18 us (7%)
  between operations  0.72 us (2%)
    all_to_all x1, blocking collectives, on_device(): lax.all_to_all(sums, ('sub', 'blk'), split_axis=0, concat_axis=0, tiled=T...  11.1 us
    pallas_call x7, Pallas kernels, call(): pl.pallas_call(body, out_shape=outs, in_specs=[spec for _, spec in inputs...  10.5 us
    ppermute x4, starting transfers between devices, swap(): return lax.ppermute(value, 'sub', pairs)  8.09 us
    all_to_all x1, starting transfers between devices, on_device(): lax.all_to_all(mortar_weight[0, 0], 'blk', split_axis=0, concat_axis=0, t...  4.22 us
    ppermute x4, waiting for transfers between devices, swap(): return lax.ppermute(value, 'sub', pairs)  3.17 us
    unnamed x10, local copies, waits for them, and re-layouts  2.87 us
    another operation x1, local copies, waits for them, and re-layouts, on_device(): blocks = stored.reshape(stored.shape[0], size, size)  2.29 us
  transfers between devices with their start and end apart: 5, of which 3 were waited for; matrix products, arithmetic and copies ran while one was open for 5% of the time, Pallas kernels for 10%

profile of v3, /device:TPU:0, one launch (start us, length us, event | category | flops | bytes accessed | tf_op | source)
XLA Modules:
  0.0 43.0 jit_solution(9992385039551705324)
XLA Ops:
  0.6 0.0 copy-start.2
  0.6 4.2 %all-to-all-start = ((f32[4,16,128]{2,1,0:T(8,128)}), f32[4,16,128]{2,1,0:T(8,128)S(1)}, u32[]{:S(2)}, u32[]{:S(2)}) async-start(f32[4,16,128]{2,1,0:T(8,128)} %bitcast.24), calls=%async_computation | async-start | bytes 65536 | tf_op jit(solution)/shard_map/all_to_all | solution.py:333
  4.9 0.8 %copy-done = s32[1,1,128,128]{3,2,1,0:T(8,128)S(1)} copy-done((s32[1,1,128,128]{3,2,1,0:T(8,128)S(1)}, s32[1,1,128,128]{3,2,1,0:T(8,128)}, u32[]{:S(2)}) %copy-start) | copy-done | bytes 65560
  5.7 0.7 %copy-done.1 = f32[1,1,96,32]{2,3,1,0:T(8,128)S(1)} copy-done((f32[1,1,96,32]{2,3,1,0:T(8,128)S(1)}, f32[1,1,96,32]{2,3,1,0:T(8,128)}, u32[]{:S(2)}) %copy-start.1) | copy-done | bytes 12312
  6.4 0.7 %copy-done.3 = s32[1,1,64]{2,1,0:T(1,128)S(1)} copy-done((s32[1,1,64]{2,1,0:T(1,128)S(1)}, s32[1,1,64]{2,1,0:T(1,128)}, u32[]{:S(2)}) %copy-start.3) | copy-done | bytes 280
  7.1 0.7 %copy-done.4 = s32[1,1,4]{2,1,0:T(1,128)S(1)} copy-done((s32[1,1,4]{2,1,0:T(1,128)S(1)}, s32[1,1,4]{2,1,0:T(1,128)}, u32[]{:S(2)}) %copy-start.4) | copy-done | bytes 40
  7.7 1.5 %shard_map.86 = (s32[128,128]{1,0:T(8,128)S(1)}, f32[32,128]{1,0:T(8,128)S(1)}, f32[64,64]{1,0:T(8,128)S(1)}, f32[64,128]{1,0:T(8,128)S(1)}, f32[64,128]{1,0:T(8,128)S(1)}) custom-call(s32[64]{0:T(128)S(1)} %bitcast.22, s32[4]{0:T(128)S(1)} %bitcast.23, s32[128,128]{1,0:T(8,128)S(1)} %bitcast.18, f32[32,96]{1,0:T(8,128)S(1)} %bitcast.19), custom_call_target="tpu_custom_call" | custom-call | flops 1000000 | bytes 1000000 | tf_op jit(solution)/shard_map/pallas_call | solution.py:21
  9.3 0.0 all-to-all-done
  9.3 0.1 shard_map.88
  9.4 5.1 %collective-permute-start = (f32[128,128]{1,0:T(8,128)S(1)}, f32[128,128]{1,0:T(8,128)S(1)}, u32[]{:S(2)}, u32[]{:S(2)}) collective-permute-start(f32[128,128]{1,0:T(8,128)S(1)} %get-tuple-element.22.to_a_ref), channel_id=1, source_target_pairs={{4,8},{8,4},{12,16},{16,12},{20,24},{24,20},{28,0},{0,28},{5,9},{9... | collective-permute-start | bytes 196616 | tf_op jit(solution)/shard_map/ppermute | solution.py:316
  14.5 0.0 collective-permute-start.1
  14.6 2.3 %reshape_squeeze.3.blocks_ref = bf16[48,96,96]{2,1,0:T(8,128)(2,1)S(1)} reshape(bf16[1,1,48,9216]{3,2,1,0:T(8,128)(2,1)} %param.8) | data formatting | bytes 1769472 | tf_op jit(solution)/shard_map/reshape;squeeze | solution.py:325
  16.9 1.4 %shard_map.87.product_ref = f32[32,128]{1,0:T(8,128)S(1)} custom-call(s32[2,16]{1,0:T(2,128)S(1)} %bitcast.20, bf16[48,96,96]{2,1,0:T(8,128)(2,1)S(1)} %reshape_squeeze.3.blocks_ref, f32[32,128]{1,0:T(8,128)S(1)} %get-tuple-element.17.field_ref), custom_call_target="tpu_custom_call" | custom-call | flops 1000000 | bytes 1000000 | tf_op jit(solution)/shard_map/pallas_call | solution.py:21
  18.3 0.0 collective-permute-done.from_a_ref
  18.3 0.5 %collective-permute-done.1.from_b_ref = f32[128,128]{1,0:T(8,128)S(1)} collective-permute-done((f32[128,128]{1,0:T(8,128)S(1)}, f32[128,128]{1,0:T(8,128)S(1)}, u32[]{:S(2)}, u32[]{:S(2)}) %collective-permute-start.1) | collective-permute-done | bytes 65568 | tf_op jit(solution)/shard_map/ppermute | solution.py:316
  18.8 3.0 %shard_map.89 = (f32[32,128]{1,0:T(8,128)S(1)}, f32[128,128]{1,0:T(8,128)S(1)}, f32[64,128]{1,0:T(8,128)S(1)}, f32[64,128]{1,0:T(8,128)S(1)}) custom-call(s32[128,128]{1,0:T(8,128)S(1)} %get-tuple-element.18.aligned_ref, f32[32,128]{1,0:T(8,128)S(1)} %shard_map.87.product_ref, f32[128,128]{1,0:T(8,128)S(1)} %get-tuple-element.22.to_a_ref, ...), custom_call_target="tpu_custom_call" | custom-call | flops 1000000 | bytes 1000000 | tf_op jit(solution)/shard_map/pallas_call | solution.py:21
  21.9 3.0 %collective-permute-start.2 = (f32[64,128]{1,0:T(8,128)S(1)}, f32[64,128]{1,0:T(8,128)S(1)}, u32[]{:S(2)}, u32[]{:S(2)}) collective-permute-start(f32[64,128]{1,0:T(8,128)S(1)} %get-tuple-element.26.side_a_ref), channel_id=1, source_target_pairs={{4,8},{8,4},{12,16},{16,12},{20,24},{24,20},{28,0},{0,28},{5,9},{9... | collective-permute-start | bytes 98312 | tf_op jit(solution)/shard_map/ppermute | solution.py:316
  24.8 0.0 collective-permute-start.3
  24.8 1.4 %shard_map.90.product_ref = f32[32,128]{1,0:T(8,128)S(1)} custom-call(s32[2,16]{1,0:T(2,128)S(1)} %bitcast.21, bf16[48,96,96]{2,1,0:T(8,128)(2,1)S(1)} %reshape_squeeze.3.blocks_ref, f32[32,128]{1,0:T(8,128)S(1)} %get-tuple-element.24.field_ref.image_ref), custom_call_target="tpu_custom_call" | custom-call | flops 1000000 | bytes 1000000 | tf_op jit(solution)/shard_map/pallas_call | solution.py:21
  26.2 2.3 %collective-permute-done.2.from_a_ref = f32[64,128]{1,0:T(8,128)S(1)} collective-permute-done((f32[64,128]{1,0:T(8,128)S(1)}, f32[64,128]{1,0:T(8,128)S(1)}, u32[]{:S(2)}, u32[]{:S(2)}) %collective-permute-start.2) | collective-permute-done | bytes 32800 | tf_op jit(solution)/shard_map/ppermute | solution.py:316
  28.5 0.3 collective-permute-done.3.from_b_ref
  28.9 2.3 %shard_map.91 = (f32[32,128]{1,0:T(8,128)S(1)}, f32[32,1,128]{2,1,0:T(1,128)S(1)}) custom-call(s32[128,128]{1,0:T(8,128)S(1)} %get-tuple-element.18.aligned_ref, f32[32,128]{1,0:T(8,128)S(1)} %shard_map.90.product_ref, f32[128,128]{1,0:T(8,128)S(1)} %get-tuple-element.25.weights_ref, f32[64,128]{1,0:T(8,128)S(1)} %get-tuple-element.26.side_a_ref, ...), custom_call_target="tpu_custom_call" | custom-call | flops 1000000 | bytes 1000000 | tf_op jit(solution)/shard_map/pallas_call | solution.py:21
  31.2 11.1 %all_to_all.10.sums_ref = f32[32,1,128]{2,1,0:T(1,128)S(1)} all-to-all(f32[32,1,128]{2,1,0:T(1,128)S(1)} %get-tuple-element.29), channel_id=1, replica_groups=mesh['sub'=8,'blk'=4] {'sub','blk'}, dimensions={0} | all-to-all | bytes 32768 | tf_op jit(solution)/shard_map/all_to_all | solution.py:386
  42.2 0.7 %shard_map.92 = (f32[32,96]{1,0:T(8,128)}, f32[32,96]{1,0:T(8,128)}) custom-call(f32[32,128]{1,0:T(8,128)S(1)} %get-tuple-element.17.field_ref, f32[32,128]{1,0:T(8,128)S(1)} %get-tuple-element.24.field_ref.image_ref, f32[32,128]{1,0:T(8,128)S(1)} %get-tuple-element.28.second_ref, f32[32,1,128]{2,1,0:T(1,128)S(1)} %all_to_all.10.sums_ref), custom_call_target="tpu_custom_call" | custom-call | flops 1000000 | bytes 1000000 | tf_op jit(solution)/shard_map/pallas_call | solution.py:21
  (5 shorter events, 0.0 us)
Async XLA Ops:
  0.6 16.2 %copy-start.2 = (s32[1,1,2,16]{3,2,1,0:T(2,128)S(1)}, s32[1,1,2,16]{3,2,1,0:T(2,128)}, u32[]{:S(2)}) copy-start(s32[1,1,2,16]{3,2,1,0:T(2,128)} %param.9) | copy-start | bytes 388
  0.6 8.6 %all-to-all-start = ((f32[4,16,128]{2,1,0:T(8,128)}), f32[4,16,128]{2,1,0:T(8,128)S(1)}, u32[]{:S(2)}, u32[]{:S(2)}) async-start(f32[4,16,128]{2,1,0:T(8,128)} %bitcast.24), calls=%async_computation | async-start | bytes 65536 | tf_op jit(solution)/shard_map/all_to_all | solution.py:333
  4.9 0.8 %copy-start = (s32[1,1,128,128]{3,2,1,0:T(8,128)S(1)}, s32[1,1,128,128]{3,2,1,0:T(8,128)}, u32[]{:S(2)}) copy-start(s32[1,1,128,128]{3,2,1,0:T(8,128)} %param.10) | copy-start | bytes 196612
  5.7 0.7 %copy-start.1 = (f32[1,1,96,32]{2,3,1,0:T(8,128)S(1)}, f32[1,1,96,32]{2,3,1,0:T(8,128)}, u32[]{:S(2)}) copy-start(f32[1,1,96,32]{2,3,1,0:T(8,128)} %param.7) | copy-start | bytes 36868
  6.4 0.7 %copy-start.3 = (s32[1,1,64]{2,1,0:T(1,128)S(1)}, s32[1,1,64]{2,1,0:T(1,128)}, u32[]{:S(2)}) copy-start(s32[1,1,64]{2,1,0:T(1,128)} %param.11) | copy-start | bytes 772
  7.1 0.7 %copy-start.4 = (s32[1,1,4]{2,1,0:T(1,128)S(1)}, s32[1,1,4]{2,1,0:T(1,128)}, u32[]{:S(2)}) copy-start(s32[1,1,4]{2,1,0:T(1,128)} %param.12) | copy-start | bytes 52
  9.4 8.8 %collective-permute-start = (f32[128,128]{1,0:T(8,128)S(1)}, f32[128,128]{1,0:T(8,128)S(1)}, u32[]{:S(2)}, u32[]{:S(2)}) collective-permute-start(f32[128,128]{1,0:T(8,128)S(1)} %get-tuple-element.22.to_a_ref), channel_id=1, source_target_pairs={{4,8},{8,4},{12,16},{16,12},{20,24},{24,20},{28,0},{0,28},{5,9},{9... | collective-permute-start | bytes 196616 | tf_op jit(solution)/shard_map/ppermute | solution.py:316
  14.5 4.3 %collective-permute-start.1 = (f32[128,128]{1,0:T(8,128)S(1)}, f32[128,128]{1,0:T(8,128)S(1)}, u32[]{:S(2)}, u32[]{:S(2)}) collective-permute-start(f32[128,128]{1,0:T(8,128)S(1)} %get-tuple-element.23.to_b_ref), channel_id=1, source_target_pairs={{0,4},{4,0},{8,12},{12,8},{16,20},{20,16},{24,28},{28,24},{1,5},{5... | collective-permute-start | bytes 196616 | tf_op jit(solution)/shard_map/ppermute | solution.py:316
  21.9 6.7 %collective-permute-start.2 = (f32[64,128]{1,0:T(8,128)S(1)}, f32[64,128]{1,0:T(8,128)S(1)}, u32[]{:S(2)}, u32[]{:S(2)}) collective-permute-start(f32[64,128]{1,0:T(8,128)S(1)} %get-tuple-element.26.side_a_ref), channel_id=1, source_target_pairs={{4,8},{8,4},{12,16},{16,12},{20,24},{24,20},{28,0},{0,28},{5,9},{9... | collective-permute-start | bytes 98312 | tf_op jit(solution)/shard_map/ppermute | solution.py:316
  24.8 4.1 %collective-permute-start.3 = (f32[64,128]{1,0:T(8,128)S(1)}, f32[64,128]{1,0:T(8,128)S(1)}, u32[]{:S(2)}, u32[]{:S(2)}) collective-permute-start(f32[64,128]{1,0:T(8,128)S(1)} %get-tuple-element.27.side_b_ref), channel_id=1, source_target_pairs={{0,4},{4,0},{8,12},{12,8},{16,20},{20,16},{24,28},{28,24},{1,5},{5... | collective-permute-start | bytes 98312 | tf_op jit(solution)/shard_map/ppermute | solution.py:316

commit v4 on v3

--- a/solution.py
+++ b/solution.py
@@ -241,11 +241,48 @@
     gather_traces(image_ref[...], aligned_ref, (side_a_ref, side_b_ref))
 
 
-def total_of(value):
-    return jnp.sum(jnp.sum(value, axis=0, keepdims=True), axis=1, keepdims=True)
-
-
-def last_kernel(
+def sums_kernel(
+    product_ref,
+    weights_ref,
+    side_a_ref,
+    side_b_ref,
+    from_a_ref,
+    from_b_ref,
+    first_a_ref,
+    first_b_ref,
+    field_ref,
+    image_ref,
+    sums_ref,
+):
+    faces = side_a_ref.shape[0]
+    field = field_ref[...]
+    image = image_ref[...]
+    product = product_ref[...]
+    with_field = jnp.sum(field * product, axis=0, keepdims=True)
+    with_image = jnp.sum(image * product, axis=0, keepdims=True)
+    for place, own, arrived, first in (
+        (slice(0, faces), side_a_ref, from_a_ref, first_a_ref),
+        (slice(faces, 2 * faces), side_b_ref, from_b_ref, first_b_ref),
+    ):
+        lam = weights_ref[place, :] * (own[...] - arrived[...])
+        with_field += jnp.sum(lam * first[:faces, :], axis=0, keepdims=True)
+        with_image += jnp.sum(lam * own[...], axis=0, keepdims=True)
+    lane = lax.broadcasted_iota(jnp.int32, (1, LANES), 1)
+    row = jnp.zeros((1, LANES), F32)
+    for k, part in enumerate(
+        (
+            jnp.sum(field * field, axis=0, keepdims=True),
+            jnp.sum(field * image, axis=0, keepdims=True),
+            jnp.sum(image * image, axis=0, keepdims=True),
+            with_field,
+            with_image,
+        )
+    ):
+        row = jnp.where(lane == k, jnp.sum(part, axis=1, keepdims=True), row)
+    sums_ref[...] = jnp.broadcast_to(row[None], sums_ref.shape)
+
+
+def second_kernel(
     size,
     aligned_ref,
     product_ref,
@@ -254,32 +291,17 @@
     side_b_ref,
     from_a_ref,
     from_b_ref,
-    field_ref,
-    image_ref,
     second_ref,
-    sums_ref,
 ):
-    block_rows = product_ref.shape[0]
-    coupled = spread_jumps(
-        block_rows,
+    second_ref[...] = product_ref[...]
+    second_ref[:, :size] = second_ref[:, :size] + spread_jumps(
+        product_ref.shape[0],
         size,
         aligned_ref,
         weights_ref,
         (side_a_ref, side_b_ref),
         (from_a_ref, from_b_ref),
     )
-    second_ref[...] = product_ref[...]
-    second_ref[:, :size] = second_ref[:, :size] + coupled
-    field = field_ref[...]
-    image = image_ref[...]
-    second = second_ref[...]
-    lane = lax.broadcasted_iota(jnp.int32, (1, LANES), 1)
-    row = jnp.zeros((1, LANES), F32)
-    for k, product in enumerate(
-        (field * field, field * image, image * image, field * second, image * second)
-    ):
-        row = jnp.where(lane == k, total_of(product), row)
-    sums_ref[...] = jnp.broadcast_to(row[None], sums_ref.shape)
 
 
 def final_kernel(field_ref, image_ref, second_ref, sums_ref, solution_ref, residual_ref):
@@ -373,15 +395,18 @@
     )
     from_a = swap(side_a, 1)
     from_b = swap(side_b, 0)
-    second, sums = call(
-        functools.partial(last_kernel, size),
-        [shape(block_rows), jax.ShapeDtypeStruct((devices, 1, LANES), F32)],
-        [
-            (value, VMEM)
-            for value in (
-                aligned, stiff(image), weights, side_a, side_b, from_a, from_b, padded, image
-            )
-        ],
+    product = stiff(image)
+    jumps = (weights, side_a, side_b, from_a, from_b)
+    (sums,) = call(
+        sums_kernel,
+        [jax.ShapeDtypeStruct((devices, 1, LANES), F32)],
+        [(value, VMEM) for value in (product, *jumps, to_a, to_b, padded, image)],
+    )
+    (second,) = call(
+        functools.partial(second_kernel, size),
+        [shape(block_rows)],
+        [(value, VMEM) for value in (aligned, product, *jumps)],
+        flops=1_000_000_000,
     )
     sums = lax.all_to_all(sums, ("sub", "blk"), split_axis=0, concat_axis=0, tiled=True)
     solution_field, residual = call(

time: 43.4 us -> 42 us (0.968)
  blocking collectives: 11.1 us -> 0 us
  waiting for transfers between devices: 3.18 us -> 8.09 us
  starting transfers between devices: 12.3 us -> 16.5 us
  Pallas kernels: 10.5 us -> 11.2 us
    all_to_all x1 -> x0, blocking collectives: 11.1 us -> none  [on_device(): lax.all_to_all(sums, ('sub', 'blk'), split_axis=0, concat_axis=0, tiled=T...]
    all_to_all x0 -> x1, waiting for transfers between devices: none -> 4.91 us  [on_device(): lax.all_to_all(sums, ('sub', 'blk'), split_axis=0, concat_axis=0, tiled=T...]
    all_to_all x0 -> x1, starting transfers between devices: none -> 4.15 us  [on_device(): lax.all_to_all(sums, ('sub', 'blk'), split_axis=0, concat_axis=0, tiled=T...]
    pallas_call x7 -> x8, Pallas kernels: 10.5 us -> 11.2 us  [call(): pl.pallas_call(body, out_shape=outs, in_specs=[spec for _, spec in inputs...]
  transfers between devices with their start and end apart: 5 -> 6, of which waited for: 3 -> 4; matrix products, arithmetic and copies ran while one was open for 5% -> 6% of each run, Pallas kernels for 10% -> 16%
where the time goes in v4:
time: 42 us; the launch traced here: 41.6 us
  starting transfers between devices  16.5 us (39%)
  Pallas kernels  11.2 us (27%)
  waiting for transfers between devices  8.09 us (19%)
  local copies, waits for them, and re-layouts  5.16 us (12%)
  between operations  0.73 us (2%)
    pallas_call x8, Pallas kernels, call(): pl.pallas_call(body, out_shape=outs, in_specs=[spec for _, spec in inputs...  11.2 us
    ppermute x4, starting transfers between devices, swap(): return lax.ppermute(value, 'sub', pairs)  8.09 us
    all_to_all x1, waiting for transfers between devices, on_device(): lax.all_to_all(sums, ('sub', 'blk'), split_axis=0, concat_axis=0, tiled=T...  4.91 us
    all_to_all x1, starting transfers between devices, on_device(): lax.all_to_all(mortar_weight[0, 0], 'blk', split_axis=0, concat_axis=0, t...  4.22 us
    all_to_all x1, starting transfers between devices, on_device(): lax.all_to_all(sums, ('sub', 'blk'), split_axis=0, concat_axis=0, tiled=T...  4.15 us
    ppermute x4, waiting for transfers between devices, swap(): return lax.ppermute(value, 'sub', pairs)  3.17 us
    unnamed x10, local copies, waits for them, and re-layouts  2.87 us
    another operation x1, local copies, waits for them, and re-layouts, on_device(): blocks = stored.reshape(stored.shape[0], size, size)  2.29 us
  transfers between devices with their start and end apart: 6, of which 4 were waited for; matrix products, arithmetic and copies ran while one was open for 6% of the time, Pallas kernels for 16%

profile of v4, /device:TPU:0, one launch (start us, length us, event | category | flops | bytes accessed | tf_op | source)
XLA Modules:
  0.0 41.6 jit_solution(12167149601564584282)
XLA Ops:
  0.6 4.2 %all-to-all-start = ((f32[4,16,128]{2,1,0:T(8,128)}), f32[4,16,128]{2,1,0:T(8,128)S(1)}, u32[]{:S(2)}, u32[]{:S(2)}) async-start(f32[4,16,128]{2,1,0:T(8,128)} %bitcast.24), calls=%async_computation | async-start | bytes 65536 | tf_op jit(solution)/shard_map/all_to_all | solution.py:355
  4.9 0.8 %copy-done = s32[1,1,128,128]{3,2,1,0:T(8,128)S(1)} copy-done((s32[1,1,128,128]{3,2,1,0:T(8,128)S(1)}, s32[1,1,128,128]{3,2,1,0:T(8,128)}, u32[]{:S(2)}) %copy-start) | copy-done | bytes 65560
  5.7 0.7 %copy-done.1 = f32[1,1,96,32]{2,3,1,0:T(8,128)S(1)} copy-done((f32[1,1,96,32]{2,3,1,0:T(8,128)S(1)}, f32[1,1,96,32]{2,3,1,0:T(8,128)}, u32[]{:S(2)}) %copy-start.1) | copy-done | bytes 12312
  6.4 0.7 %copy-done.3 = s32[1,1,64]{2,1,0:T(1,128)S(1)} copy-done((s32[1,1,64]{2,1,0:T(1,128)S(1)}, s32[1,1,64]{2,1,0:T(1,128)}, u32[]{:S(2)}) %copy-start.3) | copy-done | bytes 280
  7.1 0.7 %copy-done.4 = s32[1,1,4]{2,1,0:T(1,128)S(1)} copy-done((s32[1,1,4]{2,1,0:T(1,128)S(1)}, s32[1,1,4]{2,1,0:T(1,128)}, u32[]{:S(2)}) %copy-start.4) | copy-done | bytes 40
  7.7 1.5 %shard_map.86 = (s32[128,128]{1,0:T(8,128)S(1)}, f32[32,128]{1,0:T(8,128)S(1)}, f32[64,64]{1,0:T(8,128)S(1)}, f32[64,128]{1,0:T(8,128)S(1)}, f32[64,128]{1,0:T(8,128)S(1)}) custom-call(s32[64]{0:T(128)S(1)} %bitcast.22, s32[4]{0:T(128)S(1)} %bitcast.23, s32[128,128]{1,0:T(8,128)S(1)} %bitcast.18, f32[32,96]{1,0:T(8,128)S(1)} %bitcast.19), custom_call_target="tpu_custom_call" | custom-call | flops 1000000 | bytes 1000000 | tf_op jit(solution)/shard_map/pallas_call | solution.py:21
  9.3 0.0 all-to-all-done
  9.3 0.1 shard_map.88
  9.4 5.1 %collective-permute-start = (f32[128,128]{1,0:T(8,128)S(1)}, f32[128,128]{1,0:T(8,128)S(1)}, u32[]{:S(2)}, u32[]{:S(2)}) collective-permute-start(f32[128,128]{1,0:T(8,128)S(1)} %get-tuple-element.20.to_a_ref.first_a_ref), channel_id=1, source_target_pairs={{4,8},{8,4},{12,16},{16,12},{20,24},{24,20},{28,0},{0,28},{5,9},{9... | collective-permute-start | bytes 196616 | tf_op jit(solution)/shard_map/ppermute | solution.py:338
  14.6 2.3 %reshape_squeeze.3.blocks_ref = bf16[48,96,96]{2,1,0:T(8,128)(2,1)S(1)} reshape(bf16[1,1,48,9216]{3,2,1,0:T(8,128)(2,1)} %param.8) | data formatting | bytes 1769472 | tf_op jit(solution)/shard_map/reshape;squeeze | solution.py:347
  16.9 1.4 %shard_map.87.product_ref = f32[32,128]{1,0:T(8,128)S(1)} custom-call(s32[2,16]{1,0:T(2,128)S(1)} %bitcast.20, bf16[48,96,96]{2,1,0:T(8,128)(2,1)S(1)} %reshape_squeeze.3.blocks_ref, f32[32,128]{1,0:T(8,128)S(1)} %get-tuple-element.15.field_ref), custom_call_target="tpu_custom_call" | custom-call | flops 1000000 | bytes 1000000 | tf_op jit(solution)/shard_map/pallas_call | solution.py:21
  18.3 0.0 collective-permute-done.from_a_ref
  18.3 0.5 %collective-permute-done.1.from_b_ref = f32[128,128]{1,0:T(8,128)S(1)} collective-permute-done((f32[128,128]{1,0:T(8,128)S(1)}, f32[128,128]{1,0:T(8,128)S(1)}, u32[]{:S(2)}, u32[]{:S(2)}) %collective-permute-start.1) | collective-permute-done | bytes 65568 | tf_op jit(solution)/shard_map/ppermute | solution.py:338
  18.8 3.0 %shard_map.89 = (f32[32,128]{1,0:T(8,128)S(1)}, f32[128,128]{1,0:T(8,128)S(1)}, f32[64,128]{1,0:T(8,128)S(1)}, f32[64,128]{1,0:T(8,128)S(1)}) custom-call(s32[128,128]{1,0:T(8,128)S(1)} %get-tuple-element.16.aligned_ref, f32[32,128]{1,0:T(8,128)S(1)} %shard_map.87.product_ref, f32[128,128]{1,0:T(8,128)S(1)} %get-tuple-element.20.to_a_ref.first_a_ref, ...), custom_call_target="tpu_custom_call" | custom-call | flops 1000000 | bytes 1000000 | tf_op jit(solution)/shard_map/pallas_call | solution.py:21
  21.9 3.0 %collective-permute-start.2 = (f32[64,128]{1,0:T(8,128)S(1)}, f32[64,128]{1,0:T(8,128)S(1)}, u32[]{:S(2)}, u32[]{:S(2)}) collective-permute-start(f32[64,128]{1,0:T(8,128)S(1)} %get-tuple-element.24.side_a_ref), channel_id=1, source_target_pairs={{4,8},{8,4},{12,16},{16,12},{20,24},{24,20},{28,0},{0,28},{5,9},{9... | collective-permute-start | bytes 98312 | tf_op jit(solution)/shard_map/ppermute | solution.py:338
  24.8 0.0 collective-permute-start.3
  24.8 1.4 %shard_map.90.product_ref = f32[32,128]{1,0:T(8,128)S(1)} custom-call(s32[2,16]{1,0:T(2,128)S(1)} %bitcast.21, bf16[48,96,96]{2,1,0:T(8,128)(2,1)S(1)} %reshape_squeeze.3.blocks_ref, f32[32,128]{1,0:T(8,128)S(1)} %get-tuple-element.22.field_ref.image_ref), custom_call_target="tpu_custom_call" | custom-call | flops 1000000 | bytes 1000000 | tf_op jit(solution)/shard_map/pallas_call | solution.py:21
  26.2 2.3 %collective-permute-done.2.from_a_ref = f32[64,128]{1,0:T(8,128)S(1)} collective-permute-done((f32[64,128]{1,0:T(8,128)S(1)}, f32[64,128]{1,0:T(8,128)S(1)}, u32[]{:S(2)}, u32[]{:S(2)}) %collective-permute-start.2) | collective-permute-done | bytes 32800 | tf_op jit(solution)/shard_map/ppermute | solution.py:338
  28.5 0.3 collective-permute-done.3.from_b_ref
  28.9 0.7 %shard_map.92 = f32[32,1,128]{2,1,0:T(1,128)} custom-call(f32[32,128]{1,0:T(8,128)S(1)} %shard_map.90.product_ref, f32[128,128]{1,0:T(8,128)S(1)} %get-tuple-element.23.weights_ref, f32[64,128]{1,0:T(8,128)S(1)} %get-tuple-element.24.side_a_ref, f32[64,128]{1,0:T(8,128)S(1)} %get-tuple-element.25.side_b_ref, ...), custom_call_target="tpu_custom_call" | custom-call | flops 1000000 | bytes 1000000 | tf_op jit(solution)/shard_map/pallas_call | solution.py:21
  29.6 4.1 %all-to-all-start.1 = ((f32[32,1,128]{2,1,0:T(1,128)}), f32[32,1,128]{2,1,0:T(1,128)S(1)}, u32[]{:S(2)}, u32[]{:S(2)}) async-start(f32[32,1,128]{2,1,0:T(1,128)} %shard_map.92), calls=%async_computation.1 | async-start | bytes 32768 | tf_op jit(solution)/shard_map/all_to_all | solution.py:411
  33.8 2.2 %shard_map.91.second_ref = f32[32,128]{1,0:T(8,128)S(1)} custom-call(s32[128,128]{1,0:T(8,128)S(1)} %get-tuple-element.16.aligned_ref, f32[32,128]{1,0:T(8,128)S(1)} %shard_map.90.product_ref, f32[128,128]{1,0:T(8,128)S(1)} %get-tuple-element.23.weights_ref, f32[64,128]{1,0:T(8,128)S(1)} %get-tuple-element.24.side_a_ref, ...), custom_call_target="tpu_custom_call" | custom-call | flops 1000000000 | bytes 1000000 | tf_op jit(solution)/shard_map/pallas_call | solution.py:21
  35.9 4.9 %all-to-all-done.1.sums_ref = f32[32,1,128]{2,1,0:T(1,128)S(1)} async-done(((f32[32,1,128]{2,1,0:T(1,128)}), f32[32,1,128]{2,1,0:T(1,128)S(1)}, u32[]{:S(2)}, u32[]{:S(2)}) %all-to-all-start.1) | async-done | bytes 16416 | tf_op jit(solution)/shard_map/all_to_all | solution.py:411
  40.8 0.7 %shard_map.93 = (f32[32,96]{1,0:T(8,128)}, f32[32,96]{1,0:T(8,128)}) custom-call(f32[32,128]{1,0:T(8,128)S(1)} %get-tuple-element.15.field_ref, f32[32,128]{1,0:T(8,128)S(1)} %get-tuple-element.22.field_ref.image_ref, f32[32,128]{1,0:T(8,128)S(1)} %shard_map.91.second_ref, f32[32,1,128]{2,1,0:T(1,128)S(1)} %all-to-all-done.1.sums_ref), custom_call_target="tpu_custom_call" | custom-call | flops 1000000 | bytes 1000000 | tf_op jit(solution)/shard_map/pallas_call | solution.py:21
  (7 shorter events, 0.0 us)
Async XLA Ops:
  0.6 16.2 %copy-start.2 = (s32[1,1,2,16]{3,2,1,0:T(2,128)S(1)}, s32[1,1,2,16]{3,2,1,0:T(2,128)}, u32[]{:S(2)}) copy-start(s32[1,1,2,16]{3,2,1,0:T(2,128)} %param.9) | copy-start | bytes 388
  0.6 8.6 %all-to-all-start = ((f32[4,16,128]{2,1,0:T(8,128)}), f32[4,16,128]{2,1,0:T(8,128)S(1)}, u32[]{:S(2)}, u32[]{:S(2)}) async-start(f32[4,16,128]{2,1,0:T(8,128)} %bitcast.24), calls=%async_computation | async-start | bytes 65536 | tf_op jit(solution)/shard_map/all_to_all | solution.py:355
  4.9 0.8 %copy-start = (s32[1,1,128,128]{3,2,1,0:T(8,128)S(1)}, s32[1,1,128,128]{3,2,1,0:T(8,128)}, u32[]{:S(2)}) copy-start(s32[1,1,128,128]{3,2,1,0:T(8,128)} %param.10) | copy-start | bytes 196612
  5.7 0.7 %copy-start.1 = (f32[1,1,96,32]{2,3,1,0:T(8,128)S(1)}, f32[1,1,96,32]{2,3,1,0:T(8,128)}, u32[]{:S(2)}) copy-start(f32[1,1,96,32]{2,3,1,0:T(8,128)} %param.7) | copy-start | bytes 36868
  6.4 0.7 %copy-start.3 = (s32[1,1,64]{2,1,0:T(1,128)S(1)}, s32[1,1,64]{2,1,0:T(1,128)}, u32[]{:S(2)}) copy-start(s32[1,1,64]{2,1,0:T(1,128)} %param.11) | copy-start | bytes 772
  7.1 0.7 %copy-start.4 = (s32[1,1,4]{2,1,0:T(1,128)S(1)}, s32[1,1,4]{2,1,0:T(1,128)}, u32[]{:S(2)}) copy-start(s32[1,1,4]{2,1,0:T(1,128)} %param.12) | copy-start | bytes 52
  9.4 8.8 %collective-permute-start = (f32[128,128]{1,0:T(8,128)S(1)}, f32[128,128]{1,0:T(8,128)S(1)}, u32[]{:S(2)}, u32[]{:S(2)}) collective-permute-start(f32[128,128]{1,0:T(8,128)S(1)} %get-tuple-element.20.to_a_ref.first_a_ref), channel_id=1, source_target_pairs={{4,8},{8,4},{12,16},{16,12},{20,24},{24,20},{28,0},{0,28},{5,9},{9... | collective-permute-start | bytes 196616 | tf_op jit(solution)/shard_map/ppermute | solution.py:338
  14.5 4.3 %collective-permute-start.1 = (f32[128,128]{1,0:T(8,128)S(1)}, f32[128,128]{1,0:T(8,128)S(1)}, u32[]{:S(2)}, u32[]{:S(2)}) collective-permute-start(f32[128,128]{1,0:T(8,128)S(1)} %get-tuple-element.21.to_b_ref.first_b_ref), channel_id=1, source_target_pairs={{0,4},{4,0},{8,12},{12,8},{16,20},{20,16},{24,28},{28,24},{1,5},{5... | collective-permute-start | bytes 196616 | tf_op jit(solution)/shard_map/ppermute | solution.py:338
  21.9 6.7 %collective-permute-start.2 = (f32[64,128]{1,0:T(8,128)S(1)}, f32[64,128]{1,0:T(8,128)S(1)}, u32[]{:S(2)}, u32[]{:S(2)}) collective-permute-start(f32[64,128]{1,0:T(8,128)S(1)} %get-tuple-element.24.side_a_ref), channel_id=1, source_target_pairs={{4,8},{8,4},{12,16},{16,12},{20,24},{24,20},{28,0},{0,28},{5,9},{9... | collective-permute-start | bytes 98312 | tf_op jit(solution)/shard_map/ppermute | solution.py:338
  24.8 4.1 %collective-permute-start.3 = (f32[64,128]{1,0:T(8,128)S(1)}, f32[64,128]{1,0:T(8,128)S(1)}, u32[]{:S(2)}, u32[]{:S(2)}) collective-permute-start(f32[64,128]{1,0:T(8,128)S(1)} %get-tuple-element.25.side_b_ref), channel_id=1, source_target_pairs={{0,4},{4,0},{8,12},{12,8},{16,20},{20,16},{24,28},{28,24},{1,5},{5... | collective-permute-start | bytes 98312 | tf_op jit(solution)/shard_map/ppermute | solution.py:338
  29.6 11.2 %all-to-all-start.1 = ((f32[32,1,128]{2,1,0:T(1,128)}), f32[32,1,128]{2,1,0:T(1,128)S(1)}, u32[]{:S(2)}, u32[]{:S(2)}) async-start(f32[32,1,128]{2,1,0:T(1,128)} %shard_map.92), calls=%async_computation.1 | async-start | bytes 32768 | tf_op jit(solution)/shard_map/all_to_all | solution.py:411

commit v5 on v4

--- a/solution.py
+++ b/solution.py
@@ -10,7 +10,6 @@
 LANES = 128
 SUBLANES = 8
 VMEM = pl.BlockSpec(memory_space=pltpu.VMEM)
-HBM = pl.BlockSpec(memory_space=pltpu.HBM)
 SMEM = pl.BlockSpec(memory_space=pltpu.SMEM)
 PARAMS = pltpu.CompilerParams(vmem_limit_bytes=32 * 1024 * 1024)
 F32 = jnp.float32
@@ -72,63 +71,51 @@
     return lax.div(index, block_rows), lax.rem(index, block_rows)
 
 
+def one_hot(place, count):
+    row = lax.broadcasted_iota(jnp.int32, (count, place.shape[1]), 0)
+    return jnp.where(row == place, 1.0, 0.0)
+
+
+def exact_dot(left, right):
+    return jnp.dot(
+        left, right, precision=lax.Precision.HIGHEST, preferred_element_type=F32
+    )
+
+
 def first_kernel(
-    partner_hbm,
-    owner_hbm,
-    rows_hbm,
-    field_hbm,
-    aligned_ref,
-    padded_ref,
-    chosen_ref,
-    side_a_ref,
-    side_b_ref,
-    partner_ref,
-    owner_ref,
-    rows_ref,
-    field_ref,
-    sems,
+    groups, packed_ref, aligned_ref, padded_ref, chosen_ref, side_a_ref, side_b_ref
 ):
-    copies = [
-        pltpu.make_async_copy(source, target, sems.at[k])
-        for k, (source, target) in enumerate(
-            (
-                (partner_hbm, partner_ref),
-                (owner_hbm, owner_ref),
-                (rows_hbm, rows_ref),
-                (field_hbm, field_ref),
-            )
-        )
-    ]
-    for copy in copies:
-        copy.start()
     faces = side_a_ref.shape[0]
-    per_group = faces // owner_ref.shape[0]
-    size = field_ref.shape[1]
+    block_rows = padded_ref.shape[0]
+    per_group = faces // groups
     parity = lax.rem(lax.axis_index("sub"), 2)
     east = pl.multiple_of((1 - parity) * faces, faces)
     west = pl.multiple_of(parity * faces, faces)
-    padded_ref[...] = jnp.zeros_like(padded_ref)
-    lane = lax.broadcasted_iota(jnp.int32, (1, chosen_ref.shape[1]), 1)
-    for copy in copies:
-        copy.wait()
-    aligned_ref[pl.ds(west, faces), :] = rows_ref[faces:, :]
-    for f in range(faces):
-        place = partner_ref[f]
-        source = owner_ref[f // per_group] * per_group + f % per_group
-        aligned_ref[pl.ds(east + place, 1), :] = rows_ref[f : f + 1, :]
-        chosen_ref[pl.ds(place, 1), :] = jnp.where(lane == source, 1.0, 0.0)
-    padded_ref[:, :size] = field_ref[...]
+    padded_ref[...] = packed_ref[2 * faces : 2 * faces + block_rows, :]
+    tail = packed_ref[2 * faces + block_rows :, :].astype(jnp.int32)
+    partner = tail[:1, :faces]
+    face = lax.broadcasted_iota(jnp.int32, (1, faces), 1)
+    source = jnp.zeros((1, faces), jnp.int32)
+    for g in range(groups):
+        inside = face - g * per_group
+        source = jnp.where(
+            (inside >= 0) & (inside < per_group), tail[1:2, g : g + 1] * per_group + inside, source
+        )
+    order = one_hot(partner, faces)
+    aligned_ref[pl.ds(west, faces), :] = packed_ref[faces : 2 * faces, :].astype(jnp.int32)
+    aligned_ref[pl.ds(east, faces), :] = exact_dot(order, packed_ref[:faces, :]).astype(jnp.int32)
+    chosen_ref[...] = lax.dot_general(
+        order.astype(BF16),
+        one_hot(source, faces).astype(BF16),
+        (((1,), (1,)), ((), ())),
+        preferred_element_type=F32,
+    )
     gather_traces(padded_ref[...], aligned_ref, (side_a_ref, side_b_ref))
 
 
 def message_kernel(held_ref, chosen_ref, side_a_ref, side_b_ref, to_a_ref, to_b_ref):
     faces = side_a_ref.shape[0]
-    own = jnp.dot(
-        chosen_ref[...],
-        held_ref[...],
-        precision=lax.Precision.HIGHEST,
-        preferred_element_type=F32,
-    )
+    own = exact_dot(chosen_ref[...], held_ref[...])
     for side, target in ((side_a_ref, to_a_ref), (side_b_ref, to_b_ref)):
         target[:faces, :] = side[...]
         target[faces:, :] = own
@@ -353,8 +340,16 @@
     devices = lax.axis_size("sub") * lax.axis_size("blk")
 
     held = lax.all_to_all(mortar_weight[0, 0], "blk", split_axis=0, concat_axis=0, tiled=True)
+    last = 2 * faces + block_rows
+
+    def placed(value, first):
+        below = last + SUBLANES - first - value.shape[0]
+        return jnp.pad(value, ((first, below), (0, LANES - value.shape[1])))
+
+    indices = placed(rows, 0) + placed(partner_face[0], last) + placed(owner_list[0], last + 1)
+    packed = indices.astype(F32) + placed(field, 2 * faces)
     aligned, padded, chosen, side_a, side_b = call(
-        first_kernel,
+        functools.partial(first_kernel, owners.shape[0]),
         [
             shape(2 * faces, jnp.int32),
             shape(block_rows),
@@ -362,14 +357,7 @@
             shape(faces),
             shape(faces),
         ],
-        [(partner, HBM), (owners, HBM), (rows, HBM), (field, HBM)],
-        scratch=[
-            pltpu.SMEM(partner.shape, jnp.int32),
-            pltpu.SMEM(owners.shape, jnp.int32),
-            pltpu.VMEM(rows.shape, jnp.int32),
-            pltpu.VMEM(field.shape, F32),
-            pltpu.SemaphoreType.DMA((4,)),
-        ],
+        [(packed, VMEM)],
     )
     to_a, to_b = call(
         message_kernel,

time: 42 us -> 39.9 us (0.950)
  local copies, waits for them, and re-layouts: 5.16 us -> 2.3 us
  waiting for transfers between devices: 8.09 us -> 10.2 us
  starting transfers between devices: 16.5 us -> 14.8 us
  other arithmetic: 0 us -> 0.9 us
  Pallas kernels: 11.2 us -> 10.7 us
    unnamed x10 -> x2, local copies, waits for them, and re-layouts: 2.87 us -> 0.01 us
    all_to_all x1, waiting for transfers between devices: 0.01 us -> 1.95 us  [on_device(): lax.all_to_all(mortar_weight[0, 0], 'blk', split_axis=0, concat_axis=0, t...]
    all_to_all x1, starting transfers between devices: 4.15 us -> 2.72 us  [on_device(): lax.all_to_all(sums, ('sub', 'blk'), split_axis=0, concat_axis=0, tiled=T...]
    add x0 -> x1, other arithmetic: none -> 0.9 us  [on_device(): packed = indices.astype(F32) + placed(field, 2 * faces)]
    pallas_call x8, Pallas kernels: 11.2 us -> 10.7 us  [call(): pl.pallas_call(body, out_shape=outs, in_specs=[spec for _, spec in inputs...]
  transfers between devices with their start and end apart: 6 -> 6, of which waited for: 4 -> 5; matrix products, arithmetic and copies ran while one was open for 6% -> 8% of each run, Pallas kernels for 16% -> 15%
where the time goes in v5:
time: 39.9 us; the launch traced here: 39.6 us
  starting transfers between devices  14.8 us (37%)
  Pallas kernels  10.7 us (27%)
  waiting for transfers between devices  10.2 us (26%)
  local copies, waits for them, and re-layouts  2.3 us (6%)
  other arithmetic  0.9 us (2%)
  between operations  0.72 us (2%)
    pallas_call x8, Pallas kernels, call(): pl.pallas_call(body, out_shape=outs, in_specs=[spec for _, spec in inputs...  10.7 us
    ppermute x4, starting transfers between devices, swap(): return lax.ppermute(value, 'sub', pairs)  7.85 us
    all_to_all x1, waiting for transfers between devices, on_device(): lax.all_to_all(sums, ('sub', 'blk'), split_axis=0, concat_axis=0, tiled=T...  4.91 us
    all_to_all x1, starting transfers between devices, on_device(): lax.all_to_all(mortar_weight[0, 0], 'blk', split_axis=0, concat_axis=0, t...  4.22 us
    ppermute x4, waiting for transfers between devices, swap(): return lax.ppermute(value, 'sub', pairs)  3.37 us
    all_to_all x1, starting transfers between devices, on_device(): lax.all_to_all(sums, ('sub', 'blk'), split_axis=0, concat_axis=0, tiled=T...  2.72 us
    another operation x1, local copies, waits for them, and re-layouts, on_device(): blocks = stored.reshape(stored.shape[0], size, size)  2.29 us
    all_to_all x1, waiting for transfers between devices, on_device(): lax.all_to_all(mortar_weight[0, 0], 'blk', split_axis=0, concat_axis=0, t...  1.95 us
  transfers between devices with their start and end apart: 6, of which 5 were waited for; matrix products, arithmetic and copies ran while one was open for 8% of the time, Pallas kernels for 15%

profile of v5, /device:TPU:0, one launch (start us, length us, event | category | flops | bytes accessed | tf_op | source)
XLA Modules:
  0.0 39.6 jit_solution(18237534924840746879)
XLA Ops:
  0.6 4.2 %all-to-all-start = ((f32[4,16,128]{2,1,0:T(8,128)}), f32[4,16,128]{2,1,0:T(8,128)S(1)}, u32[]{:S(2)}, u32[]{:S(2)}) async-start(f32[4,16,128]{2,1,0:T(8,128)} %bitcast.21), calls=%async_computation | async-start | bytes 65536 | tf_op jit(solution)/shard_map/all_to_all | solution.py:342
  4.8 0.9 %pad_add_fusion.packed_ref = f32[168,128]{1,0:T(8,128)S(1)} fusion(f32[32,96]{1,0:T(8,128)} %bitcast.22, s32[1,4]{1,0:T(1,128)} %bitcast.23, s32[1,64]{1,0:T(1,128)} %bitcast.24, s32[128,128]{1,0:T(8,128)} %bitcast.20), kind=kLoop, calls=%fused_computation | loop fusion | flops 86016 | bytes 164112 | tf_op jit(solution)/shard_map/add | solution.py:350
  5.8 0.0 copy-start
  5.8 1.1 %shard_map.86 = (s32[128,128]{1,0:T(8,128)S(1)}, f32[32,128]{1,0:T(8,128)S(1)}, f32[64,64]{1,0:T(8,128)S(1)}, f32[64,128]{1,0:T(8,128)S(1)}, f32[64,128]{1,0:T(8,128)S(1)}) custom-call(f32[168,128]{1,0:T(8,128)S(1)} %pad_add_fusion.packed_ref), custom_call_target="tpu_custom_call" | custom-call | flops 1000000 | bytes 1000000 | tf_op jit(solution)/shard_map/pallas_call | solution.py:20
  6.8 1.9 %all-to-all-done = f32[4,16,128]{2,1,0:T(8,128)S(1)} async-done(((f32[4,16,128]{2,1,0:T(8,128)}), f32[4,16,128]{2,1,0:T(8,128)S(1)}, u32[]{:S(2)}, u32[]{:S(2)}) %all-to-all-start) | async-done | bytes 32800 | tf_op jit(solution)/shard_map/all_to_all | solution.py:342
  8.8 0.1 shard_map.88
  8.9 5.1 %collective-permute-start = (f32[128,128]{1,0:T(8,128)S(1)}, f32[128,128]{1,0:T(8,128)S(1)}, u32[]{:S(2)}, u32[]{:S(2)}) collective-permute-start(f32[128,128]{1,0:T(8,128)S(1)} %get-tuple-element.20.to_a_ref.first_a_ref), channel_id=1, source_target_pairs={{4,8},{8,4},{12,16},{16,12},{20,24},{24,20},{28,0},{0,28},{5,9},{9... | collective-permute-start | bytes 196616 | tf_op jit(solution)/shard_map/ppermute | solution.py:325
  14.0 0.0 collective-permute-start.1
  14.0 2.3 %reshape_squeeze.3.blocks_ref = bf16[48,96,96]{2,1,0:T(8,128)(2,1)S(1)} reshape(bf16[1,1,48,9216]{3,2,1,0:T(8,128)(2,1)} %param.8) | data formatting | bytes 1769472 | tf_op jit(solution)/shard_map/reshape;squeeze | solution.py:334
  16.3 0.0 copy-done
  16.3 1.4 %shard_map.87.product_ref = f32[32,128]{1,0:T(8,128)S(1)} custom-call(s32[2,16]{1,0:T(2,128)S(1)} %bitcast.18, bf16[48,96,96]{2,1,0:T(8,128)(2,1)S(1)} %reshape_squeeze.3.blocks_ref, f32[32,128]{1,0:T(8,128)S(1)} %get-tuple-element.15.field_ref), custom_call_target="tpu_custom_call" | custom-call | flops 1000000 | bytes 1000000 | tf_op jit(solution)/shard_map/pallas_call | solution.py:20
  17.8 0.0 collective-permute-done.from_a_ref
  17.8 0.5 %collective-permute-done.1.from_b_ref = f32[128,128]{1,0:T(8,128)S(1)} collective-permute-done((f32[128,128]{1,0:T(8,128)S(1)}, f32[128,128]{1,0:T(8,128)S(1)}, u32[]{:S(2)}, u32[]{:S(2)}) %collective-permute-start.1) | collective-permute-done | bytes 65568 | tf_op jit(solution)/shard_map/ppermute | solution.py:325
  18.3 3.0 %shard_map.89 = (f32[32,128]{1,0:T(8,128)S(1)}, f32[128,128]{1,0:T(8,128)S(1)}, f32[64,128]{1,0:T(8,128)S(1)}, f32[64,128]{1,0:T(8,128)S(1)}) custom-call(s32[128,128]{1,0:T(8,128)S(1)} %get-tuple-element.16.aligned_ref, f32[32,128]{1,0:T(8,128)S(1)} %shard_map.87.product_ref, f32[128,128]{1,0:T(8,128)S(1)} %get-tuple-element.20.to_a_ref.first_a_ref, ...), custom_call_target="tpu_custom_call" | custom-call | flops 1000000 | bytes 1000000 | tf_op jit(solution)/shard_map/pallas_call | solution.py:20
  21.3 2.8 %collective-permute-start.2 = (f32[64,128]{1,0:T(8,128)S(1)}, f32[64,128]{1,0:T(8,128)S(1)}, u32[]{:S(2)}, u32[]{:S(2)}) collective-permute-start(f32[64,128]{1,0:T(8,128)S(1)} %get-tuple-element.24.side_a_ref), channel_id=1, source_target_pairs={{4,8},{8,4},{12,16},{16,12},{20,24},{24,20},{28,0},{0,28},{5,9},{9... | collective-permute-start | bytes 98312 | tf_op jit(solution)/shard_map/ppermute | solution.py:325
  24.1 0.0 collective-permute-start.3
  24.1 1.4 %shard_map.90.product_ref = f32[32,128]{1,0:T(8,128)S(1)} custom-call(s32[2,16]{1,0:T(2,128)S(1)} %bitcast.19, bf16[48,96,96]{2,1,0:T(8,128)(2,1)S(1)} %reshape_squeeze.3.blocks_ref, f32[32,128]{1,0:T(8,128)S(1)} %get-tuple-element.22.field_ref.image_ref), custom_call_target="tpu_custom_call" | custom-call | flops 1000000 | bytes 1000000 | tf_op jit(solution)/shard_map/pallas_call | solution.py:20
  25.5 2.5 %collective-permute-done.2.from_a_ref = f32[64,128]{1,0:T(8,128)S(1)} collective-permute-done((f32[64,128]{1,0:T(8,128)S(1)}, f32[64,128]{1,0:T(8,128)S(1)}, u32[]{:S(2)}, u32[]{:S(2)}) %collective-permute-start.2) | collective-permute-done | bytes 32800 | tf_op jit(solution)/shard_map/ppermute | solution.py:325
  28.0 0.3 collective-permute-done.3.from_b_ref
  28.4 0.7 %shard_map.92 = f32[32,1,128]{2,1,0:T(1,128)} custom-call(f32[32,128]{1,0:T(8,128)S(1)} %shard_map.90.product_ref, f32[128,128]{1,0:T(8,128)S(1)} %get-tuple-element.23.weights_ref, f32[64,128]{1,0:T(8,128)S(1)} %get-tuple-element.24.side_a_ref, f32[64,128]{1,0:T(8,128)S(1)} %get-tuple-element.25.side_b_ref, ...), custom_call_target="tpu_custom_call" | custom-call | flops 1000000 | bytes 1000000 | tf_op jit(solution)/shard_map/pallas_call | solution.py:20
  29.1 2.7 %all-to-all-start.1 = ((f32[32,1,128]{2,1,0:T(1,128)}), f32[32,1,128]{2,1,0:T(1,128)S(1)}, u32[]{:S(2)}, u32[]{:S(2)}) async-start(f32[32,1,128]{2,1,0:T(1,128)} %shard_map.92), calls=%async_computation.1 | async-start | bytes 32768 | tf_op jit(solution)/shard_map/all_to_all | solution.py:399
  31.8 2.2 %shard_map.91.second_ref = f32[32,128]{1,0:T(8,128)S(1)} custom-call(s32[128,128]{1,0:T(8,128)S(1)} %get-tuple-element.16.aligned_ref, f32[32,128]{1,0:T(8,128)S(1)} %shard_map.90.product_ref, f32[128,128]{1,0:T(8,128)S(1)} %get-tuple-element.23.weights_ref, f32[64,128]{1,0:T(8,128)S(1)} %get-tuple-element.24.side_a_ref, ...), custom_call_target="tpu_custom_call" | custom-call | flops 1000000000 | bytes 1000000 | tf_op jit(solution)/shard_map/pallas_call | solution.py:20
  34.0 4.9 %all-to-all-done.1.sums_ref = f32[32,1,128]{2,1,0:T(1,128)S(1)} async-done(((f32[32,1,128]{2,1,0:T(1,128)}), f32[32,1,128]{2,1,0:T(1,128)S(1)}, u32[]{:S(2)}, u32[]{:S(2)}) %all-to-all-start.1) | async-done | bytes 16416 | tf_op jit(solution)/shard_map/all_to_all | solution.py:399
  38.9 0.7 %shard_map.93 = (f32[32,96]{1,0:T(8,128)}, f32[32,96]{1,0:T(8,128)}) custom-call(f32[32,128]{1,0:T(8,128)S(1)} %get-tuple-element.15.field_ref, f32[32,128]{1,0:T(8,128)S(1)} %get-tuple-element.22.field_ref.image_ref, f32[32,128]{1,0:T(8,128)S(1)} %shard_map.91.second_ref, f32[32,1,128]{2,1,0:T(1,128)S(1)} %all-to-all-done.1.sums_ref), custom_call_target="tpu_custom_call" | custom-call | flops 1000000 | bytes 1000000 | tf_op jit(solution)/shard_map/pallas_call | solution.py:20
Async XLA Ops:
  0.6 8.2 %all-to-all-start = ((f32[4,16,128]{2,1,0:T(8,128)}), f32[4,16,128]{2,1,0:T(8,128)S(1)}, u32[]{:S(2)}, u32[]{:S(2)}) async-start(f32[4,16,128]{2,1,0:T(8,128)} %bitcast.21), calls=%async_computation | async-start | bytes 65536 | tf_op jit(solution)/shard_map/all_to_all | solution.py:342
  5.8 10.6 %copy-start = (s32[1,1,2,16]{3,2,1,0:T(2,128)S(1)}, s32[1,1,2,16]{3,2,1,0:T(2,128)}, u32[]{:S(2)}) copy-start(s32[1,1,2,16]{3,2,1,0:T(2,128)} %param.9) | copy-start | bytes 388
  8.9 8.8 %collective-permute-start = (f32[128,128]{1,0:T(8,128)S(1)}, f32[128,128]{1,0:T(8,128)S(1)}, u32[]{:S(2)}, u32[]{:S(2)}) collective-permute-start(f32[128,128]{1,0:T(8,128)S(1)} %get-tuple-element.20.to_a_ref.first_a_ref), channel_id=1, source_target_pairs={{4,8},{8,4},{12,16},{16,12},{20,24},{24,20},{28,0},{0,28},{5,9},{9... | collective-permute-start | bytes 196616 | tf_op jit(solution)/shard_map/ppermute | solution.py:325
  14.0 4.3 %collective-permute-start.1 = (f32[128,128]{1,0:T(8,128)S(1)}, f32[128,128]{1,0:T(8,128)S(1)}, u32[]{:S(2)}, u32[]{:S(2)}) collective-permute-start(f32[128,128]{1,0:T(8,128)S(1)} %get-tuple-element.21.to_b_ref.first_b_ref), channel_id=1, source_target_pairs={{0,4},{4,0},{8,12},{12,8},{16,20},{20,16},{24,28},{28,24},{1,5},{5... | collective-permute-start | bytes 196616 | tf_op jit(solution)/shard_map/ppermute | solution.py:325
  21.3 6.7 %collective-permute-start.2 = (f32[64,128]{1,0:T(8,128)S(1)}, f32[64,128]{1,0:T(8,128)S(1)}, u32[]{:S(2)}, u32[]{:S(2)}) collective-permute-start(f32[64,128]{1,0:T(8,128)S(1)} %get-tuple-element.24.side_a_ref), channel_id=1, source_target_pairs={{4,8},{8,4},{12,16},{16,12},{20,24},{24,20},{28,0},{0,28},{5,9},{9... | collective-permute-start | bytes 98312 | tf_op jit(solution)/shard_map/ppermute | solution.py:325
  24.1 4.3 %collective-permute-start.3 = (f32[64,128]{1,0:T(8,128)S(1)}, f32[64,128]{1,0:T(8,128)S(1)}, u32[]{:S(2)}, u32[]{:S(2)}) collective-permute-start(f32[64,128]{1,0:T(8,128)S(1)} %get-tuple-element.25.side_b_ref), channel_id=1, source_target_pairs={{0,4},{4,0},{8,12},{12,8},{16,20},{20,16},{24,28},{28,24},{1,5},{5... | collective-permute-start | bytes 98312 | tf_op jit(solution)/shard_map/ppermute | solution.py:325
  29.1 9.8 %all-to-all-start.1 = ((f32[32,1,128]{2,1,0:T(1,128)}), f32[32,1,128]{2,1,0:T(1,128)S(1)}, u32[]{:S(2)}, u32[]{:S(2)}) async-start(f32[32,1,128]{2,1,0:T(1,128)} %shard_map.92), calls=%async_computation.1 | async-start | bytes 32768 | tf_op jit(solution)/shard_map/all_to_all | solution.py:399

commit v6 on v5

--- a/solution.py
+++ b/solution.py
@@ -1,4 +1,5 @@
 import functools
+import math
 
 import jax
 import jax.numpy as jnp
@@ -121,67 +122,102 @@
         target[faces:, :] = own
 
 
-def stiffness_kernel(pairs_ref, blocks_ref, field_ref, out_ref, pieces, sums):
+def stiffness_kernel(size, pairs_ref, blocks_ref, field_ref, out_ref, ends, mixed):
     block_rows = field_ref.shape[0]
-    size = blocks_ref.shape[1]
     count = pairs_ref.shape[1]
-    high, low = halves(field_ref[...])
-    pieces[...] = jnp.zeros_like(pieces)
-    pieces[pl.ds(0, block_rows, stride=SUBLANES), :] = high
-    pieces[pl.ds(1, block_rows, stride=SUBLANES), :] = low
-
-    def times(row, block, contract):
-        left = pieces[pl.ds(pl.multiple_of(row * SUBLANES, SUBLANES), SUBLANES), :]
-        return lax.dot_general(
-            left[:, :size].astype(BF16),
-            block,
-            (((1,), (contract,)), ((), ())),
-            preferred_element_type=F32,
-        )
-
-    def add(row, value):
-        place = pl.ds(pl.multiple_of(row * SUBLANES, SUBLANES), SUBLANES)
-        sums[place, :size] = sums[place, :size] + value
-
-    sums[...] = jnp.zeros_like(sums)
-    for i in range(block_rows):
-        sums[i * SUBLANES : (i + 1) * SUBLANES, :size] = times(i, blocks_ref[i], 1)
+    width = math.lcm(size, LANES)
+    tiles = width // LANES
+    segments = width // size
     for p in range(count):
-        first = pairs_ref[0, p]
-        other = pairs_ref[1, p]
-        block = blocks_ref[block_rows + p]
-        add(first, times(other, block, 1))
-        add(other, times(first, block, 0))
-    out_ref[...] = (
-        sums[pl.ds(0, block_rows, stride=SUBLANES), :]
-        + sums[pl.ds(1, block_rows, stride=SUBLANES), :]
-    )
+        ends[p : p + 1, :] = field_ref[pl.ds(pairs_ref[1, p], 1), :]
+        ends[count + p : count + p + 1, :] = field_ref[pl.ds(pairs_ref[0, p], 1), :]
+    right = jnp.concatenate([field_ref[...], ends[:count, :]], axis=0)
+    left = ends[count:, :]
+
+    def place(position):
+        segment = sum(jnp.where(position >= k * size, 1, 0) for k in range(1, segments))
+        return segment, position - segment * size
+
+    def lanes_of(value, index):
+        slabs = [
+            jnp.take_along_axis(
+                value[k : k + SUBLANES, :], index, axis=1, mode="promise_in_bounds"
+            )
+            for k in range(0, value.shape[0], SUBLANES)
+        ]
+        return jnp.concatenate(slabs, axis=0)
+
+    lane = lax.broadcasted_iota(jnp.int32, (SUBLANES, LANES), 1)
+    places = [place(lane + t * LANES) for t in range(tiles)]
+    repeated = jnp.concatenate([lanes_of(right, inside) for _, inside in places], axis=1)
+    segment, inside = place(lax.broadcasted_iota(jnp.int32, (width, LANES), 0))
+    column = lax.broadcasted_iota(jnp.int32, (width, LANES), 1)
+    add_segments = jnp.where(segment == column % segments, 1.0, 0.0).astype(BF16)
+    fold = jnp.where(inside == column, 1.0, 0.0)
+    dof_group = lax.broadcasted_iota(jnp.int32, (block_rows + count, LANES), 1) // segments
+
+    def step(g, carry):
+        total, turned = carry
+        stored = blocks_ref[:, pl.ds(pl.multiple_of(g * width, LANES), width)].astype(F32)
+        product = stored * repeated
+        high = product.astype(BF16)
+        low = (product - high.astype(F32)).astype(BF16)
+        sums = jnp.dot(
+            jnp.concatenate([high, low], axis=0), add_segments, preferred_element_type=F32
+        )
+        sums = sums[: block_rows + count] + sums[block_rows + count :]
+        total = jnp.where(dof_group == g, sums, total)
+        across = [lanes_of(left, g * segments + segment) for segment, _ in places]
+        turned = turned + stored[block_rows:] * jnp.concatenate(across, axis=1)
+        return total, turned
+
+    total, turned = lax.fori_loop(
+        0,
+        size // segments,
+        step,
+        (jnp.zeros((block_rows + count, LANES), F32), jnp.zeros((count, width), F32)),
+        unroll=4,
+    )
+    ends[:count, :] = total[block_rows:]
+    ends[count:, :] = exact_dot(turned, fold)
+    for p in range(count):
+        mixed[pl.ds(pairs_ref[0, p], 1), :] = ends[p : p + 1, :]
+        mixed[pl.ds(pairs_ref[1, p], 1), :] = ends[count + p : count + p + 1, :]
+    out_ref[...] = total[:block_rows] + mixed[...]
 
 
 def spread_jumps(block_rows, size, aligned_ref, weights_ref, own, arrived):
     faces = weights_ref.shape[0] // 2
-    dof_of = lax.broadcasted_iota(jnp.int32, (size, LANES), 0)
-    row_of = lax.broadcasted_iota(jnp.int32, (block_rows, LANES), 0)
+    dof_of = lax.broadcasted_iota(jnp.int32, (size, LANES), 0).astype(F32).astype(BF16)
+    row_of = lax.broadcasted_iota(jnp.int32, (block_rows, LANES), 0).astype(F32).astype(BF16)
+    none = jnp.zeros((), BF16)
+    one = jnp.ones((), BF16)
+
+    def widened(value, f, rows):
+        slab = jnp.broadcast_to(value[f : f + 1, :], (2 * SUBLANES, LANES)).astype(BF16)
+        return jnp.concatenate([slab] * (rows // (2 * SUBLANES)), axis=0)
 
     def step(k, total, side):
         place = tile(side * faces // SUBLANES + k)
         lam = weights_ref[place, :] * (own[side][tile(k), :] - arrived[side][tile(k), :])
         high, low = halves(lam)
         dof, row = split(aligned_ref[place, :], block_rows)
+        dof = dof.astype(F32)
+        row = row.astype(F32)
         left = []
         right = []
         for f in range(SUBLANES):
-            here = row_of == row[f : f + 1, :]
+            here = row_of == widened(row, f, block_rows)
             left.append(
                 jnp.concatenate(
                     [
-                        jnp.where(here, high[f : f + 1, :], 0.0),
-                        jnp.where(here, low[f : f + 1, :], 0.0),
+                        jnp.where(here, widened(high, f, block_rows), none),
+                        jnp.where(here, widened(low, f, block_rows), none),
                     ],
                     axis=0,
-                ).astype(BF16)
+                )
             )
-            right.append(jnp.where(dof_of == dof[f : f + 1, :], 1.0, 0.0).astype(BF16))
+            right.append(jnp.where(dof_of == widened(dof, f, size), one, none))
         return total + lax.dot_general(
             jnp.concatenate(left, axis=1),
             jnp.concatenate(right, axis=1),
@@ -330,8 +366,7 @@
 ):
     field = right_side[0, 0].T
     block_rows, size = field.shape
-    stored = stiffness[0, 0]
-    blocks = stored.reshape(stored.shape[0], size, size)
+    blocks = stiffness[0, 0]
     pairs = block_pairs[0, 0]
     rows = trace_rows[0, 0]
     partner = partner_face[0, 0]
@@ -369,10 +404,13 @@
 
     def stiff(vector):
         (product,) = call(
-            stiffness_kernel,
+            functools.partial(stiffness_kernel, size),
             [shape(block_rows)],
             [(pairs, SMEM), (blocks, VMEM), (vector, VMEM)],
-            scratch=[pltpu.VMEM((block_rows * SUBLANES, LANES), F32)] * 2,
+            scratch=[
+                pltpu.VMEM((2 * pairs.shape[1], LANES), F32),
+                pltpu.VMEM((block_rows, LANES), F32),
+            ],
         )
         return product
 

time: 39.9 us -> 40.1 us (level)
  waiting for transfers between devices: 10.2 us -> 8.33 us
  Pallas kernels: 10.7 us -> 12.5 us
    unnamed x2 -> x12, local copies, waits for them, and re-layouts: 0.01 us -> 2.52 us
    another operation x1 -> x0, local copies, waits for them, and re-layouts: 2.29 us -> none  [on_device(): blocks = stored.reshape(stored.shape[0], size, size)]
    pallas_call x8, Pallas kernels: 10.7 us -> 12.5 us  [call(): pl.pallas_call(body, out_shape=outs, in_specs=[spec for _, spec in inputs...]
    ppermute x4, waiting for transfers between devices: 3.37 us -> 1.9 us  [swap(): return lax.ppermute(value, 'sub', pairs)]
    all_to_all x1, waiting for transfers between devices: 1.95 us -> 1.46 us  [on_device(): lax.all_to_all(mortar_weight[0, 0], 'blk', split_axis=0, concat_axis=0, t...]
  transfers between devices with their start and end apart: 6 -> 6, of which waited for: 5 -> 4; matrix products, arithmetic and copies ran while one was open for 8% -> 2% of each run, Pallas kernels for 15% -> 20%
where the time goes in v6:
time: 40.1 us; the launch traced here: 39.7 us
  starting transfers between devices  14.9 us (37%)
  Pallas kernels  12.5 us (31%)
  waiting for transfers between devices  8.33 us (21%)
  local copies, waits for them, and re-layouts  2.52 us (6%)
  other arithmetic  0.73 us (2%)
  between operations  0.7 us (2%)
    pallas_call x8, Pallas kernels, call(): pl.pallas_call(body, out_shape=outs, in_specs=[spec for _, spec in inputs...  12.5 us
    ppermute x4, starting transfers between devices, swap(): return lax.ppermute(value, 'sub', pairs)  7.85 us
    all_to_all x1, waiting for transfers between devices, on_device(): lax.all_to_all(sums, ('sub', 'blk'), split_axis=0, concat_axis=0, tiled=T...  4.96 us
    all_to_all x1, starting transfers between devices, on_device(): lax.all_to_all(mortar_weight[0, 0], 'blk', split_axis=0, concat_axis=0, t...  4.35 us
    all_to_all x1, starting transfers between devices, on_device(): lax.all_to_all(sums, ('sub', 'blk'), split_axis=0, concat_axis=0, tiled=T...  2.73 us
    unnamed x12, local copies, waits for them, and re-layouts  2.52 us
    ppermute x4, waiting for transfers between devices, swap(): return lax.ppermute(value, 'sub', pairs)  1.9 us
    all_to_all x1, waiting for transfers between devices, on_device(): lax.all_to_all(mortar_weight[0, 0], 'blk', split_axis=0, concat_axis=0, t...  1.46 us
  transfers between devices with their start and end apart: 6, of which 4 were waited for; matrix products, arithmetic and copies ran while one was open for 2% of the time, Pallas kernels for 20%

profile of v6, /device:TPU:0, one launch (start us, length us, event | category | flops | bytes accessed | tf_op | source)
XLA Modules:
  0.0 39.7 jit_solution(8784767932601579627)
XLA Ops:
  0.6 4.4 %all-to-all-start = ((f32[4,16,128]{2,1,0:T(8,128)}), f32[4,16,128]{2,1,0:T(8,128)S(1)}, u32[]{:S(2)}, u32[]{:S(2)}) async-start(f32[4,16,128]{2,1,0:T(8,128)} %bitcast.22), calls=%async_computation | async-start | bytes 65536 | tf_op jit(solution)/shard_map/all_to_all | solution.py:377
  5.0 0.6 %copy-done.4 = s32[1,1,4]{2,1,0:T(1,128)S(1)} copy-done((s32[1,1,4]{2,1,0:T(1,128)S(1)}, s32[1,1,4]{2,1,0:T(1,128)}, u32[]{:S(2)}) %copy-start.4) | copy-done | bytes 40
  5.6 0.0 copy-done.5
  5.7 0.7 %pad_add_fusion.packed_ref = f32[168,128]{1,0:T(8,128)S(1)} fusion(f32[32,96]{1,0:T(8,128)} %bitcast.23, s32[1,4]{1,0:T(1,128)S(1)} %bitcast.24, s32[1,64]{1,0:T(1,128)S(1)} %bitcast.25, s32[128,128]{1,0:T(8,128)S(1)} %bitcast.21), kind=kLoop, calls=%fused_computation | loop fusion | flops 86016 | bytes 164112 | tf_op jit(solution)/shard_map/add | solution.py:385
  6.4 1.1 %shard_map.86 = (s32[128,128]{1,0:T(8,128)S(1)}, f32[32,128]{1,0:T(8,128)S(1)}, f32[64,64]{1,0:T(8,128)S(1)}, f32[64,128]{1,0:T(8,128)S(1)}, f32[64,128]{1,0:T(8,128)S(1)}) custom-call(f32[168,128]{1,0:T(8,128)S(1)} %pad_add_fusion.packed_ref), custom_call_target="tpu_custom_call" | custom-call | flops 1000000 | bytes 1000000 | tf_op jit(solution)/shard_map/pallas_call | solution.py:21
  7.5 1.5 %all-to-all-done = f32[4,16,128]{2,1,0:T(8,128)S(1)} async-done(((f32[4,16,128]{2,1,0:T(8,128)}), f32[4,16,128]{2,1,0:T(8,128)S(1)}, u32[]{:S(2)}, u32[]{:S(2)}) %all-to-all-start) | async-done | bytes 32800 | tf_op jit(solution)/shard_map/all_to_all | solution.py:377
  8.9 0.1 shard_map.88
  9.1 5.1 %collective-permute-start = (f32[128,128]{1,0:T(8,128)S(1)}, f32[128,128]{1,0:T(8,128)S(1)}, u32[]{:S(2)}, u32[]{:S(2)}) collective-permute-start(f32[128,128]{1,0:T(8,128)S(1)} %get-tuple-element.20.to_a_ref.first_a_ref), channel_id=1, source_target_pairs={{4,8},{8,4},{12,16},{16,12},{20,24},{24,20},{28,0},{0,28},{5,9},{9... | collective-permute-start | bytes 196616 | tf_op jit(solution)/shard_map/ppermute | solution.py:361
  14.2 0.0 collective-permute-start.1
  14.2 0.7 %copy-done.2 = s32[1,1,2,16]{3,2,1,0:T(2,128)S(1)} copy-done((s32[1,1,2,16]{3,2,1,0:T(2,128)S(1)}, s32[1,1,2,16]{3,2,1,0:T(2,128)}, u32[]{:S(2)}) %copy-start.2) | copy-done | bytes 152
  14.9 1.2 %copy-done = bf16[1,1,48,9216]{3,2,1,0:T(8,128)(2,1)S(1)} copy-done((bf16[1,1,48,9216]{3,2,1,0:T(8,128)(2,1)S(1)}, bf16[1,1,48,9216]{3,2,1,0:T(8,128)(2,1)}, u32[]{:S(2)}) %copy-start) | copy-done | bytes 884760
  16.0 2.4 %shard_map.87.product_ref = f32[32,128]{1,0:T(8,128)S(1)} custom-call(s32[2,16]{1,0:T(2,128)S(1)} %bitcast.19, bf16[48,9216]{1,0:T(8,128)(2,1)S(1)} %bitcast.16, f32[32,128]{1,0:T(8,128)S(1)} %get-tuple-element.15.field_ref), custom_call_target="tpu_custom_call" | custom-call | flops 1000000 | bytes 1000000 | tf_op jit(solution)/shard_map/pallas_call | solution.py:21
  18.4 0.0 collective-permute-done.from_a_ref
  18.4 0.0 collective-permute-done.1.from_b_ref
  18.4 3.0 %shard_map.89 = (f32[32,128]{1,0:T(8,128)S(1)}, f32[128,128]{1,0:T(8,128)S(1)}, f32[64,128]{1,0:T(8,128)S(1)}, f32[64,128]{1,0:T(8,128)S(1)}) custom-call(s32[128,128]{1,0:T(8,128)S(1)} %get-tuple-element.16.aligned_ref, f32[32,128]{1,0:T(8,128)S(1)} %shard_map.87.product_ref, f32[128,128]{1,0:T(8,128)S(1)} %get-tuple-element.20.to_a_ref.first_a_ref, ...), custom_call_target="tpu_custom_call" | custom-call | flops 1000000 | bytes 1000000 | tf_op jit(solution)/shard_map/pallas_call | solution.py:21
  21.4 2.8 %collective-permute-start.2 = (f32[64,128]{1,0:T(8,128)S(1)}, f32[64,128]{1,0:T(8,128)S(1)}, u32[]{:S(2)}, u32[]{:S(2)}) collective-permute-start(f32[64,128]{1,0:T(8,128)S(1)} %get-tuple-element.24.side_a_ref), channel_id=1, source_target_pairs={{4,8},{8,4},{12,16},{16,12},{20,24},{24,20},{28,0},{0,28},{5,9},{9... | collective-permute-start | bytes 98312 | tf_op jit(solution)/shard_map/ppermute | solution.py:361
  24.2 2.4 %shard_map.90.product_ref = f32[32,128]{1,0:T(8,128)S(1)} custom-call(s32[2,16]{1,0:T(2,128)S(1)} %bitcast.20, bf16[48,9216]{1,0:T(8,128)(2,1)S(1)} %bitcast.17, f32[32,128]{1,0:T(8,128)S(1)} %get-tuple-element.22.field_ref.image_ref), custom_call_target="tpu_custom_call" | custom-call | flops 1000000 | bytes 1000000 | tf_op jit(solution)/shard_map/pallas_call | solution.py:21
  26.6 1.6 %collective-permute-done.2.from_a_ref = f32[64,128]{1,0:T(8,128)S(1)} collective-permute-done((f32[64,128]{1,0:T(8,128)S(1)}, f32[64,128]{1,0:T(8,128)S(1)}, u32[]{:S(2)}, u32[]{:S(2)}) %collective-permute-start.2) | collective-permute-done | bytes 32800 | tf_op jit(solution)/shard_map/ppermute | solution.py:361
  28.1 0.3 collective-permute-done.3.from_b_ref
  28.4 0.7 %shard_map.92 = f32[32,1,128]{2,1,0:T(1,128)} custom-call(f32[32,128]{1,0:T(8,128)S(1)} %shard_map.90.product_ref, f32[128,128]{1,0:T(8,128)S(1)} %get-tuple-element.23.weights_ref, f32[64,128]{1,0:T(8,128)S(1)} %get-tuple-element.24.side_a_ref, f32[64,128]{1,0:T(8,128)S(1)} %get-tuple-element.25.side_b_ref, ...), custom_call_target="tpu_custom_call" | custom-call | flops 1000000 | bytes 1000000 | tf_op jit(solution)/shard_map/pallas_call | solution.py:21
  29.2 2.7 %all-to-all-start.1 = ((f32[32,1,128]{2,1,0:T(1,128)}), f32[32,1,128]{2,1,0:T(1,128)S(1)}, u32[]{:S(2)}, u32[]{:S(2)}) async-start(f32[32,1,128]{2,1,0:T(1,128)} %shard_map.92), calls=%async_computation.1 | async-start | bytes 32768 | tf_op jit(solution)/shard_map/all_to_all | solution.py:437
  31.9 2.1 %shard_map.91.second_ref = f32[32,128]{1,0:T(8,128)S(1)} custom-call(s32[128,128]{1,0:T(8,128)S(1)} %get-tuple-element.16.aligned_ref, f32[32,128]{1,0:T(8,128)S(1)} %shard_map.90.product_ref, f32[128,128]{1,0:T(8,128)S(1)} %get-tuple-element.23.weights_ref, f32[64,128]{1,0:T(8,128)S(1)} %get-tuple-element.24.side_a_ref, ...), custom_call_target="tpu_custom_call" | custom-call | flops 1000000000 | bytes 1000000 | tf_op jit(solution)/shard_map/pallas_call | solution.py:21
  34.0 5.0 %all-to-all-done.1.sums_ref = f32[32,1,128]{2,1,0:T(1,128)S(1)} async-done(((f32[32,1,128]{2,1,0:T(1,128)}), f32[32,1,128]{2,1,0:T(1,128)S(1)}, u32[]{:S(2)}, u32[]{:S(2)}) %all-to-all-start.1) | async-done | bytes 16416 | tf_op jit(solution)/shard_map/all_to_all | solution.py:437
  39.0 0.7 %shard_map.93 = (f32[32,96]{1,0:T(8,128)}, f32[32,96]{1,0:T(8,128)}) custom-call(f32[32,128]{1,0:T(8,128)S(1)} %get-tuple-element.15.field_ref, f32[32,128]{1,0:T(8,128)S(1)} %get-tuple-element.22.field_ref.image_ref, f32[32,128]{1,0:T(8,128)S(1)} %shard_map.91.second_ref, f32[32,1,128]{2,1,0:T(1,128)S(1)} %all-to-all-done.1.sums_ref), custom_call_target="tpu_custom_call" | custom-call | flops 1000000 | bytes 1000000 | tf_op jit(solution)/shard_map/pallas_call | solution.py:21
  (9 shorter events, 0.0 us)
Async XLA Ops:
  0.6 4.4 %copy-start.3 = (s32[1,1,128,128]{3,2,1,0:T(8,128)S(1)}, s32[1,1,128,128]{3,2,1,0:T(8,128)}, u32[]{:S(2)}) copy-start(s32[1,1,128,128]{3,2,1,0:T(8,128)} %param.10) | copy-start | bytes 196612
  0.6 8.3 %all-to-all-start = ((f32[4,16,128]{2,1,0:T(8,128)}), f32[4,16,128]{2,1,0:T(8,128)S(1)}, u32[]{:S(2)}, u32[]{:S(2)}) async-start(f32[4,16,128]{2,1,0:T(8,128)} %bitcast.22), calls=%async_computation | async-start | bytes 65536 | tf_op jit(solution)/shard_map/all_to_all | solution.py:377
  5.0 0.7 %copy-start.4 = (s32[1,1,4]{2,1,0:T(1,128)S(1)}, s32[1,1,4]{2,1,0:T(1,128)}, u32[]{:S(2)}) copy-start(s32[1,1,4]{2,1,0:T(1,128)} %param.12) | copy-start | bytes 52
  5.0 0.7 %copy-start.5 = (s32[1,1,64]{2,1,0:T(1,128)S(1)}, s32[1,1,64]{2,1,0:T(1,128)}, u32[]{:S(2)}) copy-start(s32[1,1,64]{2,1,0:T(1,128)} %param.11) | copy-start | bytes 772
  9.1 9.3 %collective-permute-start = (f32[128,128]{1,0:T(8,128)S(1)}, f32[128,128]{1,0:T(8,128)S(1)}, u32[]{:S(2)}, u32[]{:S(2)}) collective-permute-start(f32[128,128]{1,0:T(8,128)S(1)} %get-tuple-element.20.to_a_ref.first_a_ref), channel_id=1, source_target_pairs={{4,8},{8,4},{12,16},{16,12},{20,24},{24,20},{28,0},{0,28},{5,9},{9... | collective-permute-start | bytes 196616 | tf_op jit(solution)/shard_map/ppermute | solution.py:361
  14.2 4.3 %collective-permute-start.1 = (f32[128,128]{1,0:T(8,128)S(1)}, f32[128,128]{1,0:T(8,128)S(1)}, u32[]{:S(2)}, u32[]{:S(2)}) collective-permute-start(f32[128,128]{1,0:T(8,128)S(1)} %get-tuple-element.21.to_b_ref.first_b_ref), channel_id=1, source_target_pairs={{0,4},{4,0},{8,12},{12,8},{16,20},{20,16},{24,28},{28,24},{1,5},{5... | collective-permute-start | bytes 196616 | tf_op jit(solution)/shard_map/ppermute | solution.py:361
  14.2 0.7 %copy-start.2 = (s32[1,1,2,16]{3,2,1,0:T(2,128)S(1)}, s32[1,1,2,16]{3,2,1,0:T(2,128)}, u32[]{:S(2)}) copy-start(s32[1,1,2,16]{3,2,1,0:T(2,128)} %param.9) | copy-start | bytes 388
  14.8 1.2 %copy-start = (bf16[1,1,48,9216]{3,2,1,0:T(8,128)(2,1)S(1)}, bf16[1,1,48,9216]{3,2,1,0:T(8,128)(2,1)}, u32[]{:S(2)}) copy-start(bf16[1,1,48,9216]{3,2,1,0:T(8,128)(2,1)} %param.8) | copy-start | bytes 2654212
  16.0 8.2 %copy-start.1 = (bf16[1,1,48,9216]{3,2,1,0:T(8,128)(2,1)S(1)}, bf16[1,1,48,9216]{3,2,1,0:T(8,128)(2,1)}, u32[]{:S(2)}) copy-start(bf16[1,1,48,9216]{3,2,1,0:T(8,128)(2,1)} %param.8) | copy-start | bytes 2654212
  21.4 6.7 %collective-permute-start.2 = (f32[64,128]{1,0:T(8,128)S(1)}, f32[64,128]{1,0:T(8,128)S(1)}, u32[]{:S(2)}, u32[]{:S(2)}) collective-permute-start(f32[64,128]{1,0:T(8,128)S(1)} %get-tuple-element.24.side_a_ref), channel_id=1, source_target_pairs={{4,8},{8,4},{12,16},{16,12},{20,24},{24,20},{28,0},{0,28},{5,9},{9... | collective-permute-start | bytes 98312 | tf_op jit(solution)/shard_map/ppermute | solution.py:361
  24.2 4.3 %collective-permute-start.3 = (f32[64,128]{1,0:T(8,128)S(1)}, f32[64,128]{1,0:T(8,128)S(1)}, u32[]{:S(2)}, u32[]{:S(2)}) collective-permute-start(f32[64,128]{1,0:T(8,128)S(1)} %get-tuple-element.25.side_b_ref), channel_id=1, source_target_pairs={{0,4},{4,0},{8,12},{12,8},{16,20},{20,16},{24,28},{28,24},{1,5},{5... | collective-permute-start | bytes 98312 | tf_op jit(solution)/shard_map/ppermute | solution.py:361
  29.2 9.8 %all-to-all-start.1 = ((f32[32,1,128]{2,1,0:T(1,128)}), f32[32,1,128]{2,1,0:T(1,128)S(1)}, u32[]{:S(2)}, u32[]{:S(2)}) async-start(f32[32,1,128]{2,1,0:T(1,128)} %shard_map.92), calls=%async_computation.1 | async-start | bytes 32768 | tf_op jit(solution)/shard_map/all_to_all | solution.py:437

commit v7 on v6

v7 whole, which is shorter than its diff:
```python
import functools
import math

import jax
import jax.numpy as jnp
from jax import lax
from jax.experimental import pallas as pl
from jax.experimental.pallas import tpu as pltpu
from jax.sharding import PartitionSpec as P

LANES = 128
SUBLANES = 8
VMEM = pl.BlockSpec(memory_space=pltpu.VMEM)
HBM = pl.BlockSpec(memory_space=pltpu.HBM)
F32 = jnp.float32
BF16 = jnp.bfloat16


def call(body, outs, inputs, scratch=(), flops=1_000_000, moved=1_000_000, limit=32 * 1024 * 1024):
    return pl.pallas_call(
        body,
        out_shape=outs,
        in_specs=[spec for _, spec in inputs],
        out_specs=[VMEM] * len(outs),
        scratch_shapes=list(scratch),
        compiler_params=pltpu.CompilerParams(vmem_limit_bytes=limit),
        cost_estimate=pl.CostEstimate(
            flops=flops, bytes_accessed=moved, transcendentals=0
        ),
    )(*[value for value, _ in inputs])


def shape(rows, dtype=F32):
    return jax.ShapeDtypeStruct((rows, LANES), dtype)


def halves(value):
    high = value.astype(BF16).astype(F32)
    return high, value - high


def gather_traces(field, rows_ref, rows_first, target):
    block_rows = field.shape[0]
    spread = [
        jnp.broadcast_to(field[i : i + 1, :], (SUBLANES, LANES)) for i in range(block_rows)
    ]
    for k in range(target.shape[0] // SUBLANES):
        index = rows_ref[rows_first + k * SUBLANES : rows_first + (k + 1) * SUBLANES, :]
        dof, row = split(index, block_rows)
        taken = jnp.zeros((SUBLANES, LANES), F32)
        for i in range(block_rows):
            here = jnp.take_along_axis(spread[i], dof, axis=1, mode="promise_in_bounds")
            taken = jnp.where(row == i, here, taken)
        target[k * SUBLANES : (k + 1) * SUBLANES, :] = taken


def tile(k):
    return pl.ds(pl.multiple_of(k * SUBLANES, SUBLANES), SUBLANES)


def split(index, block_rows):
    if block_rows & (block_rows - 1) == 0:
        shift = block_rows.bit_length() - 1
        return index >> shift, index & (block_rows - 1)
    return lax.div(index, block_rows), lax.rem(index, block_rows)


def one_hot(place, count):
    row = lax.broadcasted_iota(jnp.int32, (count, place.shape[1]), 0)
    return jnp.where(row == place, 1.0, 0.0)


def exact_dot(left, right):
    return jnp.dot(
        left, right, precision=lax.Precision.HIGHEST, preferred_element_type=F32
    )


def first_kernel(
    groups, packed_ref, aligned_ref, padded_ref, chosen_ref, side_a_ref
):
    faces = side_a_ref.shape[0]
    block_rows = padded_ref.shape[0]
    per_group = faces // groups
    parity = lax.rem(lax.axis_index("sub"), 2)
    east = pl.multiple_of((1 - parity) * faces, faces)
    west = pl.multiple_of(parity * faces, faces)
    padded_ref[...] = packed_ref[2 * faces : 2 * faces + block_rows, :]
    tail = packed_ref[2 * faces + block_rows :, :].astype(jnp.int32)
    partner = tail[:1, :faces]
    face = lax.broadcasted_iota(jnp.int32, (1, faces), 1)
    source = jnp.zeros((1, faces), jnp.int32)
    for g in range(groups):
        inside = face - g * per_group
        source = jnp.where(
            (inside >= 0) & (inside < per_group), tail[1:2, g : g + 1] * per_group + inside, source
        )
    order = one_hot(partner, faces)
    aligned_ref[pl.ds(west, faces), :] = packed_ref[faces : 2 * faces, :].astype(jnp.int32)
    aligned_ref[pl.ds(east, faces), :] = exact_dot(order, packed_ref[:faces, :]).astype(jnp.int32)
    chosen_ref[...] = lax.dot_general(
        order.astype(BF16),
        one_hot(source, faces).astype(BF16),
        (((1,), (1,)), ((), ())),
        preferred_element_type=F32,
    )
    gather_traces(padded_ref[...], aligned_ref, 0, side_a_ref)


def far_message_kernel(held_ref, chosen_ref, side_a_ref, to_a_ref):
    faces = side_a_ref.shape[0]
    to_a_ref[:faces, :] = side_a_ref[...]
    to_a_ref[faces : 2 * faces, :] = exact_dot(chosen_ref[...], held_ref[...])
    to_a_ref[2 * faces :, :] = jnp.zeros_like(to_a_ref[2 * faces :, :])


def near_message_kernel(aligned_ref, padded_ref, to_a_ref, to_b_ref):
    faces = to_b_ref.shape[0] // 2
    to_b_ref[faces:, :] = to_a_ref[faces : 2 * faces, :]
    gather_traces(padded_ref[...], aligned_ref, faces, to_b_ref.at[:faces, :])


def near_traces_kernel(aligned_ref, image_ref, side_b_ref):
    gather_traces(image_ref[...], aligned_ref, side_b_ref.shape[0], side_b_ref)


def stiffness_kernel(
    size, count, pieces, packed_ref, field_ref, blocks_hbm, out_ref, blocks_ref, sems
):
    block_rows = field_ref.shape[0]
    width = math.lcm(size, LANES)
    tiles = width // LANES
    segments = width // size
    groups = size // segments // pieces
    copies = []
    for k in range(pieces):
        part = slice(k * groups * width, (k + 1) * groups * width)
        copies.append(
            pltpu.make_async_copy(blocks_hbm.at[:, part], blocks_ref.at[:, part], sems.at[k])
        )
        copies[-1].start()

    def place(position):
        segment = sum(jnp.where(position >= k * size, 1, 0) for k in range(1, segments))
        return segment, position - segment * size

    def lanes_of(value, index):
        slabs = [
            jnp.take_along_axis(
                value[k : k + SUBLANES, :], index, axis=1, mode="promise_in_bounds"
            )
            for k in range(0, value.shape[0], SUBLANES)
        ]
        return jnp.concatenate(slabs, axis=0)

    tail = packed_ref[packed_ref.shape[0] - SUBLANES :, :].astype(jnp.int32)
    first_of, other_of = (one_hot(tail[k : k + 1, :count], block_rows) for k in (2, 3))
    field = field_ref[...]
    left, other = (
        lax.dot_general(
            ends,
            field,
            (((0,), (0,)), ((), ())),
            precision=lax.Precision.HIGHEST,
            preferred_element_type=F32,
        )
        for ends in (first_of, other_of)
    )
    right = jnp.concatenate([field, other], axis=0)
    lane = lax.broadcasted_iota(jnp.int32, (SUBLANES, LANES), 1)
    places = [place(lane + t * LANES) for t in range(tiles)]
    repeated = jnp.concatenate([lanes_of(right, inside) for _, inside in places], axis=1)
    segment, inside = place(lax.broadcasted_iota(jnp.int32, (width, LANES), 0))
    column = lax.broadcasted_iota(jnp.int32, (width, LANES), 1)
    add_segments = jnp.where(segment == column % segments, 1.0, 0.0).astype(BF16)
    fold = jnp.where(inside == column, 1.0, 0.0)
    rows = block_rows + count
    dof_group = lax.broadcasted_iota(jnp.int32, (rows, LANES), 1) // segments
    total = jnp.zeros((rows, LANES), F32)
    turned = jnp.zeros((count, width), F32)
    for k in range(pieces):
        copies[k].wait()
        stack = []
        for g in range(k * groups, (k + 1) * groups):
            stored = blocks_ref[:, g * width : (g + 1) * width].astype(F32)
            product = stored * repeated
            high = product.astype(BF16)
            stack += [high, (product - high.astype(F32)).astype(BF16)]
            across = [lanes_of(left, g * segments + segment) for segment, _ in places]
            turned = turned + stored[block_rows:] * jnp.concatenate(across, axis=1)
        sums = jnp.dot(
            jnp.concatenate(stack, axis=0), add_segments, preferred_element_type=F32
        )
        for n in range(groups):
            both = sums[2 * n * rows : 2 * (n + 1) * rows]
            total = jnp.where(dof_group == k * groups + n, both[:rows] + both[rows:], total)
    out_ref[...] = (
        total[:block_rows]
        + exact_dot(first_of, total[block_rows:])
        + exact_dot(other_of, exact_dot(turned, fold))
    )


def spread_jumps(size, faces, rows_ref, rows_first, weights_ref, own_ref, arrived_ref, block_rows):
    dof_of = lax.broadcasted_iota(jnp.int32, (size, LANES), 0).astype(F32).astype(BF16)
    row_of = lax.broadcasted_iota(jnp.int32, (block_rows, LANES), 0).astype(F32).astype(BF16)
    none = jnp.zeros((), BF16)
    one = jnp.ones((), BF16)

    def widened(value, f, rows):
        slab = jnp.broadcast_to(value[f : f + 1, :], (2 * SUBLANES, LANES)).astype(BF16)
        return jnp.concatenate([slab] * (rows // (2 * SUBLANES)), axis=0)

    def step(k, total):
        lam = weights_ref[tile(k), :] * (own_ref[tile(k), :] - arrived_ref[tile(k), :])
        high, low = halves(lam)
        dof, row = split(rows_ref[tile(rows_first // SUBLANES + k), :], block_rows)
        dof = dof.astype(F32)
        row = row.astype(F32)
        left = []
        right = []
        for f in range(SUBLANES):
            here = row_of == widened(row, f, block_rows)
            left.append(
                jnp.concatenate(
                    [
                        jnp.where(here, widened(high, f, block_rows), none),
                        jnp.where(here, widened(low, f, block_rows), none),
                    ],
                    axis=0,
                )
            )
            right.append(jnp.where(dof_of == widened(dof, f, size), one, none))
        return total + lax.dot_general(
            jnp.concatenate(left, axis=1),
            jnp.concatenate(right, axis=1),
            (((1,), (1,)), ((), ())),
            preferred_element_type=F32,
        )

    total = lax.fori_loop(
        0, faces // SUBLANES, step, jnp.zeros((2 * block_rows, size), F32), unroll=8
    )
    return total[:block_rows] + total[block_rows:]


def near_kernel(size, aligned_ref, product_ref, to_ref, from_ref, partial_ref, weights_ref):
    block_rows = product_ref.shape[0]
    faces = weights_ref.shape[0]
    odd = lax.rem(lax.axis_index("sub"), 2) == 1
    weights_ref[...] = jnp.where(odd, from_ref[faces:, :], to_ref[faces:, :])
    partial_ref[...] = product_ref[...]
    partial_ref[:, :size] = partial_ref[:, :size] + spread_jumps(
        size, faces, aligned_ref, faces, weights_ref, to_ref, from_ref, block_rows
    )


def far_kernel(
    size,
    aligned_ref,
    partial_ref,
    to_ref,
    from_ref,
    image_ref,
    weights_ref,
    side_a_ref,
):
    block_rows = partial_ref.shape[0]
    faces = weights_ref.shape[0]
    odd = lax.rem(lax.axis_index("sub"), 2) == 1
    weights_ref[...] = jnp.where(
        odd, to_ref[faces : 2 * faces, :], from_ref[faces : 2 * faces, :]
    )
    image_ref[...] = partial_ref[...]
    image_ref[:, :size] = image_ref[:, :size] + spread_jumps(
        size, faces, aligned_ref, 0, weights_ref, to_ref, from_ref, block_rows
    )
    gather_traces(image_ref[...], aligned_ref, 0, side_a_ref.at[:faces, :])
    side_a_ref[faces:, :] = jnp.zeros_like(side_a_ref[faces:, :])


def column_sums(value):
    return jnp.sum(value, axis=0, keepdims=True)


def jump_sums(weights_ref, own_ref, arrived_ref, first_ref):
    faces = slice(0, weights_ref.shape[0])
    own = own_ref[faces, :]
    lam = weights_ref[...] * (own - arrived_ref[faces, :])
    return column_sums(lam * first_ref[faces, :]), column_sums(lam * own)


def near_sums_kernel(
    product_ref, weights_ref, own_ref, arrived_ref, first_ref, field_ref, image_ref, rows_ref
):
    field = field_ref[...]
    image = image_ref[...]
    product = product_ref[...]
    with_field, with_image = jump_sums(weights_ref, own_ref, arrived_ref, first_ref)
    parts = [
        column_sums(field * field),
        column_sums(field * image),
        column_sums(image * image),
        column_sums(field * product) + with_field,
        column_sums(image * product) + with_image,
    ]
    parts += [jnp.zeros_like(parts[0])] * (SUBLANES - len(parts))
    rows_ref[...] = jnp.concatenate(parts, axis=0)


def sums_kernel(rows_ref, weights_ref, own_ref, arrived_ref, first_ref, sums_ref):
    with_field, with_image = jump_sums(weights_ref, own_ref, arrived_ref, first_ref)
    row = lax.broadcasted_iota(jnp.int32, (SUBLANES, LANES), 0)
    rows = rows_ref[...] + jnp.where(row == 3, with_field, jnp.where(row == 4, with_image, 0.0))
    lane = lax.broadcasted_iota(jnp.int32, (SUBLANES, LANES), 1)
    whole = jnp.sum(rows, axis=1, keepdims=True)
    packed = column_sums(jnp.where(lane == row, whole, 0.0))
    sums_ref[...] = jnp.broadcast_to(packed[None], sums_ref.shape)


def second_kernel(
    size,
    aligned_ref,
    product_ref,
    weights_a_ref,
    weights_b_ref,
    side_a_ref,
    side_b_ref,
    from_a_ref,
    from_b_ref,
    second_ref,
):
    block_rows = product_ref.shape[0]
    faces = weights_a_ref.shape[0]
    second_ref[...] = product_ref[...]
    second_ref[:, :size] = (
        second_ref[:, :size]
        + spread_jumps(
            size, faces, aligned_ref, 0, weights_a_ref, side_a_ref, from_a_ref, block_rows
        )
        + spread_jumps(
            size, faces, aligned_ref, faces, weights_b_ref, side_b_ref, from_b_ref, block_rows
        )
    )


def final_kernel(field_ref, image_ref, second_ref, sums_ref, solution_ref, residual_ref):
    size = solution_ref.shape[1]
    row = jnp.sum(sums_ref[...], axis=0)
    lane = lax.broadcasted_iota(jnp.int32, (1, LANES), 1)

    def entry(k):
        return jnp.sum(jnp.where(lane == k, row, 0.0), axis=1, keepdims=True)

    bb, bq, qq, bw, qw = (entry(k) for k in range(5))
    field = field_ref[:, :size]
    image = image_ref[:, :size]
    second = second_ref[:, :size]
    alpha = bb / bq
    norm = bb - alpha * (2.0 * bq - alpha * qq)
    beta = norm / bb
    grown = 1.0 + beta
    energy = grown * (grown * bq - alpha * (bw + qq)) + alpha * alpha * qw
    alpha_next = norm / energy
    residual = field - alpha * image
    direction = residual + beta * field
    moved = (image - alpha * second) + beta * image
    solution_ref[...] = alpha * field + alpha_next * direction
    residual_ref[...] = residual - alpha_next * moved


def swap(value, odd):
    count = lax.axis_size("sub")
    pairs = []
    for first in range(odd, count, 2):
        second = (first + 1) % count
        pairs += [(first, second), (second, first)]
    return lax.ppermute(value, "sub", pairs)


def on_device(
    right_side, stiffness, block_pairs, trace_rows, partner_face, owner_list, mortar_weight
):
    field = right_side[0, 0].T
    block_rows, size = field.shape
    blocks = stiffness[0, 0]
    pairs = block_pairs[0, 0]
    rows = trace_rows[0, 0]
    partner = partner_face[0, 0]
    owners = owner_list[0, 0]
    faces = partner.shape[0]
    devices = lax.axis_size("sub") * lax.axis_size("blk")

    held = lax.all_to_all(mortar_weight[0, 0], "blk", split_axis=0, concat_axis=0, tiled=True)
    last = 2 * faces + block_rows

    def placed(value, first):
        below = last + SUBLANES - first - value.shape[0]
        return jnp.pad(value, ((first, below), (0, LANES - value.shape[1])))

    indices = (
        placed(rows, 0)
        + placed(partner_face[0], last)
        + placed(owner_list[0], last + 1)
        + placed(pairs, last + 2)
    )
    packed = indices.astype(F32) + placed(field, 2 * faces)
    aligned, padded, chosen, side_a = call(
        functools.partial(first_kernel, owners.shape[0]),
        [
            shape(2 * faces, jnp.int32),
            shape(block_rows),
            jax.ShapeDtypeStruct((faces, faces), F32),
            shape(faces),
        ],
        [(packed, VMEM)],
    )
    (to_a,) = call(
        far_message_kernel,
        [shape(2 * faces + SUBLANES)],
        [(value, VMEM) for value in (held.reshape(faces, LANES), chosen, side_a)],
    )
    from_a = swap(to_a, 1)
    (to_b,) = call(
        near_message_kernel,
        [shape(2 * faces)],
        [(value, VMEM) for value in (aligned, padded, to_a)],
    )
    from_b = swap(to_b, 0)
    pieces = next(k for k in (6, 4, 3, 2, 1) if size * size // math.lcm(size, LANES) % k == 0)

    def stiff(vector):
        (product,) = call(
            functools.partial(stiffness_kernel, size, pairs.shape[1], pieces),
            [shape(block_rows)],
            [(packed, VMEM), (vector, VMEM), (blocks, HBM)],
            scratch=[pltpu.VMEM(blocks.shape, BF16), pltpu.SemaphoreType.DMA((pieces,))],
            limit=66_300_000,
        )
        return product

    partial, weights_b = call(
        functools.partial(near_kernel, size),
        [shape(block_rows), shape(faces)],
        [(value, VMEM) for value in (aligned, stiff(padded), to_b, from_b)],
        flops=1,
        moved=1,
    )
    image, weights_a, side_a = call(
        functools.partial(far_kernel, size),
        [shape(block_rows), shape(faces), shape(faces + SUBLANES)],
        [(value, VMEM) for value in (aligned, partial, to_a, from_a)],
    )
    from_a = swap(side_a, 1)
    (side_b,) = call(
        near_traces_kernel, [shape(faces)], [(aligned, VMEM), (image, VMEM)]
    )
    from_b = swap(side_b, 0)
    product = stiff(image)
    (sums,) = call(
        near_sums_kernel,
        [shape(SUBLANES)],
        [(value, VMEM) for value in (product, weights_b, side_b, from_b, to_b, padded, image)],
        flops=1,
        moved=1,
    )
    (sums,) = call(
        sums_kernel,
        [jax.ShapeDtypeStruct((devices, 1, LANES), F32)],
        [(value, VMEM) for value in (sums, weights_a, side_a, from_a, to_a)],
    )
    (second,) = call(
        functools.partial(second_kernel, size),
        [shape(block_rows)],
        [
            (value, VMEM)
            for value in (
                aligned, product, weights_a, weights_b, side_a, side_b, from_a, from_b
            )
        ],
        flops=1_000_000_000,
    )
    sums = lax.all_to_all(sums, ("sub", "blk"), split_axis=0, concat_axis=0, tiled=True)
    solution_field, residual = call(
        final_kernel,
        [jax.ShapeDtypeStruct((block_rows, size), F32)] * 2,
        [(padded, VMEM), (image, VMEM), (second, VMEM), (sums, VMEM)],
    )
    return (solution_field.T[None, None], residual.T[None, None])


def solution(mesh):
    in_specs = (
        P("sub", "blk", None, None),
        P("sub", "blk", None, None),
        P("sub", "blk", None, None),
        P("sub", "blk", None, None),
        P("sub", "blk", None),
        P("sub", "blk", None),
        P("sub", "blk", None, None, None),
    )
    out_specs = (P("sub", "blk", None, None), P("sub", "blk", None, None))
    return jax.shard_map(
        on_device, mesh=mesh, in_specs=in_specs, out_specs=out_specs, check_vma=False
    )
```

time: 40.1 us -> 42.4 us (1.057)
  Pallas kernels: 12.5 us -> 15 us
  waiting for transfers between devices: 8.33 us -> 7.78 us
    pallas_call x8 -> x12, Pallas kernels: 12.5 us -> 15 us  [call(): pl.pallas_call(body, out_shape=outs, in_specs=[spec for _, spec in inputs...]
    ppermute x4, waiting for transfers between devices: 1.9 us -> 0.01 us  [swap(): return lax.ppermute(value, 'sub', pairs)]
    all_to_all x1, waiting for transfers between devices: 4.96 us -> 5.82 us  [on_device(): lax.all_to_all(sums, ('sub', 'blk'), split_axis=0, concat_axis=0, tiled=T...]
    all_to_all x1, starting transfers between devices: 2.73 us -> 3.55 us  [on_device(): lax.all_to_all(sums, ('sub', 'blk'), split_axis=0, concat_axis=0, tiled=T...]
    all_to_all x1, waiting for transfers between devices: 1.46 us -> 1.96 us  [on_device(): lax.all_to_all(mortar_weight[0, 0], 'blk', split_axis=0, concat_axis=0, t...]
    ppermute x4, starting transfers between devices: 7.85 us -> 7.39 us  [swap(): return lax.ppermute(value, 'sub', pairs)]
    unnamed x12 -> x24, local copies, waits for them, and re-layouts: 2.52 us -> 2.15 us
  transfers between devices with their start and end apart: 6 -> 6, of which waited for: 4 -> 2; matrix products, arithmetic and copies ran while one was open for 2% -> 2% of each run, Pallas kernels for 20% -> 29%
where the time goes in v7:
time: 42.4 us; the launch traced here: 41.8 us
  starting transfers between devices  15.3 us (36%)
  Pallas kernels  15 us (35%)
  waiting for transfers between devices  7.78 us (18%)
  local copies, waits for them, and re-layouts  2.15 us (5%)
  between operations  0.84 us (2%)
  other arithmetic  0.73 us (2%)
    pallas_call x12, Pallas kernels, call(): pl.pallas_call(body, out_shape=outs, in_specs=[spec for _, spec in inputs...  15 us
    ppermute x4, starting transfers between devices, swap(): return lax.ppermute(value, 'sub', pairs)  7.39 us
    all_to_all x1, waiting for transfers between devices, on_device(): lax.all_to_all(sums, ('sub', 'blk'), split_axis=0, concat_axis=0, tiled=T...  5.82 us
    all_to_all x1, starting transfers between devices, on_device(): lax.all_to_all(mortar_weight[0, 0], 'blk', split_axis=0, concat_axis=0, t...  4.35 us
    all_to_all x1, starting transfers between devices, on_device(): lax.all_to_all(sums, ('sub', 'blk'), split_axis=0, concat_axis=0, tiled=T...  3.55 us
    unnamed x24, local copies, waits for them, and re-layouts  2.15 us
    all_to_all x1, waiting for transfers between devices, on_device(): lax.all_to_all(mortar_weight[0, 0], 'blk', split_axis=0, concat_axis=0, t...  1.96 us
  transfers between devices with their start and end apart: 6, of which 2 were waited for; matrix products, arithmetic and copies ran while one was open for 2% of the time, Pallas kernels for 29%

profile of v7, /device:TPU:0, one launch (start us, length us, event | category | flops | bytes accessed | tf_op | source)
XLA Modules:
  0.0 41.8 jit_solution(17297428954927800176)
XLA Ops:
  0.6 4.4 %all-to-all-start = ((f32[4,16,128]{2,1,0:T(8,128)}), f32[4,16,128]{2,1,0:T(8,128)S(1)}, u32[]{:S(2)}, u32[]{:S(2)}) async-start(f32[4,16,128]{2,1,0:T(8,128)} %bitcast.20), calls=%async_computation | async-start | bytes 65536 | tf_op jit(solution)/shard_map/all_to_all | solution.py:394
  5.0 0.6 %copy-done.11 = s32[1,1,64]{2,1,0:T(1,128)S(1)} copy-done((s32[1,1,64]{2,1,0:T(1,128)S(1)}, s32[1,1,64]{2,1,0:T(1,128)}, u32[]{:S(2)}) %copy-start.11) | copy-done | bytes 280
  5.6 0.0 copy-done.9
  5.7 0.7 %pad_add_fusion.packed_ref = f32[168,128]{1,0:T(8,128)S(1)} fusion(f32[32,96]{1,0:T(8,128)} %bitcast.21, s32[2,16]{1,0:T(2,128)S(1)} %bitcast.22, s32[1,4]{1,0:T(1,128)S(1)} %bitcast.23, s32[1,64]{1,0:T(1,128)S(1)} %bitcast.24, s32[128,128]{1,0:T(8,128)S(1)} %bitcast.19), kind=kLoop, calls=%fused_computation | loop fusion | flops 107520 | bytes 164240 | tf_op jit(solution)/shard_map/add | solution.py:407
  6.4 0.5 %shard_map.86 = (s32[128,128]{1,0:T(8,128)S(1)}, f32[32,128]{1,0:T(8,128)S(1)}, f32[64,64]{1,0:T(8,128)S(1)}, f32[64,128]{1,0:T(8,128)S(1)}) custom-call(f32[168,128]{1,0:T(8,128)S(1)} %pad_add_fusion.packed_ref), custom_call_target="tpu_custom_call" | custom-call | flops 1000000 | bytes 1000000 | tf_op jit(solution)/shard_map/pallas_call | solution.py:20
  7.0 2.0 %all-to-all-done = f32[4,16,128]{2,1,0:T(8,128)S(1)} async-done(((f32[4,16,128]{2,1,0:T(8,128)}), f32[4,16,128]{2,1,0:T(8,128)S(1)}, u32[]{:S(2)}, u32[]{:S(2)}) %all-to-all-start) | async-done | bytes 32800 | tf_op jit(solution)/shard_map/all_to_all | solution.py:394
  8.9 0.1 shard_map.88.to_a_ref.to_ref.first_ref
  9.1 5.1 %collective-permute-start.1 = (f32[136,128]{1,0:T(8,128)S(1)}, f32[136,128]{1,0:T(8,128)S(1)}, u32[]{:S(2)}, u32[]{:S(2)}) collective-permute-start(f32[136,128]{1,0:T(8,128)S(1)} %shard_map.88.to_a_ref.to_ref.first_ref), channel_id=1, source_target_pairs={{4,8},{8,4},{12,16},{16,12},{20,24},{24,20},{28,0},{0,28},{5,9},{9... | collective-permute-start | bytes 208904 | tf_op jit(solution)/shard_map/ppermute | solution.py:378
  14.2 0.4 shard_map.89.to_ref.first_ref
  14.6 0.1 collective-permute-start
  14.6 4.5 %shard_map.87.product_ref = f32[32,128]{1,0:T(8,128)} custom-call(f32[168,128]{1,0:T(8,128)} %copy-done, f32[32,128]{1,0:T(8,128)} %copy-done.3, bf16[48,9216]{1,0:T(8,128)(2,1)} %bitcast.17), custom_call_target="tpu_custom_call" | custom-call | flops 1000000 | bytes 1000000 | tf_op jit(solution)/shard_map/pallas_call | solution.py:20
  19.2 0.7 %copy-done.7 = f32[32,128]{1,0:T(8,128)S(1)} copy-done((f32[32,128]{1,0:T(8,128)S(1)}, f32[32,128]{1,0:T(8,128)}, u32[]{:S(2)}) %copy-start.7) | copy-done | bytes 16408
  19.9 0.7 %shard_map.90 = (f32[32,128]{1,0:T(8,128)S(1)}, f32[64,128]{1,0:T(8,128)S(1)}) custom-call(s32[128,128]{1,0:T(8,128)S(1)} %get-tuple-element.14.aligned_ref, f32[32,128]{1,0:T(8,128)S(1)} %copy-done.7, f32[128,128]{1,0:T(8,128)S(1)} %shard_map.89.to_ref.first_ref, f32[128,128]{1,0:T(8,128)S(1)} %collective-permute-done.from_ref), custom_call_target="tpu_custom_call" | custom-call | flops 1 | bytes 1 | tf_op jit(solution)/shard_map/pallas_call | solution.py:20
  20.6 1.1 %shard_map.91 = (f32[32,128]{1,0:T(8,128)S(1)}, f32[64,128]{1,0:T(8,128)S(1)}, f32[72,128]{1,0:T(8,128)S(1)}) custom-call(s32[128,128]{1,0:T(8,128)S(1)} %get-tuple-element.14.aligned_ref, f32[32,128]{1,0:T(8,128)S(1)} %get-tuple-element.17.partial_ref, f32[136,128]{1,0:T(8,128)S(1)} %shard_map.88.to_a_ref.to_ref.first_ref, ...), custom_call_target="tpu_custom_call" | custom-call | flops 1000000 | bytes 1000000 | tf_op jit(solution)/shard_map/pallas_call | solution.py:20
  21.7 2.0 %collective-permute-start.2 = (f32[72,128]{1,0:T(8,128)S(1)}, f32[72,128]{1,0:T(8,128)S(1)}, u32[]{:S(2)}, u32[]{:S(2)}) collective-permute-start(f32[72,128]{1,0:T(8,128)S(1)} %get-tuple-element.21.side_a_ref.own_ref), channel_id=1, source_target_pairs={{4,8},{8,4},{12,16},{16,12},{20,24},{24,20},{28,0},{0,28},{5,9},{9... | collective-permute-start | bytes 110600 | tf_op jit(solution)/shard_map/ppermute | solution.py:378
  23.7 0.4 shard_map.93.side_b_ref.own_ref
  24.1 0.3 collective-permute-start.3
  24.4 4.5 %shard_map.92.product_ref = f32[32,128]{1,0:T(8,128)} custom-call(f32[168,128]{1,0:T(8,128)} %copy-done, f32[32,128]{1,0:T(8,128)} %copy-done.1, bf16[48,9216]{1,0:T(8,128)(2,1)} %bitcast.18), custom_call_target="tpu_custom_call" | custom-call | flops 1000000 | bytes 1000000 | tf_op jit(solution)/shard_map/pallas_call | solution.py:20
  28.9 0.7 %copy-done.5 = f32[32,128]{1,0:T(8,128)S(1)} copy-done((f32[32,128]{1,0:T(8,128)S(1)}, f32[32,128]{1,0:T(8,128)}, u32[]{:S(2)}) %copy-start.5) | copy-done | bytes 16408
  29.7 0.7 %shard_map.96 = f32[32,1,128]{2,1,0:T(1,128)} custom-call(f32[8,128]{1,0:T(8,128)S(1)} %shard_map.95.rows_ref, f32[64,128]{1,0:T(8,128)S(1)} %get-tuple-element.19.weights_a_ref.weights_ref, f32[72,128]{1,0:T(8,128)S(1)} %get-tuple-element.21.side_a_ref.own_ref, f32[72,128]{1,0:T(8,128)S(1)} %collective-permute-done.2.from_a_ref.arrived_ref, ...), custom_call_target="tpu_custom_call" | custom-call | flops 1000000 | bytes 1000000 | tf_op jit(solution)/shard_map/pallas_call | solution.py:20
  30.4 3.6 %all-to-all-start.1 = ((f32[32,1,128]{2,1,0:T(1,128)}), f32[32,1,128]{2,1,0:T(1,128)S(1)}, u32[]{:S(2)}, u32[]{:S(2)}) async-start(f32[32,1,128]{2,1,0:T(1,128)} %shard_map.96), calls=%async_computation.1 | async-start | bytes 32768 | tf_op jit(solution)/shard_map/all_to_all | solution.py:483
  34.0 1.2 %shard_map.94.second_ref = f32[32,128]{1,0:T(8,128)S(1)} custom-call(s32[128,128]{1,0:T(8,128)S(1)} %get-tuple-element.14.aligned_ref, f32[32,128]{1,0:T(8,128)S(1)} %copy-done.6, f32[64,128]{1,0:T(8,128)S(1)} %get-tuple-element.19.weights_a_ref.weights_ref, f32[64,128]{1,0:T(8,128)S(1)} %get-tuple-element.20.weights_b_ref.weights_ref, ...), custom_call_target="tpu_custom_call" | custom-call | flops 1000000000 | bytes 1000000 | tf_op jit(solution)/shard_map/pallas_call | solution.py:20
  35.2 5.8 %all-to-all-done.1.sums_ref = f32[32,1,128]{2,1,0:T(1,128)S(1)} async-done(((f32[32,1,128]{2,1,0:T(1,128)}), f32[32,1,128]{2,1,0:T(1,128)S(1)}, u32[]{:S(2)}, u32[]{:S(2)}) %all-to-all-start.1) | async-done | bytes 16416 | tf_op jit(solution)/shard_map/all_to_all | solution.py:483
  41.0 0.7 %shard_map.97 = (f32[32,96]{1,0:T(8,128)}, f32[32,96]{1,0:T(8,128)}) custom-call(f32[32,128]{1,0:T(8,128)S(1)} %copy-done.4, f32[32,128]{1,0:T(8,128)S(1)} %copy-done.2, f32[32,128]{1,0:T(8,128)S(1)} %shard_map.94.second_ref, f32[32,1,128]{2,1,0:T(1,128)S(1)} %all-to-all-done.1.sums_ref), custom_call_target="tpu_custom_call" | custom-call | flops 1000000 | bytes 1000000 | tf_op jit(solution)/shard_map/pallas_call | solution.py:20
  (25 shorter events, 0.1 us)
Async XLA Ops:
  0.6 4.4 %copy-start.8 = (s32[1,1,128,128]{3,2,1,0:T(8,128)S(1)}, s32[1,1,128,128]{3,2,1,0:T(8,128)}, u32[]{:S(2)}) copy-start(s32[1,1,128,128]{3,2,1,0:T(8,128)} %param.10) | copy-start | bytes 196612
  0.6 8.3 %all-to-all-start = ((f32[4,16,128]{2,1,0:T(8,128)}), f32[4,16,128]{2,1,0:T(8,128)S(1)}, u32[]{:S(2)}, u32[]{:S(2)}) async-start(f32[4,16,128]{2,1,0:T(8,128)} %bitcast.20), calls=%async_computation | async-start | bytes 65536 | tf_op jit(solution)/shard_map/all_to_all | solution.py:394
  5.0 0.7 %copy-start.11 = (s32[1,1,64]{2,1,0:T(1,128)S(1)}, s32[1,1,64]{2,1,0:T(1,128)}, u32[]{:S(2)}) copy-start(s32[1,1,64]{2,1,0:T(1,128)} %param.11) | copy-start | bytes 772
  5.0 0.7 %copy-start.9 = (s32[1,1,2,16]{3,2,1,0:T(2,128)S(1)}, s32[1,1,2,16]{3,2,1,0:T(2,128)}, u32[]{:S(2)}) copy-start(s32[1,1,2,16]{3,2,1,0:T(2,128)} %param.9) | copy-start | bytes 388
  5.0 0.7 %copy-start.10 = (s32[1,1,4]{2,1,0:T(1,128)S(1)}, s32[1,1,4]{2,1,0:T(1,128)}, u32[]{:S(2)}) copy-start(s32[1,1,4]{2,1,0:T(1,128)} %param.12) | copy-start | bytes 52
  6.4 2.7 %copy-start = (f32[168,128]{1,0:T(8,128)}, f32[168,128]{1,0:T(8,128)S(1)}, u32[]{:S(2)}) copy-start(f32[168,128]{1,0:T(8,128)S(1)} %pad_add_fusion.packed_ref) | copy-start | bytes 258052
  7.0 7.2 %copy-start.3 = (f32[32,128]{1,0:T(8,128)}, f32[32,128]{1,0:T(8,128)S(1)}, u32[]{:S(2)}) copy-start(f32[32,128]{1,0:T(8,128)S(1)} %get-tuple-element.13.field_ref.padded_ref) | copy-start | bytes 49156
  9.1 11.5 %collective-permute-start.1 = (f32[136,128]{1,0:T(8,128)S(1)}, f32[136,128]{1,0:T(8,128)S(1)}, u32[]{:S(2)}, u32[]{:S(2)}) collective-permute-start(f32[136,128]{1,0:T(8,128)S(1)} %shard_map.88.to_a_ref.to_ref.first_ref), channel_id=1, source_target_pairs={{4,8},{8,4},{12,16},{16,12},{20,24},{24,20},{28,0},{0,28},{5,9},{9... | collective-permute-start | bytes 208904 | tf_op jit(solution)/shard_map/ppermute | solution.py:378
  14.6 4.6 %collective-permute-start = (f32[128,128]{1,0:T(8,128)S(1)}, f32[128,128]{1,0:T(8,128)S(1)}, u32[]{:S(2)}, u32[]{:S(2)}) collective-permute-start(f32[128,128]{1,0:T(8,128)S(1)} %shard_map.89.to_ref.first_ref), channel_id=1, source_target_pairs={{0,4},{4,0},{8,12},{12,8},{16,20},{20,16},{24,28},{28,24},{1,5},{5... | collective-permute-start | bytes 196616 | tf_op jit(solution)/shard_map/ppermute | solution.py:378
  19.2 0.7 %copy-start.7 = (f32[32,128]{1,0:T(8,128)S(1)}, f32[32,128]{1,0:T(8,128)}, u32[]{:S(2)}) copy-start(f32[32,128]{1,0:T(8,128)} %shard_map.87.product_ref) | copy-start | bytes 49156
  21.7 2.3 %copy-start.1 = (f32[32,128]{1,0:T(8,128)}, f32[32,128]{1,0:T(8,128)S(1)}, u32[]{:S(2)}) copy-start(f32[32,128]{1,0:T(8,128)S(1)} %get-tuple-element.18.field_ref.image_ref) | copy-start | bytes 49156
  21.7 7.9 %collective-permute-start.2 = (f32[72,128]{1,0:T(8,128)S(1)}, f32[72,128]{1,0:T(8,128)S(1)}, u32[]{:S(2)}, u32[]{:S(2)}) collective-permute-start(f32[72,128]{1,0:T(8,128)S(1)} %get-tuple-element.21.side_a_ref.own_ref), channel_id=1, source_target_pairs={{4,8},{8,4},{12,16},{16,12},{20,24},{24,20},{28,0},{0,28},{5,9},{9... | collective-permute-start | bytes 110600 | tf_op jit(solution)/shard_map/ppermute | solution.py:378
  24.1 4.8 %copy-start.4 = (f32[32,128]{1,0:T(8,128)S(1)}, f32[32,128]{1,0:T(8,128)}, u32[]{:S(2)}) copy-start(f32[32,128]{1,0:T(8,128)} %copy-done.3) | copy-start | bytes 49156
  24.1 4.8 %collective-permute-start.3 = (f32[64,128]{1,0:T(8,128)S(1)}, f32[64,128]{1,0:T(8,128)S(1)}, u32[]{:S(2)}, u32[]{:S(2)}) collective-permute-start(f32[64,128]{1,0:T(8,128)S(1)} %shard_map.93.side_b_ref.own_ref), channel_id=1, source_target_pairs={{0,4},{4,0},{8,12},{12,8},{16,20},{20,16},{24,28},{28,24},{1,5},{5... | collective-permute-start | bytes 98312 | tf_op jit(solution)/shard_map/ppermute | solution.py:378
  24.4 4.5 %copy-start.2 = (f32[32,128]{1,0:T(8,128)S(1)}, f32[32,128]{1,0:T(8,128)}, u32[]{:S(2)}) copy-start(f32[32,128]{1,0:T(8,128)} %copy-done.1) | copy-start | bytes 49156
  28.9 0.7 %copy-start.5 = (f32[32,128]{1,0:T(8,128)S(1)}, f32[32,128]{1,0:T(8,128)}, u32[]{:S(2)}) copy-start(f32[32,128]{1,0:T(8,128)} %shard_map.92.product_ref) | copy-start | bytes 49156
  30.4 3.6 %copy-start.6 = (f32[32,128]{1,0:T(8,128)S(1)}, f32[32,128]{1,0:T(8,128)}, u32[]{:S(2)}) copy-start(f32[32,128]{1,0:T(8,128)} %shard_map.92.product_ref) | copy-start | bytes 49156
  30.4 10.6 %all-to-all-start.1 = ((f32[32,1,128]{2,1,0:T(1,128)}), f32[32,1,128]{2,1,0:T(1,128)S(1)}, u32[]{:S(2)}, u32[]{:S(2)}) async-start(f32[32,1,128]{2,1,0:T(1,128)} %shard_map.96), calls=%async_computation.1 | async-start | bytes 32768 | tf_op jit(solution)/shard_map/all_to_all | solution.py:483

commit v8 on v7

--- a/solution.py
+++ b/solution.py
@@ -1,5 +1,4 @@
 import functools
-import math
 
 import jax
 import jax.numpy as jnp
@@ -11,19 +10,19 @@
 LANES = 128
 SUBLANES = 8
 VMEM = pl.BlockSpec(memory_space=pltpu.VMEM)
-HBM = pl.BlockSpec(memory_space=pltpu.HBM)
+SMEM = pl.BlockSpec(memory_space=pltpu.SMEM)
 F32 = jnp.float32
 BF16 = jnp.bfloat16
 
 
-def call(body, outs, inputs, scratch=(), flops=1_000_000, moved=1_000_000, limit=32 * 1024 * 1024):
+def call(body, outs, inputs, scratch=(), flops=1_000_000, moved=1_000_000):
     return pl.pallas_call(
         body,
         out_shape=outs,
         in_specs=[spec for _, spec in inputs],
         out_specs=[VMEM] * len(outs),
         scratch_shapes=list(scratch),
-        compiler_params=pltpu.CompilerParams(vmem_limit_bytes=limit),
+        compiler_params=pltpu.CompilerParams(vmem_limit_bytes=32 * 1024 * 1024),
         cost_estimate=pl.CostEstimate(
             flops=flops, bytes_accessed=moved, transcendentals=0
         ),
@@ -124,80 +123,40 @@
     gather_traces(image_ref[...], aligned_ref, side_b_ref.shape[0], side_b_ref)
 
 
-def stiffness_kernel(
-    size, count, pieces, packed_ref, field_ref, blocks_hbm, out_ref, blocks_ref, sems
-):
+def stiffness_kernel(pairs_ref, blocks_ref, field_ref, out_ref, pieces, sums):
     block_rows = field_ref.shape[0]
-    width = math.lcm(size, LANES)
-    tiles = width // LANES
-    segments = width // size
-    groups = size // segments // pieces
-    copies = []
-    for k in range(pieces):
-        part = slice(k * groups * width, (k + 1) * groups * width)
-        copies.append(
-            pltpu.make_async_copy(blocks_hbm.at[:, part], blocks_ref.at[:, part], sems.at[k])
-        )
-        copies[-1].start()
-
-    def place(position):
-        segment = sum(jnp.where(position >= k * size, 1, 0) for k in range(1, segments))
-        return segment, position - segment * size
-
-    def lanes_of(value, index):
-        slabs = [
-            jnp.take_along_axis(
-                value[k : k + SUBLANES, :], index, axis=1, mode="promise_in_bounds"
-            )
-            for k in range(0, value.shape[0], SUBLANES)
-        ]
-        return jnp.concatenate(slabs, axis=0)
-
-    tail = packed_ref[packed_ref.shape[0] - SUBLANES :, :].astype(jnp.int32)
-    first_of, other_of = (one_hot(tail[k : k + 1, :count], block_rows) for k in (2, 3))
-    field = field_ref[...]
-    left, other = (
-        lax.dot_general(
-            ends,
-            field,
-            (((0,), (0,)), ((), ())),
-            precision=lax.Precision.HIGHEST,
+    size = blocks_ref.shape[1]
+    count = pairs_ref.shape[1]
+    high, low = halves(field_ref[...])
+    pieces[...] = jnp.zeros_like(pieces)
+    pieces[pl.ds(0, block_rows, stride=SUBLANES), :] = high
+    pieces[pl.ds(1, block_rows, stride=SUBLANES), :] = low
+
+    def times(row, block, contract):
+        left = pieces[pl.ds(pl.multiple_of(row * SUBLANES, SUBLANES), SUBLANES), :]
+        return lax.dot_general(
+            left[:, :size].astype(BF16),
+            block,
+            (((1,), (contract,)), ((), ())),
             preferred_element_type=F32,
         )
-        for ends in (first_of, other_of)
-    )
-    right = jnp.concatenate([field, other], axis=0)
-    lane = lax.broadcasted_iota(jnp.int32, (SUBLANES, LANES), 1)
-    places = [place(lane + t * LANES) for t in range(tiles)]
-    repeated = jnp.concatenate([lanes_of(right, inside) for _, inside in places], axis=1)
-    segment, inside = place(lax.broadcasted_iota(jnp.int32, (width, LANES), 0))
-    column = lax.broadcasted_iota(jnp.int32, (width, LANES), 1)
-    add_segments = jnp.where(segment == column % segments, 1.0, 0.0).astype(BF16)
-    fold = jnp.where(inside == column, 1.0, 0.0)
-    rows = block_rows + count
-    dof_group = lax.broadcasted_iota(jnp.int32, (rows, LANES), 1) // segments
-    total = jnp.zeros((rows, LANES), F32)
-    turned = jnp.zeros((count, width), F32)
-    for k in range(pieces):
-        copies[k].wait()
-        stack = []
-        for g in range(k * groups, (k + 1) * groups):
-            stored = blocks_ref[:, g * width : (g + 1) * width].astype(F32)
-            product = stored * repeated
-            high = product.astype(BF16)
-            stack += [high, (product - high.astype(F32)).astype(BF16)]
-            across = [lanes_of(left, g * segments + segment) for segment, _ in places]
-            turned = turned + stored[block_rows:] * jnp.concatenate(across, axis=1)
-        sums = jnp.dot(
-            jnp.concatenate(stack, axis=0), add_segments, preferred_element_type=F32
-        )
-        for n in range(groups):
-            both = sums[2 * n * rows : 2 * (n + 1) * rows]
-            total = jnp.where(dof_group == k * groups + n, both[:rows] + both[rows:], total)
+
+    def add(row, value):
+        place = pl.ds(pl.multiple_of(row * SUBLANES, SUBLANES), SUBLANES)
+        sums[place, :size] = sums[place, :size] + value
+
+    sums[...] = jnp.zeros_like(sums)
+    for i in range(block_rows):
+        sums[i * SUBLANES : (i + 1) * SUBLANES, :size] = times(i, blocks_ref[i], 1)
+    for p in range(count):
+        first = pairs_ref[0, p]
+        other = pairs_ref[1, p]
+        block = blocks_ref[block_rows + p]
+        add(first, times(other, block, 1))
+        add(other, times(first, block, 0))
     out_ref[...] = (
-        total[:block_rows]
-        + exact_dot(first_of, total[block_rows:])
-        + exact_dot(other_of, exact_dot(turned, fold))
+        sums[pl.ds(0, block_rows, stride=SUBLANES), :]
+        + sums[pl.ds(1, block_rows, stride=SUBLANES), :]
     )
 
 
@@ -383,7 +342,8 @@
 ):
     field = right_side[0, 0].T
     block_rows, size = field.shape
-    blocks = stiffness[0, 0]
+    stored = stiffness[0, 0]
+    blocks = stored.reshape(stored.shape[0], size, size)
     pairs = block_pairs[0, 0]
     rows = trace_rows[0, 0]
     partner = partner_face[0, 0]
@@ -398,12 +358,7 @@
         below = last + SUBLANES - first - value.shape[0]
         return jnp.pad(value, ((first, below), (0, LANES - value.shape[1])))
 
-    indices = (
-        placed(rows, 0)
-        + placed(partner_face[0], last)
-        + placed(owner_list[0], last + 1)
-        + placed(pairs, last + 2)
-    )
+    indices = placed(rows, 0) + placed(partner_face[0], last) + placed(owner_list[0], last + 1)
     packed = indices.astype(F32) + placed(field, 2 * faces)
     aligned, padded, chosen, side_a = call(
         functools.partial(first_kernel, owners.shape[0]),
@@ -427,15 +382,12 @@
         [(value, VMEM) for value in (aligned, padded, to_a)],
     )
     from_b = swap(to_b, 0)
-    pieces = next(k for k in (6, 4, 3, 2, 1) if size * size // math.lcm(size, LANES) % k == 0)
-
     def stiff(vector):
         (product,) = call(
-            functools.partial(stiffness_kernel, size, pairs.shape[1], pieces),
+            stiffness_kernel,
             [shape(block_rows)],
-            [(packed, VMEM), (vector, VMEM), (blocks, HBM)],
-            scratch=[pltpu.VMEM(blocks.shape, BF16), pltpu.SemaphoreType.DMA((pieces,))],
-            limit=66_300_000,
+            [(pairs, SMEM), (blocks, VMEM), (vector, VMEM)],
+            scratch=[pltpu.VMEM((block_rows * SUBLANES, LANES), F32)] * 2,
         )
         return product
 

time: 42.4 us -> 39 us (0.920)
  Pallas kernels: 15 us -> 8.77 us
  waiting for transfers between devices: 7.78 us -> 12 us
  starting transfers between devices: 15.3 us -> 13.9 us
    pallas_call x12, Pallas kernels: 15 us -> 8.77 us  [call(): pl.pallas_call(body, out_shape=outs, in_specs=[spec for _, spec in inputs...]
    ppermute x4, waiting for transfers between devices: 0.01 us -> 3.71 us  [swap(): return lax.ppermute(value, 'sub', pairs)]
    another operation x0 -> x1, local copies, waits for them, and re-layouts: none -> 2.3 us  [on_device(): blocks = stored.reshape(stored.shape[0], size, size)]
    unnamed x24 -> x2, local copies, waits for them, and re-layouts: 2.15 us -> 0.02 us
    all_to_all x1, starting transfers between devices: 3.55 us -> 2.82 us  [on_device(): lax.all_to_all(sums, ('sub', 'blk'), split_axis=0, concat_axis=0, tiled=T...]
    all_to_all x1, waiting for transfers between devices: 1.96 us -> 2.5 us  [on_device(): lax.all_to_all(mortar_weight[0, 0], 'blk', split_axis=0, concat_axis=0, t...]
    ppermute x4, starting transfers between devices: 7.39 us -> 6.89 us  [swap(): return lax.ppermute(value, 'sub', pairs)]
  transfers between devices with their start and end apart: 6 -> 6, of which waited for: 2 -> 5; matrix products, arithmetic and copies ran while one was open for 2% -> 8% of each run, Pallas kernels for 29% -> 16%
where the time goes in v8:
time: 39 us; the launch traced here: 38.7 us
  starting transfers between devices  13.9 us (36%)
  waiting for transfers between devices  12 us (31%)
  Pallas kernels  8.77 us (22%)
  local copies, waits for them, and re-layouts  2.31 us (6%)
  other arithmetic  0.9 us (2%)
  between operations  0.74 us (2%)
    pallas_call x12, Pallas kernels, call(): pl.pallas_call(body, out_shape=outs, in_specs=[spec for _, spec in inputs...  8.77 us
    ppermute x4, starting transfers between devices, swap(): return lax.ppermute(value, 'sub', pairs)  6.89 us
    all_to_all x1, waiting for transfers between devices, on_device(): lax.all_to_all(sums, ('sub', 'blk'), split_axis=0, concat_axis=0, tiled=T...  5.83 us
    all_to_all x1, starting transfers between devices, on_device(): lax.all_to_all(mortar_weight[0, 0], 'blk', split_axis=0, concat_axis=0, t...  4.22 us
    ppermute x4, waiting for transfers between devices, swap(): return lax.ppermute(value, 'sub', pairs)  3.71 us
    all_to_all x1, starting transfers between devices, on_device(): lax.all_to_all(sums, ('sub', 'blk'), split_axis=0, concat_axis=0, tiled=T...  2.82 us
    all_to_all x1, waiting for transfers between devices, on_device(): lax.all_to_all(mortar_weight[0, 0], 'blk', split_axis=0, concat_axis=0, t...  2.5 us
    another operation x1, local copies, waits for them, and re-layouts, on_device(): blocks = stored.reshape(stored.shape[0], size, size)  2.3 us
  transfers between devices with their start and end apart: 6, of which 5 were waited for; matrix products, arithmetic and copies ran while one was open for 8% of the time, Pallas kernels for 16%

profile of v8, /device:TPU:0, one launch (start us, length us, event | category | flops | bytes accessed | tf_op | source)
XLA Modules:
  0.0 38.7 jit_solution(7248668146497267848)
XLA Ops:
  0.6 4.2 %all-to-all-start = ((f32[4,16,128]{2,1,0:T(8,128)}), f32[4,16,128]{2,1,0:T(8,128)S(1)}, u32[]{:S(2)}, u32[]{:S(2)}) async-start(f32[4,16,128]{2,1,0:T(8,128)} %bitcast.21), calls=%async_computation | async-start | bytes 65536 | tf_op jit(solution)/shard_map/all_to_all | solution.py:354
  4.8 0.9 %pad_add_fusion.packed_ref = f32[168,128]{1,0:T(8,128)S(1)} fusion(f32[32,96]{1,0:T(8,128)} %bitcast.22, s32[1,4]{1,0:T(1,128)} %bitcast.23, s32[1,64]{1,0:T(1,128)} %bitcast.24, s32[128,128]{1,0:T(8,128)} %bitcast.20), kind=kLoop, calls=%fused_computation | loop fusion | flops 86016 | bytes 164112 | tf_op jit(solution)/shard_map/add | solution.py:362
  5.8 0.5 %shard_map.86 = (s32[128,128]{1,0:T(8,128)S(1)}, f32[32,128]{1,0:T(8,128)S(1)}, f32[64,64]{1,0:T(8,128)S(1)}, f32[64,128]{1,0:T(8,128)S(1)}) custom-call(f32[168,128]{1,0:T(8,128)S(1)} %pad_add_fusion.packed_ref), custom_call_target="tpu_custom_call" | custom-call | flops 1000000 | bytes 1000000 | tf_op jit(solution)/shard_map/pallas_call | solution.py:19
  6.3 2.5 %all-to-all-done = f32[4,16,128]{2,1,0:T(8,128)S(1)} async-done(((f32[4,16,128]{2,1,0:T(8,128)}), f32[4,16,128]{2,1,0:T(8,128)S(1)}, u32[]{:S(2)}, u32[]{:S(2)}) %all-to-all-start) | async-done | bytes 32800 | tf_op jit(solution)/shard_map/all_to_all | solution.py:354
  8.8 0.1 shard_map.88.to_a_ref.to_ref.first_ref
  9.0 5.1 %collective-permute-start.1 = (f32[136,128]{1,0:T(8,128)S(1)}, f32[136,128]{1,0:T(8,128)S(1)}, u32[]{:S(2)}, u32[]{:S(2)}) collective-permute-start(f32[136,128]{1,0:T(8,128)S(1)} %shard_map.88.to_a_ref.to_ref.first_ref), channel_id=1, source_target_pairs={{4,8},{8,4},{12,16},{16,12},{20,24},{24,20},{28,0},{0,28},{5,9},{9... | collective-permute-start | bytes 208904 | tf_op jit(solution)/shard_map/ppermute | solution.py:337
  14.1 0.4 shard_map.89.to_ref.first_ref
  14.4 0.1 collective-permute-start
  14.5 2.3 %reshape_squeeze.3.blocks_ref = bf16[48,96,96]{2,1,0:T(8,128)(2,1)S(1)} reshape(bf16[1,1,48,9216]{3,2,1,0:T(8,128)(2,1)} %param.8) | data formatting | bytes 1769472 | tf_op jit(solution)/shard_map/reshape;squeeze | solution.py:346
  16.8 1.4 %shard_map.87.product_ref = f32[32,128]{1,0:T(8,128)S(1)} custom-call(s32[2,16]{1,0:T(2,128)S(1)} %bitcast.18, bf16[48,96,96]{2,1,0:T(8,128)(2,1)S(1)} %reshape_squeeze.3.blocks_ref, f32[32,128]{1,0:T(8,128)S(1)} %get-tuple-element.13.field_ref.padded_ref), custom_call_target="tpu_custom_call" | custom-call | flops 1000000 | bytes 1000000 | tf_op jit(solution)/shard_map/pallas_call | solution.py:19
  18.2 0.5 %collective-permute-done.from_ref = f32[128,128]{1,0:T(8,128)S(1)} collective-permute-done((f32[128,128]{1,0:T(8,128)S(1)}, f32[128,128]{1,0:T(8,128)S(1)}, u32[]{:S(2)}, u32[]{:S(2)}) %collective-permute-start) | collective-permute-done | bytes 65568 | tf_op jit(solution)/shard_map/ppermute | solution.py:337
  18.8 0.7 %shard_map.90 = (f32[32,128]{1,0:T(8,128)S(1)}, f32[64,128]{1,0:T(8,128)S(1)}) custom-call(s32[128,128]{1,0:T(8,128)S(1)} %get-tuple-element.14.aligned_ref, f32[32,128]{1,0:T(8,128)S(1)} %shard_map.87.product_ref, f32[128,128]{1,0:T(8,128)S(1)} %shard_map.89.to_ref.first_ref, f32[128,128]{1,0:T(8,128)S(1)} %collective-permute-done.from_ref), custom_call_target="tpu_custom_call" | custom-call | flops 1 | bytes 1 | tf_op jit(solution)/shard_map/pallas_call | solution.py:19
  19.5 1.1 %shard_map.91 = (f32[32,128]{1,0:T(8,128)S(1)}, f32[64,128]{1,0:T(8,128)S(1)}, f32[72,128]{1,0:T(8,128)S(1)}) custom-call(s32[128,128]{1,0:T(8,128)S(1)} %get-tuple-element.14.aligned_ref, f32[32,128]{1,0:T(8,128)S(1)} %get-tuple-element.17.partial_ref, f32[136,128]{1,0:T(8,128)S(1)} %shard_map.88.to_a_ref.to_ref.first_ref, ...), custom_call_target="tpu_custom_call" | custom-call | flops 1000000 | bytes 1000000 | tf_op jit(solution)/shard_map/pallas_call | solution.py:19
  20.6 1.7 %collective-permute-start.2 = (f32[72,128]{1,0:T(8,128)S(1)}, f32[72,128]{1,0:T(8,128)S(1)}, u32[]{:S(2)}, u32[]{:S(2)}) collective-permute-start(f32[72,128]{1,0:T(8,128)S(1)} %get-tuple-element.21.side_a_ref.own_ref), channel_id=1, source_target_pairs={{4,8},{8,4},{12,16},{16,12},{20,24},{24,20},{28,0},{0,28},{5,9},{9... | collective-permute-start | bytes 110600 | tf_op jit(solution)/shard_map/ppermute | solution.py:337
  22.3 0.4 shard_map.93.side_b_ref.own_ref
  22.6 0.1 collective-permute-start.3
  22.7 1.4 %shard_map.92.product_ref = f32[32,128]{1,0:T(8,128)S(1)} custom-call(s32[2,16]{1,0:T(2,128)S(1)} %bitcast.19, bf16[48,96,96]{2,1,0:T(8,128)(2,1)S(1)} %reshape_squeeze.3.blocks_ref, f32[32,128]{1,0:T(8,128)S(1)} %get-tuple-element.18.field_ref.image_ref), custom_call_target="tpu_custom_call" | custom-call | flops 1000000 | bytes 1000000 | tf_op jit(solution)/shard_map/pallas_call | solution.py:19
  24.1 2.5 %collective-permute-done.3.from_b_ref.arrived_ref = f32[64,128]{1,0:T(8,128)S(1)} collective-permute-done((f32[64,128]{1,0:T(8,128)S(1)}, f32[64,128]{1,0:T(8,128)S(1)}, u32[]{:S(2)}, u32[]{:S(2)}) %collective-permute-start.3) | collective-permute-done | bytes 32800 | tf_op jit(solution)/shard_map/ppermute | solution.py:337
  26.6 0.7 %collective-permute-done.2.from_a_ref.arrived_ref = f32[72,128]{1,0:T(8,128)S(1)} collective-permute-done((f32[72,128]{1,0:T(8,128)S(1)}, f32[72,128]{1,0:T(8,128)S(1)}, u32[]{:S(2)}, u32[]{:S(2)}) %collective-permute-start.2) | collective-permute-done | bytes 36896 | tf_op jit(solution)/shard_map/ppermute | solution.py:337
  27.3 0.7 %shard_map.96 = f32[32,1,128]{2,1,0:T(1,128)} custom-call(f32[8,128]{1,0:T(8,128)S(1)} %shard_map.95.rows_ref, f32[64,128]{1,0:T(8,128)S(1)} %get-tuple-element.19.weights_a_ref.weights_ref, f32[72,128]{1,0:T(8,128)S(1)} %get-tuple-element.21.side_a_ref.own_ref, f32[72,128]{1,0:T(8,128)S(1)} %collective-permute-done.2.from_a_ref.arrived_ref, ...), custom_call_target="tpu_custom_call" | custom-call | flops 1000000 | bytes 1000000 | tf_op jit(solution)/shard_map/pallas_call | solution.py:19
  28.0 2.8 %all-to-all-start.1 = ((f32[32,1,128]{2,1,0:T(1,128)}), f32[32,1,128]{2,1,0:T(1,128)S(1)}, u32[]{:S(2)}, u32[]{:S(2)}) async-start(f32[32,1,128]{2,1,0:T(1,128)} %shard_map.96), calls=%async_computation.1 | async-start | bytes 32768 | tf_op jit(solution)/shard_map/all_to_all | solution.py:435
  30.9 1.2 %shard_map.94.second_ref = f32[32,128]{1,0:T(8,128)S(1)} custom-call(s32[128,128]{1,0:T(8,128)S(1)} %get-tuple-element.14.aligned_ref, f32[32,128]{1,0:T(8,128)S(1)} %shard_map.92.product_ref, f32[64,128]{1,0:T(8,128)S(1)} %get-tuple-element.19.weights_a_ref.weights_ref, f32[64,128]{1,0:T(8,128)S(1)} %get-tuple-element.20.weights_b_ref.weights_ref, ...), custom_call_target="tpu_custom_call" | custom-call | flops 1000000000 | bytes 1000000 | tf_op jit(solution)/shard_map/pallas_call | solution.py:19
  32.1 5.8 %all-to-all-done.1.sums_ref = f32[32,1,128]{2,1,0:T(1,128)S(1)} async-done(((f32[32,1,128]{2,1,0:T(1,128)}), f32[32,1,128]{2,1,0:T(1,128)S(1)}, u32[]{:S(2)}, u32[]{:S(2)}) %all-to-all-start.1) | async-done | bytes 16416 | tf_op jit(solution)/shard_map/all_to_all | solution.py:435
  37.9 0.7 %shard_map.97 = (f32[32,96]{1,0:T(8,128)}, f32[32,96]{1,0:T(8,128)}) custom-call(f32[32,128]{1,0:T(8,128)S(1)} %get-tuple-element.13.field_ref.padded_ref, f32[32,128]{1,0:T(8,128)S(1)} %get-tuple-element.18.field_ref.image_ref, f32[32,128]{1,0:T(8,128)S(1)} %shard_map.94.second_ref, f32[32,1,128]{2,1,0:T(1,128)S(1)} %all-to-all-done.1.sums_ref), custom_call_target="tpu_custom_call" | custom-call | flops 1000000 | bytes 1000000 | tf_op jit(solution)/shard_map/pallas_call | solution.py:19
  (4 shorter events, 0.0 us)
Async XLA Ops:
  0.6 8.2 %all-to-all-start = ((f32[4,16,128]{2,1,0:T(8,128)}), f32[4,16,128]{2,1,0:T(8,128)S(1)}, u32[]{:S(2)}, u32[]{:S(2)}) async-start(f32[4,16,128]{2,1,0:T(8,128)} %bitcast.21), calls=%async_computation | async-start | bytes 65536 | tf_op jit(solution)/shard_map/all_to_all | solution.py:354
  8.9 7.9 %copy-start = (s32[1,1,2,16]{3,2,1,0:T(2,128)S(1)}, s32[1,1,2,16]{3,2,1,0:T(2,128)}, u32[]{:S(2)}) copy-start(s32[1,1,2,16]{3,2,1,0:T(2,128)} %param.9) | copy-start | bytes 388
  9.0 10.5 %collective-permute-start.1 = (f32[136,128]{1,0:T(8,128)S(1)}, f32[136,128]{1,0:T(8,128)S(1)}, u32[]{:S(2)}, u32[]{:S(2)}) collective-permute-start(f32[136,128]{1,0:T(8,128)S(1)} %shard_map.88.to_a_ref.to_ref.first_ref), channel_id=1, source_target_pairs={{4,8},{8,4},{12,16},{16,12},{20,24},{24,20},{28,0},{0,28},{5,9},{9... | collective-permute-start | bytes 208904 | tf_op jit(solution)/shard_map/ppermute | solution.py:337
  14.4 4.3 %collective-permute-start = (f32[128,128]{1,0:T(8,128)S(1)}, f32[128,128]{1,0:T(8,128)S(1)}, u32[]{:S(2)}, u32[]{:S(2)}) collective-permute-start(f32[128,128]{1,0:T(8,128)S(1)} %shard_map.89.to_ref.first_ref), channel_id=1, source_target_pairs={{0,4},{4,0},{8,12},{12,8},{16,20},{20,16},{24,28},{28,24},{1,5},{5... | collective-permute-start | bytes 196616 | tf_op jit(solution)/shard_map/ppermute | solution.py:337
  20.6 6.7 %collective-permute-start.2 = (f32[72,128]{1,0:T(8,128)S(1)}, f32[72,128]{1,0:T(8,128)S(1)}, u32[]{:S(2)}, u32[]{:S(2)}) collective-permute-start(f32[72,128]{1,0:T(8,128)S(1)} %get-tuple-element.21.side_a_ref.own_ref), channel_id=1, source_target_pairs={{4,8},{8,4},{12,16},{16,12},{20,24},{24,20},{28,0},{0,28},{5,9},{9... | collective-permute-start | bytes 110600 | tf_op jit(solution)/shard_map/ppermute | solution.py:337
  22.6 4.0 %collective-permute-start.3 = (f32[64,128]{1,0:T(8,128)S(1)}, f32[64,128]{1,0:T(8,128)S(1)}, u32[]{:S(2)}, u32[]{:S(2)}) collective-permute-start(f32[64,128]{1,0:T(8,128)S(1)} %shard_map.93.side_b_ref.own_ref), channel_id=1, source_target_pairs={{0,4},{4,0},{8,12},{12,8},{16,20},{20,16},{24,28},{28,24},{1,5},{5... | collective-permute-start | bytes 98312 | tf_op jit(solution)/shard_map/ppermute | solution.py:337
  28.0 9.9 %all-to-all-start.1 = ((f32[32,1,128]{2,1,0:T(1,128)}), f32[32,1,128]{2,1,0:T(1,128)S(1)}, u32[]{:S(2)}, u32[]{:S(2)}) async-start(f32[32,1,128]{2,1,0:T(1,128)} %shard_map.96), calls=%async_computation.1 | async-start | bytes 32768 | tf_op jit(solution)/shard_map/all_to_all | solution.py:435

commit v9 on v8

--- a/solution.py
+++ b/solution.py
@@ -81,6 +81,7 @@
     faces = side_a_ref.shape[0]
     block_rows = padded_ref.shape[0]
     per_group = faces // groups
+    slot = lax.axis_index("blk")
     parity = lax.rem(lax.axis_index("sub"), 2)
     east = pl.multiple_of((1 - parity) * faces, faces)
     west = pl.multiple_of(parity * faces, faces)
@@ -92,7 +93,9 @@
     for g in range(groups):
         inside = face - g * per_group
         source = jnp.where(
-            (inside >= 0) & (inside < per_group), tail[1:2, g : g + 1] * per_group + inside, source
+            (inside >= 0) & (inside < per_group),
+            (groups - 1 - (tail[1:2, g : g + 1] ^ slot)) * per_group + inside,
+            source,
         )
     order = one_hot(partner, faces)
     aligned_ref[pl.ds(west, faces), :] = packed_ref[faces : 2 * faces, :].astype(jnp.int32)
@@ -106,10 +109,18 @@
     gather_traces(padded_ref[...], aligned_ref, 0, side_a_ref)
 
 
-def far_message_kernel(held_ref, chosen_ref, side_a_ref, to_a_ref):
+def blocks_kernel(weights_ref, *block_refs):
+    slot = lax.axis_index("blk")
+    for place, block_ref in enumerate(block_refs):
+        block_ref[...] = weights_ref[slot ^ (len(block_refs) - 1 - place)]
+
+
+def far_message_kernel(chosen_ref, side_a_ref, *refs):
     faces = side_a_ref.shape[0]
+    *block_refs, to_a_ref = refs
+    held = jnp.concatenate([block_ref[...] for block_ref in block_refs], axis=0)
     to_a_ref[:faces, :] = side_a_ref[...]
-    to_a_ref[faces : 2 * faces, :] = exact_dot(chosen_ref[...], held_ref[...])
+    to_a_ref[faces : 2 * faces, :] = exact_dot(chosen_ref[...], held)
     to_a_ref[2 * faces :, :] = jnp.zeros_like(to_a_ref[2 * faces :, :])
 
 
@@ -337,6 +348,11 @@
     return lax.ppermute(value, "sub", pairs)
 
 
+def swap_slots(value, k):
+    count = lax.axis_size("blk")
+    return lax.ppermute(value, "blk", [(slot, slot ^ k) for slot in range(count)])
+
+
 def on_device(
     right_side, stiffness, block_pairs, trace_rows, partner_face, owner_list, mortar_weight
 ):
@@ -351,7 +367,15 @@
     faces = partner.shape[0]
     devices = lax.axis_size("sub") * lax.axis_size("blk")
 
-    held = lax.all_to_all(mortar_weight[0, 0], "blk", split_axis=0, concat_axis=0, tiled=True)
+    held = call(
+        blocks_kernel,
+        [shape(mortar_weight.shape[3])] * mortar_weight.shape[2],
+        [(mortar_weight[0, 0], VMEM)],
+    )
+    held = [
+        swap_slots(block, k) if k else block
+        for k, block in zip(reversed(range(len(held))), held)
+    ]
     last = 2 * faces + block_rows
 
     def placed(value, first):
@@ -373,7 +397,7 @@
     (to_a,) = call(
         far_message_kernel,
         [shape(2 * faces + SUBLANES)],
-        [(value, VMEM) for value in (held.reshape(faces, LANES), chosen, side_a)],
+        [(value, VMEM) for value in (chosen, side_a, *held)],
     )
     from_a = swap(to_a, 1)
     (to_b,) = call(

time: 39 us -> 37.2 us (0.954)
  starting transfers between devices: 13.9 us -> 12.3 us
  waiting for transfers between devices: 12 us -> 11.1 us
  local copies, waits for them, and re-layouts: 2.31 us -> 3.07 us
    all_to_all x1 -> x0, starting transfers between devices: 4.22 us -> none  [on_device(): lax.all_to_all(mortar_weight[0, 0], 'blk', split_axis=0, concat_axis=0, t...]
    ppermute x0 -> x3, starting transfers between devices: none -> 3.06 us  [swap_slots(): lax.ppermute(value, 'blk', [(slot, slot ^ k) for slot in range(count)])]
    all_to_all x1 -> x0, waiting for transfers between devices: 2.5 us -> none  [on_device(): lax.all_to_all(mortar_weight[0, 0], 'blk', split_axis=0, concat_axis=0, t...]
    ppermute x0 -> x3, waiting for transfers between devices: none -> 1.52 us  [swap_slots(): lax.ppermute(value, 'blk', [(slot, slot ^ k) for slot in range(count)])]
    unnamed x2 -> x4, local copies, waits for them, and re-layouts: 0.02 us -> 0.77 us
    ppermute x4, starting transfers between devices: 6.89 us -> 6.42 us  [swap(): return lax.ppermute(value, 'sub', pairs)]
    pallas_call x12 -> x13, Pallas kernels: 8.77 us -> 8.77 us  [call(): pl.pallas_call(body, out_shape=outs, in_specs=[spec for _, spec in inputs...]
  transfers between devices with their start and end apart: 6 -> 8, of which waited for: 5 -> 5; matrix products, arithmetic and copies ran while one was open for 8% -> 9% of each run, Pallas kernels for 16% -> 16%
where the time goes in v9:
time: 37.2 us; the launch traced here: 36.9 us
  starting transfers between devices  12.3 us (33%)
  waiting for transfers between devices  11.1 us (30%)
  Pallas kernels  8.77 us (24%)
  local copies, waits for them, and re-layouts  3.07 us (8%)
  other arithmetic  0.9 us (2%)
  between operations  0.76 us (2%)
    pallas_call x13, Pallas kernels, call(): pl.pallas_call(body, out_shape=outs, in_specs=[spec for _, spec in inputs...  8.77 us
    ppermute x4, starting transfers between devices, swap(): return lax.ppermute(value, 'sub', pairs)  6.42 us
    all_to_all x1, waiting for transfers between devices, on_device(): lax.all_to_all(sums, ('sub', 'blk'), split_axis=0, concat_axis=0, tiled=T...  5.83 us
    ppermute x4, waiting for transfers between devices, swap(): return lax.ppermute(value, 'sub', pairs)  3.71 us
    ppermute x3, starting transfers between devices, swap_slots(): lax.ppermute(value, 'blk', [(slot, slot ^ k) for slot in range(count)])  3.06 us
    all_to_all x1, starting transfers between devices, on_device(): lax.all_to_all(sums, ('sub', 'blk'), split_axis=0, concat_axis=0, tiled=T...  2.85 us
    another operation x1, local copies, waits for them, and re-layouts, on_device(): blocks = stored.reshape(stored.shape[0], size, size)  2.3 us
    ppermute x3, waiting for transfers between devices, swap_slots(): lax.ppermute(value, 'blk', [(slot, slot ^ k) for slot in range(count)])  1.52 us
  transfers between devices with their start and end apart: 8, of which 5 were waited for; matrix products, arithmetic and copies ran while one was open for 9% of the time, Pallas kernels for 16%

profile of v9, /device:TPU:0, one launch (start us, length us, event | category | flops | bytes accessed | tf_op | source)
XLA Modules:
  0.0 36.9 jit_solution(2363071647619744616)
XLA Ops:
  0.6 0.7 %copy-done = f32[1,1,4,16,128]{4,3,2,1,0:T(8,128)S(1)} copy-done((f32[1,1,4,16,128]{4,3,2,1,0:T(8,128)S(1)}, f32[1,1,4,16,128]{4,3,2,1,0:T(8,128)}, u32[]{:S(2)}) %copy-start) | copy-done | bytes 32792
  1.4 2.4 %collective-permute-start = (f32[16,128]{1,0:T(8,128)S(1)}, f32[16,128]{1,0:T(8,128)S(1)}, u32[]{:S(2)}, u32[]{:S(2)}) collective-permute-start(f32[16,128]{1,0:T(8,128)S(1)} %get-tuple-element.21), channel_id=1, source_target_pairs={{0,3},{1,2},{2,1},{3,0},{4,7},{5,6},{6,5},{7,4},{8,11},{9,10},{10,... | collective-permute-start | bytes 24584 | tf_op jit(solution)/shard_map/ppermute | solution.py:353
  3.8 0.6 %collective-permute-start.1 = (f32[16,128]{1,0:T(8,128)S(1)}, f32[16,128]{1,0:T(8,128)S(1)}, u32[]{:S(2)}, u32[]{:S(2)}) collective-permute-start(f32[16,128]{1,0:T(8,128)S(1)} %get-tuple-element.22), channel_id=1, source_target_pairs={{0,2},{1,3},{2,0},{3,1},{4,6},{5,7},{6,4},{7,5},{8,10},{9,11},{10,... | collective-permute-start | bytes 24584 | tf_op jit(solution)/shard_map/ppermute | solution.py:353
  4.5 0.9 %pad_add_fusion.packed_ref = f32[168,128]{1,0:T(8,128)S(1)} fusion(f32[32,96]{1,0:T(8,128)} %bitcast.20, s32[1,4]{1,0:T(1,128)} %bitcast.21, s32[1,64]{1,0:T(1,128)} %bitcast.22, s32[128,128]{1,0:T(8,128)} %bitcast.19), kind=kLoop, calls=%fused_computation | loop fusion | flops 86016 | bytes 164112 | tf_op jit(solution)/shard_map/add | solution.py:386
  5.4 0.5 %shard_map.86 = (s32[128,128]{1,0:T(8,128)S(1)}, f32[32,128]{1,0:T(8,128)S(1)}, f32[64,64]{1,0:T(8,128)S(1)}, f32[64,128]{1,0:T(8,128)S(1)}) custom-call(f32[168,128]{1,0:T(8,128)S(1)} %pad_add_fusion.packed_ref), custom_call_target="tpu_custom_call" | custom-call | flops 1000000 | bytes 1000000 | tf_op jit(solution)/shard_map/pallas_call | solution.py:19
  5.9 1.5 %collective-permute-done.1.refs_1_ = f32[16,128]{1,0:T(8,128)S(1)} collective-permute-done((f32[16,128]{1,0:T(8,128)S(1)}, f32[16,128]{1,0:T(8,128)S(1)}, u32[]{:S(2)}, u32[]{:S(2)}) %collective-permute-start.1) | collective-permute-done | bytes 8224 | tf_op jit(solution)/shard_map/ppermute | solution.py:353
  7.4 0.1 shard_map.89.to_a_ref.to_ref.first_ref
  7.6 4.6 %collective-permute-start.4 = (f32[136,128]{1,0:T(8,128)S(1)}, f32[136,128]{1,0:T(8,128)S(1)}, u32[]{:S(2)}, u32[]{:S(2)}) collective-permute-start(f32[136,128]{1,0:T(8,128)S(1)} %shard_map.89.to_a_ref.to_ref.first_ref), channel_id=1, source_target_pairs={{4,8},{8,4},{12,16},{16,12},{20,24},{24,20},{28,0},{0,28},{5,9},{9... | collective-permute-start | bytes 208904 | tf_op jit(solution)/shard_map/ppermute | solution.py:348
  12.2 0.4 shard_map.90.to_ref.first_ref
  12.7 2.3 %reshape_squeeze.3.blocks_ref = bf16[48,96,96]{2,1,0:T(8,128)(2,1)S(1)} reshape(bf16[1,1,48,9216]{3,2,1,0:T(8,128)(2,1)} %param.8) | data formatting | bytes 1769472 | tf_op jit(solution)/shard_map/reshape;squeeze | solution.py:362
  15.0 1.4 %shard_map.87.product_ref = f32[32,128]{1,0:T(8,128)S(1)} custom-call(s32[2,16]{1,0:T(2,128)S(1)} %bitcast.17, bf16[48,96,96]{2,1,0:T(8,128)(2,1)S(1)} %reshape_squeeze.3.blocks_ref, f32[32,128]{1,0:T(8,128)S(1)} %get-tuple-element.17.field_ref.padded_ref), custom_call_target="tpu_custom_call" | custom-call | flops 1000000 | bytes 1000000 | tf_op jit(solution)/shard_map/pallas_call | solution.py:19
  16.4 0.5 %collective-permute-done.3.from_ref = f32[128,128]{1,0:T(8,128)S(1)} collective-permute-done((f32[128,128]{1,0:T(8,128)S(1)}, f32[128,128]{1,0:T(8,128)S(1)}, u32[]{:S(2)}, u32[]{:S(2)}) %collective-permute-start.3) | collective-permute-done | bytes 65568 | tf_op jit(solution)/shard_map/ppermute | solution.py:348
  16.9 0.7 %shard_map.91 = (f32[32,128]{1,0:T(8,128)S(1)}, f32[64,128]{1,0:T(8,128)S(1)}) custom-call(s32[128,128]{1,0:T(8,128)S(1)} %get-tuple-element.18.aligned_ref, f32[32,128]{1,0:T(8,128)S(1)} %shard_map.87.product_ref, f32[128,128]{1,0:T(8,128)S(1)} %shard_map.90.to_ref.first_ref, f32[128,128]{1,0:T(8,128)S(1)} %collective-permute-done.3.from_ref), custom_call_target="tpu_custom_call" | custom-call | flops 1 | bytes 1 | tf_op jit(solution)/shard_map/pallas_call | solution.py:19
  17.6 1.1 %shard_map.92 = (f32[32,128]{1,0:T(8,128)S(1)}, f32[64,128]{1,0:T(8,128)S(1)}, f32[72,128]{1,0:T(8,128)S(1)}) custom-call(s32[128,128]{1,0:T(8,128)S(1)} %get-tuple-element.18.aligned_ref, f32[32,128]{1,0:T(8,128)S(1)} %get-tuple-element.25.partial_ref, f32[136,128]{1,0:T(8,128)S(1)} %shard_map.89.to_a_ref.to_ref.first_ref, ...), custom_call_target="tpu_custom_call" | custom-call | flops 1000000 | bytes 1000000 | tf_op jit(solution)/shard_map/pallas_call | solution.py:19
  18.8 1.7 %collective-permute-start.5 = (f32[72,128]{1,0:T(8,128)S(1)}, f32[72,128]{1,0:T(8,128)S(1)}, u32[]{:S(2)}, u32[]{:S(2)}) collective-permute-start(f32[72,128]{1,0:T(8,128)S(1)} %get-tuple-element.29.side_a_ref.own_ref), channel_id=1, source_target_pairs={{4,8},{8,4},{12,16},{16,12},{20,24},{24,20},{28,0},{0,28},{5,9},{9... | collective-permute-start | bytes 110600 | tf_op jit(solution)/shard_map/ppermute | solution.py:348
  20.4 0.4 shard_map.94.side_b_ref.own_ref
  20.9 1.4 %shard_map.93.product_ref = f32[32,128]{1,0:T(8,128)S(1)} custom-call(s32[2,16]{1,0:T(2,128)S(1)} %bitcast.18, bf16[48,96,96]{2,1,0:T(8,128)(2,1)S(1)} %reshape_squeeze.3.blocks_ref, f32[32,128]{1,0:T(8,128)S(1)} %get-tuple-element.26.field_ref.image_ref), custom_call_target="tpu_custom_call" | custom-call | flops 1000000 | bytes 1000000 | tf_op jit(solution)/shard_map/pallas_call | solution.py:19
  22.3 2.5 %collective-permute-done.6.from_b_ref.arrived_ref = f32[64,128]{1,0:T(8,128)S(1)} collective-permute-done((f32[64,128]{1,0:T(8,128)S(1)}, f32[64,128]{1,0:T(8,128)S(1)}, u32[]{:S(2)}, u32[]{:S(2)}) %collective-permute-start.6) | collective-permute-done | bytes 32800 | tf_op jit(solution)/shard_map/ppermute | solution.py:348
  24.8 0.7 %collective-permute-done.5.from_a_ref.arrived_ref = f32[72,128]{1,0:T(8,128)S(1)} collective-permute-done((f32[72,128]{1,0:T(8,128)S(1)}, f32[72,128]{1,0:T(8,128)S(1)}, u32[]{:S(2)}, u32[]{:S(2)}) %collective-permute-start.5) | collective-permute-done | bytes 36896 | tf_op jit(solution)/shard_map/ppermute | solution.py:348
  25.5 0.7 %shard_map.97 = f32[32,1,128]{2,1,0:T(1,128)} custom-call(f32[8,128]{1,0:T(8,128)S(1)} %shard_map.96.rows_ref, f32[64,128]{1,0:T(8,128)S(1)} %get-tuple-element.27.weights_a_ref.weights_ref, f32[72,128]{1,0:T(8,128)S(1)} %get-tuple-element.29.side_a_ref.own_ref, f32[72,128]{1,0:T(8,128)S(1)} %collective-permute-done.5.from_a_ref.arrived_ref, ...), custom_call_target="tpu_custom_call" | custom-call | flops 1000000 | bytes 1000000 | tf_op jit(solution)/shard_map/pallas_call | solution.py:19
  26.2 2.8 %all-to-all-start = ((f32[32,1,128]{2,1,0:T(1,128)}), f32[32,1,128]{2,1,0:T(1,128)S(1)}, u32[]{:S(2)}, u32[]{:S(2)}) async-start(f32[32,1,128]{2,1,0:T(1,128)} %shard_map.97), calls=%async_computation | async-start | bytes 32768 | tf_op jit(solution)/shard_map/all_to_all | solution.py:459
  29.1 1.2 %shard_map.95.second_ref = f32[32,128]{1,0:T(8,128)S(1)} custom-call(s32[128,128]{1,0:T(8,128)S(1)} %get-tuple-element.18.aligned_ref, f32[32,128]{1,0:T(8,128)S(1)} %shard_map.93.product_ref, f32[64,128]{1,0:T(8,128)S(1)} %get-tuple-element.27.weights_a_ref.weights_ref, f32[64,128]{1,0:T(8,128)S(1)} %get-tuple-element.28.weights_b_ref.weights_ref, ...), custom_call_target="tpu_custom_call" | custom-call | flops 1000000000 | bytes 1000000 | tf_op jit(solution)/shard_map/pallas_call | solution.py:19
  30.3 5.8 %all-to-all-done.sums_ref = f32[32,1,128]{2,1,0:T(1,128)S(1)} async-done(((f32[32,1,128]{2,1,0:T(1,128)}), f32[32,1,128]{2,1,0:T(1,128)S(1)}, u32[]{:S(2)}, u32[]{:S(2)}) %all-to-all-start) | async-done | bytes 16416 | tf_op jit(solution)/shard_map/all_to_all | solution.py:459
  36.1 0.7 %shard_map.98 = (f32[32,96]{1,0:T(8,128)}, f32[32,96]{1,0:T(8,128)}) custom-call(f32[32,128]{1,0:T(8,128)S(1)} %get-tuple-element.17.field_ref.padded_ref, f32[32,128]{1,0:T(8,128)S(1)} %get-tuple-element.26.field_ref.image_ref, f32[32,128]{1,0:T(8,128)S(1)} %shard_map.95.second_ref, f32[32,1,128]{2,1,0:T(1,128)S(1)} %all-to-all-done.sums_ref), custom_call_target="tpu_custom_call" | custom-call | flops 1000000 | bytes 1000000 | tf_op jit(solution)/shard_map/pallas_call | solution.py:19
  (11 shorter events, 0.3 us)
Async XLA Ops:
  0.6 0.8 %copy-start = (f32[1,1,4,16,128]{4,3,2,1,0:T(8,128)S(1)}, f32[1,1,4,16,128]{4,3,2,1,0:T(8,128)}, u32[]{:S(2)}) copy-start(f32[1,1,4,16,128]{4,3,2,1,0:T(8,128)} %param.13) | copy-start | bytes 98308
  1.4 4.5 %collective-permute-start = (f32[16,128]{1,0:T(8,128)S(1)}, f32[16,128]{1,0:T(8,128)S(1)}, u32[]{:S(2)}, u32[]{:S(2)}) collective-permute-start(f32[16,128]{1,0:T(8,128)S(1)} %get-tuple-element.21), channel_id=1, source_target_pairs={{0,3},{1,2},{2,1},{3,0},{4,7},{5,6},{6,5},{7,4},{8,11},{9,10},{10,... | collective-permute-start | bytes 24584 | tf_op jit(solution)/shard_map/ppermute | solution.py:353
  3.8 3.7 %collective-permute-start.1 = (f32[16,128]{1,0:T(8,128)S(1)}, f32[16,128]{1,0:T(8,128)S(1)}, u32[]{:S(2)}, u32[]{:S(2)}) collective-permute-start(f32[16,128]{1,0:T(8,128)S(1)} %get-tuple-element.22), channel_id=1, source_target_pairs={{0,2},{1,3},{2,0},{3,1},{4,6},{5,7},{6,4},{7,5},{8,10},{9,11},{10,... | collective-permute-start | bytes 24584 | tf_op jit(solution)/shard_map/ppermute | solution.py:353
  4.4 3.1 %collective-permute-start.2 = (f32[16,128]{1,0:T(8,128)S(1)}, f32[16,128]{1,0:T(8,128)S(1)}, u32[]{:S(2)}, u32[]{:S(2)}) collective-permute-start(f32[16,128]{1,0:T(8,128)S(1)} %get-tuple-element.23), channel_id=1, source_target_pairs={{0,1},{1,0},{2,3},{3,2},{4,5},{5,4},{6,7},{7,6},{8,9},{9,8},{10,11... | collective-permute-start | bytes 24584 | tf_op jit(solution)/shard_map/ppermute | solution.py:353
  7.6 7.4 %copy-start.1 = (s32[1,1,2,16]{3,2,1,0:T(2,128)S(1)}, s32[1,1,2,16]{3,2,1,0:T(2,128)}, u32[]{:S(2)}) copy-start(s32[1,1,2,16]{3,2,1,0:T(2,128)} %param.9) | copy-start | bytes 388
  7.6 10.0 %collective-permute-start.4 = (f32[136,128]{1,0:T(8,128)S(1)}, f32[136,128]{1,0:T(8,128)S(1)}, u32[]{:S(2)}, u32[]{:S(2)}) collective-permute-start(f32[136,128]{1,0:T(8,128)S(1)} %shard_map.89.to_a_ref.to_ref.first_ref), channel_id=1, source_target_pairs={{4,8},{8,4},{12,16},{16,12},{20,24},{24,20},{28,0},{0,28},{5,9},{9... | collective-permute-start | bytes 208904 | tf_op jit(solution)/shard_map/ppermute | solution.py:348
  12.6 4.3 %collective-permute-start.3 = (f32[128,128]{1,0:T(8,128)S(1)}, f32[128,128]{1,0:T(8,128)S(1)}, u32[]{:S(2)}, u32[]{:S(2)}) collective-permute-start(f32[128,128]{1,0:T(8,128)S(1)} %shard_map.90.to_ref.first_ref), channel_id=1, source_target_pairs={{0,4},{4,0},{8,12},{12,8},{16,20},{20,16},{24,28},{28,24},{1,5},{5... | collective-permute-start | bytes 196616 | tf_op jit(solution)/shard_map/ppermute | solution.py:348
  18.8 6.7 %collective-permute-start.5 = (f32[72,128]{1,0:T(8,128)S(1)}, f32[72,128]{1,0:T(8,128)S(1)}, u32[]{:S(2)}, u32[]{:S(2)}) collective-permute-start(f32[72,128]{1,0:T(8,128)S(1)} %get-tuple-element.29.side_a_ref.own_ref), channel_id=1, source_target_pairs={{4,8},{8,4},{12,16},{16,12},{20,24},{24,20},{28,0},{0,28},{5,9},{9... | collective-permute-start | bytes 110600 | tf_op jit(solution)/shard_map/ppermute | solution.py:348
  20.8 4.0 %collective-permute-start.6 = (f32[64,128]{1,0:T(8,128)S(1)}, f32[64,128]{1,0:T(8,128)S(1)}, u32[]{:S(2)}, u32[]{:S(2)}) collective-permute-start(f32[64,128]{1,0:T(8,128)S(1)} %shard_map.94.side_b_ref.own_ref), channel_id=1, source_target_pairs={{0,4},{4,0},{8,12},{12,8},{16,20},{20,16},{24,28},{28,24},{1,5},{5... | collective-permute-start | bytes 98312 | tf_op jit(solution)/shard_map/ppermute | solution.py:348
  26.2 9.9 %all-to-all-start = ((f32[32,1,128]{2,1,0:T(1,128)}), f32[32,1,128]{2,1,0:T(1,128)S(1)}, u32[]{:S(2)}, u32[]{:S(2)}) async-start(f32[32,1,128]{2,1,0:T(1,128)} %shard_map.97), calls=%async_computation | async-start | bytes 32768 | tf_op jit(solution)/shard_map/all_to_all | solution.py:459

commit v10 on v8

--- a/solution.py
+++ b/solution.py
@@ -76,23 +76,27 @@
 
 
 def first_kernel(
-    groups, packed_ref, aligned_ref, padded_ref, chosen_ref, side_a_ref
+    groups, packed_ref, aligned_ref, padded_ref, chosen_ref, side_a_ref, side_b_ref
 ):
     faces = side_a_ref.shape[0]
     block_rows = padded_ref.shape[0]
     per_group = faces // groups
+    slot = lax.axis_index("blk")
     parity = lax.rem(lax.axis_index("sub"), 2)
     east = pl.multiple_of((1 - parity) * faces, faces)
     west = pl.multiple_of(parity * faces, faces)
     padded_ref[...] = packed_ref[2 * faces : 2 * faces + block_rows, :]
-    tail = packed_ref[2 * faces + block_rows :, :].astype(jnp.int32)
+    last = 2 * faces + block_rows
+    tail = packed_ref[last : last + SUBLANES, :].astype(jnp.int32)
     partner = tail[:1, :faces]
     face = lax.broadcasted_iota(jnp.int32, (1, faces), 1)
     source = jnp.zeros((1, faces), jnp.int32)
     for g in range(groups):
         inside = face - g * per_group
         source = jnp.where(
-            (inside >= 0) & (inside < per_group), tail[1:2, g : g + 1] * per_group + inside, source
+            (inside >= 0) & (inside < per_group),
+            (tail[1:2, g : g + 1] ^ slot) * per_group + inside,
+            source,
         )
     order = one_hot(partner, faces)
     aligned_ref[pl.ds(west, faces), :] = packed_ref[faces : 2 * faces, :].astype(jnp.int32)
@@ -104,19 +108,22 @@
         preferred_element_type=F32,
     )
     gather_traces(padded_ref[...], aligned_ref, 0, side_a_ref)
-
-
-def far_message_kernel(held_ref, chosen_ref, side_a_ref, to_a_ref):
+    gather_traces(padded_ref[...], aligned_ref, faces, side_b_ref)
+
+
+def message_kernel(first, packed_ref, chosen_ref, side_a_ref, side_b_ref, *refs):
     faces = side_a_ref.shape[0]
-    to_a_ref[:faces, :] = side_a_ref[...]
-    to_a_ref[faces : 2 * faces, :] = exact_dot(chosen_ref[...], held_ref[...])
-    to_a_ref[2 * faces :, :] = jnp.zeros_like(to_a_ref[2 * faces :, :])
-
-
-def near_message_kernel(aligned_ref, padded_ref, to_a_ref, to_b_ref):
-    faces = to_b_ref.shape[0] // 2
-    to_b_ref[faces:, :] = to_a_ref[faces : 2 * faces, :]
-    gather_traces(padded_ref[...], aligned_ref, faces, to_b_ref.at[:faces, :])
+    *weight_refs, to_a_ref, to_b_ref = refs
+    slot = lax.axis_index("blk")
+    per_group = weight_refs[0].shape[1]
+    kept = pl.ds(pl.multiple_of(first + slot * per_group, SUBLANES), per_group)
+    held = jnp.concatenate(
+        [packed_ref[kept, :]] + [weight_ref[slot] for weight_ref in weight_refs], axis=0
+    )
+    own = exact_dot(chosen_ref[...], held)
+    for side_ref, to_ref in ((side_a_ref, to_a_ref), (side_b_ref, to_b_ref)):
+        to_ref[:faces, :] = side_ref[...]
+        to_ref[faces:, :] = own
 
 
 def near_traces_kernel(aligned_ref, image_ref, side_b_ref):
@@ -337,6 +344,11 @@
     return lax.ppermute(value, "sub", pairs)
 
 
+def swap_slots(value, k):
+    count = lax.axis_size("blk")
+    return lax.ppermute(value, "blk", [(slot, slot ^ k) for slot in range(count)])
+
+
 def on_device(
     right_side, stiffness, block_pairs, trace_rows, partner_face, owner_list, mortar_weight
 ):
@@ -351,37 +363,39 @@
     faces = partner.shape[0]
     devices = lax.axis_size("sub") * lax.axis_size("blk")
 
-    held = lax.all_to_all(mortar_weight[0, 0], "blk", split_axis=0, concat_axis=0, tiled=True)
+    own_weights = mortar_weight[0, 0]
+    held = [swap_slots(own_weights, k) for k in range(1, own_weights.shape[0])]
     last = 2 * faces + block_rows
 
     def placed(value, first):
-        below = last + SUBLANES - first - value.shape[0]
+        below = last + SUBLANES + faces - first - value.shape[0]
         return jnp.pad(value, ((first, below), (0, LANES - value.shape[1])))
 
     indices = placed(rows, 0) + placed(partner_face[0], last) + placed(owner_list[0], last + 1)
-    packed = indices.astype(F32) + placed(field, 2 * faces)
-    aligned, padded, chosen, side_a = call(
+    packed = (
+        indices.astype(F32)
+        + placed(field, 2 * faces)
+        + placed(own_weights.reshape(faces, LANES), last + SUBLANES)
+    )
+    aligned, padded, chosen, side_a, side_b = call(
         functools.partial(first_kernel, owners.shape[0]),
         [
             shape(2 * faces, jnp.int32),
             shape(block_rows),
             jax.ShapeDtypeStruct((faces, faces), F32),
             shape(faces),
+            shape(faces),
         ],
         [(packed, VMEM)],
     )
-    (to_a,) = call(
-        far_message_kernel,
-        [shape(2 * faces + SUBLANES)],
-        [(value, VMEM) for value in (held.reshape(faces, LANES), chosen, side_a)],
-    )
+    to_a, to_b = call(
+        functools.partial(message_kernel, last + SUBLANES),
+        [shape(2 * faces), shape(2 * faces)],
+        [(value, VMEM) for value in (packed, chosen, side_a, side_b, *held)],
+    )
+    from_b = swap(to_b, 0)
     from_a = swap(to_a, 1)
-    (to_b,) = call(
-        near_message_kernel,
-        [shape(2 * faces)],
-        [(value, VMEM) for value in (aligned, padded, to_a)],
-    )
-    from_b = swap(to_b, 0)
+
     def stiff(vector):
         (product,) = call(
             stiffness_kernel,

time: 39 us -> 37.2 us (0.954)
  waiting for transfers between devices: 12 us -> 10.2 us
    all_to_all x1 -> x0, starting transfers between devices: 4.22 us -> none  [on_device(): lax.all_to_all(mortar_weight[0, 0], 'blk', split_axis=0, concat_axis=0, t...]
    ppermute x0 -> x3, starting transfers between devices: none -> 3.12 us  [swap_slots(): lax.ppermute(value, 'blk', [(slot, slot ^ k) for slot in range(count)])]
    all_to_all x1 -> x0, waiting for transfers between devices: 2.5 us -> none  [on_device(): lax.all_to_all(mortar_weight[0, 0], 'blk', split_axis=0, concat_axis=0, t...]
    ppermute x0 -> x3, waiting for transfers between devices: none -> 1.74 us  [swap_slots(): lax.ppermute(value, 'blk', [(slot, slot ^ k) for slot in range(count)])]
    ppermute x4, waiting for transfers between devices: 3.71 us -> 2.65 us  [swap(): return lax.ppermute(value, 'sub', pairs)]
    ppermute x4, starting transfers between devices: 6.89 us -> 7.75 us  [swap(): return lax.ppermute(value, 'sub', pairs)]
    all_to_all x1, starting transfers between devices: 2.82 us -> 3.24 us  [on_device(): lax.all_to_all(sums, ('sub', 'blk'), split_axis=0, concat_axis=0, tiled=T...]
    pallas_call x12 -> x11, Pallas kernels: 8.77 us -> 8.73 us  [call(): pl.pallas_call(body, out_shape=outs, in_specs=[spec for _, spec in inputs...]
  transfers between devices with their start and end apart: 6 -> 8, of which waited for: 5 -> 3; matrix products, arithmetic and copies ran while one was open for 8% -> 9% of each run, Pallas kernels for 16% -> 16%
where the time goes in v10:
time: 37.2 us; the launch traced here: 37 us
  starting transfers between devices  14.1 us (38%)
  waiting for transfers between devices  10.2 us (27%)
  Pallas kernels  8.73 us (23%)
  local copies, waits for them, and re-layouts  2.29 us (6%)
  other arithmetic  0.92 us (2%)
  between operations  0.74 us (2%)
    pallas_call x11, Pallas kernels, call(): pl.pallas_call(body, out_shape=outs, in_specs=[spec for _, spec in inputs...  8.73 us
    ppermute x4, starting transfers between devices, swap(): return lax.ppermute(value, 'sub', pairs)  7.75 us
    all_to_all x1, waiting for transfers between devices, on_device(): lax.all_to_all(sums, ('sub', 'blk'), split_axis=0, concat_axis=0, tiled=T...  5.83 us
    all_to_all x1, starting transfers between devices, on_device(): lax.all_to_all(sums, ('sub', 'blk'), split_axis=0, concat_axis=0, tiled=T...  3.24 us
    ppermute x3, starting transfers between devices, swap_slots(): lax.ppermute(value, 'blk', [(slot, slot ^ k) for slot in range(count)])  3.12 us
    ppermute x4, waiting for transfers between devices, swap(): return lax.ppermute(value, 'sub', pairs)  2.65 us
    another operation x1, local copies, waits for them, and re-layouts, on_device(): blocks = stored.reshape(stored.shape[0], size, size)  2.29 us
    ppermute x3, waiting for transfers between devices, swap_slots(): lax.ppermute(value, 'blk', [(slot, slot ^ k) for slot in range(count)])  1.74 us
  transfers between devices with their start and end apart: 8, of which 3 were waited for; matrix products, arithmetic and copies ran while one was open for 9% of the time, Pallas kernels for 16%

profile of v10, /device:TPU:0, one launch (start us, length us, event | category | flops | bytes accessed | tf_op | source)
XLA Modules:
  0.0 37.0 jit_solution(4143759965330460204)
XLA Ops:
  0.6 2.4 %collective-permute-start.2 = (f32[4,16,128]{2,1,0:T(8,128)}, f32[4,16,128]{2,1,0:T(8,128)S(1)}, u32[]{:S(2)}, u32[]{:S(2)}) collective-permute-start(f32[4,16,128]{2,1,0:T(8,128)} %bitcast.20), channel_id=1, source_target_pairs={{0,3},{1,2},{2,1},{3,0},{4,7},{5,6},{6,5},{7,4},{8,11},{9,10},{10,... | collective-permute-start | bytes 98312 | tf_op jit(solution)/shard_map/ppermute | solution.py:349
  3.1 0.6 %collective-permute-start.1 = (f32[4,16,128]{2,1,0:T(8,128)}, f32[4,16,128]{2,1,0:T(8,128)S(1)}, u32[]{:S(2)}, u32[]{:S(2)}) collective-permute-start(f32[4,16,128]{2,1,0:T(8,128)} %bitcast.21), channel_id=1, source_target_pairs={{0,2},{1,3},{2,0},{3,1},{4,6},{5,7},{6,4},{7,5},{8,10},{9,11},{10,... | collective-permute-start | bytes 98312 | tf_op jit(solution)/shard_map/ppermute | solution.py:349
  3.7 0.0 collective-permute-start
  3.8 0.9 %pad_add_fusion.packed_ref = f32[232,128]{1,0:T(8,128)S(1)} fusion(f32[64,128]{1,0:T(8,128)} %bitcast.23, f32[32,96]{1,0:T(8,128)} %bitcast.24, s32[1,4]{1,0:T(1,128)} %bitcast.25, s32[1,64]{1,0:T(1,128)} %bitcast.26, s32[128,128]{1,0:T(8,128)} %bitcast.19), kind=kLoop, calls=%fused_computation | loop fusion | flops 148480 | bytes 229648 | tf_op jit(solution)/shard_map/add | solution.py:376
  4.7 0.8 %shard_map.86 = (s32[128,128]{1,0:T(8,128)S(1)}, f32[32,128]{1,0:T(8,128)S(1)}, f32[64,64]{1,0:T(8,128)S(1)}, f32[64,128]{1,0:T(8,128)S(1)}, f32[64,128]{1,0:T(8,128)S(1)}) custom-call(f32[232,128]{1,0:T(8,128)S(1)} %pad_add_fusion.packed_ref), custom_call_target="tpu_custom_call" | custom-call | flops 1000000 | bytes 1000000 | tf_op jit(solution)/shard_map/pallas_call | solution.py:19
  5.5 1.7 %collective-permute-done.1.refs_1_ = f32[4,16,128]{2,1,0:T(8,128)S(1)} collective-permute-done((f32[4,16,128]{2,1,0:T(8,128)}, f32[4,16,128]{2,1,0:T(8,128)S(1)}, u32[]{:S(2)}, u32[]{:S(2)}) %collective-permute-start.1) | collective-permute-done | bytes 32800 | tf_op jit(solution)/shard_map/ppermute | solution.py:349
  7.3 0.0 collective-permute-done.refs_0_
  7.3 0.2 shard_map.88
  7.4 1.6 %collective-permute-start.3 = (f32[128,128]{1,0:T(8,128)S(1)}, f32[128,128]{1,0:T(8,128)S(1)}, u32[]{:S(2)}, u32[]{:S(2)}) collective-permute-start(f32[128,128]{1,0:T(8,128)S(1)} %get-tuple-element.21.to_ref.first_ref), channel_id=1, source_target_pairs={{0,4},{4,0},{8,12},{12,8},{16,20},{20,16},{24,28},{28,24},{1,5},{5... | collective-permute-start | bytes 196616 | tf_op jit(solution)/shard_map/ppermute | solution.py:344
  9.0 3.5 %collective-permute-start.4 = (f32[128,128]{1,0:T(8,128)S(1)}, f32[128,128]{1,0:T(8,128)S(1)}, u32[]{:S(2)}, u32[]{:S(2)}) collective-permute-start(f32[128,128]{1,0:T(8,128)S(1)} %get-tuple-element.23.to_ref.first_ref), channel_id=1, source_target_pairs={{4,8},{8,4},{12,16},{16,12},{20,24},{24,20},{28,0},{0,28},{5,9},{9... | collective-permute-start | bytes 196616 | tf_op jit(solution)/shard_map/ppermute | solution.py:344
  12.5 2.3 %reshape_squeeze.7.blocks_ref = bf16[48,96,96]{2,1,0:T(8,128)(2,1)S(1)} reshape(bf16[1,1,48,9216]{3,2,1,0:T(8,128)(2,1)} %param.8) | data formatting | bytes 1769472 | tf_op jit(solution)/shard_map/reshape;squeeze | solution.py:358
  14.8 1.4 %shard_map.87.product_ref = f32[32,128]{1,0:T(8,128)S(1)} custom-call(s32[2,16]{1,0:T(2,128)S(1)} %bitcast.17, bf16[48,96,96]{2,1,0:T(8,128)(2,1)S(1)} %reshape_squeeze.7.blocks_ref, f32[32,128]{1,0:T(8,128)S(1)} %get-tuple-element.16.field_ref), custom_call_target="tpu_custom_call" | custom-call | flops 1000000 | bytes 1000000 | tf_op jit(solution)/shard_map/pallas_call | solution.py:19
  16.3 0.7 %shard_map.89 = (f32[32,128]{1,0:T(8,128)S(1)}, f32[64,128]{1,0:T(8,128)S(1)}) custom-call(s32[128,128]{1,0:T(8,128)S(1)} %get-tuple-element.17.aligned_ref, f32[32,128]{1,0:T(8,128)S(1)} %shard_map.87.product_ref, f32[128,128]{1,0:T(8,128)S(1)} %get-tuple-element.21.to_ref.first_ref, f32[128,128]{1,0:T(8,128)S(1)} %collective-permute-done.3.from_ref), custom_call_target="tpu_custom_call" | custom-call | flops 1 | bytes 1 | tf_op jit(solution)/shard_map/pallas_call | solution.py:19
  17.0 1.1 %shard_map.90 = (f32[32,128]{1,0:T(8,128)S(1)}, f32[64,128]{1,0:T(8,128)S(1)}, f32[72,128]{1,0:T(8,128)S(1)}) custom-call(s32[128,128]{1,0:T(8,128)S(1)} %get-tuple-element.17.aligned_ref, f32[32,128]{1,0:T(8,128)S(1)} %get-tuple-element.22.partial_ref, f32[128,128]{1,0:T(8,128)S(1)} %get-tuple-element.23.to_ref.first_ref, ...), custom_call_target="tpu_custom_call" | custom-call | flops 1000000 | bytes 1000000 | tf_op jit(solution)/shard_map/pallas_call | solution.py:19
  18.1 2.6 %collective-permute-start.5 = (f32[72,128]{1,0:T(8,128)S(1)}, f32[72,128]{1,0:T(8,128)S(1)}, u32[]{:S(2)}, u32[]{:S(2)}) collective-permute-start(f32[72,128]{1,0:T(8,128)S(1)} %get-tuple-element.27.side_a_ref.own_ref), channel_id=1, source_target_pairs={{4,8},{8,4},{12,16},{16,12},{20,24},{24,20},{28,0},{0,28},{5,9},{9... | collective-permute-start | bytes 110600 | tf_op jit(solution)/shard_map/ppermute | solution.py:344
  20.7 0.4 shard_map.92.side_b_ref.own_ref
  21.0 0.1 collective-permute-start.6
  21.1 1.4 %shard_map.91.product_ref = f32[32,128]{1,0:T(8,128)S(1)} custom-call(s32[2,16]{1,0:T(2,128)S(1)} %bitcast.18, bf16[48,96,96]{2,1,0:T(8,128)(2,1)S(1)} %reshape_squeeze.7.blocks_ref, f32[32,128]{1,0:T(8,128)S(1)} %get-tuple-element.24.field_ref.image_ref), custom_call_target="tpu_custom_call" | custom-call | flops 1000000 | bytes 1000000 | tf_op jit(solution)/shard_map/pallas_call | solution.py:19
  22.5 2.6 %collective-permute-done.6.from_b_ref.arrived_ref = f32[64,128]{1,0:T(8,128)S(1)} collective-permute-done((f32[64,128]{1,0:T(8,128)S(1)}, f32[64,128]{1,0:T(8,128)S(1)}, u32[]{:S(2)}, u32[]{:S(2)}) %collective-permute-start.6) | collective-permute-done | bytes 32800 | tf_op jit(solution)/shard_map/ppermute | solution.py:344
  25.2 0.7 %shard_map.95 = f32[32,1,128]{2,1,0:T(1,128)} custom-call(f32[8,128]{1,0:T(8,128)S(1)} %shard_map.94.rows_ref, f32[64,128]{1,0:T(8,128)S(1)} %get-tuple-element.25.weights_a_ref.weights_ref, f32[72,128]{1,0:T(8,128)S(1)} %get-tuple-element.27.side_a_ref.own_ref, f32[72,128]{1,0:T(8,128)S(1)} %collective-permute-done.5.from_a_ref.arrived_ref, ...), custom_call_target="tpu_custom_call" | custom-call | flops 1000000 | bytes 1000000 | tf_op jit(solution)/shard_map/pallas_call | solution.py:19
  25.9 3.2 %all-to-all-start = ((f32[32,1,128]{2,1,0:T(1,128)}), f32[32,1,128]{2,1,0:T(1,128)S(1)}, u32[]{:S(2)}, u32[]{:S(2)}) async-start(f32[32,1,128]{2,1,0:T(1,128)} %shard_map.95), calls=%async_computation | async-start | bytes 32768 | tf_op jit(solution)/shard_map/all_to_all | solution.py:449
  29.2 1.2 %shard_map.93.second_ref = f32[32,128]{1,0:T(8,128)S(1)} custom-call(s32[128,128]{1,0:T(8,128)S(1)} %get-tuple-element.17.aligned_ref, f32[32,128]{1,0:T(8,128)S(1)} %shard_map.91.product_ref, f32[64,128]{1,0:T(8,128)S(1)} %get-tuple-element.25.weights_a_ref.weights_ref, f32[64,128]{1,0:T(8,128)S(1)} %get-tuple-element.26.weights_b_ref.weights_ref, ...), custom_call_target="tpu_custom_call" | custom-call | flops 1000000000 | bytes 1000000 | tf_op jit(solution)/shard_map/pallas_call | solution.py:19
  30.4 5.8 %all-to-all-done.sums_ref = f32[32,1,128]{2,1,0:T(1,128)S(1)} async-done(((f32[32,1,128]{2,1,0:T(1,128)}), f32[32,1,128]{2,1,0:T(1,128)S(1)}, u32[]{:S(2)}, u32[]{:S(2)}) %all-to-all-start) | async-done | bytes 16416 | tf_op jit(solution)/shard_map/all_to_all | solution.py:449
  36.3 0.7 %shard_map.96 = (f32[32,96]{1,0:T(8,128)}, f32[32,96]{1,0:T(8,128)}) custom-call(f32[32,128]{1,0:T(8,128)S(1)} %get-tuple-element.16.field_ref, f32[32,128]{1,0:T(8,128)S(1)} %get-tuple-element.24.field_ref.image_ref, f32[32,128]{1,0:T(8,128)S(1)} %shard_map.93.second_ref, f32[32,1,128]{2,1,0:T(1,128)S(1)} %all-to-all-done.sums_ref), custom_call_target="tpu_custom_call" | custom-call | flops 1000000 | bytes 1000000 | tf_op jit(solution)/shard_map/pallas_call | solution.py:19
  (7 shorter events, 0.0 us)
Async XLA Ops:
  0.6 4.9 %collective-permute-start.2 = (f32[4,16,128]{2,1,0:T(8,128)}, f32[4,16,128]{2,1,0:T(8,128)S(1)}, u32[]{:S(2)}, u32[]{:S(2)}) collective-permute-start(f32[4,16,128]{2,1,0:T(8,128)} %bitcast.20), channel_id=1, source_target_pairs={{0,3},{1,2},{2,1},{3,0},{4,7},{5,6},{6,5},{7,4},{8,11},{9,10},{10,... | collective-permute-start | bytes 98312 | tf_op jit(solution)/shard_map/ppermute | solution.py:349
  3.1 4.2 %collective-permute-start.1 = (f32[4,16,128]{2,1,0:T(8,128)}, f32[4,16,128]{2,1,0:T(8,128)S(1)}, u32[]{:S(2)}, u32[]{:S(2)}) collective-permute-start(f32[4,16,128]{2,1,0:T(8,128)} %bitcast.21), channel_id=1, source_target_pairs={{0,2},{1,3},{2,0},{3,1},{4,6},{5,7},{6,4},{7,5},{8,10},{9,11},{10,... | collective-permute-start | bytes 98312 | tf_op jit(solution)/shard_map/ppermute | solution.py:349
  3.7 3.5 %collective-permute-start = (f32[4,16,128]{2,1,0:T(8,128)}, f32[4,16,128]{2,1,0:T(8,128)S(1)}, u32[]{:S(2)}, u32[]{:S(2)}) collective-permute-start(f32[4,16,128]{2,1,0:T(8,128)} %bitcast.22), channel_id=1, source_target_pairs={{0,1},{1,0},{2,3},{3,2},{4,5},{5,4},{6,7},{7,6},{8,9},{9,8},{10,11... | collective-permute-start | bytes 98312 | tf_op jit(solution)/shard_map/ppermute | solution.py:349
  7.3 7.6 %copy-start = (s32[1,1,2,16]{3,2,1,0:T(2,128)S(1)}, s32[1,1,2,16]{3,2,1,0:T(2,128)}, u32[]{:S(2)}) copy-start(s32[1,1,2,16]{3,2,1,0:T(2,128)} %param.9) | copy-start | bytes 388
  7.4 8.8 %collective-permute-start.3 = (f32[128,128]{1,0:T(8,128)S(1)}, f32[128,128]{1,0:T(8,128)S(1)}, u32[]{:S(2)}, u32[]{:S(2)}) collective-permute-start(f32[128,128]{1,0:T(8,128)S(1)} %get-tuple-element.21.to_ref.first_ref), channel_id=1, source_target_pairs={{0,4},{4,0},{8,12},{12,8},{16,20},{20,16},{24,28},{28,24},{1,5},{5... | collective-permute-start | bytes 196616 | tf_op jit(solution)/shard_map/ppermute | solution.py:344
  9.0 8.0 %collective-permute-start.4 = (f32[128,128]{1,0:T(8,128)S(1)}, f32[128,128]{1,0:T(8,128)S(1)}, u32[]{:S(2)}, u32[]{:S(2)}) collective-permute-start(f32[128,128]{1,0:T(8,128)S(1)} %get-tuple-element.23.to_ref.first_ref), channel_id=1, source_target_pairs={{4,8},{8,4},{12,16},{16,12},{20,24},{24,20},{28,0},{0,28},{5,9},{9... | collective-permute-start | bytes 196616 | tf_op jit(solution)/shard_map/ppermute | solution.py:344
  18.1 7.1 %collective-permute-start.5 = (f32[72,128]{1,0:T(8,128)S(1)}, f32[72,128]{1,0:T(8,128)S(1)}, u32[]{:S(2)}, u32[]{:S(2)}) collective-permute-start(f32[72,128]{1,0:T(8,128)S(1)} %get-tuple-element.27.side_a_ref.own_ref), channel_id=1, source_target_pairs={{4,8},{8,4},{12,16},{16,12},{20,24},{24,20},{28,0},{0,28},{5,9},{9... | collective-permute-start | bytes 110600 | tf_op jit(solution)/shard_map/ppermute | solution.py:344
  21.0 4.1 %collective-permute-start.6 = (f32[64,128]{1,0:T(8,128)S(1)}, f32[64,128]{1,0:T(8,128)S(1)}, u32[]{:S(2)}, u32[]{:S(2)}) collective-permute-start(f32[64,128]{1,0:T(8,128)S(1)} %shard_map.92.side_b_ref.own_ref), channel_id=1, source_target_pairs={{0,4},{4,0},{8,12},{12,8},{16,20},{20,16},{24,28},{28,24},{1,5},{5... | collective-permute-start | bytes 98312 | tf_op jit(solution)/shard_map/ppermute | solution.py:344
  25.9 10.3 %all-to-all-start = ((f32[32,1,128]{2,1,0:T(1,128)}), f32[32,1,128]{2,1,0:T(1,128)S(1)}, u32[]{:S(2)}, u32[]{:S(2)}) async-start(f32[32,1,128]{2,1,0:T(1,128)} %shard_map.95), calls=%async_computation | async-start | bytes 32768 | tf_op jit(solution)/shard_map/all_to_all | solution.py:449

commit v11 on v10

--- a/solution.py
+++ b/solution.py
@@ -121,9 +121,10 @@
         [packed_ref[kept, :]] + [weight_ref[slot] for weight_ref in weight_refs], axis=0
     )
     own = exact_dot(chosen_ref[...], held)
+    to_a_ref[2 * faces :, :] = jnp.zeros_like(to_a_ref[2 * faces :, :])
     for side_ref, to_ref in ((side_a_ref, to_a_ref), (side_b_ref, to_b_ref)):
         to_ref[:faces, :] = side_ref[...]
-        to_ref[faces:, :] = own
+        to_ref[faces : 2 * faces, :] = own
 
 
 def near_traces_kernel(aligned_ref, image_ref, side_b_ref):
@@ -198,15 +199,16 @@
             )
             right.append(jnp.where(dof_of == widened(dof, f, size), one, none))
         return total + lax.dot_general(
+            jnp.concatenate(right, axis=1),
             jnp.concatenate(left, axis=1),
-            jnp.concatenate(right, axis=1),
             (((1,), (1,)), ((), ())),
             preferred_element_type=F32,
         )
 
     total = lax.fori_loop(
-        0, faces // SUBLANES, step, jnp.zeros((2 * block_rows, size), F32), unroll=8
-    )
+        0, faces // SUBLANES, step, jnp.zeros((size, 2 * block_rows), F32), unroll=8
+    )
+    total = total.T
     return total[:block_rows] + total[block_rows:]
 
 
@@ -390,7 +392,7 @@
     )
     to_a, to_b = call(
         functools.partial(message_kernel, last + SUBLANES),
-        [shape(2 * faces), shape(2 * faces)],
+        [shape(2 * faces + SUBLANES), shape(2 * faces)],
         [(value, VMEM) for value in (packed, chosen, side_a, side_b, *held)],
     )
     from_b = swap(to_b, 0)

time: 37.2 us -> 36.8 us (0.989)
  starting transfers between devices: 14.1 us -> 13 us
  waiting for transfers between devices: 10.2 us -> 11.2 us
    ppermute x4, starting transfers between devices: 7.75 us -> 6.82 us  [swap(): return lax.ppermute(value, 'sub', pairs)]
    ppermute x4, waiting for transfers between devices: 2.65 us -> 3.44 us  [swap(): return lax.ppermute(value, 'sub', pairs)]
  transfers between devices with their start and end apart: 8 -> 8, of which waited for: 3 -> 4; matrix products, arithmetic and copies ran while one was open for 9% -> 9% of each run, Pallas kernels for 16% -> 16%
where the time goes in v11:
time: 36.8 us; the launch traced here: 36.6 us
  starting transfers between devices  13 us (35%)
  waiting for transfers between devices  11.2 us (30%)
  Pallas kernels  8.4 us (23%)
  local copies, waits for them, and re-layouts  2.29 us (6%)
  other arithmetic  0.92 us (2%)
  between operations  0.74 us (2%)
    pallas_call x11, Pallas kernels, call(): pl.pallas_call(body, out_shape=outs, in_specs=[spec for _, spec in inputs...  8.4 us
    ppermute x4, starting transfers between devices, swap(): return lax.ppermute(value, 'sub', pairs)  6.82 us
    all_to_all x1, waiting for transfers between devices, on_device(): lax.all_to_all(sums, ('sub', 'blk'), split_axis=0, concat_axis=0, tiled=T...  6.04 us
    ppermute x4, waiting for transfers between devices, swap(): return lax.ppermute(value, 'sub', pairs)  3.44 us
    ppermute x3, starting transfers between devices, swap_slots(): lax.ppermute(value, 'blk', [(slot, slot ^ k) for slot in range(count)])  3.12 us
    all_to_all x1, starting transfers between devices, on_device(): lax.all_to_all(sums, ('sub', 'blk'), split_axis=0, concat_axis=0, tiled=T...  3.05 us
    another operation x1, local copies, waits for them, and re-layouts, on_device(): blocks = stored.reshape(stored.shape[0], size, size)  2.29 us
    ppermute x3, waiting for transfers between devices, swap_slots(): lax.ppermute(value, 'blk', [(slot, slot ^ k) for slot in range(count)])  1.74 us
  transfers between devices with their start and end apart: 8, of which 4 were waited for; matrix products, arithmetic and copies ran while one was open for 9% of the time, Pallas kernels for 16%

profile of v11, /device:TPU:0, one launch (start us, length us, event | category | flops | bytes accessed | tf_op | source)
XLA Modules:
  0.0 36.6 jit_solution(8162853109699505815)
XLA Ops:
  0.6 2.4 %collective-permute-start.2 = (f32[4,16,128]{2,1,0:T(8,128)}, f32[4,16,128]{2,1,0:T(8,128)S(1)}, u32[]{:S(2)}, u32[]{:S(2)}) collective-permute-start(f32[4,16,128]{2,1,0:T(8,128)} %bitcast.20), channel_id=1, source_target_pairs={{0,3},{1,2},{2,1},{3,0},{4,7},{5,6},{6,5},{7,4},{8,11},{9,10},{10,... | collective-permute-start | bytes 98312 | tf_op jit(solution)/shard_map/ppermute | solution.py:351
  3.1 0.6 %collective-permute-start.1 = (f32[4,16,128]{2,1,0:T(8,128)}, f32[4,16,128]{2,1,0:T(8,128)S(1)}, u32[]{:S(2)}, u32[]{:S(2)}) collective-permute-start(f32[4,16,128]{2,1,0:T(8,128)} %bitcast.21), channel_id=1, source_target_pairs={{0,2},{1,3},{2,0},{3,1},{4,6},{5,7},{6,4},{7,5},{8,10},{9,11},{10,... | collective-permute-start | bytes 98312 | tf_op jit(solution)/shard_map/ppermute | solution.py:351
  3.7 0.0 collective-permute-start
  3.8 0.9 %pad_add_fusion.packed_ref = f32[232,128]{1,0:T(8,128)S(1)} fusion(f32[64,128]{1,0:T(8,128)} %bitcast.23, f32[32,96]{1,0:T(8,128)} %bitcast.24, s32[1,4]{1,0:T(1,128)} %bitcast.25, s32[1,64]{1,0:T(1,128)} %bitcast.26, s32[128,128]{1,0:T(8,128)} %bitcast.19), kind=kLoop, calls=%fused_computation | loop fusion | flops 148480 | bytes 229648 | tf_op jit(solution)/shard_map/add | solution.py:378
  4.7 0.8 %shard_map.86 = (s32[128,128]{1,0:T(8,128)S(1)}, f32[32,128]{1,0:T(8,128)S(1)}, f32[64,64]{1,0:T(8,128)S(1)}, f32[64,128]{1,0:T(8,128)S(1)}, f32[64,128]{1,0:T(8,128)S(1)}) custom-call(f32[232,128]{1,0:T(8,128)S(1)} %pad_add_fusion.packed_ref), custom_call_target="tpu_custom_call" | custom-call | flops 1000000 | bytes 1000000 | tf_op jit(solution)/shard_map/pallas_call | solution.py:19
  5.5 1.7 %collective-permute-done.1.refs_1_ = f32[4,16,128]{2,1,0:T(8,128)S(1)} collective-permute-done((f32[4,16,128]{2,1,0:T(8,128)}, f32[4,16,128]{2,1,0:T(8,128)S(1)}, u32[]{:S(2)}, u32[]{:S(2)}) %collective-permute-start.1) | collective-permute-done | bytes 32800 | tf_op jit(solution)/shard_map/ppermute | solution.py:351
  7.3 0.2 shard_map.88
  7.4 4.6 %collective-permute-start.4 = (f32[136,128]{1,0:T(8,128)S(1)}, f32[136,128]{1,0:T(8,128)S(1)}, u32[]{:S(2)}, u32[]{:S(2)}) collective-permute-start(f32[136,128]{1,0:T(8,128)S(1)} %get-tuple-element.23.to_ref.first_ref), channel_id=1, source_target_pairs={{4,8},{8,4},{12,16},{16,12},{20,24},{24,20},{28,0},{0,28},{5,9},{9... | collective-permute-start | bytes 208904 | tf_op jit(solution)/shard_map/ppermute | solution.py:346
  12.0 2.3 %reshape_squeeze.7.blocks_ref = bf16[48,96,96]{2,1,0:T(8,128)(2,1)S(1)} reshape(bf16[1,1,48,9216]{3,2,1,0:T(8,128)(2,1)} %param.8) | data formatting | bytes 1769472 | tf_op jit(solution)/shard_map/reshape;squeeze | solution.py:360
  14.3 1.4 %shard_map.87.product_ref = f32[32,128]{1,0:T(8,128)S(1)} custom-call(s32[2,16]{1,0:T(2,128)S(1)} %bitcast.17, bf16[48,96,96]{2,1,0:T(8,128)(2,1)S(1)} %reshape_squeeze.7.blocks_ref, f32[32,128]{1,0:T(8,128)S(1)} %get-tuple-element.16.field_ref), custom_call_target="tpu_custom_call" | custom-call | flops 1000000 | bytes 1000000 | tf_op jit(solution)/shard_map/pallas_call | solution.py:19
  15.8 0.5 %collective-permute-done.3.from_ref = f32[128,128]{1,0:T(8,128)S(1)} collective-permute-done((f32[128,128]{1,0:T(8,128)S(1)}, f32[128,128]{1,0:T(8,128)S(1)}, u32[]{:S(2)}, u32[]{:S(2)}) %collective-permute-start.3) | collective-permute-done | bytes 65568 | tf_op jit(solution)/shard_map/ppermute | solution.py:346
  16.3 0.6 %shard_map.89 = (f32[32,128]{1,0:T(8,128)S(1)}, f32[64,128]{1,0:T(8,128)S(1)}) custom-call(s32[128,128]{1,0:T(8,128)S(1)} %get-tuple-element.17.aligned_ref, f32[32,128]{1,0:T(8,128)S(1)} %shard_map.87.product_ref, f32[128,128]{1,0:T(8,128)S(1)} %get-tuple-element.21.to_ref.first_ref, f32[128,128]{1,0:T(8,128)S(1)} %collective-permute-done.3.from_ref), custom_call_target="tpu_custom_call" | custom-call | flops 1 | bytes 1 | tf_op jit(solution)/shard_map/pallas_call | solution.py:19
  16.9 0.0 collective-permute-done.4.from_ref
  16.9 1.1 %shard_map.90 = (f32[32,128]{1,0:T(8,128)S(1)}, f32[64,128]{1,0:T(8,128)S(1)}, f32[72,128]{1,0:T(8,128)S(1)}) custom-call(s32[128,128]{1,0:T(8,128)S(1)} %get-tuple-element.17.aligned_ref, f32[32,128]{1,0:T(8,128)S(1)} %get-tuple-element.22.partial_ref, f32[136,128]{1,0:T(8,128)S(1)} %get-tuple-element.23.to_ref.first_ref, ...), custom_call_target="tpu_custom_call" | custom-call | flops 1000000 | bytes 1000000 | tf_op jit(solution)/shard_map/pallas_call | solution.py:19
  18.0 2.1 %collective-permute-start.5 = (f32[72,128]{1,0:T(8,128)S(1)}, f32[72,128]{1,0:T(8,128)S(1)}, u32[]{:S(2)}, u32[]{:S(2)}) collective-permute-start(f32[72,128]{1,0:T(8,128)S(1)} %get-tuple-element.27.side_a_ref.own_ref), channel_id=1, source_target_pairs={{4,8},{8,4},{12,16},{16,12},{20,24},{24,20},{28,0},{0,28},{5,9},{9... | collective-permute-start | bytes 110600 | tf_op jit(solution)/shard_map/ppermute | solution.py:346
  20.2 0.4 shard_map.92.side_b_ref.own_ref
  20.5 0.1 collective-permute-start.6
  20.6 1.4 %shard_map.91.product_ref = f32[32,128]{1,0:T(8,128)S(1)} custom-call(s32[2,16]{1,0:T(2,128)S(1)} %bitcast.18, bf16[48,96,96]{2,1,0:T(8,128)(2,1)S(1)} %reshape_squeeze.7.blocks_ref, f32[32,128]{1,0:T(8,128)S(1)} %get-tuple-element.24.field_ref.image_ref), custom_call_target="tpu_custom_call" | custom-call | flops 1000000 | bytes 1000000 | tf_op jit(solution)/shard_map/pallas_call | solution.py:19
  22.0 2.9 %collective-permute-done.6.from_b_ref.arrived_ref = f32[64,128]{1,0:T(8,128)S(1)} collective-permute-done((f32[64,128]{1,0:T(8,128)S(1)}, f32[64,128]{1,0:T(8,128)S(1)}, u32[]{:S(2)}, u32[]{:S(2)}) %collective-permute-start.6) | collective-permute-done | bytes 32800 | tf_op jit(solution)/shard_map/ppermute | solution.py:346
  25.0 0.7 %shard_map.95 = f32[32,1,128]{2,1,0:T(1,128)} custom-call(f32[8,128]{1,0:T(8,128)S(1)} %shard_map.94.rows_ref, f32[64,128]{1,0:T(8,128)S(1)} %get-tuple-element.25.weights_a_ref.weights_ref, f32[72,128]{1,0:T(8,128)S(1)} %get-tuple-element.27.side_a_ref.own_ref, f32[72,128]{1,0:T(8,128)S(1)} %collective-permute-done.5.from_a_ref.arrived_ref, ...), custom_call_target="tpu_custom_call" | custom-call | flops 1000000 | bytes 1000000 | tf_op jit(solution)/shard_map/pallas_call | solution.py:19
  25.7 3.0 %all-to-all-start = ((f32[32,1,128]{2,1,0:T(1,128)}), f32[32,1,128]{2,1,0:T(1,128)S(1)}, u32[]{:S(2)}, u32[]{:S(2)}) async-start(f32[32,1,128]{2,1,0:T(1,128)} %shard_map.95), calls=%async_computation | async-start | bytes 32768 | tf_op jit(solution)/shard_map/all_to_all | solution.py:451
  28.7 1.0 %shard_map.93.second_ref = f32[32,128]{1,0:T(8,128)S(1)} custom-call(s32[128,128]{1,0:T(8,128)S(1)} %get-tuple-element.17.aligned_ref, f32[32,128]{1,0:T(8,128)S(1)} %shard_map.91.product_ref, f32[64,128]{1,0:T(8,128)S(1)} %get-tuple-element.25.weights_a_ref.weights_ref, f32[64,128]{1,0:T(8,128)S(1)} %get-tuple-element.26.weights_b_ref.weights_ref, ...), custom_call_target="tpu_custom_call" | custom-call | flops 1000000000 | bytes 1000000 | tf_op jit(solution)/shard_map/pallas_call | solution.py:19
  29.8 6.0 %all-to-all-done.sums_ref = f32[32,1,128]{2,1,0:T(1,128)S(1)} async-done(((f32[32,1,128]{2,1,0:T(1,128)}), f32[32,1,128]{2,1,0:T(1,128)S(1)}, u32[]{:S(2)}, u32[]{:S(2)}) %all-to-all-start) | async-done | bytes 16416 | tf_op jit(solution)/shard_map/all_to_all | solution.py:451
  35.8 0.7 %shard_map.96 = (f32[32,96]{1,0:T(8,128)}, f32[32,96]{1,0:T(8,128)}) custom-call(f32[32,128]{1,0:T(8,128)S(1)} %get-tuple-element.16.field_ref, f32[32,128]{1,0:T(8,128)S(1)} %get-tuple-element.24.field_ref.image_ref, f32[32,128]{1,0:T(8,128)S(1)} %shard_map.93.second_ref, f32[32,1,128]{2,1,0:T(1,128)S(1)} %all-to-all-done.sums_ref), custom_call_target="tpu_custom_call" | custom-call | flops 1000000 | bytes 1000000 | tf_op jit(solution)/shard_map/pallas_call | solution.py:19
  (7 shorter events, 0.0 us)
Async XLA Ops:
  0.6 4.9 %collective-permute-start.2 = (f32[4,16,128]{2,1,0:T(8,128)}, f32[4,16,128]{2,1,0:T(8,128)S(1)}, u32[]{:S(2)}, u32[]{:S(2)}) collective-permute-start(f32[4,16,128]{2,1,0:T(8,128)} %bitcast.20), channel_id=1, source_target_pairs={{0,3},{1,2},{2,1},{3,0},{4,7},{5,6},{6,5},{7,4},{8,11},{9,10},{10,... | collective-permute-start | bytes 98312 | tf_op jit(solution)/shard_map/ppermute | solution.py:351
  3.1 4.2 %collective-permute-start.1 = (f32[4,16,128]{2,1,0:T(8,128)}, f32[4,16,128]{2,1,0:T(8,128)S(1)}, u32[]{:S(2)}, u32[]{:S(2)}) collective-permute-start(f32[4,16,128]{2,1,0:T(8,128)} %bitcast.21), channel_id=1, source_target_pairs={{0,2},{1,3},{2,0},{3,1},{4,6},{5,7},{6,4},{7,5},{8,10},{9,11},{10,... | collective-permute-start | bytes 98312 | tf_op jit(solution)/shard_map/ppermute | solution.py:351
  3.7 3.5 %collective-permute-start = (f32[4,16,128]{2,1,0:T(8,128)}, f32[4,16,128]{2,1,0:T(8,128)S(1)}, u32[]{:S(2)}, u32[]{:S(2)}) collective-permute-start(f32[4,16,128]{2,1,0:T(8,128)} %bitcast.22), channel_id=1, source_target_pairs={{0,1},{1,0},{2,3},{3,2},{4,5},{5,4},{6,7},{7,6},{8,9},{9,8},{10,11... | collective-permute-start | bytes 98312 | tf_op jit(solution)/shard_map/ppermute | solution.py:351
  7.3 7.1 %copy-start = (s32[1,1,2,16]{3,2,1,0:T(2,128)S(1)}, s32[1,1,2,16]{3,2,1,0:T(2,128)}, u32[]{:S(2)}) copy-start(s32[1,1,2,16]{3,2,1,0:T(2,128)} %param.9) | copy-start | bytes 388
  7.4 9.5 %collective-permute-start.4 = (f32[136,128]{1,0:T(8,128)S(1)}, f32[136,128]{1,0:T(8,128)S(1)}, u32[]{:S(2)}, u32[]{:S(2)}) collective-permute-start(f32[136,128]{1,0:T(8,128)S(1)} %get-tuple-element.23.to_ref.first_ref), channel_id=1, source_target_pairs={{4,8},{8,4},{12,16},{16,12},{20,24},{24,20},{28,0},{0,28},{5,9},{9... | collective-permute-start | bytes 208904 | tf_op jit(solution)/shard_map/ppermute | solution.py:346
  12.0 4.3 %collective-permute-start.3 = (f32[128,128]{1,0:T(8,128)S(1)}, f32[128,128]{1,0:T(8,128)S(1)}, u32[]{:S(2)}, u32[]{:S(2)}) collective-permute-start(f32[128,128]{1,0:T(8,128)S(1)} %get-tuple-element.21.to_ref.first_ref), channel_id=1, source_target_pairs={{0,4},{4,0},{8,12},{12,8},{16,20},{20,16},{24,28},{28,24},{1,5},{5... | collective-permute-start | bytes 196616 | tf_op jit(solution)/shard_map/ppermute | solution.py:346
  18.0 6.9 %collective-permute-start.5 = (f32[72,128]{1,0:T(8,128)S(1)}, f32[72,128]{1,0:T(8,128)S(1)}, u32[]{:S(2)}, u32[]{:S(2)}) collective-permute-start(f32[72,128]{1,0:T(8,128)S(1)} %get-tuple-element.27.side_a_ref.own_ref), channel_id=1, source_target_pairs={{4,8},{8,4},{12,16},{16,12},{20,24},{24,20},{28,0},{0,28},{5,9},{9... | collective-permute-start | bytes 110600 | tf_op jit(solution)/shard_map/ppermute | solution.py:346
  20.5 4.4 %collective-permute-start.6 = (f32[64,128]{1,0:T(8,128)S(1)}, f32[64,128]{1,0:T(8,128)S(1)}, u32[]{:S(2)}, u32[]{:S(2)}) collective-permute-start(f32[64,128]{1,0:T(8,128)S(1)} %shard_map.92.side_b_ref.own_ref), channel_id=1, source_target_pairs={{0,4},{4,0},{8,12},{12,8},{16,20},{20,16},{24,28},{28,24},{1,5},{5... | collective-permute-start | bytes 98312 | tf_op jit(solution)/shard_map/ppermute | solution.py:346
  25.7 10.1 %all-to-all-start = ((f32[32,1,128]{2,1,0:T(1,128)}), f32[32,1,128]{2,1,0:T(1,128)S(1)}, u32[]{:S(2)}, u32[]{:S(2)}) async-start(f32[32,1,128]{2,1,0:T(1,128)} %shard_map.95), calls=%async_computation | async-start | bytes 32768 | tf_op jit(solution)/shard_map/all_to_all | solution.py:451

commit v12 on v11

--- a/solution.py
+++ b/solution.py
@@ -73,6 +73,10 @@
     return jnp.dot(
         left, right, precision=lax.Precision.HIGHEST, preferred_element_type=F32
     )
+
+
+def block_place(k, groups):
+    return jnp.where(k == 0, 0, groups - k)
 
 
 def first_kernel(
@@ -95,7 +99,7 @@
         inside = face - g * per_group
         source = jnp.where(
             (inside >= 0) & (inside < per_group),
-            (tail[1:2, g : g + 1] ^ slot) * per_group + inside,
+            block_place(tail[1:2, g : g + 1] ^ slot, groups) * per_group + inside,
             source,
         )
     order = one_hot(partner, faces)
@@ -113,7 +117,7 @@
 
 def message_kernel(first, packed_ref, chosen_ref, side_a_ref, side_b_ref, *refs):
     faces = side_a_ref.shape[0]
-    *weight_refs, to_a_ref, to_b_ref = refs
+    *weight_refs, odd_a_ref, odd_b_ref, even_a_ref, even_b_ref = refs
     slot = lax.axis_index("blk")
     per_group = weight_refs[0].shape[1]
     kept = pl.ds(pl.multiple_of(first + slot * per_group, SUBLANES), per_group)
@@ -121,14 +125,16 @@
         [packed_ref[kept, :]] + [weight_ref[slot] for weight_ref in weight_refs], axis=0
     )
     own = exact_dot(chosen_ref[...], held)
-    to_a_ref[2 * faces :, :] = jnp.zeros_like(to_a_ref[2 * faces :, :])
-    for side_ref, to_ref in ((side_a_ref, to_a_ref), (side_b_ref, to_b_ref)):
-        to_ref[:faces, :] = side_ref[...]
+    for side_ref, to_refs in (
+        (side_a_ref, (odd_a_ref, even_a_ref)),
+        (side_b_ref, (odd_b_ref, even_b_ref)),
+    ):
+        for to_ref in to_refs:
+            to_ref[:faces, :] = side_ref[...]
+    for to_ref in (odd_a_ref, odd_b_ref, even_b_ref):
         to_ref[faces : 2 * faces, :] = own
-
-
-def near_traces_kernel(aligned_ref, image_ref, side_b_ref):
-    gather_traces(image_ref[...], aligned_ref, side_b_ref.shape[0], side_b_ref)
+    for to_ref in (odd_a_ref, odd_b_ref):
+        to_ref[2 * faces :, :] = jnp.zeros_like(to_ref[2 * faces :, :])
 
 
 def stiffness_kernel(pairs_ref, blocks_ref, field_ref, out_ref, pieces, sums):
@@ -168,7 +174,7 @@
     )
 
 
-def spread_jumps(size, faces, rows_ref, rows_first, weights_ref, own_ref, arrived_ref, block_rows):
+def spread_jumps(size, block_rows, rows_ref, rows_first, jumps):
     dof_of = lax.broadcasted_iota(jnp.int32, (size, LANES), 0).astype(F32).astype(BF16)
     row_of = lax.broadcasted_iota(jnp.int32, (block_rows, LANES), 0).astype(F32).astype(BF16)
     none = jnp.zeros((), BF16)
@@ -178,10 +184,11 @@
         slab = jnp.broadcast_to(value[f : f + 1, :], (2 * SUBLANES, LANES)).astype(BF16)
         return jnp.concatenate([slab] * (rows // (2 * SUBLANES)), axis=0)
 
-    def step(k, total):
-        lam = weights_ref[tile(k), :] * (own_ref[tile(k), :] - arrived_ref[tile(k), :])
+    total = jnp.zeros((size, 2 * block_rows), F32)
+    for k, lam in enumerate(jumps):
         high, low = halves(lam)
-        dof, row = split(rows_ref[tile(rows_first // SUBLANES + k), :], block_rows)
+        place = slice(rows_first + k * SUBLANES, rows_first + (k + 1) * SUBLANES)
+        dof, row = split(rows_ref[place, :], block_rows)
         dof = dof.astype(F32)
         row = row.astype(F32)
         left = []
@@ -198,73 +205,165 @@
                 )
             )
             right.append(jnp.where(dof_of == widened(dof, f, size), one, none))
-        return total + lax.dot_general(
+        total = total + lax.dot_general(
             jnp.concatenate(right, axis=1),
             jnp.concatenate(left, axis=1),
             (((1,), (1,)), ((), ())),
             preferred_element_type=F32,
         )
-
-    total = lax.fori_loop(
-        0, faces // SUBLANES, step, jnp.zeros((size, 2 * block_rows), F32), unroll=8
-    )
     total = total.T
     return total[:block_rows] + total[block_rows:]
 
 
-def near_kernel(size, aligned_ref, product_ref, to_ref, from_ref, partial_ref, weights_ref):
-    block_rows = product_ref.shape[0]
-    faces = weights_ref.shape[0]
+def weighted_jumps(faces, weights_ref, own_ref, *arrived_refs):
     odd = lax.rem(lax.axis_index("sub"), 2) == 1
-    weights_ref[...] = jnp.where(odd, from_ref[faces:, :], to_ref[faces:, :])
-    partial_ref[...] = product_ref[...]
-    partial_ref[:, :size] = partial_ref[:, :size] + spread_jumps(
-        size, faces, aligned_ref, faces, weights_ref, to_ref, from_ref, block_rows
-    )
-
-
-def far_kernel(
+    for k in range(0, faces, SUBLANES):
+        place = slice(k, k + SUBLANES)
+        arrived = arrived_refs[0][place, :]
+        if len(arrived_refs) > 1:
+            arrived = jnp.where(odd, arrived_refs[1][place, :], arrived)
+        yield weights_ref[place, :] * (own_ref[place, :] - arrived)
+
+
+def near_kernel(
     size,
+    faces,
+    aligned_ref,
+    product_ref,
+    to_ref,
+    even_from_a_ref,
+    even_from_b_ref,
+    odd_from_b_ref,
+    partial_ref,
+    weights_a_ref,
+    weights_b_ref,
+    arrived_ref,
+):
+    odd = lax.rem(lax.axis_index("sub"), 2) == 1
+    own = to_ref[faces : 2 * faces, :]
+    weights_a_ref[...] = jnp.where(odd, own, even_from_a_ref[faces : 2 * faces, :])
+    weights_b_ref[...] = jnp.where(odd, odd_from_b_ref[faces : 2 * faces, :], own)
+    arrived_ref[...] = jnp.where(odd, odd_from_b_ref[:faces, :], even_from_b_ref[:faces, :])
+
+    @pl.when(odd)
+    def _():
+        partial_ref[...] = product_ref[...]
+        partial_ref[:, :size] = partial_ref[:, :size] + spread_jumps(
+            size,
+            product_ref.shape[0],
+            aligned_ref,
+            faces,
+            weighted_jumps(faces, weights_b_ref, to_ref, arrived_ref),
+        )
+
+
+def odd_kernel(
+    size,
+    faces,
     aligned_ref,
     partial_ref,
+    weights_ref,
     to_ref,
     from_ref,
     image_ref,
-    weights_ref,
     side_a_ref,
-):
-    block_rows = partial_ref.shape[0]
-    faces = weights_ref.shape[0]
+    side_b_ref,
+):
+    @pl.when(lax.rem(lax.axis_index("sub"), 2) == 1)
+    def _():
+        image_ref[...] = partial_ref[...]
+        image_ref[:, :size] = image_ref[:, :size] + spread_jumps(
+            size,
+            partial_ref.shape[0],
+            aligned_ref,
+            0,
+            weighted_jumps(faces, weights_ref, to_ref, from_ref),
+        )
+        gather_traces(image_ref[...], aligned_ref, 0, side_a_ref.at[:faces, :])
+        gather_traces(image_ref[...], aligned_ref, faces, side_b_ref)
+        side_a_ref[faces:, :] = jnp.zeros_like(side_a_ref[faces:, :])
+
+
+def even_kernel(
+    size,
+    faces,
+    aligned_ref,
+    product_ref,
+    weights_a_ref,
+    weights_b_ref,
+    to_a_ref,
+    to_b_ref,
+    from_a_ref,
+    from_b_ref,
+    odd_image_ref,
+    odd_a_ref,
+    odd_b_ref,
+    image_ref,
+    side_a_ref,
+    side_b_ref,
+):
     odd = lax.rem(lax.axis_index("sub"), 2) == 1
-    weights_ref[...] = jnp.where(
-        odd, to_ref[faces : 2 * faces, :], from_ref[faces : 2 * faces, :]
-    )
-    image_ref[...] = partial_ref[...]
-    image_ref[:, :size] = image_ref[:, :size] + spread_jumps(
-        size, faces, aligned_ref, 0, weights_ref, to_ref, from_ref, block_rows
-    )
-    gather_traces(image_ref[...], aligned_ref, 0, side_a_ref.at[:faces, :])
-    side_a_ref[faces:, :] = jnp.zeros_like(side_a_ref[faces:, :])
+
+    @pl.when(odd)
+    def _():
+        image_ref[...] = odd_image_ref[...]
+        side_a_ref[...] = odd_a_ref[:faces, :]
+        side_b_ref[...] = odd_b_ref[...]
+
+    @pl.when(jnp.logical_not(odd))
+    def _():
+        image_ref[...] = product_ref[...]
+        coupled = [
+            spread_jumps(
+                size,
+                product_ref.shape[0],
+                aligned_ref,
+                first,
+                weighted_jumps(faces, weights_ref, to_ref, from_ref),
+            )
+            for first, weights_ref, to_ref, from_ref in (
+                (0, weights_a_ref, to_a_ref, from_a_ref),
+                (faces, weights_b_ref, to_b_ref, from_b_ref),
+            )
+        ]
+        image_ref[:, :size] = image_ref[:, :size] + (coupled[0] + coupled[1])
+        gather_traces(image_ref[...], aligned_ref, 0, side_a_ref)
+        gather_traces(image_ref[...], aligned_ref, faces, side_b_ref)
 
 
 def column_sums(value):
     return jnp.sum(value, axis=0, keepdims=True)
 
 
-def jump_sums(weights_ref, own_ref, arrived_ref, first_ref):
-    faces = slice(0, weights_ref.shape[0])
-    own = own_ref[faces, :]
-    lam = weights_ref[...] * (own - arrived_ref[faces, :])
-    return column_sums(lam * first_ref[faces, :]), column_sums(lam * own)
+def jump_sums(faces, weights_ref, own_ref, arrived_ref, first_ref, first_arrived_ref):
+    even = lax.rem(lax.axis_index("sub"), 2) == 0
+    place = slice(0, faces)
+    jump = own_ref[place, :] - arrived_ref[place, :]
+    first = first_ref[place, :] - first_arrived_ref[place, :]
+    lam = weights_ref[...] * jump
+    return tuple(
+        jnp.where(even, column_sums(lam * value), 0.0) for value in (first, jump)
+    )
 
 
 def near_sums_kernel(
-    product_ref, weights_ref, own_ref, arrived_ref, first_ref, field_ref, image_ref, rows_ref
+    faces,
+    product_ref,
+    weights_ref,
+    own_ref,
+    arrived_ref,
+    first_ref,
+    first_arrived_ref,
+    field_ref,
+    image_ref,
+    rows_ref,
 ):
     field = field_ref[...]
     image = image_ref[...]
     product = product_ref[...]
-    with_field, with_image = jump_sums(weights_ref, own_ref, arrived_ref, first_ref)
+    with_field, with_image = jump_sums(
+        faces, weights_ref, own_ref, arrived_ref, first_ref, first_arrived_ref
+    )
     parts = [
         column_sums(field * field),
         column_sums(field * image),
@@ -276,8 +375,12 @@
     rows_ref[...] = jnp.concatenate(parts, axis=0)
 
 
-def sums_kernel(rows_ref, weights_ref, own_ref, arrived_ref, first_ref, sums_ref):
-    with_field, with_image = jump_sums(weights_ref, own_ref, arrived_ref, first_ref)
+def sums_kernel(
+    faces, rows_ref, weights_ref, own_ref, arrived_ref, first_ref, first_arrived_ref, sums_ref
+):
+    with_field, with_image = jump_sums(
+        faces, weights_ref, own_ref, arrived_ref, first_ref, first_arrived_ref
+    )
     row = lax.broadcasted_iota(jnp.int32, (SUBLANES, LANES), 0)
     rows = rows_ref[...] + jnp.where(row == 3, with_field, jnp.where(row == 4, with_image, 0.0))
     lane = lax.broadcasted_iota(jnp.int32, (SUBLANES, LANES), 1)
@@ -294,22 +397,29 @@
     weights_b_ref,
     side_a_ref,
     side_b_ref,
-    from_a_ref,
-    from_b_ref,
+    even_from_a_ref,
+    even_from_b_ref,
+    odd_from_a_ref,
+    odd_from_b_ref,
     second_ref,
 ):
     block_rows = product_ref.shape[0]
-    faces = weights_a_ref.shape[0]
+    faces = side_a_ref.shape[0]
     second_ref[...] = product_ref[...]
-    second_ref[:, :size] = (
-        second_ref[:, :size]
-        + spread_jumps(
-            size, faces, aligned_ref, 0, weights_a_ref, side_a_ref, from_a_ref, block_rows
-        )
-        + spread_jumps(
-            size, faces, aligned_ref, faces, weights_b_ref, side_b_ref, from_b_ref, block_rows
-        )
-    )
+    coupled = [
+        spread_jumps(
+            size,
+            block_rows,
+            aligned_ref,
+            first,
+            weighted_jumps(faces, weights_ref, own_ref, even_from_ref, odd_from_ref),
+        )
+        for first, weights_ref, own_ref, even_from_ref, odd_from_ref in (
+            (0, weights_a_ref, side_a_ref, even_from_a_ref, odd_from_a_ref),
+            (faces, weights_b_ref, side_b_ref, even_from_b_ref, odd_from_b_ref),
+        )
+    ]
+    second_ref[:, :size] = second_ref[:, :size] + (coupled[0] + coupled[1])
 
 
 def final_kernel(field_ref, image_ref, second_ref, sums_ref, solution_ref, residual_ref):
@@ -337,12 +447,9 @@
     residual_ref[...] = residual - alpha_next * moved
 
 
-def swap(value, odd):
+def across(value, parity, steps):
     count = lax.axis_size("sub")
-    pairs = []
-    for first in range(odd, count, 2):
-        second = (first + 1) % count
-        pairs += [(first, second), (second, first)]
+    pairs = [(source, (source + steps) % count) for source in range(parity, count, 2)]
     return lax.ppermute(value, "sub", pairs)
 
 
@@ -366,7 +473,7 @@
     devices = lax.axis_size("sub") * lax.axis_size("blk")
 
     own_weights = mortar_weight[0, 0]
-    held = [swap_slots(own_weights, k) for k in range(1, own_weights.shape[0])]
+    held = [swap_slots(own_weights, k) for k in range(own_weights.shape[0] - 1, 0, -1)]
     last = 2 * faces + block_rows
 
     def placed(value, first):
@@ -390,13 +497,20 @@
         ],
         [(packed, VMEM)],
     )
-    to_a, to_b = call(
+    to_a, to_b, even_a, even_b = call(
         functools.partial(message_kernel, last + SUBLANES),
-        [shape(2 * faces + SUBLANES), shape(2 * faces)],
+        [
+            shape(2 * faces + 2 * SUBLANES),
+            shape(2 * faces + SUBLANES),
+            shape(faces),
+            shape(2 * faces),
+        ],
         [(value, VMEM) for value in (packed, chosen, side_a, side_b, *held)],
     )
-    from_b = swap(to_b, 0)
-    from_a = swap(to_a, 1)
+    even_from_a = across(to_a, 1, 1)
+    even_from_b = across(to_b, 1, -1)
+    odd_from_b = across(even_b, 0, 1)
+    odd_from_a = across(even_a, 0, -1)
 
     def stiff(vector):
         (product,) = call(
@@ -407,35 +521,70 @@
         )
         return product
 
-    partial, weights_b = call(
-        functools.partial(near_kernel, size),
-        [shape(block_rows), shape(faces)],
-        [(value, VMEM) for value in (aligned, stiff(padded), to_b, from_b)],
+    product = stiff(padded)
+    partial, weights_a, weights_b, from_b = call(
+        functools.partial(near_kernel, size, faces),
+        [shape(block_rows)] + [shape(faces)] * 3,
+        [
+            (value, VMEM)
+            for value in (aligned, product, to_b, even_from_a, even_from_b, odd_from_b)
+        ],
         flops=1,
         moved=1,
     )
-    image, weights_a, side_a = call(
-        functools.partial(far_kernel, size),
-        [shape(block_rows), shape(faces), shape(faces + SUBLANES)],
-        [(value, VMEM) for value in (aligned, partial, to_a, from_a)],
-    )
-    from_a = swap(side_a, 1)
-    (side_b,) = call(
-        near_traces_kernel, [shape(faces)], [(aligned, VMEM), (image, VMEM)]
-    )
-    from_b = swap(side_b, 0)
+    odd_image, odd_a, odd_b = call(
+        functools.partial(odd_kernel, size, faces),
+        [shape(block_rows), shape(faces + SUBLANES), shape(faces)],
+        [(value, VMEM) for value in (aligned, partial, weights_a, to_a, odd_from_a)],
+        flops=1,
+        moved=1,
+    )
+    second_from_a = across(odd_a, 1, 1)
+    second_from_b = across(odd_b, 1, -1)
+    image, side_a, side_b = call(
+        functools.partial(even_kernel, size, faces),
+        [shape(block_rows)] + [shape(faces)] * 2,
+        [
+            (value, VMEM)
+            for value in (
+                aligned,
+                product,
+                weights_a,
+                weights_b,
+                to_a,
+                to_b,
+                even_from_a,
+                from_b,
+                odd_image,
+                odd_a,
+                odd_b,
+            )
+        ],
+        flops=1,
+        moved=1,
+    )
+    third_from_b = across(side_b, 0, 1)
+    third_from_a = across(side_a, 0, -1)
     product = stiff(image)
     (sums,) = call(
-        near_sums_kernel,
+        functools.partial(near_sums_kernel, faces),
         [shape(SUBLANES)],
-        [(value, VMEM) for value in (product, weights_b, side_b, from_b, to_b, padded, image)],
+        [
+            (value, VMEM)
+            for value in (
+                product, weights_b, side_b, second_from_b, to_b, from_b, padded, image
+            )
+        ],
         flops=1,
         moved=1,
     )
     (sums,) = call(
-        sums_kernel,
+        functools.partial(sums_kernel, faces),
         [jax.ShapeDtypeStruct((devices, 1, LANES), F32)],
-        [(value, VMEM) for value in (sums, weights_a, side_a, from_a, to_a)],
+        [
+            (value, VMEM)
+            for value in (sums, weights_a, side_a, second_from_a, to_a, even_from_a)
+        ],
     )
     (second,) = call(
         functools.partial(second_kernel, size),
@@ -443,7 +592,16 @@
         [
             (value, VMEM)
             for value in (
-                aligned, product, weights_a, weights_b, side_a, side_b, from_a, from_b
+                aligned,
+                product,
+                weights_a,
+                weights_b,
+                side_a,
+                side_b,
+                second_from_a,
+                second_from_b,
+                third_from_a,
+                third_from_b,
             )
         ],
         flops=1_000_000_000,

time: 36.8 us -> 46.9 us (1.27)
  starting transfers between devices: 13 us -> 26.5 us
  waiting for transfers between devices: 11.2 us -> 7.77 us
    ppermute x4 -> x8, starting transfers between devices: 6.82 us -> 20.8 us  [across(): return lax.ppermute(value, 'sub', pairs)]
    ppermute x4 -> x8, waiting for transfers between devices: 3.44 us -> 0.02 us  [across(): return lax.ppermute(value, 'sub', pairs)]
    all_to_all x1, starting transfers between devices: 3.05 us -> 2.54 us  [on_device(): lax.all_to_all(sums, ('sub', 'blk'), split_axis=0, concat_axis=0, tiled=T...]
  transfers between devices with their start and end apart: 8 -> 12, of which waited for: 4 -> 2; matrix products, arithmetic and copies ran while one was open for 9% -> 7% of each run, Pallas kernels for 16% -> 16%
where the time goes in v12:
time: 46.9 us; the launch traced here: 46.5 us
  starting transfers between devices  26.5 us (57%)
  Pallas kernels  8.2 us (17%)
  waiting for transfers between devices  7.77 us (17%)
  local copies, waits for them, and re-layouts  2.3 us (5%)
  other arithmetic  0.92 us (2%)
  between operations  0.86 us (2%)
    ppermute x8, starting transfers between devices, across(): return lax.ppermute(value, 'sub', pairs)  20.8 us
    pallas_call x11, Pallas kernels, call(): pl.pallas_call(body, out_shape=outs, in_specs=[spec for _, spec in inputs...  8.2 us
    all_to_all x1, waiting for transfers between devices, on_device(): lax.all_to_all(sums, ('sub', 'blk'), split_axis=0, concat_axis=0, tiled=T...  6.01 us
    ppermute x3, starting transfers between devices, swap_slots(): lax.ppermute(value, 'blk', [(slot, slot ^ k) for slot in range(count)])  3.12 us
    all_to_all x1, starting transfers between devices, on_device(): lax.all_to_all(sums, ('sub', 'blk'), split_axis=0, concat_axis=0, tiled=T...  2.54 us
    another operation x1, local copies, waits for them, and re-layouts, on_device(): blocks = stored.reshape(stored.shape[0], size, size)  2.3 us
    ppermute x3, waiting for transfers between devices, swap_slots(): lax.ppermute(value, 'blk', [(slot, slot ^ k) for slot in range(count)])  1.74 us
  transfers between devices with their start and end apart: 12, of which 2 were waited for; matrix products, arithmetic and copies ran while one was open for 7% of the time, Pallas kernels for 16%

profile of v12, /device:TPU:0, one launch (start us, length us, event | category | flops | bytes accessed | tf_op | source)
XLA Modules:
  0.0 46.5 jit_solution(16039947503487447686)
XLA Ops:
  0.6 2.4 %collective-permute-start = (f32[4,16,128]{2,1,0:T(8,128)}, f32[4,16,128]{2,1,0:T(8,128)S(1)}, u32[]{:S(2)}, u32[]{:S(2)}) collective-permute-start(f32[4,16,128]{2,1,0:T(8,128)} %bitcast.20), channel_id=1, source_target_pairs={{0,3},{1,2},{2,1},{3,0},{4,7},{5,6},{6,5},{7,4},{8,11},{9,10},{10,... | collective-permute-start | bytes 98312 | tf_op jit(solution)/shard_map/ppermute | solution.py:458
  3.1 0.6 %collective-permute-start.1 = (f32[4,16,128]{2,1,0:T(8,128)}, f32[4,16,128]{2,1,0:T(8,128)S(1)}, u32[]{:S(2)}, u32[]{:S(2)}) collective-permute-start(f32[4,16,128]{2,1,0:T(8,128)} %bitcast.21), channel_id=1, source_target_pairs={{0,2},{1,3},{2,0},{3,1},{4,6},{5,7},{6,4},{7,5},{8,10},{9,11},{10,... | collective-permute-start | bytes 98312 | tf_op jit(solution)/shard_map/ppermute | solution.py:458
  3.7 0.0 collective-permute-start.2
  3.8 0.9 %pad_add_fusion.packed_ref = f32[232,128]{1,0:T(8,128)S(1)} fusion(f32[64,128]{1,0:T(8,128)} %bitcast.23, f32[32,96]{1,0:T(8,128)} %bitcast.24, s32[1,4]{1,0:T(1,128)} %bitcast.25, s32[1,64]{1,0:T(1,128)} %bitcast.26, s32[128,128]{1,0:T(8,128)} %bitcast.19), kind=kLoop, calls=%fused_computation | loop fusion | flops 148480 | bytes 229648 | tf_op jit(solution)/shard_map/add | solution.py:485
  4.7 0.8 %shard_map.86 = (s32[128,128]{1,0:T(8,128)S(1)}, f32[32,128]{1,0:T(8,128)S(1)}, f32[64,64]{1,0:T(8,128)S(1)}, f32[64,128]{1,0:T(8,128)S(1)}, f32[64,128]{1,0:T(8,128)S(1)}) custom-call(f32[232,128]{1,0:T(8,128)S(1)} %pad_add_fusion.packed_ref), custom_call_target="tpu_custom_call" | custom-call | flops 1000000 | bytes 1000000 | tf_op jit(solution)/shard_map/pallas_call | solution.py:19
  5.5 1.7 %collective-permute-done.1.refs_1_ = f32[4,16,128]{2,1,0:T(8,128)S(1)} collective-permute-done((f32[4,16,128]{2,1,0:T(8,128)}, f32[4,16,128]{2,1,0:T(8,128)S(1)}, u32[]{:S(2)}, u32[]{:S(2)}) %collective-permute-start.1) | collective-permute-done | bytes 32800 | tf_op jit(solution)/shard_map/ppermute | solution.py:458
  7.3 0.2 shard_map.88
  7.4 1.3 %collective-permute-start.3 = (f32[144,128]{1,0:T(8,128)S(1)}, f32[144,128]{1,0:T(8,128)S(1)}, u32[]{:S(2)}, u32[]{:S(2)}) collective-permute-start(f32[144,128]{1,0:T(8,128)S(1)} %get-tuple-element.29.to_ref.to_a_ref.first_ref), channel_id=1, source_target_pairs={{4,8},{12,16},{20,24},{28,0},{5,9},{13,17},{21,25},{29,1},{6,10},{... | collective-permute-start | bytes 221192 | tf_op jit(solution)/shard_map/ppermute | solution.py:453
  8.7 1.3 %collective-permute-start.4 = (f32[136,128]{1,0:T(8,128)S(1)}, f32[136,128]{1,0:T(8,128)S(1)}, u32[]{:S(2)}, u32[]{:S(2)}) collective-permute-start(f32[136,128]{1,0:T(8,128)S(1)} %get-tuple-element.28.to_ref.to_b_ref.first_ref), channel_id=1, source_target_pairs={{4,0},{12,8},{20,16},{28,24},{5,1},{13,9},{21,17},{29,25},{6,2},{1... | collective-permute-start | bytes 208904 | tf_op jit(solution)/shard_map/ppermute | solution.py:453
  10.0 5.6 %collective-permute-start.5 = (f32[128,128]{1,0:T(8,128)S(1)}, f32[128,128]{1,0:T(8,128)S(1)}, u32[]{:S(2)}, u32[]{:S(2)}) collective-permute-start(f32[128,128]{1,0:T(8,128)S(1)} %get-tuple-element.30), channel_id=1, source_target_pairs={{0,4},{8,12},{16,20},{24,28},{1,5},{9,13},{17,21},{25,29},{2,6},{1... | collective-permute-start | bytes 196616 | tf_op jit(solution)/shard_map/ppermute | solution.py:453
  15.6 3.3 %collective-permute-start.6 = (f32[64,128]{1,0:T(8,128)S(1)}, f32[64,128]{1,0:T(8,128)S(1)}, u32[]{:S(2)}, u32[]{:S(2)}) collective-permute-start(f32[64,128]{1,0:T(8,128)S(1)} %get-tuple-element.35), channel_id=1, source_target_pairs={{0,28},{8,4},{16,12},{24,20},{1,29},{9,5},{17,13},{25,21},{2,30},{... | collective-permute-start | bytes 98312 | tf_op jit(solution)/shard_map/ppermute | solution.py:453
  18.9 2.3 %reshape_squeeze.7.blocks_ref = bf16[48,96,96]{2,1,0:T(8,128)(2,1)S(1)} reshape(bf16[1,1,48,9216]{3,2,1,0:T(8,128)(2,1)} %param.8) | data formatting | bytes 1769472 | tf_op jit(solution)/shard_map/reshape;squeeze | solution.py:467
  21.2 1.4 %shard_map.87.product_ref = f32[32,128]{1,0:T(8,128)S(1)} custom-call(s32[2,16]{1,0:T(2,128)S(1)} %bitcast.17, bf16[48,96,96]{2,1,0:T(8,128)(2,1)S(1)} %reshape_squeeze.7.blocks_ref, f32[32,128]{1,0:T(8,128)S(1)} %get-tuple-element.23.field_ref), custom_call_target="tpu_custom_call" | custom-call | flops 1000000 | bytes 1000000 | tf_op jit(solution)/shard_map/pallas_call | solution.py:19
  22.8 1.3 %collective-permute-start.7 = (f32[72,128]{1,0:T(8,128)S(1)}, f32[72,128]{1,0:T(8,128)S(1)}, u32[]{:S(2)}, u32[]{:S(2)}) collective-permute-start(f32[72,128]{1,0:T(8,128)S(1)} %get-tuple-element.37.odd_a_ref), channel_id=1, source_target_pairs={{4,8},{12,16},{20,24},{28,0},{5,9},{13,17},{21,25},{29,1},{6,10},{... | collective-permute-start | bytes 110600 | tf_op jit(solution)/shard_map/ppermute | solution.py:453
  24.1 1.3 %collective-permute-start.8 = (f32[64,128]{1,0:T(8,128)S(1)}, f32[64,128]{1,0:T(8,128)S(1)}, u32[]{:S(2)}, u32[]{:S(2)}) collective-permute-start(f32[64,128]{1,0:T(8,128)S(1)} %get-tuple-element.38.odd_b_ref), channel_id=1, source_target_pairs={{4,0},{12,8},{20,16},{28,24},{5,1},{13,9},{21,17},{29,25},{6,2},{1... | collective-permute-start | bytes 98312 | tf_op jit(solution)/shard_map/ppermute | solution.py:453
  25.4 1.8 %shard_map.91 = (f32[32,128]{1,0:T(8,128)S(1)}, f32[64,128]{1,0:T(8,128)S(1)}, f32[64,128]{1,0:T(8,128)S(1)}) custom-call(s32[128,128]{1,0:T(8,128)S(1)} %get-tuple-element.24.aligned_ref, f32[32,128]{1,0:T(8,128)S(1)} %shard_map.87.product_ref, f32[64,128]{1,0:T(8,128)S(1)} %get-tuple-element.31.weights_ref.weights_a_ref, ...), custom_call_target="tpu_custom_call" | custom-call | flops 1 | bytes 1 | tf_op jit(solution)/shard_map/pallas_call | solution.py:19
  27.2 2.8 %collective-permute-start.10 = (f32[64,128]{1,0:T(8,128)S(1)}, f32[64,128]{1,0:T(8,128)S(1)}, u32[]{:S(2)}, u32[]{:S(2)}) collective-permute-start(f32[64,128]{1,0:T(8,128)S(1)} %get-tuple-element.41.side_b_ref.own_ref), channel_id=1, source_target_pairs={{0,4},{8,12},{16,20},{24,28},{1,5},{9,13},{17,21},{25,29},{2,6},{1... | collective-permute-start | bytes 98312 | tf_op jit(solution)/shard_map/ppermute | solution.py:453
  29.9 4.0 %collective-permute-start.9 = (f32[64,128]{1,0:T(8,128)S(1)}, f32[64,128]{1,0:T(8,128)S(1)}, u32[]{:S(2)}, u32[]{:S(2)}) collective-permute-start(f32[64,128]{1,0:T(8,128)S(1)} %get-tuple-element.40.side_a_ref.own_ref), channel_id=1, source_target_pairs={{0,28},{8,4},{16,12},{24,20},{1,29},{9,5},{17,13},{25,21},{2,30},{... | collective-permute-start | bytes 98312 | tf_op jit(solution)/shard_map/ppermute | solution.py:453
  33.9 1.4 %shard_map.92.product_ref = f32[32,128]{1,0:T(8,128)S(1)} custom-call(s32[2,16]{1,0:T(2,128)S(1)} %bitcast.18, bf16[48,96,96]{2,1,0:T(8,128)(2,1)S(1)} %reshape_squeeze.7.blocks_ref, f32[32,128]{1,0:T(8,128)S(1)} %get-tuple-element.39.field_ref.image_ref), custom_call_target="tpu_custom_call" | custom-call | flops 1000000 | bytes 1000000 | tf_op jit(solution)/shard_map/pallas_call | solution.py:19
  35.4 0.7 %shard_map.95 = f32[32,1,128]{2,1,0:T(1,128)} custom-call(f32[8,128]{1,0:T(8,128)S(1)} %shard_map.94.rows_ref, f32[64,128]{1,0:T(8,128)S(1)} %get-tuple-element.31.weights_ref.weights_a_ref, f32[64,128]{1,0:T(8,128)S(1)} %get-tuple-element.40.side_a_ref.own_ref, f32[72,128]{1,0:T(8,128)S(1)} %collective-permute-done.7.even_from_a_ref.arrived_ref, ...), custom_call_target="tpu_custom_call" | custom-call | flops 1000000 | bytes 1000000 | tf_op jit(solution)/shard_map/pallas_call | solution.py:19
  36.1 2.5 %all-to-all-start = ((f32[32,1,128]{2,1,0:T(1,128)}), f32[32,1,128]{2,1,0:T(1,128)S(1)}, u32[]{:S(2)}, u32[]{:S(2)}) async-start(f32[32,1,128]{2,1,0:T(1,128)} %shard_map.95), calls=%async_computation | async-start | bytes 32768 | tf_op jit(solution)/shard_map/all_to_all | solution.py:609
  38.7 1.0 %shard_map.93.second_ref = f32[32,128]{1,0:T(8,128)S(1)} custom-call(s32[128,128]{1,0:T(8,128)S(1)} %get-tuple-element.24.aligned_ref, f32[32,128]{1,0:T(8,128)S(1)} %shard_map.92.product_ref, f32[64,128]{1,0:T(8,128)S(1)} %get-tuple-element.31.weights_ref.weights_a_ref, f32[64,128]{1,0:T(8,128)S(1)} %get-tuple-element.32.weights_b_ref.weights_ref, ...), custom_call_target="tpu_custom_call" | custom-call | flops 1000000000 | bytes 1000000 | tf_op jit(solution)/shard_map/pallas_call | solution.py:19
  39.8 6.0 %all-to-all-done.sums_ref = f32[32,1,128]{2,1,0:T(1,128)S(1)} async-done(((f32[32,1,128]{2,1,0:T(1,128)}), f32[32,1,128]{2,1,0:T(1,128)S(1)}, u32[]{:S(2)}, u32[]{:S(2)}) %all-to-all-start) | async-done | bytes 16416 | tf_op jit(solution)/shard_map/all_to_all | solution.py:609
  45.8 0.8 %shard_map.96 = (f32[32,96]{1,0:T(8,128)}, f32[32,96]{1,0:T(8,128)}) custom-call(f32[32,128]{1,0:T(8,128)S(1)} %get-tuple-element.23.field_ref, f32[32,128]{1,0:T(8,128)S(1)} %get-tuple-element.39.field_ref.image_ref, f32[32,128]{1,0:T(8,128)S(1)} %shard_map.93.second_ref, f32[32,1,128]{2,1,0:T(1,128)S(1)} %all-to-all-done.sums_ref), custom_call_target="tpu_custom_call" | custom-call | flops 1000000 | bytes 1000000 | tf_op jit(solution)/shard_map/pallas_call | solution.py:19
  (15 shorter events, 0.1 us)
Async XLA Ops:
  0.6 4.9 %collective-permute-start = (f32[4,16,128]{2,1,0:T(8,128)}, f32[4,16,128]{2,1,0:T(8,128)S(1)}, u32[]{:S(2)}, u32[]{:S(2)}) collective-permute-start(f32[4,16,128]{2,1,0:T(8,128)} %bitcast.20), channel_id=1, source_target_pairs={{0,3},{1,2},{2,1},{3,0},{4,7},{5,6},{6,5},{7,4},{8,11},{9,10},{10,... | collective-permute-start | bytes 98312 | tf_op jit(solution)/shard_map/ppermute | solution.py:458
  3.1 4.2 %collective-permute-start.1 = (f32[4,16,128]{2,1,0:T(8,128)}, f32[4,16,128]{2,1,0:T(8,128)S(1)}, u32[]{:S(2)}, u32[]{:S(2)}) collective-permute-start(f32[4,16,128]{2,1,0:T(8,128)} %bitcast.21), channel_id=1, source_target_pairs={{0,2},{1,3},{2,0},{3,1},{4,6},{5,7},{6,4},{7,5},{8,10},{9,11},{10,... | collective-permute-start | bytes 98312 | tf_op jit(solution)/shard_map/ppermute | solution.py:458
  3.7 3.5 %collective-permute-start.2 = (f32[4,16,128]{2,1,0:T(8,128)}, f32[4,16,128]{2,1,0:T(8,128)S(1)}, u32[]{:S(2)}, u32[]{:S(2)}) collective-permute-start(f32[4,16,128]{2,1,0:T(8,128)} %bitcast.22), channel_id=1, source_target_pairs={{0,1},{1,0},{2,3},{3,2},{4,5},{5,4},{6,7},{7,6},{8,9},{9,8},{10,11... | collective-permute-start | bytes 98312 | tf_op jit(solution)/shard_map/ppermute | solution.py:458
  7.3 14.0 %copy-start = (s32[1,1,2,16]{3,2,1,0:T(2,128)S(1)}, s32[1,1,2,16]{3,2,1,0:T(2,128)}, u32[]{:S(2)}) copy-start(s32[1,1,2,16]{3,2,1,0:T(2,128)} %param.9) | copy-start | bytes 388
  7.4 15.2 %collective-permute-start.3 = (f32[144,128]{1,0:T(8,128)S(1)}, f32[144,128]{1,0:T(8,128)S(1)}, u32[]{:S(2)}, u32[]{:S(2)}) collective-permute-start(f32[144,128]{1,0:T(8,128)S(1)} %get-tuple-element.29.to_ref.to_a_ref.first_ref), channel_id=1, source_target_pairs={{4,8},{12,16},{20,24},{28,0},{5,9},{13,17},{21,25},{29,1},{6,10},{... | collective-permute-start | bytes 221192 | tf_op jit(solution)/shard_map/ppermute | solution.py:453
  8.7 13.9 %collective-permute-start.4 = (f32[136,128]{1,0:T(8,128)S(1)}, f32[136,128]{1,0:T(8,128)S(1)}, u32[]{:S(2)}, u32[]{:S(2)}) collective-permute-start(f32[136,128]{1,0:T(8,128)S(1)} %get-tuple-element.28.to_ref.to_b_ref.first_ref), channel_id=1, source_target_pairs={{4,0},{12,8},{20,16},{28,24},{5,1},{13,9},{21,17},{29,25},{6,2},{1... | collective-permute-start | bytes 208904 | tf_op jit(solution)/shard_map/ppermute | solution.py:453
  10.0 12.6 %collective-permute-start.5 = (f32[128,128]{1,0:T(8,128)S(1)}, f32[128,128]{1,0:T(8,128)S(1)}, u32[]{:S(2)}, u32[]{:S(2)}) collective-permute-start(f32[128,128]{1,0:T(8,128)S(1)} %get-tuple-element.30), channel_id=1, source_target_pairs={{0,4},{8,12},{16,20},{24,28},{1,5},{9,13},{17,21},{25,29},{2,6},{1... | collective-permute-start | bytes 196616 | tf_op jit(solution)/shard_map/ppermute | solution.py:453
  15.6 7.1 %collective-permute-start.6 = (f32[64,128]{1,0:T(8,128)S(1)}, f32[64,128]{1,0:T(8,128)S(1)}, u32[]{:S(2)}, u32[]{:S(2)}) collective-permute-start(f32[64,128]{1,0:T(8,128)S(1)} %get-tuple-element.35), channel_id=1, source_target_pairs={{0,28},{8,4},{16,12},{24,20},{1,29},{9,5},{17,13},{25,21},{2,30},{... | collective-permute-start | bytes 98312 | tf_op jit(solution)/shard_map/ppermute | solution.py:453
  22.8 12.7 %collective-permute-start.7 = (f32[72,128]{1,0:T(8,128)S(1)}, f32[72,128]{1,0:T(8,128)S(1)}, u32[]{:S(2)}, u32[]{:S(2)}) collective-permute-start(f32[72,128]{1,0:T(8,128)S(1)} %get-tuple-element.37.odd_a_ref), channel_id=1, source_target_pairs={{4,8},{12,16},{20,24},{28,0},{5,9},{13,17},{21,25},{29,1},{6,10},{... | collective-permute-start | bytes 110600 | tf_op jit(solution)/shard_map/ppermute | solution.py:453
  24.1 11.3 %collective-permute-start.8 = (f32[64,128]{1,0:T(8,128)S(1)}, f32[64,128]{1,0:T(8,128)S(1)}, u32[]{:S(2)}, u32[]{:S(2)}) collective-permute-start(f32[64,128]{1,0:T(8,128)S(1)} %get-tuple-element.38.odd_b_ref), channel_id=1, source_target_pairs={{4,0},{12,8},{20,16},{28,24},{5,1},{13,9},{21,17},{29,25},{6,2},{1... | collective-permute-start | bytes 98312 | tf_op jit(solution)/shard_map/ppermute | solution.py:453
  27.2 11.5 %collective-permute-start.10 = (f32[64,128]{1,0:T(8,128)S(1)}, f32[64,128]{1,0:T(8,128)S(1)}, u32[]{:S(2)}, u32[]{:S(2)}) collective-permute-start(f32[64,128]{1,0:T(8,128)S(1)} %get-tuple-element.41.side_b_ref.own_ref), channel_id=1, source_target_pairs={{0,4},{8,12},{16,20},{24,28},{1,5},{9,13},{17,21},{25,29},{2,6},{1... | collective-permute-start | bytes 98312 | tf_op jit(solution)/shard_map/ppermute | solution.py:453
  29.9 8.8 %collective-permute-start.9 = (f32[64,128]{1,0:T(8,128)S(1)}, f32[64,128]{1,0:T(8,128)S(1)}, u32[]{:S(2)}, u32[]{:S(2)}) collective-permute-start(f32[64,128]{1,0:T(8,128)S(1)} %get-tuple-element.40.side_a_ref.own_ref), channel_id=1, source_target_pairs={{0,28},{8,4},{16,12},{24,20},{1,29},{9,5},{17,13},{25,21},{2,30},{... | collective-permute-start | bytes 98312 | tf_op jit(solution)/shard_map/ppermute | solution.py:453
  36.1 9.6 %all-to-all-start = ((f32[32,1,128]{2,1,0:T(1,128)}), f32[32,1,128]{2,1,0:T(1,128)S(1)}, u32[]{:S(2)}, u32[]{:S(2)}) async-start(f32[32,1,128]{2,1,0:T(1,128)} %shard_map.95), calls=%async_computation | async-start | bytes 32768 | tf_op jit(solution)/shard_map/all_to_all | solution.py:609

commit v13 on v11

--- a/solution.py
+++ b/solution.py
@@ -75,10 +75,14 @@
     )
 
 
+def block_place(k, groups):
+    return jnp.where(k == 0, 0, groups - k)
+
+
 def first_kernel(
-    groups, packed_ref, aligned_ref, padded_ref, chosen_ref, side_a_ref, side_b_ref
+    groups, packed_ref, aligned_ref, padded_ref, choice_ref, to_a_ref, to_b_ref
 ):
-    faces = side_a_ref.shape[0]
+    faces = aligned_ref.shape[0] // 2
     block_rows = padded_ref.shape[0]
     per_group = faces // groups
     slot = lax.axis_index("blk")
@@ -95,36 +99,33 @@
         inside = face - g * per_group
         source = jnp.where(
             (inside >= 0) & (inside < per_group),
-            (tail[1:2, g : g + 1] ^ slot) * per_group + inside,
+            block_place(tail[1:2, g : g + 1] ^ slot, groups) * per_group + inside,
             source,
         )
     order = one_hot(partner, faces)
     aligned_ref[pl.ds(west, faces), :] = packed_ref[faces : 2 * faces, :].astype(jnp.int32)
     aligned_ref[pl.ds(east, faces), :] = exact_dot(order, packed_ref[:faces, :]).astype(jnp.int32)
-    chosen_ref[...] = lax.dot_general(
+    choice_ref[...] = jnp.zeros_like(choice_ref)
+    choice_ref[:1, :faces] = lax.dot_general(
+        source.astype(F32).astype(BF16),
         order.astype(BF16),
-        one_hot(source, faces).astype(BF16),
         (((1,), (1,)), ((), ())),
         preferred_element_type=F32,
     )
-    gather_traces(padded_ref[...], aligned_ref, 0, side_a_ref)
-    gather_traces(padded_ref[...], aligned_ref, faces, side_b_ref)
-
-
-def message_kernel(first, packed_ref, chosen_ref, side_a_ref, side_b_ref, *refs):
-    faces = side_a_ref.shape[0]
-    *weight_refs, to_a_ref, to_b_ref = refs
+    for first, to_ref in ((0, to_a_ref), (faces, to_b_ref)):
+        gather_traces(padded_ref[...], aligned_ref, first, to_ref.at[:faces, :])
+        to_ref[faces : faces + SUBLANES, :] = choice_ref[...]
+    to_a_ref[faces + SUBLANES :, :] = jnp.zeros((SUBLANES, LANES), F32)
+
+
+def blocks_kernel(first, packed_ref, last_ref, *block_refs):
     slot = lax.axis_index("blk")
-    per_group = weight_refs[0].shape[1]
-    kept = pl.ds(pl.multiple_of(first + slot * per_group, SUBLANES), per_group)
-    held = jnp.concatenate(
-        [packed_ref[kept, :]] + [weight_ref[slot] for weight_ref in weight_refs], axis=0
-    )
-    own = exact_dot(chosen_ref[...], held)
-    to_a_ref[2 * faces :, :] = jnp.zeros_like(to_a_ref[2 * faces :, :])
-    for side_ref, to_ref in ((side_a_ref, to_a_ref), (side_b_ref, to_b_ref)):
-        to_ref[:faces, :] = side_ref[...]
-        to_ref[faces : 2 * faces, :] = own
+    per_group = last_ref.shape[1]
+    for place, block_ref in enumerate(block_refs):
+        k = slot ^ (len(block_refs) - place)
+        kept = pl.ds(pl.multiple_of(first + k * per_group, SUBLANES), per_group)
+        block_ref[:per_group, :] = packed_ref[kept, :]
+        block_ref[per_group:, :] = last_ref[k]
 
 
 def near_traces_kernel(aligned_ref, image_ref, side_b_ref):
@@ -212,36 +213,51 @@
     return total[:block_rows] + total[block_rows:]
 
 
-def near_kernel(size, aligned_ref, product_ref, to_ref, from_ref, partial_ref, weights_ref):
+def image_kernel(
+    size,
+    first,
+    packed_ref,
+    last_ref,
+    choice_ref,
+    aligned_ref,
+    product_ref,
+    to_a_ref,
+    to_b_ref,
+    from_a_ref,
+    from_b_ref,
+    *refs,
+):
+    *block_refs, image_ref, weights_a_ref, weights_b_ref, side_a_ref = refs
     block_rows = product_ref.shape[0]
-    faces = weights_ref.shape[0]
+    faces = weights_a_ref.shape[0]
+    per_group = last_ref.shape[1]
+    slot = lax.axis_index("blk")
     odd = lax.rem(lax.axis_index("sub"), 2) == 1
-    weights_ref[...] = jnp.where(odd, from_ref[faces:, :], to_ref[faces:, :])
-    partial_ref[...] = product_ref[...]
-    partial_ref[:, :size] = partial_ref[:, :size] + spread_jumps(
-        size, faces, aligned_ref, faces, weights_ref, to_ref, from_ref, block_rows
-    )
-
-
-def far_kernel(
-    size,
-    aligned_ref,
-    partial_ref,
-    to_ref,
-    from_ref,
-    image_ref,
-    weights_ref,
-    side_a_ref,
-):
-    block_rows = partial_ref.shape[0]
-    faces = weights_ref.shape[0]
-    odd = lax.rem(lax.axis_index("sub"), 2) == 1
-    weights_ref[...] = jnp.where(
-        odd, to_ref[faces : 2 * faces, :], from_ref[faces : 2 * faces, :]
-    )
-    image_ref[...] = partial_ref[...]
-    image_ref[:, :size] = image_ref[:, :size] + spread_jumps(
-        size, faces, aligned_ref, 0, weights_ref, to_ref, from_ref, block_rows
+    kept = pl.ds(pl.multiple_of(first + slot * per_group, SUBLANES), per_group)
+    place = slice(faces, faces + SUBLANES)
+    choice = jnp.where(odd, from_b_ref[place, :], from_a_ref[place, :])
+    own, last = (
+        lax.dot_general(
+            one_hot(row[:1, :faces].astype(jnp.int32), faces),
+            jnp.concatenate([block] + [block_ref[part, :] for block_ref in block_refs], axis=0),
+            (((0,), (0,)), ((), ())),
+            precision=lax.Precision.HIGHEST,
+            preferred_element_type=F32,
+        )
+        for row, block, part in (
+            (choice_ref[...], packed_ref[kept, :], slice(0, per_group)),
+            (choice, last_ref[slot], slice(per_group, 2 * per_group)),
+        )
+    )
+    weights_a_ref[...] = jnp.where(odd, own, last)
+    weights_b_ref[...] = jnp.where(odd, last, own)
+    image_ref[...] = product_ref[...]
+    image_ref[:, :size] = (
+        image_ref[:, :size]
+        + spread_jumps(size, faces, aligned_ref, 0, weights_a_ref, to_a_ref, from_a_ref, block_rows)
+        + spread_jumps(
+            size, faces, aligned_ref, faces, weights_b_ref, to_b_ref, from_b_ref, block_rows
+        )
     )
     gather_traces(image_ref[...], aligned_ref, 0, side_a_ref.at[:faces, :])
     side_a_ref[faces:, :] = jnp.zeros_like(side_a_ref[faces:, :])
@@ -346,6 +362,12 @@
     return lax.ppermute(value, "sub", pairs)
 
 
+def from_behind(value, axis, steps):
+    count = lax.axis_size(axis)
+    pairs = [(source, (source + steps) % count) for source in range(count)]
+    return lax.ppermute(value, axis, pairs)
+
+
 def swap_slots(value, k):
     count = lax.axis_size("blk")
     return lax.ppermute(value, "blk", [(slot, slot ^ k) for slot in range(count)])
@@ -366,7 +388,7 @@
     devices = lax.axis_size("sub") * lax.axis_size("blk")
 
     own_weights = mortar_weight[0, 0]
-    held = [swap_slots(own_weights, k) for k in range(1, own_weights.shape[0])]
+    last_weights = from_behind(own_weights, "sub", 1)
     last = 2 * faces + block_rows
 
     def placed(value, first):
@@ -379,24 +401,30 @@
         + placed(field, 2 * faces)
         + placed(own_weights.reshape(faces, LANES), last + SUBLANES)
     )
-    aligned, padded, chosen, side_a, side_b = call(
+    aligned, padded, choice, to_a, to_b = call(
         functools.partial(first_kernel, owners.shape[0]),
         [
             shape(2 * faces, jnp.int32),
             shape(block_rows),
-            jax.ShapeDtypeStruct((faces, faces), F32),
-            shape(faces),
-            shape(faces),
+            shape(SUBLANES),
+            shape(faces + 2 * SUBLANES),
+            shape(faces + SUBLANES),
         ],
         [(packed, VMEM)],
     )
-    to_a, to_b = call(
-        functools.partial(message_kernel, last + SUBLANES),
-        [shape(2 * faces + SUBLANES), shape(2 * faces)],
-        [(value, VMEM) for value in (packed, chosen, side_a, side_b, *held)],
-    )
+    from_a = swap(to_a, 1)
     from_b = swap(to_b, 0)
-    from_a = swap(to_a, 1)
+    slots, per_group, _ = own_weights.shape
+    blocks_to = call(
+        functools.partial(blocks_kernel, last + SUBLANES),
+        [shape(2 * per_group)] * (slots - 1),
+        [(packed, VMEM), (last_weights, VMEM)],
+        flops=1,
+        moved=1,
+    )
+    blocks_from = [
+        swap_slots(block, k) for k, block in zip(range(slots - 1, 0, -1), blocks_to)
+    ]
 
     def stiff(vector):
         (product,) = call(
@@ -407,17 +435,24 @@
         )
         return product
 
-    partial, weights_b = call(
-        functools.partial(near_kernel, size),
-        [shape(block_rows), shape(faces)],
-        [(value, VMEM) for value in (aligned, stiff(padded), to_b, from_b)],
-        flops=1,
-        moved=1,
-    )
-    image, weights_a, side_a = call(
-        functools.partial(far_kernel, size),
-        [shape(block_rows), shape(faces), shape(faces + SUBLANES)],
-        [(value, VMEM) for value in (aligned, partial, to_a, from_a)],
+    image, weights_a, weights_b, side_a = call(
+        functools.partial(image_kernel, size, last + SUBLANES),
+        [shape(block_rows), shape(faces), shape(faces), shape(faces + SUBLANES)],
+        [
+            (value, VMEM)
+            for value in (
+                packed,
+                last_weights,
+                choice,
+                aligned,
+                stiff(padded),
+                to_a,
+                to_b,
+                from_a,
+                from_b,
+                *blocks_from,
+            )
+        ],
     )
     from_a = swap(side_a, 1)
     (side_b,) = call(

time: 36.8 us -> 36.2 us (0.984)
  waiting for transfers between devices: 11.2 us -> 8.79 us
  starting transfers between devices: 13 us -> 14.9 us
    ppermute x0 -> x1, starting transfers between devices: none -> 3.02 us  [from_behind(): return lax.ppermute(value, axis, pairs)]
    ppermute x3, waiting for transfers between devices: 1.74 us -> 0.01 us  [swap_slots(): lax.ppermute(value, 'blk', [(slot, slot ^ k) for slot in range(count)])]
    ppermute x3, starting transfers between devices: 3.12 us -> 1.88 us  [swap_slots(): lax.ppermute(value, 'blk', [(slot, slot ^ k) for slot in range(count)])]
    ppermute x4, waiting for transfers between devices: 3.44 us -> 2.49 us  [swap(): return lax.ppermute(value, 'sub', pairs)]
    all_to_all x1, starting transfers between devices: 3.05 us -> 3.56 us  [on_device(): lax.all_to_all(sums, ('sub', 'blk'), split_axis=0, concat_axis=0, tiled=T...]
    pallas_call x11 -> x10, Pallas kernels: 8.4 us -> 8.26 us  [call(): pl.pallas_call(body, out_shape=outs, in_specs=[spec for _, spec in inputs...]
  transfers between devices with their start and end apart: 8 -> 9, of which waited for: 4 -> 3; matrix products, arithmetic and copies ran while one was open for 9% -> 9% of each run, Pallas kernels for 16% -> 14%
where the time goes in v13:
time: 36.2 us; the launch traced here: 36 us
  starting transfers between devices  14.9 us (41%)
  waiting for transfers between devices  8.79 us (24%)
  Pallas kernels  8.26 us (23%)
  local copies, waits for them, and re-layouts  2.3 us (6%)
  other arithmetic  0.92 us (3%)
  between operations  0.77 us (2%)
    pallas_call x10, Pallas kernels, call(): pl.pallas_call(body, out_shape=outs, in_specs=[spec for _, spec in inputs...  8.26 us
    ppermute x4, starting transfers between devices, swap(): return lax.ppermute(value, 'sub', pairs)  6.48 us
    all_to_all x1, waiting for transfers between devices, on_device(): lax.all_to_all(sums, ('sub', 'blk'), split_axis=0, concat_axis=0, tiled=T...  6.04 us
    all_to_all x1, starting transfers between devices, on_device(): lax.all_to_all(sums, ('sub', 'blk'), split_axis=0, concat_axis=0, tiled=T...  3.56 us
    ppermute x1, starting transfers between devices, from_behind(): return lax.ppermute(value, axis, pairs)  3.02 us
    ppermute x4, waiting for transfers between devices, swap(): return lax.ppermute(value, 'sub', pairs)  2.49 us
    another operation x1, local copies, waits for them, and re-layouts, on_device(): blocks = stored.reshape(stored.shape[0], size, size)  2.29 us
    ppermute x3, starting transfers between devices, swap_slots(): lax.ppermute(value, 'blk', [(slot, slot ^ k) for slot in range(count)])  1.88 us
  transfers between devices with their start and end apart: 9, of which 3 were waited for; matrix products, arithmetic and copies ran while one was open for 9% of the time, Pallas kernels for 14%

profile of v13, /device:TPU:0, one launch (start us, length us, event | category | flops | bytes accessed | tf_op | source)
XLA Modules:
  0.0 36.0 jit_solution(1397289986748442643)
XLA Ops:
  0.6 3.0 %collective-permute-start = (f32[4,16,128]{2,1,0:T(8,128)}, f32[4,16,128]{2,1,0:T(8,128)S(1)}, u32[]{:S(2)}, u32[]{:S(2)}) collective-permute-start(f32[4,16,128]{2,1,0:T(8,128)} %bitcast.20), channel_id=1, source_target_pairs={{0,4},{4,8},{8,12},{12,16},{16,20},{20,24},{24,28},{28,0},{1,5},{5... | collective-permute-start | bytes 98312 | tf_op jit(solution)/shard_map/ppermute | solution.py:368
  3.7 0.9 %pad_add_fusion.packed_ref = f32[232,128]{1,0:T(8,128)S(1)} fusion(f32[64,128]{1,0:T(8,128)} %bitcast.21, f32[32,96]{1,0:T(8,128)} %bitcast.22, s32[1,4]{1,0:T(1,128)} %bitcast.23, s32[1,64]{1,0:T(1,128)} %bitcast.24, s32[128,128]{1,0:T(8,128)} %bitcast.19), kind=kLoop, calls=%fused_computation | loop fusion | flops 148480 | bytes 229648 | tf_op jit(solution)/shard_map/add | solution.py:400
  4.6 0.0 copy-start
  4.6 0.8 %shard_map.86 = (s32[128,128]{1,0:T(8,128)S(1)}, f32[32,128]{1,0:T(8,128)S(1)}, f32[8,128]{1,0:T(8,128)S(1)}, f32[80,128]{1,0:T(8,128)S(1)}, f32[72,128]{1,0:T(8,128)S(1)}) custom-call(f32[232,128]{1,0:T(8,128)S(1)} %pad_add_fusion.packed_ref), custom_call_target="tpu_custom_call" | custom-call | flops 1000000 | bytes 1000000 | tf_op jit(solution)/shard_map/pallas_call | solution.py:19
  5.4 3.1 %collective-permute-start.1 = (f32[80,128]{1,0:T(8,128)S(1)}, f32[80,128]{1,0:T(8,128)S(1)}, u32[]{:S(2)}, u32[]{:S(2)}) collective-permute-start(f32[80,128]{1,0:T(8,128)S(1)} %get-tuple-element.19.to_a_ref.first_ref), channel_id=1, source_target_pairs={{4,8},{8,4},{12,16},{16,12},{20,24},{24,20},{28,0},{0,28},{5,9},{9... | collective-permute-start | bytes 122888 | tf_op jit(solution)/shard_map/ppermute | solution.py:362
  8.5 0.2 collective-permute-done.last_ref
  8.8 0.5 %collective-permute-start.3 = (f32[32,128]{1,0:T(8,128)S(1)}, f32[32,128]{1,0:T(8,128)S(1)}, u32[]{:S(2)}, u32[]{:S(2)}) collective-permute-start(f32[32,128]{1,0:T(8,128)S(1)} %get-tuple-element.21), channel_id=1, source_target_pairs={{0,3},{1,2},{2,1},{3,0},{4,7},{5,6},{6,5},{7,4},{8,11},{9,10},{10,... | collective-permute-start | bytes 49160 | tf_op jit(solution)/shard_map/ppermute | solution.py:373
  9.3 1.2 %collective-permute-start.4 = (f32[32,128]{1,0:T(8,128)S(1)}, f32[32,128]{1,0:T(8,128)S(1)}, u32[]{:S(2)}, u32[]{:S(2)}) collective-permute-start(f32[32,128]{1,0:T(8,128)S(1)} %get-tuple-element.22), channel_id=1, source_target_pairs={{0,2},{1,3},{2,0},{3,1},{4,6},{5,7},{6,4},{7,5},{8,10},{9,11},{10,... | collective-permute-start | bytes 49160 | tf_op jit(solution)/shard_map/ppermute | solution.py:373
  10.5 0.2 collective-permute-start.5
  10.7 2.3 %reshape_squeeze.7.blocks_ref = bf16[48,96,96]{2,1,0:T(8,128)(2,1)S(1)} reshape(bf16[1,1,48,9216]{3,2,1,0:T(8,128)(2,1)} %param.8) | data formatting | bytes 1769472 | tf_op jit(solution)/shard_map/reshape;squeeze | solution.py:382
  13.0 1.4 %shard_map.87.product_ref = f32[32,128]{1,0:T(8,128)S(1)} custom-call(s32[2,16]{1,0:T(2,128)S(1)} %bitcast.17, bf16[48,96,96]{2,1,0:T(8,128)(2,1)S(1)} %reshape_squeeze.7.blocks_ref, f32[32,128]{1,0:T(8,128)S(1)} %get-tuple-element.16.field_ref), custom_call_target="tpu_custom_call" | custom-call | flops 1000000 | bytes 1000000 | tf_op jit(solution)/shard_map/pallas_call | solution.py:19
  14.4 0.0 collective-permute-done.2.from_b_ref
  14.4 0.0 collective-permute-done.4.refs_1_
  14.5 1.7 %shard_map.89 = (f32[32,128]{1,0:T(8,128)S(1)}, f32[64,128]{1,0:T(8,128)S(1)}, f32[64,128]{1,0:T(8,128)S(1)}, f32[72,128]{1,0:T(8,128)S(1)}) custom-call(f32[232,128]{1,0:T(8,128)S(1)} %pad_add_fusion.packed_ref, f32[4,16,128]{2,1,0:T(8,128)S(1)} %collective-permute-done.last_ref, f32[8,128]{1,0:T(8,128)S(1)} %get-tuple-element.17.choice_ref, ...), custom_call_target="tpu_custom_call" | custom-call | flops 1000000 | bytes 1000000 | tf_op jit(solution)/shard_map/pallas_call | solution.py:19
  16.2 3.3 %collective-permute-start.6 = (f32[72,128]{1,0:T(8,128)S(1)}, f32[72,128]{1,0:T(8,128)S(1)}, u32[]{:S(2)}, u32[]{:S(2)}) collective-permute-start(f32[72,128]{1,0:T(8,128)S(1)} %get-tuple-element.27.side_a_ref.own_ref), channel_id=1, source_target_pairs={{4,8},{8,4},{12,16},{16,12},{20,24},{24,20},{28,0},{0,28},{5,9},{9... | collective-permute-start | bytes 110600 | tf_op jit(solution)/shard_map/ppermute | solution.py:362
  19.5 0.4 shard_map.91.side_b_ref.own_ref
  19.8 0.1 collective-permute-start.7
  19.9 1.4 %shard_map.90.product_ref = f32[32,128]{1,0:T(8,128)S(1)} custom-call(s32[2,16]{1,0:T(2,128)S(1)} %bitcast.18, bf16[48,96,96]{2,1,0:T(8,128)(2,1)S(1)} %reshape_squeeze.7.blocks_ref, f32[32,128]{1,0:T(8,128)S(1)} %get-tuple-element.24.field_ref.image_ref), custom_call_target="tpu_custom_call" | custom-call | flops 1000000 | bytes 1000000 | tf_op jit(solution)/shard_map/pallas_call | solution.py:19
  21.3 2.5 %collective-permute-done.7.from_b_ref.arrived_ref = f32[64,128]{1,0:T(8,128)S(1)} collective-permute-done((f32[64,128]{1,0:T(8,128)S(1)}, f32[64,128]{1,0:T(8,128)S(1)}, u32[]{:S(2)}, u32[]{:S(2)}) %collective-permute-start.7) | collective-permute-done | bytes 32800 | tf_op jit(solution)/shard_map/ppermute | solution.py:362
  23.9 0.7 %shard_map.94 = f32[32,1,128]{2,1,0:T(1,128)} custom-call(f32[8,128]{1,0:T(8,128)S(1)} %shard_map.93.rows_ref, f32[64,128]{1,0:T(8,128)S(1)} %get-tuple-element.25.weights_a_ref.weights_ref, f32[72,128]{1,0:T(8,128)S(1)} %get-tuple-element.27.side_a_ref.own_ref, f32[72,128]{1,0:T(8,128)S(1)} %collective-permute-done.6.from_a_ref.arrived_ref, ...), custom_call_target="tpu_custom_call" | custom-call | flops 1000000 | bytes 1000000 | tf_op jit(solution)/shard_map/pallas_call | solution.py:19
  24.6 3.6 %all-to-all-start = ((f32[32,1,128]{2,1,0:T(1,128)}), f32[32,1,128]{2,1,0:T(1,128)S(1)}, u32[]{:S(2)}, u32[]{:S(2)}) async-start(f32[32,1,128]{2,1,0:T(1,128)} %shard_map.94), calls=%async_computation | async-start | bytes 32768 | tf_op jit(solution)/shard_map/all_to_all | solution.py:486
  28.2 1.0 %shard_map.92.second_ref = f32[32,128]{1,0:T(8,128)S(1)} custom-call(s32[128,128]{1,0:T(8,128)S(1)} %get-tuple-element.18.aligned_ref, f32[32,128]{1,0:T(8,128)S(1)} %shard_map.90.product_ref, f32[64,128]{1,0:T(8,128)S(1)} %get-tuple-element.25.weights_a_ref.weights_ref, f32[64,128]{1,0:T(8,128)S(1)} %get-tuple-element.26.weights_b_ref.weights_ref, ...), custom_call_target="tpu_custom_call" | custom-call | flops 1000000000 | bytes 1000000 | tf_op jit(solution)/shard_map/pallas_call | solution.py:19
  29.2 6.0 %all-to-all-done.sums_ref = f32[32,1,128]{2,1,0:T(1,128)S(1)} async-done(((f32[32,1,128]{2,1,0:T(1,128)}), f32[32,1,128]{2,1,0:T(1,128)S(1)}, u32[]{:S(2)}, u32[]{:S(2)}) %all-to-all-start) | async-done | bytes 16416 | tf_op jit(solution)/shard_map/all_to_all | solution.py:486
  35.2 0.7 %shard_map.95 = (f32[32,96]{1,0:T(8,128)}, f32[32,96]{1,0:T(8,128)}) custom-call(f32[32,128]{1,0:T(8,128)S(1)} %get-tuple-element.16.field_ref, f32[32,128]{1,0:T(8,128)S(1)} %get-tuple-element.24.field_ref.image_ref, f32[32,128]{1,0:T(8,128)S(1)} %shard_map.92.second_ref, f32[32,1,128]{2,1,0:T(1,128)S(1)} %all-to-all-done.sums_ref), custom_call_target="tpu_custom_call" | custom-call | flops 1000000 | bytes 1000000 | tf_op jit(solution)/shard_map/pallas_call | solution.py:19
  (8 shorter events, 0.0 us)
Async XLA Ops:
  0.6 8.2 %collective-permute-start = (f32[4,16,128]{2,1,0:T(8,128)}, f32[4,16,128]{2,1,0:T(8,128)S(1)}, u32[]{:S(2)}, u32[]{:S(2)}) collective-permute-start(f32[4,16,128]{2,1,0:T(8,128)} %bitcast.20), channel_id=1, source_target_pairs={{0,4},{4,8},{8,12},{12,16},{16,20},{20,24},{24,28},{28,0},{1,5},{5... | collective-permute-start | bytes 98312 | tf_op jit(solution)/shard_map/ppermute | solution.py:368
  4.6 8.4 %copy-start = (s32[1,1,2,16]{3,2,1,0:T(2,128)S(1)}, s32[1,1,2,16]{3,2,1,0:T(2,128)}, u32[]{:S(2)}) copy-start(s32[1,1,2,16]{3,2,1,0:T(2,128)} %param.9) | copy-start | bytes 388
  5.4 9.0 %collective-permute-start.1 = (f32[80,128]{1,0:T(8,128)S(1)}, f32[80,128]{1,0:T(8,128)S(1)}, u32[]{:S(2)}, u32[]{:S(2)}) collective-permute-start(f32[80,128]{1,0:T(8,128)S(1)} %get-tuple-element.19.to_a_ref.first_ref), channel_id=1, source_target_pairs={{4,8},{8,4},{12,16},{16,12},{20,24},{24,20},{28,0},{0,28},{5,9},{9... | collective-permute-start | bytes 122888 | tf_op jit(solution)/shard_map/ppermute | solution.py:362
  8.5 5.9 %collective-permute-start.2 = (f32[72,128]{1,0:T(8,128)S(1)}, f32[72,128]{1,0:T(8,128)S(1)}, u32[]{:S(2)}, u32[]{:S(2)}) collective-permute-start(f32[72,128]{1,0:T(8,128)S(1)} %get-tuple-element.20.to_b_ref.first_ref), channel_id=1, source_target_pairs={{0,4},{4,0},{8,12},{12,8},{16,20},{20,16},{24,28},{28,24},{1,5},{5... | collective-permute-start | bytes 110600 | tf_op jit(solution)/shard_map/ppermute | solution.py:362
  8.8 5.6 %collective-permute-start.3 = (f32[32,128]{1,0:T(8,128)S(1)}, f32[32,128]{1,0:T(8,128)S(1)}, u32[]{:S(2)}, u32[]{:S(2)}) collective-permute-start(f32[32,128]{1,0:T(8,128)S(1)} %get-tuple-element.21), channel_id=1, source_target_pairs={{0,3},{1,2},{2,1},{3,0},{4,7},{5,6},{6,5},{7,4},{8,11},{9,10},{10,... | collective-permute-start | bytes 49160 | tf_op jit(solution)/shard_map/ppermute | solution.py:373
  9.3 5.2 %collective-permute-start.4 = (f32[32,128]{1,0:T(8,128)S(1)}, f32[32,128]{1,0:T(8,128)S(1)}, u32[]{:S(2)}, u32[]{:S(2)}) collective-permute-start(f32[32,128]{1,0:T(8,128)S(1)} %get-tuple-element.22), channel_id=1, source_target_pairs={{0,2},{1,3},{2,0},{3,1},{4,6},{5,7},{6,4},{7,5},{8,10},{9,11},{10,... | collective-permute-start | bytes 49160 | tf_op jit(solution)/shard_map/ppermute | solution.py:373
  10.5 3.9 %collective-permute-start.5 = (f32[32,128]{1,0:T(8,128)S(1)}, f32[32,128]{1,0:T(8,128)S(1)}, u32[]{:S(2)}, u32[]{:S(2)}) collective-permute-start(f32[32,128]{1,0:T(8,128)S(1)} %get-tuple-element.23), channel_id=1, source_target_pairs={{0,1},{1,0},{2,3},{3,2},{4,5},{5,4},{6,7},{7,6},{8,9},{9,8},{10,11... | collective-permute-start | bytes 49160 | tf_op jit(solution)/shard_map/ppermute | solution.py:373
  16.2 7.7 %collective-permute-start.6 = (f32[72,128]{1,0:T(8,128)S(1)}, f32[72,128]{1,0:T(8,128)S(1)}, u32[]{:S(2)}, u32[]{:S(2)}) collective-permute-start(f32[72,128]{1,0:T(8,128)S(1)} %get-tuple-element.27.side_a_ref.own_ref), channel_id=1, source_target_pairs={{4,8},{8,4},{12,16},{16,12},{20,24},{24,20},{28,0},{0,28},{5,9},{9... | collective-permute-start | bytes 110600 | tf_op jit(solution)/shard_map/ppermute | solution.py:362
  19.8 4.0 %collective-permute-start.7 = (f32[64,128]{1,0:T(8,128)S(1)}, f32[64,128]{1,0:T(8,128)S(1)}, u32[]{:S(2)}, u32[]{:S(2)}) collective-permute-start(f32[64,128]{1,0:T(8,128)S(1)} %shard_map.91.side_b_ref.own_ref), channel_id=1, source_target_pairs={{0,4},{4,0},{8,12},{12,8},{16,20},{20,16},{24,28},{28,24},{1,5},{5... | collective-permute-start | bytes 98312 | tf_op jit(solution)/shard_map/ppermute | solution.py:362
  24.6 10.6 %all-to-all-start = ((f32[32,1,128]{2,1,0:T(1,128)}), f32[32,1,128]{2,1,0:T(1,128)S(1)}, u32[]{:S(2)}, u32[]{:S(2)}) async-start(f32[32,1,128]{2,1,0:T(1,128)} %shard_map.94), calls=%async_computation | async-start | bytes 32768 | tf_op jit(solution)/shard_map/all_to_all | solution.py:486

commit v14 on v13

--- a/solution.py
+++ b/solution.py
@@ -1,4 +1,5 @@
 import functools
+import math
 
 import jax
 import jax.numpy as jnp
@@ -10,7 +11,6 @@
 LANES = 128
 SUBLANES = 8
 VMEM = pl.BlockSpec(memory_space=pltpu.VMEM)
-SMEM = pl.BlockSpec(memory_space=pltpu.SMEM)
 F32 = jnp.float32
 BF16 = jnp.bfloat16
 
@@ -132,40 +132,71 @@
     gather_traces(image_ref[...], aligned_ref, side_b_ref.shape[0], side_b_ref)
 
 
-def stiffness_kernel(pairs_ref, blocks_ref, field_ref, out_ref, pieces, sums):
+def stiffness_kernel(size, pairs_ref, blocks_ref, field_ref, out_ref):
     block_rows = field_ref.shape[0]
-    size = blocks_ref.shape[1]
     count = pairs_ref.shape[1]
-    high, low = halves(field_ref[...])
-    pieces[...] = jnp.zeros_like(pieces)
-    pieces[pl.ds(0, block_rows, stride=SUBLANES), :] = high
-    pieces[pl.ds(1, block_rows, stride=SUBLANES), :] = low
-
-    def times(row, block, contract):
-        left = pieces[pl.ds(pl.multiple_of(row * SUBLANES, SUBLANES), SUBLANES), :]
-        return lax.dot_general(
-            left[:, :size].astype(BF16),
-            block,
-            (((1,), (contract,)), ((), ())),
+    rows = block_rows + count
+    width = math.lcm(size, LANES)
+    tiles = width // LANES
+    segments = width // size
+    groups = size // segments
+    batch = next(k for k in (4, 3, 2, 1) if groups % k == 0)
+
+    def place(position):
+        segment = sum(jnp.where(position >= k * size, 1, 0) for k in range(1, segments))
+        return segment, position - segment * size
+
+    def lanes_of(value, index):
+        slabs = [
+            jnp.take_along_axis(
+                value[k : k + SUBLANES, :], index, axis=1, mode="promise_in_bounds"
+            )
+            for k in range(0, value.shape[0], SUBLANES)
+        ]
+        return jnp.concatenate(slabs, axis=0)
+
+    field = field_ref[...]
+    first_of, other_of = (one_hot(pairs_ref[k : k + 1, :], block_rows) for k in (0, 1))
+    left, other = (
+        lax.dot_general(
+            ends,
+            field,
+            (((0,), (0,)), ((), ())),
+            precision=lax.Precision.HIGHEST,
             preferred_element_type=F32,
         )
-
-    def add(row, value):
-        place = pl.ds(pl.multiple_of(row * SUBLANES, SUBLANES), SUBLANES)
-        sums[place, :size] = sums[place, :size] + value
-
-    sums[...] = jnp.zeros_like(sums)
-    for i in range(block_rows):
-        sums[i * SUBLANES : (i + 1) * SUBLANES, :size] = times(i, blocks_ref[i], 1)
-    for p in range(count):
-        first = pairs_ref[0, p]
-        other = pairs_ref[1, p]
-        block = blocks_ref[block_rows + p]
-        add(first, times(other, block, 1))
-        add(other, times(first, block, 0))
+        for ends in (first_of, other_of)
+    )
+    right = jnp.concatenate([field, other], axis=0)
+    lane = lax.broadcasted_iota(jnp.int32, (SUBLANES, LANES), 1)
+    places = [place(lane + t * LANES) for t in range(tiles)]
+    repeated = jnp.concatenate([lanes_of(right, inside) for _, inside in places], axis=1)
+    segment, inside = place(lax.broadcasted_iota(jnp.int32, (width, LANES), 0))
+    column = lax.broadcasted_iota(jnp.int32, (width, LANES), 1)
+    add_segments = jnp.where(segment == column % segments, 1.0, 0.0).astype(BF16)
+    fold = jnp.where(inside == column, 1.0, 0.0)
+    dof_group = lax.broadcasted_iota(jnp.int32, (rows, LANES), 1) // segments
+    total = jnp.zeros((rows, LANES), F32)
+    turned = jnp.zeros((count, width), F32)
+    for base in range(0, groups, batch):
+        stack = []
+        for g in range(base, base + batch):
+            stored = blocks_ref[:, g * width : (g + 1) * width]
+            product = stored * repeated
+            high = product.astype(BF16)
+            stack += [high, (product - high.astype(F32)).astype(BF16)]
+            spread = [lanes_of(left, g * segments + segment) for segment, _ in places]
+            turned = turned + stored[block_rows:] * jnp.concatenate(spread, axis=1)
+        sums = jnp.dot(
+            jnp.concatenate(stack, axis=0), add_segments, preferred_element_type=F32
+        )
+        for n in range(batch):
+            both = sums[2 * n * rows : 2 * (n + 1) * rows]
+            total = jnp.where(dof_group == base + n, both[:rows] + both[rows:], total)
     out_ref[...] = (
-        sums[pl.ds(0, block_rows, stride=SUBLANES), :]
-        + sums[pl.ds(1, block_rows, stride=SUBLANES), :]
+        total[:block_rows]
+        + exact_dot(first_of, total[block_rows:])
+        + exact_dot(other_of, exact_dot(turned, fold))
     )
 
 
@@ -378,8 +409,7 @@
 ):
     field = right_side[0, 0].T
     block_rows, size = field.shape
-    stored = stiffness[0, 0]
-    blocks = stored.reshape(stored.shape[0], size, size)
+    blocks = stiffness[0, 0].astype(F32)
     pairs = block_pairs[0, 0]
     rows = trace_rows[0, 0]
     partner = partner_face[0, 0]
@@ -428,10 +458,9 @@
 
     def stiff(vector):
         (product,) = call(
-            stiffness_kernel,
+            functools.partial(stiffness_kernel, size),
             [shape(block_rows)],
-            [(pairs, SMEM), (blocks, VMEM), (vector, VMEM)],
-            scratch=[pltpu.VMEM((block_rows * SUBLANES, LANES), F32)] * 2,
+            [(pairs, VMEM), (blocks, VMEM), (vector, VMEM)],
         )
         return product
 

time: 36.2 us -> 36.2 us (level)
  local copies, waits for them, and re-layouts: 2.3 us -> 0.01 us
  other arithmetic: 0.92 us -> 2.2 us
  starting transfers between devices: 14.9 us -> 15.9 us
    another operation x1 -> x0, local copies, waits for them, and re-layouts: 2.29 us -> none  [on_device(): blocks = stored.reshape(stored.shape[0], size, size)]
    convert_element_type x0 -> x1, other arithmetic: none -> 1.28 us  [on_device(): blocks = stiffness[0, 0].astype(F32)]
    ppermute x4, starting transfers between devices: 6.48 us -> 7.28 us  [swap(): return lax.ppermute(value, 'sub', pairs)]
    ppermute x4, waiting for transfers between devices: 2.49 us -> 2.89 us  [swap(): return lax.ppermute(value, 'sub', pairs)]
  transfers between devices with their start and end apart: 9 -> 9, of which waited for: 3 -> 3; matrix products, arithmetic and copies ran while one was open for 9% -> 6% of each run, Pallas kernels for 14% -> 14%
where the time goes in v14:
time: 36.2 us; the launch traced here: 36 us
  starting transfers between devices  15.9 us (44%)
  waiting for transfers between devices  8.94 us (25%)
  Pallas kernels  8.26 us (23%)
  other arithmetic  2.2 us (6%)
  between operations  0.74 us (2%)
    pallas_call x10, Pallas kernels, call(): pl.pallas_call(body, out_shape=outs, in_specs=[spec for _, spec in inputs...  8.26 us
    ppermute x4, starting transfers between devices, swap(): return lax.ppermute(value, 'sub', pairs)  7.28 us
    all_to_all x1, waiting for transfers between devices, on_device(): lax.all_to_all(sums, ('sub', 'blk'), split_axis=0, concat_axis=0, tiled=T...  6.04 us
    all_to_all x1, starting transfers between devices, on_device(): lax.all_to_all(sums, ('sub', 'blk'), split_axis=0, concat_axis=0, tiled=T...  3.64 us
    ppermute x1, starting transfers between devices, from_behind(): return lax.ppermute(value, axis, pairs)  3.02 us
    ppermute x4, waiting for transfers between devices, swap(): return lax.ppermute(value, 'sub', pairs)  2.89 us
    ppermute x3, starting transfers between devices, swap_slots(): lax.ppermute(value, 'blk', [(slot, slot ^ k) for slot in range(count)])  1.92 us
    convert_element_type x1, other arithmetic, on_device(): blocks = stiffness[0, 0].astype(F32)  1.28 us
  transfers between devices with their start and end apart: 9, of which 3 were waited for; matrix products, arithmetic and copies ran while one was open for 6% of the time, Pallas kernels for 14%

profile of v14, /device:TPU:0, one launch (start us, length us, event | category | flops | bytes accessed | tf_op | source)
XLA Modules:
  0.0 36.0 jit_solution(13876338893417749784)
XLA Ops:
  0.6 3.0 %collective-permute-start = (f32[4,16,128]{2,1,0:T(8,128)}, f32[4,16,128]{2,1,0:T(8,128)S(1)}, u32[]{:S(2)}, u32[]{:S(2)}) collective-permute-start(f32[4,16,128]{2,1,0:T(8,128)} %bitcast.21), channel_id=1, source_target_pairs={{0,4},{4,8},{8,12},{12,16},{16,20},{20,24},{24,28},{28,0},{1,5},{5... | collective-permute-start | bytes 98312 | tf_op jit(solution)/shard_map/ppermute | solution.py:399
  3.7 0.9 %pad_add_fusion.packed_ref = f32[232,128]{1,0:T(8,128)S(1)} fusion(f32[64,128]{1,0:T(8,128)} %bitcast.22, f32[32,96]{1,0:T(8,128)} %bitcast.23, s32[1,4]{1,0:T(1,128)} %bitcast.24, s32[1,64]{1,0:T(1,128)} %bitcast.25, s32[128,128]{1,0:T(8,128)} %bitcast.20), kind=kLoop, calls=%fused_computation.1 | loop fusion | flops 148480 | bytes 229648 | tf_op jit(solution)/shard_map/add | solution.py:430
  4.6 0.8 %shard_map.86 = (s32[128,128]{1,0:T(8,128)S(1)}, f32[32,128]{1,0:T(8,128)S(1)}, f32[8,128]{1,0:T(8,128)S(1)}, f32[80,128]{1,0:T(8,128)S(1)}, f32[72,128]{1,0:T(8,128)S(1)}) custom-call(f32[232,128]{1,0:T(8,128)S(1)} %pad_add_fusion.packed_ref), custom_call_target="tpu_custom_call" | custom-call | flops 1000000 | bytes 1000000 | tf_op jit(solution)/shard_map/pallas_call | solution.py:19
  5.4 1.6 %collective-permute-start.2 = (f32[72,128]{1,0:T(8,128)S(1)}, f32[72,128]{1,0:T(8,128)S(1)}, u32[]{:S(2)}, u32[]{:S(2)}) collective-permute-start(f32[72,128]{1,0:T(8,128)S(1)} %get-tuple-element.20.to_b_ref.first_ref), channel_id=1, source_target_pairs={{0,4},{4,0},{8,12},{12,8},{16,20},{20,16},{24,28},{28,24},{1,5},{5... | collective-permute-start | bytes 110600 | tf_op jit(solution)/shard_map/ppermute | solution.py:393
  7.0 3.5 %collective-permute-start.1 = (f32[80,128]{1,0:T(8,128)S(1)}, f32[80,128]{1,0:T(8,128)S(1)}, u32[]{:S(2)}, u32[]{:S(2)}) collective-permute-start(f32[80,128]{1,0:T(8,128)S(1)} %get-tuple-element.19.to_a_ref.first_ref), channel_id=1, source_target_pairs={{4,8},{8,4},{12,16},{16,12},{20,24},{24,20},{28,0},{0,28},{5,9},{9... | collective-permute-start | bytes 122888 | tf_op jit(solution)/shard_map/ppermute | solution.py:393
  10.6 0.0 collective-permute-done.last_ref
  10.6 0.1 collective-permute-start.3
  10.7 1.5 %collective-permute-start.4 = (f32[32,128]{1,0:T(8,128)S(1)}, f32[32,128]{1,0:T(8,128)S(1)}, u32[]{:S(2)}, u32[]{:S(2)}) collective-permute-start(f32[32,128]{1,0:T(8,128)S(1)} %get-tuple-element.22), channel_id=1, source_target_pairs={{0,2},{1,3},{2,0},{3,1},{4,6},{5,7},{6,4},{7,5},{8,10},{9,11},{10,... | collective-permute-start | bytes 49160 | tf_op jit(solution)/shard_map/ppermute | solution.py:404
  12.2 0.3 collective-permute-start.5
  12.5 1.3 %bitcast_convert_fusion.blocks_ref = f32[48,9216]{1,0:T(8,128)S(1)} fusion(bf16[1,1,48,9216]{3,2,1,0:T(8,128)(2,1)} %param.8), kind=kLoop, calls=%fused_computation | loop fusion | flops 442368 | bytes 2654208 | tf_op jit(solution)/shard_map/convert_element_type | solution.py:412
  13.8 1.4 %shard_map.87.product_ref = f32[32,128]{1,0:T(8,128)S(1)} custom-call(s32[2,16]{1,0:T(2,128)S(1)} %bitcast.18, f32[48,9216]{1,0:T(8,128)S(1)} %bitcast_convert_fusion.blocks_ref, f32[32,128]{1,0:T(8,128)S(1)} %get-tuple-element.16.field_ref), custom_call_target="tpu_custom_call" | custom-call | flops 1000000 | bytes 1000000 | tf_op jit(solution)/shard_map/pallas_call | solution.py:19
  15.2 0.0 collective-permute-done.1.from_a_ref
  15.2 1.7 %shard_map.89 = (f32[32,128]{1,0:T(8,128)S(1)}, f32[64,128]{1,0:T(8,128)S(1)}, f32[64,128]{1,0:T(8,128)S(1)}, f32[72,128]{1,0:T(8,128)S(1)}) custom-call(f32[232,128]{1,0:T(8,128)S(1)} %pad_add_fusion.packed_ref, f32[4,16,128]{2,1,0:T(8,128)S(1)} %collective-permute-done.last_ref, f32[8,128]{1,0:T(8,128)S(1)} %get-tuple-element.17.choice_ref, ...), custom_call_target="tpu_custom_call" | custom-call | flops 1000000 | bytes 1000000 | tf_op jit(solution)/shard_map/pallas_call | solution.py:19
  17.0 2.1 %collective-permute-start.6 = (f32[72,128]{1,0:T(8,128)S(1)}, f32[72,128]{1,0:T(8,128)S(1)}, u32[]{:S(2)}, u32[]{:S(2)}) collective-permute-start(f32[72,128]{1,0:T(8,128)S(1)} %get-tuple-element.27.side_a_ref.own_ref), channel_id=1, source_target_pairs={{4,8},{8,4},{12,16},{16,12},{20,24},{24,20},{28,0},{0,28},{5,9},{9... | collective-permute-start | bytes 110600 | tf_op jit(solution)/shard_map/ppermute | solution.py:393
  19.1 0.4 shard_map.91.side_b_ref.own_ref
  19.4 0.1 collective-permute-start.7
  19.5 1.4 %shard_map.90.product_ref = f32[32,128]{1,0:T(8,128)S(1)} custom-call(s32[2,16]{1,0:T(2,128)S(1)} %bitcast.19, f32[48,9216]{1,0:T(8,128)S(1)} %bitcast_convert_fusion.blocks_ref, f32[32,128]{1,0:T(8,128)S(1)} %get-tuple-element.24.field_ref.image_ref), custom_call_target="tpu_custom_call" | custom-call | flops 1000000 | bytes 1000000 | tf_op jit(solution)/shard_map/pallas_call | solution.py:19
  20.9 2.5 %collective-permute-done.7.from_b_ref.arrived_ref = f32[64,128]{1,0:T(8,128)S(1)} collective-permute-done((f32[64,128]{1,0:T(8,128)S(1)}, f32[64,128]{1,0:T(8,128)S(1)}, u32[]{:S(2)}, u32[]{:S(2)}) %collective-permute-start.7) | collective-permute-done | bytes 32800 | tf_op jit(solution)/shard_map/ppermute | solution.py:393
  23.5 0.4 collective-permute-done.6.from_a_ref.arrived_ref
  23.8 0.7 %shard_map.94 = f32[32,1,128]{2,1,0:T(1,128)} custom-call(f32[8,128]{1,0:T(8,128)S(1)} %shard_map.93.rows_ref, f32[64,128]{1,0:T(8,128)S(1)} %get-tuple-element.25.weights_a_ref.weights_ref, f32[72,128]{1,0:T(8,128)S(1)} %get-tuple-element.27.side_a_ref.own_ref, f32[72,128]{1,0:T(8,128)S(1)} %collective-permute-done.6.from_a_ref.arrived_ref, ...), custom_call_target="tpu_custom_call" | custom-call | flops 1000000 | bytes 1000000 | tf_op jit(solution)/shard_map/pallas_call | solution.py:19
  24.5 3.6 %all-to-all-start = ((f32[32,1,128]{2,1,0:T(1,128)}), f32[32,1,128]{2,1,0:T(1,128)S(1)}, u32[]{:S(2)}, u32[]{:S(2)}) async-start(f32[32,1,128]{2,1,0:T(1,128)} %shard_map.94), calls=%async_computation | async-start | bytes 32768 | tf_op jit(solution)/shard_map/all_to_all | solution.py:515
  28.2 1.0 %shard_map.92.second_ref = f32[32,128]{1,0:T(8,128)S(1)} custom-call(s32[128,128]{1,0:T(8,128)S(1)} %get-tuple-element.18.aligned_ref, f32[32,128]{1,0:T(8,128)S(1)} %shard_map.90.product_ref, f32[64,128]{1,0:T(8,128)S(1)} %get-tuple-element.25.weights_a_ref.weights_ref, f32[64,128]{1,0:T(8,128)S(1)} %get-tuple-element.26.weights_b_ref.weights_ref, ...), custom_call_target="tpu_custom_call" | custom-call | flops 1000000000 | bytes 1000000 | tf_op jit(solution)/shard_map/pallas_call | solution.py:19
  29.2 6.0 %all-to-all-done.sums_ref = f32[32,1,128]{2,1,0:T(1,128)S(1)} async-done(((f32[32,1,128]{2,1,0:T(1,128)}), f32[32,1,128]{2,1,0:T(1,128)S(1)}, u32[]{:S(2)}, u32[]{:S(2)}) %all-to-all-start) | async-done | bytes 16416 | tf_op jit(solution)/shard_map/all_to_all | solution.py:515
  35.3 0.7 %shard_map.95 = (f32[32,96]{1,0:T(8,128)}, f32[32,96]{1,0:T(8,128)}) custom-call(f32[32,128]{1,0:T(8,128)S(1)} %get-tuple-element.16.field_ref, f32[32,128]{1,0:T(8,128)S(1)} %get-tuple-element.24.field_ref.image_ref, f32[32,128]{1,0:T(8,128)S(1)} %shard_map.92.second_ref, f32[32,1,128]{2,1,0:T(1,128)S(1)} %all-to-all-done.sums_ref), custom_call_target="tpu_custom_call" | custom-call | flops 1000000 | bytes 1000000 | tf_op jit(solution)/shard_map/pallas_call | solution.py:19
  (8 shorter events, 0.0 us)
Async XLA Ops:
  0.6 13.1 %copy-start = (s32[1,1,2,16]{3,2,1,0:T(2,128)S(1)}, s32[1,1,2,16]{3,2,1,0:T(2,128)}, u32[]{:S(2)}) copy-start(s32[1,1,2,16]{3,2,1,0:T(2,128)} %param.9) | copy-start | bytes 388
  0.6 9.9 %collective-permute-start = (f32[4,16,128]{2,1,0:T(8,128)}, f32[4,16,128]{2,1,0:T(8,128)S(1)}, u32[]{:S(2)}, u32[]{:S(2)}) collective-permute-start(f32[4,16,128]{2,1,0:T(8,128)} %bitcast.21), channel_id=1, source_target_pairs={{0,4},{4,8},{8,12},{12,16},{16,20},{20,24},{24,28},{28,0},{1,5},{5... | collective-permute-start | bytes 98312 | tf_op jit(solution)/shard_map/ppermute | solution.py:399
  5.4 9.8 %collective-permute-start.2 = (f32[72,128]{1,0:T(8,128)S(1)}, f32[72,128]{1,0:T(8,128)S(1)}, u32[]{:S(2)}, u32[]{:S(2)}) collective-permute-start(f32[72,128]{1,0:T(8,128)S(1)} %get-tuple-element.20.to_b_ref.first_ref), channel_id=1, source_target_pairs={{0,4},{4,0},{8,12},{12,8},{16,20},{20,16},{24,28},{28,24},{1,5},{5... | collective-permute-start | bytes 110600 | tf_op jit(solution)/shard_map/ppermute | solution.py:393
  7.0 8.2 %collective-permute-start.1 = (f32[80,128]{1,0:T(8,128)S(1)}, f32[80,128]{1,0:T(8,128)S(1)}, u32[]{:S(2)}, u32[]{:S(2)}) collective-permute-start(f32[80,128]{1,0:T(8,128)S(1)} %get-tuple-element.19.to_a_ref.first_ref), channel_id=1, source_target_pairs={{4,8},{8,4},{12,16},{16,12},{20,24},{24,20},{28,0},{0,28},{5,9},{9... | collective-permute-start | bytes 122888 | tf_op jit(solution)/shard_map/ppermute | solution.py:393
  10.6 4.7 %collective-permute-start.3 = (f32[32,128]{1,0:T(8,128)S(1)}, f32[32,128]{1,0:T(8,128)S(1)}, u32[]{:S(2)}, u32[]{:S(2)}) collective-permute-start(f32[32,128]{1,0:T(8,128)S(1)} %get-tuple-element.21), channel_id=1, source_target_pairs={{0,3},{1,2},{2,1},{3,0},{4,7},{5,6},{6,5},{7,4},{8,11},{9,10},{10,... | collective-permute-start | bytes 49160 | tf_op jit(solution)/shard_map/ppermute | solution.py:404
  10.7 4.5 %collective-permute-start.4 = (f32[32,128]{1,0:T(8,128)S(1)}, f32[32,128]{1,0:T(8,128)S(1)}, u32[]{:S(2)}, u32[]{:S(2)}) collective-permute-start(f32[32,128]{1,0:T(8,128)S(1)} %get-tuple-element.22), channel_id=1, source_target_pairs={{0,2},{1,3},{2,0},{3,1},{4,6},{5,7},{6,4},{7,5},{8,10},{9,11},{10,... | collective-permute-start | bytes 49160 | tf_op jit(solution)/shard_map/ppermute | solution.py:404
  12.2 3.0 %collective-permute-start.5 = (f32[32,128]{1,0:T(8,128)S(1)}, f32[32,128]{1,0:T(8,128)S(1)}, u32[]{:S(2)}, u32[]{:S(2)}) collective-permute-start(f32[32,128]{1,0:T(8,128)S(1)} %get-tuple-element.23), channel_id=1, source_target_pairs={{0,1},{1,0},{2,3},{3,2},{4,5},{5,4},{6,7},{7,6},{8,9},{9,8},{10,11... | collective-permute-start | bytes 49160 | tf_op jit(solution)/shard_map/ppermute | solution.py:404
  17.0 6.8 %collective-permute-start.6 = (f32[72,128]{1,0:T(8,128)S(1)}, f32[72,128]{1,0:T(8,128)S(1)}, u32[]{:S(2)}, u32[]{:S(2)}) collective-permute-start(f32[72,128]{1,0:T(8,128)S(1)} %get-tuple-element.27.side_a_ref.own_ref), channel_id=1, source_target_pairs={{4,8},{8,4},{12,16},{16,12},{20,24},{24,20},{28,0},{0,28},{5,9},{9... | collective-permute-start | bytes 110600 | tf_op jit(solution)/shard_map/ppermute | solution.py:393
  19.4 4.0 %collective-permute-start.7 = (f32[64,128]{1,0:T(8,128)S(1)}, f32[64,128]{1,0:T(8,128)S(1)}, u32[]{:S(2)}, u32[]{:S(2)}) collective-permute-start(f32[64,128]{1,0:T(8,128)S(1)} %shard_map.91.side_b_ref.own_ref), channel_id=1, source_target_pairs={{0,4},{4,0},{8,12},{12,8},{16,20},{20,16},{24,28},{28,24},{1,5},{5... | collective-permute-start | bytes 98312 | tf_op jit(solution)/shard_map/ppermute | solution.py:393
  24.5 10.7 %all-to-all-start = ((f32[32,1,128]{2,1,0:T(1,128)}), f32[32,1,128]{2,1,0:T(1,128)S(1)}, u32[]{:S(2)}, u32[]{:S(2)}) async-start(f32[32,1,128]{2,1,0:T(1,128)} %shard_map.94), calls=%async_computation | async-start | bytes 32768 | tf_op jit(solution)/shard_map/all_to_all | solution.py:515

commit v15 on v14

--- a/solution.py
+++ b/solution.py
@@ -115,7 +115,6 @@
     for first, to_ref in ((0, to_a_ref), (faces, to_b_ref)):
         gather_traces(padded_ref[...], aligned_ref, first, to_ref.at[:faces, :])
         to_ref[faces : faces + SUBLANES, :] = choice_ref[...]
-    to_a_ref[faces + SUBLANES :, :] = jnp.zeros((SUBLANES, LANES), F32)
 
 
 def blocks_kernel(first, packed_ref, last_ref, *block_refs):
@@ -437,7 +436,7 @@
             shape(2 * faces, jnp.int32),
             shape(block_rows),
             shape(SUBLANES),
-            shape(faces + 2 * SUBLANES),
+            shape(faces + SUBLANES),
             shape(faces + SUBLANES),
         ],
         [(packed, VMEM)],

time: 36.2 us -> 35.2 us (0.972)
  starting transfers between devices: 15.9 us -> 14.9 us
    ppermute x4, starting transfers between devices: 7.28 us -> 6.46 us  [swap(): return lax.ppermute(value, 'sub', pairs)]
where the time goes in v15:
time: 35.2 us; the launch traced here: 35 us
  starting transfers between devices  14.9 us (42%)
  waiting for transfers between devices  8.84 us (25%)
  Pallas kernels  8.25 us (23%)
  other arithmetic  2.2 us (6%)
  between operations  0.74 us (2%)
    pallas_call x10, Pallas kernels, call(): pl.pallas_call(body, out_shape=outs, in_specs=[spec for _, spec in inputs...  8.25 us
    ppermute x4, starting transfers between devices, swap(): return lax.ppermute(value, 'sub', pairs)  6.46 us
    all_to_all x1, waiting for transfers between devices, on_device(): lax.all_to_all(sums, ('sub', 'blk'), split_axis=0, concat_axis=0, tiled=T...  6.04 us
    all_to_all x1, starting transfers between devices, on_device(): lax.all_to_all(sums, ('sub', 'blk'), split_axis=0, concat_axis=0, tiled=T...  3.56 us
    ppermute x1, starting transfers between devices, from_behind(): return lax.ppermute(value, axis, pairs)  3.02 us
    ppermute x4, waiting for transfers between devices, swap(): return lax.ppermute(value, 'sub', pairs)  2.53 us
    ppermute x3, starting transfers between devices, swap_slots(): lax.ppermute(value, 'blk', [(slot, slot ^ k) for slot in range(count)])  1.88 us
    convert_element_type x1, other arithmetic, on_device(): blocks = stiffness[0, 0].astype(F32)  1.28 us
  transfers between devices with their start and end apart: 9, of which 3 were waited for; matrix products, arithmetic and copies ran while one was open for 6% of the time, Pallas kernels for 14%

profile of v15, /device:TPU:0, one launch (start us, length us, event | category | flops | bytes accessed | tf_op | source)
XLA Modules:
  0.0 35.0 jit_solution(2796453466534777451)
XLA Ops:
  0.6 3.0 %collective-permute-start = (f32[4,16,128]{2,1,0:T(8,128)}, f32[4,16,128]{2,1,0:T(8,128)S(1)}, u32[]{:S(2)}, u32[]{:S(2)}) collective-permute-start(f32[4,16,128]{2,1,0:T(8,128)} %bitcast.21), channel_id=1, source_target_pairs={{0,4},{4,8},{8,12},{12,16},{16,20},{20,24},{24,28},{28,0},{1,5},{5... | collective-permute-start | bytes 98312 | tf_op jit(solution)/shard_map/ppermute | solution.py:398
  3.7 0.9 %pad_add_fusion.packed_ref = f32[232,128]{1,0:T(8,128)S(1)} fusion(f32[64,128]{1,0:T(8,128)} %bitcast.22, f32[32,96]{1,0:T(8,128)} %bitcast.23, s32[1,4]{1,0:T(1,128)} %bitcast.24, s32[1,64]{1,0:T(1,128)} %bitcast.25, s32[128,128]{1,0:T(8,128)} %bitcast.20), kind=kLoop, calls=%fused_computation.1 | loop fusion | flops 148480 | bytes 229648 | tf_op jit(solution)/shard_map/add | solution.py:429
  4.6 0.8 %shard_map.86 = (s32[128,128]{1,0:T(8,128)S(1)}, f32[32,128]{1,0:T(8,128)S(1)}, f32[8,128]{1,0:T(8,128)S(1)}, f32[72,128]{1,0:T(8,128)S(1)}, f32[72,128]{1,0:T(8,128)S(1)}) custom-call(f32[232,128]{1,0:T(8,128)S(1)} %pad_add_fusion.packed_ref), custom_call_target="tpu_custom_call" | custom-call | flops 1000000 | bytes 1000000 | tf_op jit(solution)/shard_map/pallas_call | solution.py:19
  5.4 3.1 %collective-permute-start.1 = (f32[72,128]{1,0:T(8,128)S(1)}, f32[72,128]{1,0:T(8,128)S(1)}, u32[]{:S(2)}, u32[]{:S(2)}) collective-permute-start(f32[72,128]{1,0:T(8,128)S(1)} %get-tuple-element.19.to_a_ref.first_ref), channel_id=1, source_target_pairs={{4,8},{8,4},{12,16},{16,12},{20,24},{24,20},{28,0},{0,28},{5,9},{9... | collective-permute-start | bytes 110600 | tf_op jit(solution)/shard_map/ppermute | solution.py:392
  8.5 0.3 collective-permute-done.last_ref
  8.8 0.5 %collective-permute-start.3 = (f32[32,128]{1,0:T(8,128)S(1)}, f32[32,128]{1,0:T(8,128)S(1)}, u32[]{:S(2)}, u32[]{:S(2)}) collective-permute-start(f32[32,128]{1,0:T(8,128)S(1)} %get-tuple-element.21), channel_id=1, source_target_pairs={{0,3},{1,2},{2,1},{3,0},{4,7},{5,6},{6,5},{7,4},{8,11},{9,10},{10,... | collective-permute-start | bytes 49160 | tf_op jit(solution)/shard_map/ppermute | solution.py:403
  9.3 1.3 %collective-permute-start.4 = (f32[32,128]{1,0:T(8,128)S(1)}, f32[32,128]{1,0:T(8,128)S(1)}, u32[]{:S(2)}, u32[]{:S(2)}) collective-permute-start(f32[32,128]{1,0:T(8,128)S(1)} %get-tuple-element.22), channel_id=1, source_target_pairs={{0,2},{1,3},{2,0},{3,1},{4,6},{5,7},{6,4},{7,5},{8,10},{9,11},{10,... | collective-permute-start | bytes 49160 | tf_op jit(solution)/shard_map/ppermute | solution.py:403
  10.5 0.2 collective-permute-start.5
  10.7 1.3 %bitcast_convert_fusion.blocks_ref = f32[48,9216]{1,0:T(8,128)S(1)} fusion(bf16[1,1,48,9216]{3,2,1,0:T(8,128)(2,1)} %param.8), kind=kLoop, calls=%fused_computation | loop fusion | flops 442368 | bytes 2654208 | tf_op jit(solution)/shard_map/convert_element_type | solution.py:411
  12.0 1.4 %shard_map.87.product_ref = f32[32,128]{1,0:T(8,128)S(1)} custom-call(s32[2,16]{1,0:T(2,128)S(1)} %bitcast.18, f32[48,9216]{1,0:T(8,128)S(1)} %bitcast_convert_fusion.blocks_ref, f32[32,128]{1,0:T(8,128)S(1)} %get-tuple-element.16.field_ref), custom_call_target="tpu_custom_call" | custom-call | flops 1000000 | bytes 1000000 | tf_op jit(solution)/shard_map/pallas_call | solution.py:19
  13.4 0.0 collective-permute-done.2.from_b_ref
  13.4 0.0 collective-permute-done.3.refs_0_
  13.4 0.0 collective-permute-done.5.refs_2_
  13.4 1.7 %shard_map.89 = (f32[32,128]{1,0:T(8,128)S(1)}, f32[64,128]{1,0:T(8,128)S(1)}, f32[64,128]{1,0:T(8,128)S(1)}, f32[72,128]{1,0:T(8,128)S(1)}) custom-call(f32[232,128]{1,0:T(8,128)S(1)} %pad_add_fusion.packed_ref, f32[4,16,128]{2,1,0:T(8,128)S(1)} %collective-permute-done.last_ref, f32[8,128]{1,0:T(8,128)S(1)} %get-tuple-element.17.choice_ref, ...), custom_call_target="tpu_custom_call" | custom-call | flops 1000000 | bytes 1000000 | tf_op jit(solution)/shard_map/pallas_call | solution.py:19
  15.2 3.3 %collective-permute-start.6 = (f32[72,128]{1,0:T(8,128)S(1)}, f32[72,128]{1,0:T(8,128)S(1)}, u32[]{:S(2)}, u32[]{:S(2)}) collective-permute-start(f32[72,128]{1,0:T(8,128)S(1)} %get-tuple-element.27.side_a_ref.own_ref), channel_id=1, source_target_pairs={{4,8},{8,4},{12,16},{16,12},{20,24},{24,20},{28,0},{0,28},{5,9},{9... | collective-permute-start | bytes 110600 | tf_op jit(solution)/shard_map/ppermute | solution.py:392
  18.5 0.4 %shard_map.91.side_b_ref.own_ref = f32[64,128]{1,0:T(8,128)S(1)} custom-call(s32[128,128]{1,0:T(8,128)S(1)} %get-tuple-element.18.aligned_ref, f32[32,128]{1,0:T(8,128)S(1)} %get-tuple-element.24.field_ref.image_ref), custom_call_target="tpu_custom_call" | custom-call | flops 1000000 | bytes 1000000 | tf_op jit(solution)/shard_map/pallas_call | solution.py:19
  18.8 0.1 collective-permute-start.7
  18.9 1.4 %shard_map.90.product_ref = f32[32,128]{1,0:T(8,128)S(1)} custom-call(s32[2,16]{1,0:T(2,128)S(1)} %bitcast.19, f32[48,9216]{1,0:T(8,128)S(1)} %bitcast_convert_fusion.blocks_ref, f32[32,128]{1,0:T(8,128)S(1)} %get-tuple-element.24.field_ref.image_ref), custom_call_target="tpu_custom_call" | custom-call | flops 1000000 | bytes 1000000 | tf_op jit(solution)/shard_map/pallas_call | solution.py:19
  20.3 2.5 %collective-permute-done.7.from_b_ref.arrived_ref = f32[64,128]{1,0:T(8,128)S(1)} collective-permute-done((f32[64,128]{1,0:T(8,128)S(1)}, f32[64,128]{1,0:T(8,128)S(1)}, u32[]{:S(2)}, u32[]{:S(2)}) %collective-permute-start.7) | collective-permute-done | bytes 32800 | tf_op jit(solution)/shard_map/ppermute | solution.py:392
  22.8 0.7 %shard_map.94 = f32[32,1,128]{2,1,0:T(1,128)} custom-call(f32[8,128]{1,0:T(8,128)S(1)} %shard_map.93.rows_ref, f32[64,128]{1,0:T(8,128)S(1)} %get-tuple-element.25.weights_a_ref.weights_ref, f32[72,128]{1,0:T(8,128)S(1)} %get-tuple-element.27.side_a_ref.own_ref, f32[72,128]{1,0:T(8,128)S(1)} %collective-permute-done.6.from_a_ref.arrived_ref, ...), custom_call_target="tpu_custom_call" | custom-call | flops 1000000 | bytes 1000000 | tf_op jit(solution)/shard_map/pallas_call | solution.py:19
  23.6 3.6 %all-to-all-start = ((f32[32,1,128]{2,1,0:T(1,128)}), f32[32,1,128]{2,1,0:T(1,128)S(1)}, u32[]{:S(2)}, u32[]{:S(2)}) async-start(f32[32,1,128]{2,1,0:T(1,128)} %shard_map.94), calls=%async_computation | async-start | bytes 32768 | tf_op jit(solution)/shard_map/all_to_all | solution.py:514
  27.1 1.0 %shard_map.92.second_ref = f32[32,128]{1,0:T(8,128)S(1)} custom-call(s32[128,128]{1,0:T(8,128)S(1)} %get-tuple-element.18.aligned_ref, f32[32,128]{1,0:T(8,128)S(1)} %shard_map.90.product_ref, f32[64,128]{1,0:T(8,128)S(1)} %get-tuple-element.25.weights_a_ref.weights_ref, f32[64,128]{1,0:T(8,128)S(1)} %get-tuple-element.26.weights_b_ref.weights_ref, ...), custom_call_target="tpu_custom_call" | custom-call | flops 1000000000 | bytes 1000000 | tf_op jit(solution)/shard_map/pallas_call | solution.py:19
  28.2 6.0 %all-to-all-done.sums_ref = f32[32,1,128]{2,1,0:T(1,128)S(1)} async-done(((f32[32,1,128]{2,1,0:T(1,128)}), f32[32,1,128]{2,1,0:T(1,128)S(1)}, u32[]{:S(2)}, u32[]{:S(2)}) %all-to-all-start) | async-done | bytes 16416 | tf_op jit(solution)/shard_map/all_to_all | solution.py:514
  34.2 0.7 %shard_map.95 = (f32[32,96]{1,0:T(8,128)}, f32[32,96]{1,0:T(8,128)}) custom-call(f32[32,128]{1,0:T(8,128)S(1)} %get-tuple-element.16.field_ref, f32[32,128]{1,0:T(8,128)S(1)} %get-tuple-element.24.field_ref.image_ref, f32[32,128]{1,0:T(8,128)S(1)} %shard_map.92.second_ref, f32[32,1,128]{2,1,0:T(1,128)S(1)} %all-to-all-done.sums_ref), custom_call_target="tpu_custom_call" | custom-call | flops 1000000 | bytes 1000000 | tf_op jit(solution)/shard_map/pallas_call | solution.py:19
  (8 shorter events, 0.0 us)
Async XLA Ops:
  0.6 11.3 %copy-start = (s32[1,1,2,16]{3,2,1,0:T(2,128)S(1)}, s32[1,1,2,16]{3,2,1,0:T(2,128)}, u32[]{:S(2)}) copy-start(s32[1,1,2,16]{3,2,1,0:T(2,128)} %param.9) | copy-start | bytes 388
  0.6 8.2 %collective-permute-start = (f32[4,16,128]{2,1,0:T(8,128)}, f32[4,16,128]{2,1,0:T(8,128)S(1)}, u32[]{:S(2)}, u32[]{:S(2)}) collective-permute-start(f32[4,16,128]{2,1,0:T(8,128)} %bitcast.21), channel_id=1, source_target_pairs={{0,4},{4,8},{8,12},{12,16},{16,20},{20,24},{24,28},{28,0},{1,5},{5... | collective-permute-start | bytes 98312 | tf_op jit(solution)/shard_map/ppermute | solution.py:398
  5.4 8.0 %collective-permute-start.1 = (f32[72,128]{1,0:T(8,128)S(1)}, f32[72,128]{1,0:T(8,128)S(1)}, u32[]{:S(2)}, u32[]{:S(2)}) collective-permute-start(f32[72,128]{1,0:T(8,128)S(1)} %get-tuple-element.19.to_a_ref.first_ref), channel_id=1, source_target_pairs={{4,8},{8,4},{12,16},{16,12},{20,24},{24,20},{28,0},{0,28},{5,9},{9... | collective-permute-start | bytes 110600 | tf_op jit(solution)/shard_map/ppermute | solution.py:392
  8.5 4.9 %collective-permute-start.2 = (f32[72,128]{1,0:T(8,128)S(1)}, f32[72,128]{1,0:T(8,128)S(1)}, u32[]{:S(2)}, u32[]{:S(2)}) collective-permute-start(f32[72,128]{1,0:T(8,128)S(1)} %get-tuple-element.20.to_b_ref.first_ref), channel_id=1, source_target_pairs={{0,4},{4,0},{8,12},{12,8},{16,20},{20,16},{24,28},{28,24},{1,5},{5... | collective-permute-start | bytes 110600 | tf_op jit(solution)/shard_map/ppermute | solution.py:392
  8.8 4.6 %collective-permute-start.3 = (f32[32,128]{1,0:T(8,128)S(1)}, f32[32,128]{1,0:T(8,128)S(1)}, u32[]{:S(2)}, u32[]{:S(2)}) collective-permute-start(f32[32,128]{1,0:T(8,128)S(1)} %get-tuple-element.21), channel_id=1, source_target_pairs={{0,3},{1,2},{2,1},{3,0},{4,7},{5,6},{6,5},{7,4},{8,11},{9,10},{10,... | collective-permute-start | bytes 49160 | tf_op jit(solution)/shard_map/ppermute | solution.py:403
  9.3 4.2 %collective-permute-start.4 = (f32[32,128]{1,0:T(8,128)S(1)}, f32[32,128]{1,0:T(8,128)S(1)}, u32[]{:S(2)}, u32[]{:S(2)}) collective-permute-start(f32[32,128]{1,0:T(8,128)S(1)} %get-tuple-element.22), channel_id=1, source_target_pairs={{0,2},{1,3},{2,0},{3,1},{4,6},{5,7},{6,4},{7,5},{8,10},{9,11},{10,... | collective-permute-start | bytes 49160 | tf_op jit(solution)/shard_map/ppermute | solution.py:403
  10.5 2.9 %collective-permute-start.5 = (f32[32,128]{1,0:T(8,128)S(1)}, f32[32,128]{1,0:T(8,128)S(1)}, u32[]{:S(2)}, u32[]{:S(2)}) collective-permute-start(f32[32,128]{1,0:T(8,128)S(1)} %get-tuple-element.23), channel_id=1, source_target_pairs={{0,1},{1,0},{2,3},{3,2},{4,5},{5,4},{6,7},{7,6},{8,9},{9,8},{10,11... | collective-permute-start | bytes 49160 | tf_op jit(solution)/shard_map/ppermute | solution.py:403
  15.2 7.6 %collective-permute-start.6 = (f32[72,128]{1,0:T(8,128)S(1)}, f32[72,128]{1,0:T(8,128)S(1)}, u32[]{:S(2)}, u32[]{:S(2)}) collective-permute-start(f32[72,128]{1,0:T(8,128)S(1)} %get-tuple-element.27.side_a_ref.own_ref), channel_id=1, source_target_pairs={{4,8},{8,4},{12,16},{16,12},{20,24},{24,20},{28,0},{0,28},{5,9},{9... | collective-permute-start | bytes 110600 | tf_op jit(solution)/shard_map/ppermute | solution.py:392
  18.8 4.0 %collective-permute-start.7 = (f32[64,128]{1,0:T(8,128)S(1)}, f32[64,128]{1,0:T(8,128)S(1)}, u32[]{:S(2)}, u32[]{:S(2)}) collective-permute-start(f32[64,128]{1,0:T(8,128)S(1)} %shard_map.91.side_b_ref.own_ref), channel_id=1, source_target_pairs={{0,4},{4,0},{8,12},{12,8},{16,20},{20,16},{24,28},{28,24},{1,5},{5... | collective-permute-start | bytes 98312 | tf_op jit(solution)/shard_map/ppermute | solution.py:392
  23.6 10.6 %all-to-all-start = ((f32[32,1,128]{2,1,0:T(1,128)}), f32[32,1,128]{2,1,0:T(1,128)S(1)}, u32[]{:S(2)}, u32[]{:S(2)}) async-start(f32[32,1,128]{2,1,0:T(1,128)} %shard_map.94), calls=%async_computation | async-start | bytes 32768 | tf_op jit(solution)/shard_map/all_to_all | solution.py:514

commit v16 on v15

--- a/solution.py
+++ b/solution.py
@@ -80,15 +80,13 @@
 
 
 def first_kernel(
-    groups, packed_ref, aligned_ref, padded_ref, choice_ref, to_a_ref, to_b_ref
+    groups, packed_ref, aligned_ref, padded_ref, choice_ref, east_ref, west_ref, to_a_ref, to_b_ref
 ):
     faces = aligned_ref.shape[0] // 2
     block_rows = padded_ref.shape[0]
     per_group = faces // groups
     slot = lax.axis_index("blk")
-    parity = lax.rem(lax.axis_index("sub"), 2)
-    east = pl.multiple_of((1 - parity) * faces, faces)
-    west = pl.multiple_of(parity * faces, faces)
+    odd = lax.rem(lax.axis_index("sub"), 2) == 1
     padded_ref[...] = packed_ref[2 * faces : 2 * faces + block_rows, :]
     last = 2 * faces + block_rows
     tail = packed_ref[last : last + SUBLANES, :].astype(jnp.int32)
@@ -103,8 +101,8 @@
             source,
         )
     order = one_hot(partner, faces)
-    aligned_ref[pl.ds(west, faces), :] = packed_ref[faces : 2 * faces, :].astype(jnp.int32)
-    aligned_ref[pl.ds(east, faces), :] = exact_dot(order, packed_ref[:faces, :]).astype(jnp.int32)
+    aligned_ref[faces:, :] = packed_ref[faces : 2 * faces, :].astype(jnp.int32)
+    aligned_ref[:faces, :] = exact_dot(order, packed_ref[:faces, :]).astype(jnp.int32)
     choice_ref[...] = jnp.zeros_like(choice_ref)
     choice_ref[:1, :faces] = lax.dot_general(
         source.astype(F32).astype(BF16),
@@ -112,9 +110,14 @@
         (((1,), (1,)), ((), ())),
         preferred_element_type=F32,
     )
-    for first, to_ref in ((0, to_a_ref), (faces, to_b_ref)):
-        gather_traces(padded_ref[...], aligned_ref, first, to_ref.at[:faces, :])
-        to_ref[faces : faces + SUBLANES, :] = choice_ref[...]
+    gather_traces(padded_ref[...], aligned_ref, 0, east_ref)
+    gather_traces(padded_ref[...], aligned_ref, faces, west_ref)
+    east = east_ref[...]
+    west = west_ref[...]
+    to_a_ref[:faces, :] = jnp.where(odd, east, west)
+    to_b_ref[:faces, :] = jnp.where(odd, west, east)
+    for to_ref in (to_a_ref, to_b_ref):
+        to_ref[faces:, :] = choice_ref[...]
 
 
 def blocks_kernel(first, packed_ref, last_ref, *block_refs):
@@ -127,8 +130,8 @@
         block_ref[per_group:, :] = last_ref[k]
 
 
-def near_traces_kernel(aligned_ref, image_ref, side_b_ref):
-    gather_traces(image_ref[...], aligned_ref, side_b_ref.shape[0], side_b_ref)
+def west_traces_kernel(aligned_ref, image_ref, west_ref):
+    gather_traces(image_ref[...], aligned_ref, west_ref.shape[0], west_ref)
 
 
 def stiffness_kernel(size, pairs_ref, blocks_ref, field_ref, out_ref):
@@ -199,7 +202,7 @@
     )
 
 
-def spread_jumps(size, faces, rows_ref, rows_first, weights_ref, own_ref, arrived_ref, block_rows):
+def spread_jumps(size, rows_ref, rows_first, weighted, block_rows):
     dof_of = lax.broadcasted_iota(jnp.int32, (size, LANES), 0).astype(F32).astype(BF16)
     row_of = lax.broadcasted_iota(jnp.int32, (block_rows, LANES), 0).astype(F32).astype(BF16)
     none = jnp.zeros((), BF16)
@@ -209,10 +212,10 @@
         slab = jnp.broadcast_to(value[f : f + 1, :], (2 * SUBLANES, LANES)).astype(BF16)
         return jnp.concatenate([slab] * (rows // (2 * SUBLANES)), axis=0)
 
-    def step(k, total):
-        lam = weights_ref[tile(k), :] * (own_ref[tile(k), :] - arrived_ref[tile(k), :])
-        high, low = halves(lam)
-        dof, row = split(rows_ref[tile(rows_first // SUBLANES + k), :], block_rows)
+    total = jnp.zeros((size, 2 * block_rows), F32)
+    for k in range(0, weighted.shape[0], SUBLANES):
+        high, low = halves(weighted[k : k + SUBLANES])
+        dof, row = split(rows_ref[rows_first + k : rows_first + k + SUBLANES, :], block_rows)
         dof = dof.astype(F32)
         row = row.astype(F32)
         left = []
@@ -229,16 +232,12 @@
                 )
             )
             right.append(jnp.where(dof_of == widened(dof, f, size), one, none))
-        return total + lax.dot_general(
+        total = total + lax.dot_general(
             jnp.concatenate(right, axis=1),
             jnp.concatenate(left, axis=1),
             (((1,), (1,)), ((), ())),
             preferred_element_type=F32,
         )
-
-    total = lax.fori_loop(
-        0, faces // SUBLANES, step, jnp.zeros((size, 2 * block_rows), F32), unroll=8
-    )
     total = total.T
     return total[:block_rows] + total[block_rows:]
 
@@ -251,83 +250,70 @@
     choice_ref,
     aligned_ref,
     product_ref,
-    to_a_ref,
-    to_b_ref,
+    east_ref,
+    west_ref,
     from_a_ref,
     from_b_ref,
     *refs,
 ):
-    *block_refs, image_ref, weights_a_ref, weights_b_ref, side_a_ref = refs
+    *block_refs, image_ref, weights_east_ref, weights_west_ref, jump_ref, next_east_ref = refs
     block_rows = product_ref.shape[0]
-    faces = weights_a_ref.shape[0]
+    faces = weights_east_ref.shape[0]
     per_group = last_ref.shape[1]
     slot = lax.axis_index("blk")
     odd = lax.rem(lax.axis_index("sub"), 2) == 1
     kept = pl.ds(pl.multiple_of(first + slot * per_group, SUBLANES), per_group)
-    place = slice(faces, faces + SUBLANES)
-    choice = jnp.where(odd, from_b_ref[place, :], from_a_ref[place, :])
-    own, last = (
-        lax.dot_general(
+    from_west = jnp.where(odd, from_b_ref[...], from_a_ref[...])
+    from_east = jnp.where(odd, from_a_ref[:faces, :], from_b_ref[:faces, :])
+    for row, block, part, weights_ref in (
+        (choice_ref[...], packed_ref[kept, :], slice(0, per_group), weights_east_ref),
+        (from_west[faces:], last_ref[slot], slice(per_group, 2 * per_group), weights_west_ref),
+    ):
+        weights_ref[...] = lax.dot_general(
             one_hot(row[:1, :faces].astype(jnp.int32), faces),
             jnp.concatenate([block] + [block_ref[part, :] for block_ref in block_refs], axis=0),
             (((0,), (0,)), ((), ())),
             precision=lax.Precision.HIGHEST,
             preferred_element_type=F32,
         )
-        for row, block, part in (
-            (choice_ref[...], packed_ref[kept, :], slice(0, per_group)),
-            (choice, last_ref[slot], slice(per_group, 2 * per_group)),
-        )
-    )
-    weights_a_ref[...] = jnp.where(odd, own, last)
-    weights_b_ref[...] = jnp.where(odd, last, own)
+    jump_ref[...] = west_ref[...] - from_west[:faces]
     image_ref[...] = product_ref[...]
     image_ref[:, :size] = (
         image_ref[:, :size]
-        + spread_jumps(size, faces, aligned_ref, 0, weights_a_ref, to_a_ref, from_a_ref, block_rows)
         + spread_jumps(
-            size, faces, aligned_ref, faces, weights_b_ref, to_b_ref, from_b_ref, block_rows
-        )
-    )
-    gather_traces(image_ref[...], aligned_ref, 0, side_a_ref.at[:faces, :])
-    side_a_ref[faces:, :] = jnp.zeros_like(side_a_ref[faces:, :])
+            size, aligned_ref, 0, weights_east_ref[...] * (east_ref[...] - from_east), block_rows
+        )
+        + spread_jumps(
+            size, aligned_ref, faces, weights_west_ref[...] * jump_ref[...], block_rows
+        )
+    )
+    gather_traces(image_ref[...], aligned_ref, 0, next_east_ref.at[:faces, :])
+    next_east_ref[faces:, :] = jnp.zeros_like(next_east_ref[faces:, :])
 
 
 def column_sums(value):
     return jnp.sum(value, axis=0, keepdims=True)
 
 
-def jump_sums(weights_ref, own_ref, arrived_ref, first_ref):
-    faces = slice(0, weights_ref.shape[0])
-    own = own_ref[faces, :]
-    lam = weights_ref[...] * (own - arrived_ref[faces, :])
-    return column_sums(lam * first_ref[faces, :]), column_sums(lam * own)
-
-
-def near_sums_kernel(
-    product_ref, weights_ref, own_ref, arrived_ref, first_ref, field_ref, image_ref, rows_ref
+def sums_kernel(
+    product_ref, weights_ref, own_ref, arrived_ref, jump_ref, field_ref, image_ref, sums_ref
 ):
     field = field_ref[...]
     image = image_ref[...]
     product = product_ref[...]
-    with_field, with_image = jump_sums(weights_ref, own_ref, arrived_ref, first_ref)
+    jump = own_ref[...] - arrived_ref[: own_ref.shape[0], :]
+    lam = weights_ref[...] * jump
     parts = [
         column_sums(field * field),
         column_sums(field * image),
         column_sums(image * image),
-        column_sums(field * product) + with_field,
-        column_sums(image * product) + with_image,
+        column_sums(field * product) + column_sums(lam * jump_ref[...]),
+        column_sums(image * product) + column_sums(lam * jump),
     ]
     parts += [jnp.zeros_like(parts[0])] * (SUBLANES - len(parts))
-    rows_ref[...] = jnp.concatenate(parts, axis=0)
-
-
-def sums_kernel(rows_ref, weights_ref, own_ref, arrived_ref, first_ref, sums_ref):
-    with_field, with_image = jump_sums(weights_ref, own_ref, arrived_ref, first_ref)
+    whole = jnp.sum(jnp.concatenate(parts, axis=0), axis=1, keepdims=True)
     row = lax.broadcasted_iota(jnp.int32, (SUBLANES, LANES), 0)
-    rows = rows_ref[...] + jnp.where(row == 3, with_field, jnp.where(row == 4, with_image, 0.0))
     lane = lax.broadcasted_iota(jnp.int32, (SUBLANES, LANES), 1)
-    whole = jnp.sum(rows, axis=1, keepdims=True)
     packed = column_sums(jnp.where(lane == row, whole, 0.0))
     sums_ref[...] = jnp.broadcast_to(packed[None], sums_ref.shape)
 
@@ -336,26 +322,31 @@
     size,
     aligned_ref,
     product_ref,
-    weights_a_ref,
-    weights_b_ref,
-    side_a_ref,
-    side_b_ref,
-    from_a_ref,
-    from_b_ref,
+    weights_east_ref,
+    weights_west_ref,
+    east_ref,
+    west_ref,
+    from_next_ref,
+    from_last_ref,
     second_ref,
 ):
     block_rows = product_ref.shape[0]
-    faces = weights_a_ref.shape[0]
+    faces = west_ref.shape[0]
     second_ref[...] = product_ref[...]
-    second_ref[:, :size] = (
-        second_ref[:, :size]
-        + spread_jumps(
-            size, faces, aligned_ref, 0, weights_a_ref, side_a_ref, from_a_ref, block_rows
-        )
-        + spread_jumps(
-            size, faces, aligned_ref, faces, weights_b_ref, side_b_ref, from_b_ref, block_rows
-        )
-    )
+    coupled = [
+        spread_jumps(
+            size,
+            aligned_ref,
+            first,
+            weights_ref[...] * (own_ref[:faces, :] - arrived_ref[:faces, :]),
+            block_rows,
+        )
+        for first, weights_ref, own_ref, arrived_ref in (
+            (0, weights_east_ref, east_ref, from_next_ref),
+            (faces, weights_west_ref, west_ref, from_last_ref),
+        )
+    ]
+    second_ref[:, :size] = second_ref[:, :size] + (coupled[0] + coupled[1])
 
 
 def final_kernel(field_ref, image_ref, second_ref, sums_ref, solution_ref, residual_ref):
@@ -430,12 +421,14 @@
         + placed(field, 2 * faces)
         + placed(own_weights.reshape(faces, LANES), last + SUBLANES)
     )
-    aligned, padded, choice, to_a, to_b = call(
+    aligned, padded, choice, east, west, to_a, to_b = call(
         functools.partial(first_kernel, owners.shape[0]),
         [
             shape(2 * faces, jnp.int32),
             shape(block_rows),
             shape(SUBLANES),
+            shape(faces),
+            shape(faces),
             shape(faces + SUBLANES),
             shape(faces + SUBLANES),
         ],
@@ -463,9 +456,9 @@
         )
         return product
 
-    image, weights_a, weights_b, side_a = call(
+    image, weights_east, weights_west, jump, east = call(
         functools.partial(image_kernel, size, last + SUBLANES),
-        [shape(block_rows), shape(faces), shape(faces), shape(faces + SUBLANES)],
+        [shape(block_rows)] + [shape(faces)] * 3 + [shape(faces + SUBLANES)],
         [
             (value, VMEM)
             for value in (
@@ -474,31 +467,25 @@
                 choice,
                 aligned,
                 stiff(padded),
-                to_a,
-                to_b,
+                east,
+                west,
                 from_a,
                 from_b,
                 *blocks_from,
             )
         ],
     )
-    from_a = swap(side_a, 1)
-    (side_b,) = call(
-        near_traces_kernel, [shape(faces)], [(aligned, VMEM), (image, VMEM)]
-    )
-    from_b = swap(side_b, 0)
+    from_last = from_behind(east, "sub", 1)
+    (west,) = call(west_traces_kernel, [shape(faces)], [(aligned, VMEM), (image, VMEM)])
+    from_next = from_behind(west, "sub", -1)
     product = stiff(image)
-    (sums,) = call(
-        near_sums_kernel,
-        [shape(SUBLANES)],
-        [(value, VMEM) for value in (product, weights_b, side_b, from_b, to_b, padded, image)],
-        flops=1,
-        moved=1,
-    )
     (sums,) = call(
         sums_kernel,
         [jax.ShapeDtypeStruct((devices, 1, LANES), F32)],
-        [(value, VMEM) for value in (sums, weights_a, side_a, from_a, to_a)],
+        [
+            (value, VMEM)
+            for value in (product, weights_west, west, from_last, jump, padded, image)
+        ],
     )
     (second,) = call(
         functools.partial(second_kernel, size),
@@ -506,7 +493,7 @@
         [
             (value, VMEM)
             for value in (
-                aligned, product, weights_a, weights_b, side_a, side_b, from_a, from_b
+                aligned, product, weights_east, weights_west, east, west, from_next, from_last
             )
         ],
         flops=1_000_000_000,

time: 35.2 us -> 33.3 us (0.946)
  waiting for transfers between devices: 8.84 us -> 6.49 us
  starting transfers between devices: 14.9 us -> 15.4 us
    ppermute x1 -> x3, starting transfers between devices: 3.02 us -> 7.85 us  [from_behind(): return lax.ppermute(value, axis, pairs)]
    ppermute x4 -> x2, starting transfers between devices: 6.46 us -> 3.12 us  [swap(): return lax.ppermute(value, 'sub', pairs)]
    ppermute x4 -> x2, waiting for transfers between devices: 2.53 us -> 0.03 us  [swap(): return lax.ppermute(value, 'sub', pairs)]
    all_to_all x1, starting transfers between devices: 3.56 us -> 2.54 us  [on_device(): lax.all_to_all(sums, ('sub', 'blk'), split_axis=0, concat_axis=0, tiled=T...]
    pallas_call x10 -> x9, Pallas kernels: 8.25 us -> 8.21 us  [call(): pl.pallas_call(body, out_shape=outs, in_specs=[spec for _, spec in inputs...]
  transfers between devices with their start and end apart: 9 -> 9, of which waited for: 3 -> 3; matrix products, arithmetic and copies ran while one was open for 6% -> 7% of each run, Pallas kernels for 14% -> 17%
where the time goes in v16:
time: 33.3 us; the launch traced here: 33 us
  starting transfers between devices  15.4 us (46%)
  Pallas kernels  8.21 us (25%)
  waiting for transfers between devices  6.49 us (19%)
  other arithmetic  2.2 us (7%)
  between operations  0.74 us (2%)
    pallas_call x9, Pallas kernels, call(): pl.pallas_call(body, out_shape=outs, in_specs=[spec for _, spec in inputs...  8.21 us
    ppermute x3, starting transfers between devices, from_behind(): return lax.ppermute(value, axis, pairs)  7.85 us
    all_to_all x1, waiting for transfers between devices, on_device(): lax.all_to_all(sums, ('sub', 'blk'), split_axis=0, concat_axis=0, tiled=T...  6.02 us
    ppermute x2, starting transfers between devices, swap(): return lax.ppermute(value, 'sub', pairs)  3.12 us
    all_to_all x1, starting transfers between devices, on_device(): lax.all_to_all(sums, ('sub', 'blk'), split_axis=0, concat_axis=0, tiled=T...  2.54 us
    ppermute x3, starting transfers between devices, swap_slots(): lax.ppermute(value, 'blk', [(slot, slot ^ k) for slot in range(count)])  1.88 us
    convert_element_type x1, other arithmetic, on_device(): blocks = stiffness[0, 0].astype(F32)  1.28 us
    add x1, other arithmetic, on_device(): indices.astype(F32) + placed(field, 2 * faces)  0.92 us
  transfers between devices with their start and end apart: 9, of which 3 were waited for; matrix products, arithmetic and copies ran while one was open for 7% of the time, Pallas kernels for 17%

profile of v16, /device:TPU:0, one launch (start us, length us, event | category | flops | bytes accessed | tf_op | source)
XLA Modules:
  0.0 33.0 jit_solution(16610120877640965609)
XLA Ops:
  0.6 3.0 %collective-permute-start = (f32[4,16,128]{2,1,0:T(8,128)}, f32[4,16,128]{2,1,0:T(8,128)S(1)}, u32[]{:S(2)}, u32[]{:S(2)}) collective-permute-start(f32[4,16,128]{2,1,0:T(8,128)} %bitcast.21), channel_id=1, source_target_pairs={{0,4},{4,8},{8,12},{12,16},{16,20},{20,24},{24,28},{28,0},{1,5},{5... | collective-permute-start | bytes 98312 | tf_op jit(solution)/shard_map/ppermute | solution.py:389
  3.7 0.9 %pad_add_fusion.packed_ref = f32[232,128]{1,0:T(8,128)S(1)} fusion(f32[64,128]{1,0:T(8,128)} %bitcast.22, f32[32,96]{1,0:T(8,128)} %bitcast.23, s32[1,4]{1,0:T(1,128)} %bitcast.24, s32[1,64]{1,0:T(1,128)} %bitcast.25, s32[128,128]{1,0:T(8,128)} %bitcast.20), kind=kLoop, calls=%fused_computation.1 | loop fusion | flops 148480 | bytes 229648 | tf_op jit(solution)/shard_map/add | solution.py:420
  4.6 0.8 %shard_map.86 = (s32[128,128]{1,0:T(8,128)S(1)}, f32[32,128]{1,0:T(8,128)S(1)}, f32[8,128]{1,0:T(8,128)S(1)}, f32[64,128]{1,0:T(8,128)S(1)}, f32[64,128]{1,0:T(8...) custom-call(f32[232,128]{1,0:T(8,128)S(1)} %pad_add_fusion.packed_ref), custom_call_target="tpu_custom_call" | custom-call | flops 1000000 | bytes 1000000 | tf_op jit(solution)/shard_map/pallas_call | solution.py:19
  5.4 3.1 %collective-permute-start.1 = (f32[72,128]{1,0:T(8,128)S(1)}, f32[72,128]{1,0:T(8,128)S(1)}, u32[]{:S(2)}, u32[]{:S(2)}) collective-permute-start(f32[72,128]{1,0:T(8,128)S(1)} %get-tuple-element.24), channel_id=1, source_target_pairs={{4,8},{8,4},{12,16},{16,12},{20,24},{24,20},{28,0},{0,28},{5,9},{9... | collective-permute-start | bytes 110600 | tf_op jit(solution)/shard_map/ppermute | solution.py:383
  8.5 0.3 collective-permute-done.last_ref
  8.8 0.5 %collective-permute-start.3 = (f32[32,128]{1,0:T(8,128)S(1)}, f32[32,128]{1,0:T(8,128)S(1)}, u32[]{:S(2)}, u32[]{:S(2)}) collective-permute-start(f32[32,128]{1,0:T(8,128)S(1)} %get-tuple-element.26), channel_id=1, source_target_pairs={{0,3},{1,2},{2,1},{3,0},{4,7},{5,6},{6,5},{7,4},{8,11},{9,10},{10,... | collective-permute-start | bytes 49160 | tf_op jit(solution)/shard_map/ppermute | solution.py:394
  9.3 1.3 %collective-permute-start.4 = (f32[32,128]{1,0:T(8,128)S(1)}, f32[32,128]{1,0:T(8,128)S(1)}, u32[]{:S(2)}, u32[]{:S(2)}) collective-permute-start(f32[32,128]{1,0:T(8,128)S(1)} %get-tuple-element.27), channel_id=1, source_target_pairs={{0,2},{1,3},{2,0},{3,1},{4,6},{5,7},{6,4},{7,5},{8,10},{9,11},{10,... | collective-permute-start | bytes 49160 | tf_op jit(solution)/shard_map/ppermute | solution.py:394
  10.5 0.2 collective-permute-start.5
  10.7 1.3 %bitcast_convert_fusion.blocks_ref = f32[48,9216]{1,0:T(8,128)S(1)} fusion(bf16[1,1,48,9216]{3,2,1,0:T(8,128)(2,1)} %param.8), kind=kLoop, calls=%fused_computation | loop fusion | flops 442368 | bytes 2654208 | tf_op jit(solution)/shard_map/convert_element_type | solution.py:402
  12.0 1.4 %shard_map.87.product_ref = f32[32,128]{1,0:T(8,128)S(1)} custom-call(s32[2,16]{1,0:T(2,128)S(1)} %bitcast.18, f32[48,9216]{1,0:T(8,128)S(1)} %bitcast_convert_fusion.blocks_ref, f32[32,128]{1,0:T(8,128)S(1)} %get-tuple-element.19.field_ref), custom_call_target="tpu_custom_call" | custom-call | flops 1000000 | bytes 1000000 | tf_op jit(solution)/shard_map/pallas_call | solution.py:19
  13.4 0.0 collective-permute-done.2.from_b_ref
  13.4 0.0 collective-permute-done.3.refs_0_
  13.4 0.0 collective-permute-done.5.refs_2_
  13.4 1.7 %shard_map.89 = (f32[32,128]{1,0:T(8,128)S(1)}, f32[64,128]{1,0:T(8,128)S(1)}, f32[64,128]{1,0:T(8,128)S(1)}, f32[64,128]{1,0:T(8,128)S(1)}, f32[72,128]{1,0:T(8,128)S(1)}) custom-call(f32[232,128]{1,0:T(8,128)S(1)} %pad_add_fusion.packed_ref, f32[4,16,128]{2,1,0:T(8,128)S(1)} %collective-permute-done.last_ref, f32[8,128]{1,0:T(8,128)S(1)} %get-tuple-element.20.choice_ref, ...), custom_call_target="tpu_custom_call" | custom-call | flops 1000000 | bytes 1000000 | tf_op jit(solution)/shard_map/pallas_call | solution.py:19
  15.2 1.9 %collective-permute-start.7 = (f32[72,128]{1,0:T(8,128)S(1)}, f32[72,128]{1,0:T(8,128)S(1)}, u32[]{:S(2)}, u32[]{:S(2)}) collective-permute-start(f32[72,128]{1,0:T(8,128)S(1)} %get-tuple-element.32.east_ref), channel_id=1, source_target_pairs={{0,4},{4,8},{8,12},{12,16},{16,20},{20,24},{24,28},{28,0},{1,5},{5... | collective-permute-start | bytes 110600 | tf_op jit(solution)/shard_map/ppermute | solution.py:389
  17.0 0.4 %shard_map.91.west_ref.own_ref = f32[64,128]{1,0:T(8,128)S(1)} custom-call(s32[128,128]{1,0:T(8,128)S(1)} %get-tuple-element.21.aligned_ref, f32[32,128]{1,0:T(8,128)S(1)} %get-tuple-element.29.field_ref.image_ref), custom_call_target="tpu_custom_call" | custom-call | flops 1000000 | bytes 1000000 | tf_op jit(solution)/shard_map/pallas_call | solution.py:19
  17.4 3.0 %collective-permute-start.6 = (f32[64,128]{1,0:T(8,128)S(1)}, f32[64,128]{1,0:T(8,128)S(1)}, u32[]{:S(2)}, u32[]{:S(2)}) collective-permute-start(f32[64,128]{1,0:T(8,128)S(1)} %shard_map.91.west_ref.own_ref), channel_id=1, source_target_pairs={{0,28},{4,0},{8,4},{12,8},{16,12},{20,16},{24,20},{28,24},{1,29},{... | collective-permute-start | bytes 98312 | tf_op jit(solution)/shard_map/ppermute | solution.py:389
  20.4 1.4 %shard_map.90.product_ref = f32[32,128]{1,0:T(8,128)S(1)} custom-call(s32[2,16]{1,0:T(2,128)S(1)} %bitcast.19, f32[48,9216]{1,0:T(8,128)S(1)} %bitcast_convert_fusion.blocks_ref, f32[32,128]{1,0:T(8,128)S(1)} %get-tuple-element.29.field_ref.image_ref), custom_call_target="tpu_custom_call" | custom-call | flops 1000000 | bytes 1000000 | tf_op jit(solution)/shard_map/pallas_call | solution.py:19
  21.8 0.2 collective-permute-done.7.from_last_ref.arrived_ref
  21.9 0.7 %shard_map.93 = f32[32,1,128]{2,1,0:T(1,128)} custom-call(f32[32,128]{1,0:T(8,128)S(1)} %shard_map.90.product_ref, f32[64,128]{1,0:T(8,128)S(1)} %get-tuple-element.31.weights_west_ref.weights_ref, f32[64,128]{1,0:T(8,128)S(1)} %shard_map.91.west_ref.own_ref, f32[72,128]{1,0:T(8,128)S(1)} %collective-permute-done.7.from_last_ref.arrived_ref, ...), custom_call_target="tpu_custom_call" | custom-call | flops 1000000 | bytes 1000000 | tf_op jit(solution)/shard_map/pallas_call | solution.py:19
  22.6 2.5 %all-to-all-start = ((f32[32,1,128]{2,1,0:T(1,128)}), f32[32,1,128]{2,1,0:T(1,128)S(1)}, u32[]{:S(2)}, u32[]{:S(2)}) async-start(f32[32,1,128]{2,1,0:T(1,128)} %shard_map.93), calls=%async_computation | async-start | bytes 32768 | tf_op jit(solution)/shard_map/all_to_all | solution.py:501
  25.2 1.0 %shard_map.92.second_ref = f32[32,128]{1,0:T(8,128)S(1)} custom-call(s32[128,128]{1,0:T(8,128)S(1)} %get-tuple-element.21.aligned_ref, f32[32,128]{1,0:T(8,128)S(1)} %shard_map.90.product_ref, f32[64,128]{1,0:T(8,128)S(1)} %get-tuple-element.30.weights_east_ref, f32[64,128]{1,0:T(8,128)S(1)} %get-tuple-element.31.weights_west_ref.weights_ref, ...), custom_call_target="tpu_custom_call" | custom-call | flops 1000000000 | bytes 1000000 | tf_op jit(solution)/shard_map/pallas_call | solution.py:19
  26.3 6.0 %all-to-all-done.sums_ref = f32[32,1,128]{2,1,0:T(1,128)S(1)} async-done(((f32[32,1,128]{2,1,0:T(1,128)}), f32[32,1,128]{2,1,0:T(1,128)S(1)}, u32[]{:S(2)}, u32[]{:S(2)}) %all-to-all-start) | async-done | bytes 16416 | tf_op jit(solution)/shard_map/all_to_all | solution.py:501
  32.3 0.7 %shard_map.94 = (f32[32,96]{1,0:T(8,128)}, f32[32,96]{1,0:T(8,128)}) custom-call(f32[32,128]{1,0:T(8,128)S(1)} %get-tuple-element.19.field_ref, f32[32,128]{1,0:T(8,128)S(1)} %get-tuple-element.29.field_ref.image_ref, f32[32,128]{1,0:T(8,128)S(1)} %shard_map.92.second_ref, f32[32,1,128]{2,1,0:T(1,128)S(1)} %all-to-all-done.sums_ref), custom_call_target="tpu_custom_call" | custom-call | flops 1000000 | bytes 1000000 | tf_op jit(solution)/shard_map/pallas_call | solution.py:19
  (7 shorter events, 0.0 us)
Async XLA Ops:
  0.6 11.3 %copy-start = (s32[1,1,2,16]{3,2,1,0:T(2,128)S(1)}, s32[1,1,2,16]{3,2,1,0:T(2,128)}, u32[]{:S(2)}) copy-start(s32[1,1,2,16]{3,2,1,0:T(2,128)} %param.9) | copy-start | bytes 388
  0.6 8.2 %collective-permute-start = (f32[4,16,128]{2,1,0:T(8,128)}, f32[4,16,128]{2,1,0:T(8,128)S(1)}, u32[]{:S(2)}, u32[]{:S(2)}) collective-permute-start(f32[4,16,128]{2,1,0:T(8,128)} %bitcast.21), channel_id=1, source_target_pairs={{0,4},{4,8},{8,12},{12,16},{16,20},{20,24},{24,28},{28,0},{1,5},{5... | collective-permute-start | bytes 98312 | tf_op jit(solution)/shard_map/ppermute | solution.py:389
  5.4 8.0 %collective-permute-start.1 = (f32[72,128]{1,0:T(8,128)S(1)}, f32[72,128]{1,0:T(8,128)S(1)}, u32[]{:S(2)}, u32[]{:S(2)}) collective-permute-start(f32[72,128]{1,0:T(8,128)S(1)} %get-tuple-element.24), channel_id=1, source_target_pairs={{4,8},{8,4},{12,16},{16,12},{20,24},{24,20},{28,0},{0,28},{5,9},{9... | collective-permute-start | bytes 110600 | tf_op jit(solution)/shard_map/ppermute | solution.py:383
  8.5 4.9 %collective-permute-start.2 = (f32[72,128]{1,0:T(8,128)S(1)}, f32[72,128]{1,0:T(8,128)S(1)}, u32[]{:S(2)}, u32[]{:S(2)}) collective-permute-start(f32[72,128]{1,0:T(8,128)S(1)} %get-tuple-element.25), channel_id=1, source_target_pairs={{0,4},{4,0},{8,12},{12,8},{16,20},{20,16},{24,28},{28,24},{1,5},{5... | collective-permute-start | bytes 110600 | tf_op jit(solution)/shard_map/ppermute | solution.py:383
  8.8 4.6 %collective-permute-start.3 = (f32[32,128]{1,0:T(8,128)S(1)}, f32[32,128]{1,0:T(8,128)S(1)}, u32[]{:S(2)}, u32[]{:S(2)}) collective-permute-start(f32[32,128]{1,0:T(8,128)S(1)} %get-tuple-element.26), channel_id=1, source_target_pairs={{0,3},{1,2},{2,1},{3,0},{4,7},{5,6},{6,5},{7,4},{8,11},{9,10},{10,... | collective-permute-start | bytes 49160 | tf_op jit(solution)/shard_map/ppermute | solution.py:394
  9.3 4.2 %collective-permute-start.4 = (f32[32,128]{1,0:T(8,128)S(1)}, f32[32,128]{1,0:T(8,128)S(1)}, u32[]{:S(2)}, u32[]{:S(2)}) collective-permute-start(f32[32,128]{1,0:T(8,128)S(1)} %get-tuple-element.27), channel_id=1, source_target_pairs={{0,2},{1,3},{2,0},{3,1},{4,6},{5,7},{6,4},{7,5},{8,10},{9,11},{10,... | collective-permute-start | bytes 49160 | tf_op jit(solution)/shard_map/ppermute | solution.py:394
  10.5 2.9 %collective-permute-start.5 = (f32[32,128]{1,0:T(8,128)S(1)}, f32[32,128]{1,0:T(8,128)S(1)}, u32[]{:S(2)}, u32[]{:S(2)}) collective-permute-start(f32[32,128]{1,0:T(8,128)S(1)} %get-tuple-element.28), channel_id=1, source_target_pairs={{0,1},{1,0},{2,3},{3,2},{4,5},{5,4},{6,7},{7,6},{8,9},{9,8},{10,11... | collective-permute-start | bytes 49160 | tf_op jit(solution)/shard_map/ppermute | solution.py:394
  15.2 6.7 %collective-permute-start.7 = (f32[72,128]{1,0:T(8,128)S(1)}, f32[72,128]{1,0:T(8,128)S(1)}, u32[]{:S(2)}, u32[]{:S(2)}) collective-permute-start(f32[72,128]{1,0:T(8,128)S(1)} %get-tuple-element.32.east_ref), channel_id=1, source_target_pairs={{0,4},{4,8},{8,12},{12,16},{16,20},{20,24},{24,28},{28,0},{1,5},{5... | collective-permute-start | bytes 110600 | tf_op jit(solution)/shard_map/ppermute | solution.py:389
  17.4 7.8 %collective-permute-start.6 = (f32[64,128]{1,0:T(8,128)S(1)}, f32[64,128]{1,0:T(8,128)S(1)}, u32[]{:S(2)}, u32[]{:S(2)}) collective-permute-start(f32[64,128]{1,0:T(8,128)S(1)} %shard_map.91.west_ref.own_ref), channel_id=1, source_target_pairs={{0,28},{4,0},{8,4},{12,8},{16,12},{20,16},{24,20},{28,24},{1,29},{... | collective-permute-start | bytes 98312 | tf_op jit(solution)/shard_map/ppermute | solution.py:389
  22.6 9.6 %all-to-all-start = ((f32[32,1,128]{2,1,0:T(1,128)}), f32[32,1,128]{2,1,0:T(1,128)S(1)}, u32[]{:S(2)}, u32[]{:S(2)}) async-start(f32[32,1,128]{2,1,0:T(1,128)} %shard_map.93), calls=%async_computation | async-start | bytes 32768 | tf_op jit(solution)/shard_map/all_to_all | solution.py:501

commit v17 on v16

--- a/solution.py
+++ b/solution.py
@@ -202,7 +202,7 @@
     )
 
 
-def spread_jumps(size, rows_ref, rows_first, weighted, block_rows):
+def spread_jumps(size, rows_ref, sides, block_rows):
     dof_of = lax.broadcasted_iota(jnp.int32, (size, LANES), 0).astype(F32).astype(BF16)
     row_of = lax.broadcasted_iota(jnp.int32, (block_rows, LANES), 0).astype(F32).astype(BF16)
     none = jnp.zeros((), BF16)
@@ -213,33 +213,50 @@
         return jnp.concatenate([slab] * (rows // (2 * SUBLANES)), axis=0)
 
     total = jnp.zeros((size, 2 * block_rows), F32)
-    for k in range(0, weighted.shape[0], SUBLANES):
-        high, low = halves(weighted[k : k + SUBLANES])
-        dof, row = split(rows_ref[rows_first + k : rows_first + k + SUBLANES, :], block_rows)
-        dof = dof.astype(F32)
-        row = row.astype(F32)
-        left = []
-        right = []
-        for f in range(SUBLANES):
-            here = row_of == widened(row, f, block_rows)
-            left.append(
-                jnp.concatenate(
-                    [
-                        jnp.where(here, widened(high, f, block_rows), none),
-                        jnp.where(here, widened(low, f, block_rows), none),
-                    ],
-                    axis=0,
+    for side, weighted in enumerate(sides):
+        for k in range(0, weighted.shape[0], SUBLANES):
+            high, low = halves(weighted[k : k + SUBLANES])
+            first = side * weighted.shape[0] + k
+            dof, row = split(rows_ref[first : first + SUBLANES, :], block_rows)
+            dof = dof.astype(F32)
+            row = row.astype(F32)
+            left = []
+            right = []
+            for f in range(SUBLANES):
+                here = row_of == widened(row, f, block_rows)
+                left.append(
+                    jnp.concatenate(
+                        [
+                            jnp.where(here, widened(high, f, block_rows), none),
+                            jnp.where(here, widened(low, f, block_rows), none),
+                        ],
+                        axis=0,
+                    )
                 )
+                right.append(jnp.where(dof_of == widened(dof, f, size), one, none))
+            total = total + lax.dot_general(
+                jnp.concatenate(right, axis=1),
+                jnp.concatenate(left, axis=1),
+                (((1,), (1,)), ((), ())),
+                preferred_element_type=F32,
             )
-            right.append(jnp.where(dof_of == widened(dof, f, size), one, none))
-        total = total + lax.dot_general(
-            jnp.concatenate(right, axis=1),
-            jnp.concatenate(left, axis=1),
-            (((1,), (1,)), ((), ())),
-            preferred_element_type=F32,
-        )
     total = total.T
     return total[:block_rows] + total[block_rows:]
+
+
+def pick_rows(choice, value):
+    high, rest = halves(value)
+    middle, low = halves(rest)
+    pieces = jnp.concatenate([high, middle, low], axis=1).astype(BF16)
+    picked = lax.dot_general(
+        one_hot(choice, value.shape[0]).astype(BF16),
+        pieces,
+        (((0,), (0,)), ((), ())),
+        preferred_element_type=F32,
+    )
+    return (
+        picked[:, :LANES] + picked[:, LANES : 2 * LANES]
+    ) + picked[:, 2 * LANES :]
 
 
 def image_kernel(
@@ -269,23 +286,20 @@
         (choice_ref[...], packed_ref[kept, :], slice(0, per_group), weights_east_ref),
         (from_west[faces:], last_ref[slot], slice(per_group, 2 * per_group), weights_west_ref),
     ):
-        weights_ref[...] = lax.dot_general(
-            one_hot(row[:1, :faces].astype(jnp.int32), faces),
+        weights_ref[...] = pick_rows(
+            row[:1, :faces].astype(jnp.int32),
             jnp.concatenate([block] + [block_ref[part, :] for block_ref in block_refs], axis=0),
-            (((0,), (0,)), ((), ())),
-            precision=lax.Precision.HIGHEST,
-            preferred_element_type=F32,
         )
     jump_ref[...] = west_ref[...] - from_west[:faces]
     image_ref[...] = product_ref[...]
-    image_ref[:, :size] = (
-        image_ref[:, :size]
-        + spread_jumps(
-            size, aligned_ref, 0, weights_east_ref[...] * (east_ref[...] - from_east), block_rows
-        )
-        + spread_jumps(
-            size, aligned_ref, faces, weights_west_ref[...] * jump_ref[...], block_rows
-        )
+    image_ref[:, :size] = image_ref[:, :size] + spread_jumps(
+        size,
+        aligned_ref,
+        (
+            weights_east_ref[...] * (east_ref[...] - from_east),
+            weights_west_ref[...] * jump_ref[...],
+        ),
+        block_rows,
     )
     gather_traces(image_ref[...], aligned_ref, 0, next_east_ref.at[:faces, :])
     next_east_ref[faces:, :] = jnp.zeros_like(next_east_ref[faces:, :])
@@ -333,20 +347,18 @@
     block_rows = product_ref.shape[0]
     faces = west_ref.shape[0]
     second_ref[...] = product_ref[...]
-    coupled = [
-        spread_jumps(
-            size,
-            aligned_ref,
-            first,
-            weights_ref[...] * (own_ref[:faces, :] - arrived_ref[:faces, :]),
-            block_rows,
-        )
-        for first, weights_ref, own_ref, arrived_ref in (
-            (0, weights_east_ref, east_ref, from_next_ref),
-            (faces, weights_west_ref, west_ref, from_last_ref),
-        )
-    ]
-    second_ref[:, :size] = second_ref[:, :size] + (coupled[0] + coupled[1])
+    second_ref[:, :size] = second_ref[:, :size] + spread_jumps(
+        size,
+        aligned_ref,
+        [
+            weights_ref[...] * (own_ref[:faces, :] - arrived_ref[:faces, :])
+            for weights_ref, own_ref, arrived_ref in (
+                (weights_east_ref, east_ref, from_next_ref),
+                (weights_west_ref, west_ref, from_last_ref),
+            )
+        ],
+        block_rows,
+    )
 
 
 def final_kernel(field_ref, image_ref, second_ref, sums_ref, solution_ref, residual_ref):

time: 33.3 us -> 33.2 us (level)
  no operation moved by 1% of the time
where the time goes in v17:
time: 33.2 us; the launch traced here: 33 us
  starting transfers between devices  15.4 us (46%)
  Pallas kernels  8.13 us (24%)
  waiting for transfers between devices  6.52 us (20%)
  other arithmetic  2.2 us (7%)
  between operations  0.73 us (2%)
    pallas_call x9, Pallas kernels, call(): pl.pallas_call(body, out_shape=outs, in_specs=[spec for _, spec in inputs...  8.13 us
    ppermute x3, starting transfers between devices, from_behind(): return lax.ppermute(value, axis, pairs)  7.85 us
    all_to_all x1, waiting for transfers between devices, on_device(): lax.all_to_all(sums, ('sub', 'blk'), split_axis=0, concat_axis=0, tiled=T...  6.05 us
    ppermute x2, starting transfers between devices, swap(): return lax.ppermute(value, 'sub', pairs)  3.12 us
    all_to_all x1, starting transfers between devices, on_device(): lax.all_to_all(sums, ('sub', 'blk'), split_axis=0, concat_axis=0, tiled=T...  2.54 us
    ppermute x3, starting transfers between devices, swap_slots(): lax.ppermute(value, 'blk', [(slot, slot ^ k) for slot in range(count)])  1.88 us
    convert_element_type x1, other arithmetic, on_device(): blocks = stiffness[0, 0].astype(F32)  1.28 us
    add x1, other arithmetic, on_device(): indices.astype(F32) + placed(field, 2 * faces)  0.92 us
  transfers between devices with their start and end apart: 9, of which 3 were waited for; matrix products, arithmetic and copies ran while one was open for 7% of the time, Pallas kernels for 17%

profile of v17, /device:TPU:0, one launch (start us, length us, event | category | flops | bytes accessed | tf_op | source)
XLA Modules:
  0.0 33.0 jit_solution(13037767811082214204)
XLA Ops:
  0.6 3.0 %collective-permute-start = (f32[4,16,128]{2,1,0:T(8,128)}, f32[4,16,128]{2,1,0:T(8,128)S(1)}, u32[]{:S(2)}, u32[]{:S(2)}) collective-permute-start(f32[4,16,128]{2,1,0:T(8,128)} %bitcast.21), channel_id=1, source_target_pairs={{0,4},{4,8},{8,12},{12,16},{16,20},{20,24},{24,28},{28,0},{1,5},{5... | collective-permute-start | bytes 98312 | tf_op jit(solution)/shard_map/ppermute | solution.py:401
  3.7 0.9 %pad_add_fusion.packed_ref = f32[232,128]{1,0:T(8,128)S(1)} fusion(f32[64,128]{1,0:T(8,128)} %bitcast.22, f32[32,96]{1,0:T(8,128)} %bitcast.23, s32[1,4]{1,0:T(1,128)} %bitcast.24, s32[1,64]{1,0:T(1,128)} %bitcast.25, s32[128,128]{1,0:T(8,128)} %bitcast.20), kind=kLoop, calls=%fused_computation.1 | loop fusion | flops 148480 | bytes 229648 | tf_op jit(solution)/shard_map/add | solution.py:432
  4.6 0.8 %shard_map.86 = (s32[128,128]{1,0:T(8,128)S(1)}, f32[32,128]{1,0:T(8,128)S(1)}, f32[8,128]{1,0:T(8,128)S(1)}, f32[64,128]{1,0:T(8,128)S(1)}, f32[64,128]{1,0:T(8...) custom-call(f32[232,128]{1,0:T(8,128)S(1)} %pad_add_fusion.packed_ref), custom_call_target="tpu_custom_call" | custom-call | flops 1000000 | bytes 1000000 | tf_op jit(solution)/shard_map/pallas_call | solution.py:19
  5.4 3.1 %collective-permute-start.1 = (f32[72,128]{1,0:T(8,128)S(1)}, f32[72,128]{1,0:T(8,128)S(1)}, u32[]{:S(2)}, u32[]{:S(2)}) collective-permute-start(f32[72,128]{1,0:T(8,128)S(1)} %get-tuple-element.24), channel_id=1, source_target_pairs={{4,8},{8,4},{12,16},{16,12},{20,24},{24,20},{28,0},{0,28},{5,9},{9... | collective-permute-start | bytes 110600 | tf_op jit(solution)/shard_map/ppermute | solution.py:395
  8.5 0.3 collective-permute-done.last_ref
  8.8 0.5 %collective-permute-start.3 = (f32[32,128]{1,0:T(8,128)S(1)}, f32[32,128]{1,0:T(8,128)S(1)}, u32[]{:S(2)}, u32[]{:S(2)}) collective-permute-start(f32[32,128]{1,0:T(8,128)S(1)} %get-tuple-element.26), channel_id=1, source_target_pairs={{0,3},{1,2},{2,1},{3,0},{4,7},{5,6},{6,5},{7,4},{8,11},{9,10},{10,... | collective-permute-start | bytes 49160 | tf_op jit(solution)/shard_map/ppermute | solution.py:406
  9.3 1.3 %collective-permute-start.4 = (f32[32,128]{1,0:T(8,128)S(1)}, f32[32,128]{1,0:T(8,128)S(1)}, u32[]{:S(2)}, u32[]{:S(2)}) collective-permute-start(f32[32,128]{1,0:T(8,128)S(1)} %get-tuple-element.27), channel_id=1, source_target_pairs={{0,2},{1,3},{2,0},{3,1},{4,6},{5,7},{6,4},{7,5},{8,10},{9,11},{10,... | collective-permute-start | bytes 49160 | tf_op jit(solution)/shard_map/ppermute | solution.py:406
  10.5 0.2 collective-permute-start.5
  10.7 1.3 %bitcast_convert_fusion.blocks_ref = f32[48,9216]{1,0:T(8,128)S(1)} fusion(bf16[1,1,48,9216]{3,2,1,0:T(8,128)(2,1)} %param.8), kind=kLoop, calls=%fused_computation | loop fusion | flops 442368 | bytes 2654208 | tf_op jit(solution)/shard_map/convert_element_type | solution.py:414
  12.0 1.4 %shard_map.87.product_ref = f32[32,128]{1,0:T(8,128)S(1)} custom-call(s32[2,16]{1,0:T(2,128)S(1)} %bitcast.18, f32[48,9216]{1,0:T(8,128)S(1)} %bitcast_convert_fusion.blocks_ref, f32[32,128]{1,0:T(8,128)S(1)} %get-tuple-element.19.field_ref), custom_call_target="tpu_custom_call" | custom-call | flops 1000000 | bytes 1000000 | tf_op jit(solution)/shard_map/pallas_call | solution.py:19
  13.4 0.0 collective-permute-done.2.from_b_ref
  13.4 0.0 collective-permute-done.3.refs_0_
  13.4 0.0 collective-permute-done.5.refs_2_
  13.4 1.7 %shard_map.89 = (f32[32,128]{1,0:T(8,128)S(1)}, f32[64,128]{1,0:T(8,128)S(1)}, f32[64,128]{1,0:T(8,128)S(1)}, f32[64,128]{1,0:T(8,128)S(1)}, f32[72,128]{1,0:T(8,128)S(1)}) custom-call(f32[232,128]{1,0:T(8,128)S(1)} %pad_add_fusion.packed_ref, f32[4,16,128]{2,1,0:T(8,128)S(1)} %collective-permute-done.last_ref, f32[8,128]{1,0:T(8,128)S(1)} %get-tuple-element.20.choice_ref, ...), custom_call_target="tpu_custom_call" | custom-call | flops 1000000 | bytes 1000000 | tf_op jit(solution)/shard_map/pallas_call | solution.py:19
  15.1 1.9 %collective-permute-start.7 = (f32[72,128]{1,0:T(8,128)S(1)}, f32[72,128]{1,0:T(8,128)S(1)}, u32[]{:S(2)}, u32[]{:S(2)}) collective-permute-start(f32[72,128]{1,0:T(8,128)S(1)} %get-tuple-element.32.east_ref), channel_id=1, source_target_pairs={{0,4},{4,8},{8,12},{12,16},{16,20},{20,24},{24,28},{28,0},{1,5},{5... | collective-permute-start | bytes 110600 | tf_op jit(solution)/shard_map/ppermute | solution.py:401
  17.0 0.4 %shard_map.91.west_ref.own_ref = f32[64,128]{1,0:T(8,128)S(1)} custom-call(s32[128,128]{1,0:T(8,128)S(1)} %get-tuple-element.21.aligned_ref, f32[32,128]{1,0:T(8,128)S(1)} %get-tuple-element.29.field_ref.image_ref), custom_call_target="tpu_custom_call" | custom-call | flops 1000000 | bytes 1000000 | tf_op jit(solution)/shard_map/pallas_call | solution.py:19
  17.4 3.0 %collective-permute-start.6 = (f32[64,128]{1,0:T(8,128)S(1)}, f32[64,128]{1,0:T(8,128)S(1)}, u32[]{:S(2)}, u32[]{:S(2)}) collective-permute-start(f32[64,128]{1,0:T(8,128)S(1)} %shard_map.91.west_ref.own_ref), channel_id=1, source_target_pairs={{0,28},{4,0},{8,4},{12,8},{16,12},{20,16},{24,20},{28,24},{1,29},{... | collective-permute-start | bytes 98312 | tf_op jit(solution)/shard_map/ppermute | solution.py:401
  20.3 1.4 %shard_map.90.product_ref = f32[32,128]{1,0:T(8,128)S(1)} custom-call(s32[2,16]{1,0:T(2,128)S(1)} %bitcast.19, f32[48,9216]{1,0:T(8,128)S(1)} %bitcast_convert_fusion.blocks_ref, f32[32,128]{1,0:T(8,128)S(1)} %get-tuple-element.29.field_ref.image_ref), custom_call_target="tpu_custom_call" | custom-call | flops 1000000 | bytes 1000000 | tf_op jit(solution)/shard_map/pallas_call | solution.py:19
  21.7 0.2 collective-permute-done.7.from_last_ref.arrived_ref
  21.9 0.7 %shard_map.93 = f32[32,1,128]{2,1,0:T(1,128)} custom-call(f32[32,128]{1,0:T(8,128)S(1)} %shard_map.90.product_ref, f32[64,128]{1,0:T(8,128)S(1)} %get-tuple-element.31.weights_west_ref.weights_ref, f32[64,128]{1,0:T(8,128)S(1)} %shard_map.91.west_ref.own_ref, f32[72,128]{1,0:T(8,128)S(1)} %collective-permute-done.7.from_last_ref.arrived_ref, ...), custom_call_target="tpu_custom_call" | custom-call | flops 1000000 | bytes 1000000 | tf_op jit(solution)/shard_map/pallas_call | solution.py:19
  22.6 2.5 %all-to-all-start = ((f32[32,1,128]{2,1,0:T(1,128)}), f32[32,1,128]{2,1,0:T(1,128)S(1)}, u32[]{:S(2)}, u32[]{:S(2)}) async-start(f32[32,1,128]{2,1,0:T(1,128)} %shard_map.93), calls=%async_computation | async-start | bytes 32768 | tf_op jit(solution)/shard_map/all_to_all | solution.py:513
  25.2 1.0 %shard_map.92.second_ref = f32[32,128]{1,0:T(8,128)S(1)} custom-call(s32[128,128]{1,0:T(8,128)S(1)} %get-tuple-element.21.aligned_ref, f32[32,128]{1,0:T(8,128)S(1)} %shard_map.90.product_ref, f32[64,128]{1,0:T(8,128)S(1)} %get-tuple-element.30.weights_east_ref, f32[64,128]{1,0:T(8,128)S(1)} %get-tuple-element.31.weights_west_ref.weights_ref, ...), custom_call_target="tpu_custom_call" | custom-call | flops 1000000000 | bytes 1000000 | tf_op jit(solution)/shard_map/pallas_call | solution.py:19
  26.2 6.0 %all-to-all-done.sums_ref = f32[32,1,128]{2,1,0:T(1,128)S(1)} async-done(((f32[32,1,128]{2,1,0:T(1,128)}), f32[32,1,128]{2,1,0:T(1,128)S(1)}, u32[]{:S(2)}, u32[]{:S(2)}) %all-to-all-start) | async-done | bytes 16416 | tf_op jit(solution)/shard_map/all_to_all | solution.py:513
  32.2 0.7 %shard_map.94 = (f32[32,96]{1,0:T(8,128)}, f32[32,96]{1,0:T(8,128)}) custom-call(f32[32,128]{1,0:T(8,128)S(1)} %get-tuple-element.19.field_ref, f32[32,128]{1,0:T(8,128)S(1)} %get-tuple-element.29.field_ref.image_ref, f32[32,128]{1,0:T(8,128)S(1)} %shard_map.92.second_ref, f32[32,1,128]{2,1,0:T(1,128)S(1)} %all-to-all-done.sums_ref), custom_call_target="tpu_custom_call" | custom-call | flops 1000000 | bytes 1000000 | tf_op jit(solution)/shard_map/pallas_call | solution.py:19
  (7 shorter events, 0.0 us)
Async XLA Ops:
  0.6 11.3 %copy-start = (s32[1,1,2,16]{3,2,1,0:T(2,128)S(1)}, s32[1,1,2,16]{3,2,1,0:T(2,128)}, u32[]{:S(2)}) copy-start(s32[1,1,2,16]{3,2,1,0:T(2,128)} %param.9) | copy-start | bytes 388
  0.6 8.2 %collective-permute-start = (f32[4,16,128]{2,1,0:T(8,128)}, f32[4,16,128]{2,1,0:T(8,128)S(1)}, u32[]{:S(2)}, u32[]{:S(2)}) collective-permute-start(f32[4,16,128]{2,1,0:T(8,128)} %bitcast.21), channel_id=1, source_target_pairs={{0,4},{4,8},{8,12},{12,16},{16,20},{20,24},{24,28},{28,0},{1,5},{5... | collective-permute-start | bytes 98312 | tf_op jit(solution)/shard_map/ppermute | solution.py:401
  5.4 8.0 %collective-permute-start.1 = (f32[72,128]{1,0:T(8,128)S(1)}, f32[72,128]{1,0:T(8,128)S(1)}, u32[]{:S(2)}, u32[]{:S(2)}) collective-permute-start(f32[72,128]{1,0:T(8,128)S(1)} %get-tuple-element.24), channel_id=1, source_target_pairs={{4,8},{8,4},{12,16},{16,12},{20,24},{24,20},{28,0},{0,28},{5,9},{9... | collective-permute-start | bytes 110600 | tf_op jit(solution)/shard_map/ppermute | solution.py:395
  8.5 4.9 %collective-permute-start.2 = (f32[72,128]{1,0:T(8,128)S(1)}, f32[72,128]{1,0:T(8,128)S(1)}, u32[]{:S(2)}, u32[]{:S(2)}) collective-permute-start(f32[72,128]{1,0:T(8,128)S(1)} %get-tuple-element.25), channel_id=1, source_target_pairs={{0,4},{4,0},{8,12},{12,8},{16,20},{20,16},{24,28},{28,24},{1,5},{5... | collective-permute-start | bytes 110600 | tf_op jit(solution)/shard_map/ppermute | solution.py:395
  8.8 4.6 %collective-permute-start.3 = (f32[32,128]{1,0:T(8,128)S(1)}, f32[32,128]{1,0:T(8,128)S(1)}, u32[]{:S(2)}, u32[]{:S(2)}) collective-permute-start(f32[32,128]{1,0:T(8,128)S(1)} %get-tuple-element.26), channel_id=1, source_target_pairs={{0,3},{1,2},{2,1},{3,0},{4,7},{5,6},{6,5},{7,4},{8,11},{9,10},{10,... | collective-permute-start | bytes 49160 | tf_op jit(solution)/shard_map/ppermute | solution.py:406
  9.3 4.2 %collective-permute-start.4 = (f32[32,128]{1,0:T(8,128)S(1)}, f32[32,128]{1,0:T(8,128)S(1)}, u32[]{:S(2)}, u32[]{:S(2)}) collective-permute-start(f32[32,128]{1,0:T(8,128)S(1)} %get-tuple-element.27), channel_id=1, source_target_pairs={{0,2},{1,3},{2,0},{3,1},{4,6},{5,7},{6,4},{7,5},{8,10},{9,11},{10,... | collective-permute-start | bytes 49160 | tf_op jit(solution)/shard_map/ppermute | solution.py:406
  10.5 2.9 %collective-permute-start.5 = (f32[32,128]{1,0:T(8,128)S(1)}, f32[32,128]{1,0:T(8,128)S(1)}, u32[]{:S(2)}, u32[]{:S(2)}) collective-permute-start(f32[32,128]{1,0:T(8,128)S(1)} %get-tuple-element.28), channel_id=1, source_target_pairs={{0,1},{1,0},{2,3},{3,2},{4,5},{5,4},{6,7},{7,6},{8,9},{9,8},{10,11... | collective-permute-start | bytes 49160 | tf_op jit(solution)/shard_map/ppermute | solution.py:406
  15.1 6.8 %collective-permute-start.7 = (f32[72,128]{1,0:T(8,128)S(1)}, f32[72,128]{1,0:T(8,128)S(1)}, u32[]{:S(2)}, u32[]{:S(2)}) collective-permute-start(f32[72,128]{1,0:T(8,128)S(1)} %get-tuple-element.32.east_ref), channel_id=1, source_target_pairs={{0,4},{4,8},{8,12},{12,16},{16,20},{20,24},{24,28},{28,0},{1,5},{5... | collective-permute-start | bytes 110600 | tf_op jit(solution)/shard_map/ppermute | solution.py:401
  17.4 7.8 %collective-permute-start.6 = (f32[64,128]{1,0:T(8,128)S(1)}, f32[64,128]{1,0:T(8,128)S(1)}, u32[]{:S(2)}, u32[]{:S(2)}) collective-permute-start(f32[64,128]{1,0:T(8,128)S(1)} %shard_map.91.west_ref.own_ref), channel_id=1, source_target_pairs={{0,28},{4,0},{8,4},{12,8},{16,12},{20,16},{24,20},{28,24},{1,29},{... | collective-permute-start | bytes 98312 | tf_op jit(solution)/shard_map/ppermute | solution.py:401
  22.6 9.6 %all-to-all-start = ((f32[32,1,128]{2,1,0:T(1,128)}), f32[32,1,128]{2,1,0:T(1,128)S(1)}, u32[]{:S(2)}, u32[]{:S(2)}) async-start(f32[32,1,128]{2,1,0:T(1,128)} %shard_map.93), calls=%async_computation | async-start | bytes 32768 | tf_op jit(solution)/shard_map/all_to_all | solution.py:513

commit v18 on v17

--- a/solution.py
+++ b/solution.py
@@ -130,11 +130,9 @@
         block_ref[per_group:, :] = last_ref[k]
 
 
-def west_traces_kernel(aligned_ref, image_ref, west_ref):
-    gather_traces(image_ref[...], aligned_ref, west_ref.shape[0], west_ref)
-
-
-def stiffness_kernel(size, pairs_ref, blocks_ref, field_ref, out_ref):
+def stiffness_kernel(size, pairs_ref, blocks_ref, field_ref, *refs):
+    *aligned_refs, out_ref = refs[:1] if len(refs) == 1 else refs[:2]
+    west_refs = refs[2:]
     block_rows = field_ref.shape[0]
     count = pairs_ref.shape[1]
     rows = block_rows + count
@@ -200,6 +198,8 @@
         + exact_dot(first_of, total[block_rows:])
         + exact_dot(other_of, exact_dot(turned, fold))
     )
+    for aligned_ref, west_ref in zip(aligned_refs, west_refs):
+        gather_traces(field, aligned_ref, west_ref.shape[0], west_ref)
 
 
 def spread_jumps(size, rows_ref, sides, block_rows):
@@ -460,14 +460,14 @@
         swap_slots(block, k) for k, block in zip(range(slots - 1, 0, -1), blocks_to)
     ]
 
-    def stiff(vector):
-        (product,) = call(
+    def stiff(vector, *ordered):
+        return call(
             functools.partial(stiffness_kernel, size),
-            [shape(block_rows)],
-            [(pairs, VMEM), (blocks, VMEM), (vector, VMEM)],
+            [shape(block_rows)] + [shape(faces)] * len(ordered),
+            [(value, VMEM) for value in (pairs, blocks, vector, *ordered)],
         )
-        return product
-
+
+    (product,) = stiff(padded)
     image, weights_east, weights_west, jump, east = call(
         functools.partial(image_kernel, size, last + SUBLANES),
         [shape(block_rows)] + [shape(faces)] * 3 + [shape(faces + SUBLANES)],
@@ -478,7 +478,7 @@
                 last_weights,
                 choice,
                 aligned,
-                stiff(padded),
+                product,
                 east,
                 west,
                 from_a,
@@ -488,9 +488,8 @@
         ],
     )
     from_last = from_behind(east, "sub", 1)
-    (west,) = call(west_traces_kernel, [shape(faces)], [(aligned, VMEM), (image, VMEM)])
+    product, west = stiff(image, aligned)
     from_next = from_behind(west, "sub", -1)
-    product = stiff(image)
     (sums,) = call(
         sums_kernel,
         [jax.ShapeDtypeStruct((devices, 1, LANES), F32)],

time: 33.2 us -> 33.2 us (level)
  waiting for transfers between devices: 6.52 us -> 6.87 us
    ppermute x3, waiting for transfers between devices: 0.43 us -> 0.8 us  [from_behind(): return lax.ppermute(value, axis, pairs)]
    pallas_call x9 -> x8, Pallas kernels: 8.13 us -> 7.82 us  [call(): pl.pallas_call(body, out_shape=outs, in_specs=[spec for _, spec in inputs...]
  transfers between devices with their start and end apart: 9 -> 9, of which waited for: 3 -> 3; matrix products, arithmetic and copies ran while one was open for 7% -> 7% of each run, Pallas kernels for 17% -> 16%
where the time goes in v18:
time: 33.2 us; the launch traced here: 33 us
  starting transfers between devices  15.3 us (46%)
  Pallas kernels  7.82 us (24%)
  waiting for transfers between devices  6.87 us (21%)
  other arithmetic  2.2 us (7%)
  between operations  0.72 us (2%)
    pallas_call x8, Pallas kernels, call(): pl.pallas_call(body, out_shape=outs, in_specs=[spec for _, spec in inputs...  7.82 us
    ppermute x3, starting transfers between devices, from_behind(): return lax.ppermute(value, axis, pairs)  7.81 us
    all_to_all x1, waiting for transfers between devices, on_device(): lax.all_to_all(sums, ('sub', 'blk'), split_axis=0, concat_axis=0, tiled=T...  6.04 us
    ppermute x2, starting transfers between devices, swap(): return lax.ppermute(value, 'sub', pairs)  3.12 us
    all_to_all x1, starting transfers between devices, on_device(): lax.all_to_all(sums, ('sub', 'blk'), split_axis=0, concat_axis=0, tiled=T...  2.54 us
    ppermute x3, starting transfers between devices, swap_slots(): lax.ppermute(value, 'blk', [(slot, slot ^ k) for slot in range(count)])  1.88 us
    convert_element_type x1, other arithmetic, on_device(): blocks = stiffness[0, 0].astype(F32)  1.28 us
    add x1, other arithmetic, on_device(): indices.astype(F32) + placed(field, 2 * faces)  0.92 us
  transfers between devices with their start and end apart: 9, of which 3 were waited for; matrix products, arithmetic and copies ran while one was open for 7% of the time, Pallas kernels for 16%

profile of v18, /device:TPU:0, one launch (start us, length us, event | category | flops | bytes accessed | tf_op | source)
XLA Modules:
  0.0 33.0 jit_solution(5599128829990657680)
XLA Ops:
  0.6 3.0 %collective-permute-start = (f32[4,16,128]{2,1,0:T(8,128)}, f32[4,16,128]{2,1,0:T(8,128)S(1)}, u32[]{:S(2)}, u32[]{:S(2)}) collective-permute-start(f32[4,16,128]{2,1,0:T(8,128)} %bitcast.21), channel_id=1, source_target_pairs={{0,4},{4,8},{8,12},{12,16},{16,20},{20,24},{24,28},{28,0},{1,5},{5... | collective-permute-start | bytes 98312 | tf_op jit(solution)/shard_map/ppermute | solution.py:401
  3.7 0.9 %pad_add_fusion.packed_ref = f32[232,128]{1,0:T(8,128)S(1)} fusion(f32[64,128]{1,0:T(8,128)} %bitcast.22, f32[32,96]{1,0:T(8,128)} %bitcast.23, s32[1,4]{1,0:T(1,128)} %bitcast.24, s32[1,64]{1,0:T(1,128)} %bitcast.25, s32[128,128]{1,0:T(8,128)} %bitcast.20), kind=kLoop, calls=%fused_computation.1 | loop fusion | flops 148480 | bytes 229648 | tf_op jit(solution)/shard_map/add | solution.py:432
  4.6 0.8 %shard_map.86 = (s32[128,128]{1,0:T(8,128)S(1)}, f32[32,128]{1,0:T(8,128)S(1)}, f32[8,128]{1,0:T(8,128)S(1)}, f32[64,128]{1,0:T(8,128)S(1)}, f32[64,128]{1,0:T(8...) custom-call(f32[232,128]{1,0:T(8,128)S(1)} %pad_add_fusion.packed_ref), custom_call_target="tpu_custom_call" | custom-call | flops 1000000 | bytes 1000000 | tf_op jit(solution)/shard_map/pallas_call | solution.py:19
  5.4 3.1 %collective-permute-start.1 = (f32[72,128]{1,0:T(8,128)S(1)}, f32[72,128]{1,0:T(8,128)S(1)}, u32[]{:S(2)}, u32[]{:S(2)}) collective-permute-start(f32[72,128]{1,0:T(8,128)S(1)} %get-tuple-element.26), channel_id=1, source_target_pairs={{4,8},{8,4},{12,16},{16,12},{20,24},{24,20},{28,0},{0,28},{5,9},{9... | collective-permute-start | bytes 110600 | tf_op jit(solution)/shard_map/ppermute | solution.py:395
  8.5 0.3 collective-permute-done.last_ref
  8.8 0.5 %collective-permute-start.3 = (f32[32,128]{1,0:T(8,128)S(1)}, f32[32,128]{1,0:T(8,128)S(1)}, u32[]{:S(2)}, u32[]{:S(2)}) collective-permute-start(f32[32,128]{1,0:T(8,128)S(1)} %get-tuple-element.28), channel_id=1, source_target_pairs={{0,3},{1,2},{2,1},{3,0},{4,7},{5,6},{6,5},{7,4},{8,11},{9,10},{10,... | collective-permute-start | bytes 49160 | tf_op jit(solution)/shard_map/ppermute | solution.py:406
  9.3 1.3 %collective-permute-start.4 = (f32[32,128]{1,0:T(8,128)S(1)}, f32[32,128]{1,0:T(8,128)S(1)}, u32[]{:S(2)}, u32[]{:S(2)}) collective-permute-start(f32[32,128]{1,0:T(8,128)S(1)} %get-tuple-element.29), channel_id=1, source_target_pairs={{0,2},{1,3},{2,0},{3,1},{4,6},{5,7},{6,4},{7,5},{8,10},{9,11},{10,... | collective-permute-start | bytes 49160 | tf_op jit(solution)/shard_map/ppermute | solution.py:406
  10.5 0.2 collective-permute-start.5
  10.7 1.3 %bitcast_convert_fusion.blocks_ref = f32[48,9216]{1,0:T(8,128)S(1)} fusion(bf16[1,1,48,9216]{3,2,1,0:T(8,128)(2,1)} %param.8), kind=kLoop, calls=%fused_computation | loop fusion | flops 442368 | bytes 2654208 | tf_op jit(solution)/shard_map/convert_element_type | solution.py:414
  12.0 1.4 %shard_map.87.product_ref = f32[32,128]{1,0:T(8,128)S(1)} custom-call(s32[2,16]{1,0:T(2,128)S(1)} %bitcast.18, f32[48,9216]{1,0:T(8,128)S(1)} %bitcast_convert_fusion.blocks_ref, f32[32,128]{1,0:T(8,128)S(1)} %get-tuple-element.21.field_ref), custom_call_target="tpu_custom_call" | custom-call | flops 1000000 | bytes 1000000 | tf_op jit(solution)/shard_map/pallas_call | solution.py:19
  13.4 0.0 collective-permute-done.2.from_b_ref
  13.4 0.0 collective-permute-done.3.refs_0_
  13.4 0.0 collective-permute-done.5.refs_2_
  13.4 1.7 %shard_map.89 = (f32[32,128]{1,0:T(8,128)S(1)}, f32[64,128]{1,0:T(8,128)S(1)}, f32[64,128]{1,0:T(8,128)S(1)}, f32[64,128]{1,0:T(8,128)S(1)}, f32[72,128]{1,0:T(8,128)S(1)}) custom-call(f32[232,128]{1,0:T(8,128)S(1)} %pad_add_fusion.packed_ref, f32[4,16,128]{2,1,0:T(8,128)S(1)} %collective-permute-done.last_ref, f32[8,128]{1,0:T(8,128)S(1)} %get-tuple-element.22.choice_ref, ...), custom_call_target="tpu_custom_call" | custom-call | flops 1000000 | bytes 1000000 | tf_op jit(solution)/shard_map/pallas_call | solution.py:19
  15.1 1.9 %collective-permute-start.7 = (f32[72,128]{1,0:T(8,128)S(1)}, f32[72,128]{1,0:T(8,128)S(1)}, u32[]{:S(2)}, u32[]{:S(2)}) collective-permute-start(f32[72,128]{1,0:T(8,128)S(1)} %get-tuple-element.35.east_ref), channel_id=1, source_target_pairs={{0,4},{4,8},{8,12},{12,16},{16,20},{20,24},{24,28},{28,0},{1,5},{5... | collective-permute-start | bytes 110600 | tf_op jit(solution)/shard_map/ppermute | solution.py:401
  17.0 1.4 %shard_map.90 = (f32[32,128]{1,0:T(8,128)S(1)}, f32[64,128]{1,0:T(8,128)S(1)}) custom-call(s32[2,16]{1,0:T(2,128)S(1)} %bitcast.19, f32[48,9216]{1,0:T(8,128)S(1)} %bitcast_convert_fusion.blocks_ref, f32[32,128]{1,0:T(8,128)S(1)} %get-tuple-element.31.field_ref.image_ref, s32[128,128]{1,0:T(8,128)S(1)} %get-tuple-element.23.aligned_ref.refs_0_), custom_call_target="tpu_custom_call" | custom-call | flops 1000000 | bytes 1000000 | tf_op jit(solution)/shard_map/pallas_call | solution.py:19
  18.4 2.9 %collective-permute-start.6 = (f32[64,128]{1,0:T(8,128)S(1)}, f32[64,128]{1,0:T(8,128)S(1)}, u32[]{:S(2)}, u32[]{:S(2)}) collective-permute-start(f32[64,128]{1,0:T(8,128)S(1)} %get-tuple-element.36.west_ref.own_ref), channel_id=1, source_target_pairs={{0,28},{4,0},{8,4},{12,8},{16,12},{20,16},{24,20},{28,24},{1,29},{... | collective-permute-start | bytes 98312 | tf_op jit(solution)/shard_map/ppermute | solution.py:401
  21.3 0.5 %collective-permute-done.7.from_last_ref.arrived_ref = f32[72,128]{1,0:T(8,128)S(1)} collective-permute-done((f32[72,128]{1,0:T(8,128)S(1)}, f32[72,128]{1,0:T(8,128)S(1)}, u32[]{:S(2)}, u32[]{:S(2)}) %collective-permute-start.7) | collective-permute-done | bytes 36896 | tf_op jit(solution)/shard_map/ppermute | solution.py:401
  21.9 0.7 %shard_map.92 = f32[32,1,128]{2,1,0:T(1,128)} custom-call(f32[32,128]{1,0:T(8,128)S(1)} %get-tuple-element.32.product_ref, f32[64,128]{1,0:T(8,128)S(1)} %get-tuple-element.34.weights_west_ref.weights_ref, f32[64,128]{1,0:T(8,128)S(1)} %get-tuple-element.36.west_ref.own_ref, f32[72,128]{1,0:T(8,128)S(1)} %collective-permute-done.7.from_last_ref.arrived_ref, ...), custom_call_target="tpu_custom_call" | custom-call | flops 1000000 | bytes 1000000 | tf_op jit(solution)/shard_map/pallas_call | solution.py:19
  22.6 2.5 %all-to-all-start = ((f32[32,1,128]{2,1,0:T(1,128)}), f32[32,1,128]{2,1,0:T(1,128)S(1)}, u32[]{:S(2)}, u32[]{:S(2)}) async-start(f32[32,1,128]{2,1,0:T(1,128)} %shard_map.92), calls=%async_computation | async-start | bytes 32768 | tf_op jit(solution)/shard_map/all_to_all | solution.py:512
  25.1 0.0 collective-permute-done.6.from_next_ref
  25.2 1.0 %shard_map.91.second_ref = f32[32,128]{1,0:T(8,128)S(1)} custom-call(s32[128,128]{1,0:T(8,128)S(1)} %get-tuple-element.23.aligned_ref.refs_0_, f32[32,128]{1,0:T(8,128)S(1)} %get-tuple-element.32.product_ref, f32[64,128]{1,0:T(8,128)S(1)} %get-tuple-element.33.weights_east_ref, f32[64,128]{1,0:T(8,128)S(1)} %get-tuple-element.34.weights_west_ref.weights_ref, ...), custom_call_target="tpu_custom_call" | custom-call | flops 1000000000 | bytes 1000000 | tf_op jit(solution)/shard_map/pallas_call | solution.py:19
  26.2 6.0 %all-to-all-done.sums_ref = f32[32,1,128]{2,1,0:T(1,128)S(1)} async-done(((f32[32,1,128]{2,1,0:T(1,128)}), f32[32,1,128]{2,1,0:T(1,128)S(1)}, u32[]{:S(2)}, u32[]{:S(2)}) %all-to-all-start) | async-done | bytes 16416 | tf_op jit(solution)/shard_map/all_to_all | solution.py:512
  32.2 0.7 %shard_map.93 = (f32[32,96]{1,0:T(8,128)}, f32[32,96]{1,0:T(8,128)}) custom-call(f32[32,128]{1,0:T(8,128)S(1)} %get-tuple-element.21.field_ref, f32[32,128]{1,0:T(8,128)S(1)} %get-tuple-element.31.field_ref.image_ref, f32[32,128]{1,0:T(8,128)S(1)} %shard_map.91.second_ref, f32[32,1,128]{2,1,0:T(1,128)S(1)} %all-to-all-done.sums_ref), custom_call_target="tpu_custom_call" | custom-call | flops 1000000 | bytes 1000000 | tf_op jit(solution)/shard_map/pallas_call | solution.py:19
  (6 shorter events, 0.0 us)
Async XLA Ops:
  0.6 11.3 %copy-start = (s32[1,1,2,16]{3,2,1,0:T(2,128)S(1)}, s32[1,1,2,16]{3,2,1,0:T(2,128)}, u32[]{:S(2)}) copy-start(s32[1,1,2,16]{3,2,1,0:T(2,128)} %param.9) | copy-start | bytes 388
  0.6 8.2 %collective-permute-start = (f32[4,16,128]{2,1,0:T(8,128)}, f32[4,16,128]{2,1,0:T(8,128)S(1)}, u32[]{:S(2)}, u32[]{:S(2)}) collective-permute-start(f32[4,16,128]{2,1,0:T(8,128)} %bitcast.21), channel_id=1, source_target_pairs={{0,4},{4,8},{8,12},{12,16},{16,20},{20,24},{24,28},{28,0},{1,5},{5... | collective-permute-start | bytes 98312 | tf_op jit(solution)/shard_map/ppermute | solution.py:401
  5.4 8.0 %collective-permute-start.1 = (f32[72,128]{1,0:T(8,128)S(1)}, f32[72,128]{1,0:T(8,128)S(1)}, u32[]{:S(2)}, u32[]{:S(2)}) collective-permute-start(f32[72,128]{1,0:T(8,128)S(1)} %get-tuple-element.26), channel_id=1, source_target_pairs={{4,8},{8,4},{12,16},{16,12},{20,24},{24,20},{28,0},{0,28},{5,9},{9... | collective-permute-start | bytes 110600 | tf_op jit(solution)/shard_map/ppermute | solution.py:395
  8.5 4.9 %collective-permute-start.2 = (f32[72,128]{1,0:T(8,128)S(1)}, f32[72,128]{1,0:T(8,128)S(1)}, u32[]{:S(2)}, u32[]{:S(2)}) collective-permute-start(f32[72,128]{1,0:T(8,128)S(1)} %get-tuple-element.27), channel_id=1, source_target_pairs={{0,4},{4,0},{8,12},{12,8},{16,20},{20,16},{24,28},{28,24},{1,5},{5... | collective-permute-start | bytes 110600 | tf_op jit(solution)/shard_map/ppermute | solution.py:395
  8.8 4.6 %collective-permute-start.3 = (f32[32,128]{1,0:T(8,128)S(1)}, f32[32,128]{1,0:T(8,128)S(1)}, u32[]{:S(2)}, u32[]{:S(2)}) collective-permute-start(f32[32,128]{1,0:T(8,128)S(1)} %get-tuple-element.28), channel_id=1, source_target_pairs={{0,3},{1,2},{2,1},{3,0},{4,7},{5,6},{6,5},{7,4},{8,11},{9,10},{10,... | collective-permute-start | bytes 49160 | tf_op jit(solution)/shard_map/ppermute | solution.py:406
  9.3 4.2 %collective-permute-start.4 = (f32[32,128]{1,0:T(8,128)S(1)}, f32[32,128]{1,0:T(8,128)S(1)}, u32[]{:S(2)}, u32[]{:S(2)}) collective-permute-start(f32[32,128]{1,0:T(8,128)S(1)} %get-tuple-element.29), channel_id=1, source_target_pairs={{0,2},{1,3},{2,0},{3,1},{4,6},{5,7},{6,4},{7,5},{8,10},{9,11},{10,... | collective-permute-start | bytes 49160 | tf_op jit(solution)/shard_map/ppermute | solution.py:406
  10.5 2.9 %collective-permute-start.5 = (f32[32,128]{1,0:T(8,128)S(1)}, f32[32,128]{1,0:T(8,128)S(1)}, u32[]{:S(2)}, u32[]{:S(2)}) collective-permute-start(f32[32,128]{1,0:T(8,128)S(1)} %get-tuple-element.30), channel_id=1, source_target_pairs={{0,1},{1,0},{2,3},{3,2},{4,5},{5,4},{6,7},{7,6},{8,9},{9,8},{10,11... | collective-permute-start | bytes 49160 | tf_op jit(solution)/shard_map/ppermute | solution.py:406
  15.1 6.8 %collective-permute-start.7 = (f32[72,128]{1,0:T(8,128)S(1)}, f32[72,128]{1,0:T(8,128)S(1)}, u32[]{:S(2)}, u32[]{:S(2)}) collective-permute-start(f32[72,128]{1,0:T(8,128)S(1)} %get-tuple-element.35.east_ref), channel_id=1, source_target_pairs={{0,4},{4,8},{8,12},{12,16},{16,20},{20,24},{24,28},{28,0},{1,5},{5... | collective-permute-start | bytes 110600 | tf_op jit(solution)/shard_map/ppermute | solution.py:401
  18.4 6.7 %collective-permute-start.6 = (f32[64,128]{1,0:T(8,128)S(1)}, f32[64,128]{1,0:T(8,128)S(1)}, u32[]{:S(2)}, u32[]{:S(2)}) collective-permute-start(f32[64,128]{1,0:T(8,128)S(1)} %get-tuple-element.36.west_ref.own_ref), channel_id=1, source_target_pairs={{0,28},{4,0},{8,4},{12,8},{16,12},{20,16},{24,20},{28,24},{1,29},{... | collective-permute-start | bytes 98312 | tf_op jit(solution)/shard_map/ppermute | solution.py:401
  22.6 9.6 %all-to-all-start = ((f32[32,1,128]{2,1,0:T(1,128)}), f32[32,1,128]{2,1,0:T(1,128)S(1)}, u32[]{:S(2)}, u32[]{:S(2)}) async-start(f32[32,1,128]{2,1,0:T(1,128)} %shard_map.92), calls=%async_computation | async-start | bytes 32768 | tf_op jit(solution)/shard_map/all_to_all | solution.py:512

commit v19 on v18

--- a/solution.py
+++ b/solution.py
@@ -101,8 +101,10 @@
             source,
         )
     order = one_hot(partner, faces)
-    aligned_ref[faces:, :] = packed_ref[faces : 2 * faces, :].astype(jnp.int32)
-    aligned_ref[:faces, :] = exact_dot(order, packed_ref[:faces, :]).astype(jnp.int32)
+    east_rows = exact_dot(order, packed_ref[:faces, :])
+    west_rows = packed_ref[faces : 2 * faces, :]
+    aligned_ref[:faces, :] = east_rows.astype(jnp.int32)
+    aligned_ref[faces:, :] = west_rows.astype(jnp.int32)
     choice_ref[...] = jnp.zeros_like(choice_ref)
     choice_ref[:1, :faces] = lax.dot_general(
         source.astype(F32).astype(BF16),
@@ -117,7 +119,9 @@
     to_a_ref[:faces, :] = jnp.where(odd, east, west)
     to_b_ref[:faces, :] = jnp.where(odd, west, east)
     for to_ref in (to_a_ref, to_b_ref):
-        to_ref[faces:, :] = choice_ref[...]
+        to_ref[faces : faces + SUBLANES, :] = choice_ref[...]
+    to_a_ref[faces + SUBLANES :, :] = jnp.where(odd, east_rows, west_rows)
+    to_b_ref[faces + SUBLANES :, :] = jnp.where(odd, west_rows, east_rows)
 
 
 def blocks_kernel(first, packed_ref, last_ref, *block_refs):
@@ -131,8 +135,7 @@
 
 
 def stiffness_kernel(size, pairs_ref, blocks_ref, field_ref, *refs):
-    *aligned_refs, out_ref = refs[:1] if len(refs) == 1 else refs[:2]
-    west_refs = refs[2:]
+    out_ref = refs[min(1, len(refs) - 1)]
     block_rows = field_ref.shape[0]
     count = pairs_ref.shape[1]
     rows = block_rows + count
@@ -198,7 +201,10 @@
         + exact_dot(first_of, total[block_rows:])
         + exact_dot(other_of, exact_dot(turned, fold))
     )
-    for aligned_ref, west_ref in zip(aligned_refs, west_refs):
+    if len(refs) > 1:
+        aligned_ref, _, copy_ref, east_ref, west_ref = refs
+        copy_ref[...] = field
+        gather_traces(field, aligned_ref, 0, east_ref)
         gather_traces(field, aligned_ref, west_ref.shape[0], west_ref)
 
 
@@ -273,7 +279,8 @@
     from_b_ref,
     *refs,
 ):
-    *block_refs, image_ref, weights_east_ref, weights_west_ref, jump_ref, next_east_ref = refs
+    *block_refs, image_ref, weights_east_ref, weights_west_ref, jump_ref = refs[:-2]
+    next_rows_ref, last_rows_ref = refs[-2:]
     block_rows = product_ref.shape[0]
     faces = weights_east_ref.shape[0]
     per_group = last_ref.shape[1]
@@ -281,10 +288,12 @@
     odd = lax.rem(lax.axis_index("sub"), 2) == 1
     kept = pl.ds(pl.multiple_of(first + slot * per_group, SUBLANES), per_group)
     from_west = jnp.where(odd, from_b_ref[...], from_a_ref[...])
-    from_east = jnp.where(odd, from_a_ref[:faces, :], from_b_ref[:faces, :])
+    from_east = jnp.where(odd, from_a_ref[...], from_b_ref[...])
+    next_rows_ref[...] = from_east[faces + SUBLANES :].astype(jnp.int32)
+    last_rows_ref[...] = from_west[faces + SUBLANES :].astype(jnp.int32)
     for row, block, part, weights_ref in (
         (choice_ref[...], packed_ref[kept, :], slice(0, per_group), weights_east_ref),
-        (from_west[faces:], last_ref[slot], slice(per_group, 2 * per_group), weights_west_ref),
+        (from_west[faces : faces + SUBLANES], last_ref[slot], slice(per_group, 2 * per_group), weights_west_ref),
     ):
         weights_ref[...] = pick_rows(
             row[:1, :faces].astype(jnp.int32),
@@ -296,13 +305,11 @@
         size,
         aligned_ref,
         (
-            weights_east_ref[...] * (east_ref[...] - from_east),
+            weights_east_ref[...] * (east_ref[...] - from_east[:faces]),
             weights_west_ref[...] * jump_ref[...],
         ),
         block_rows,
     )
-    gather_traces(image_ref[...], aligned_ref, 0, next_east_ref.at[:faces, :])
-    next_east_ref[faces:, :] = jnp.zeros_like(next_east_ref[faces:, :])
 
 
 def column_sums(value):
@@ -310,12 +317,22 @@
 
 
 def sums_kernel(
-    product_ref, weights_ref, own_ref, arrived_ref, jump_ref, field_ref, image_ref, sums_ref
+    product_ref,
+    weights_ref,
+    own_ref,
+    rows_ref,
+    last_ref,
+    jump_ref,
+    field_ref,
+    image_ref,
+    sums_ref,
+    arrived_ref,
 ):
     field = field_ref[...]
     image = image_ref[...]
     product = product_ref[...]
-    jump = own_ref[...] - arrived_ref[: own_ref.shape[0], :]
+    gather_traces(last_ref[...], rows_ref, 0, arrived_ref)
+    jump = own_ref[...] - arrived_ref[...]
     lam = weights_ref[...] * jump
     parts = [
         column_sums(field * field),
@@ -340,18 +357,20 @@
     weights_west_ref,
     east_ref,
     west_ref,
-    from_next_ref,
+    rows_ref,
+    next_ref,
     from_last_ref,
     second_ref,
+    from_next_ref,
 ):
     block_rows = product_ref.shape[0]
-    faces = west_ref.shape[0]
+    gather_traces(next_ref[...], rows_ref, 0, from_next_ref)
     second_ref[...] = product_ref[...]
     second_ref[:, :size] = second_ref[:, :size] + spread_jumps(
         size,
         aligned_ref,
         [
-            weights_ref[...] * (own_ref[:faces, :] - arrived_ref[:faces, :])
+            weights_ref[...] * (own_ref[...] - arrived_ref[...])
             for weights_ref, own_ref, arrived_ref in (
                 (weights_east_ref, east_ref, from_next_ref),
                 (weights_west_ref, west_ref, from_last_ref),
@@ -441,8 +460,8 @@
             shape(SUBLANES),
             shape(faces),
             shape(faces),
-            shape(faces + SUBLANES),
-            shape(faces + SUBLANES),
+            shape(2 * faces + SUBLANES),
+            shape(2 * faces + SUBLANES),
         ],
         [(packed, VMEM)],
     )
@@ -463,14 +482,14 @@
     def stiff(vector, *ordered):
         return call(
             functools.partial(stiffness_kernel, size),
-            [shape(block_rows)] + [shape(faces)] * len(ordered),
+            [shape(block_rows)] * (1 + len(ordered)) + [shape(faces)] * (2 * len(ordered)),
             [(value, VMEM) for value in (pairs, blocks, vector, *ordered)],
         )
 
     (product,) = stiff(padded)
-    image, weights_east, weights_west, jump, east = call(
+    image, weights_east, weights_west, jump, next_rows, last_rows = call(
         functools.partial(image_kernel, size, last + SUBLANES),
-        [shape(block_rows)] + [shape(faces)] * 3 + [shape(faces + SUBLANES)],
+        [shape(block_rows)] + [shape(faces)] * 3 + [shape(faces, jnp.int32)] * 2,
         [
             (value, VMEM)
             for value in (
@@ -487,15 +506,15 @@
             )
         ],
     )
-    from_last = from_behind(east, "sub", 1)
-    product, west = stiff(image, aligned)
-    from_next = from_behind(west, "sub", -1)
-    (sums,) = call(
+    from_last = from_behind(image, "sub", 1)
+    product, copied, east, west = stiff(image, aligned)
+    from_next = from_behind(copied, "sub", -1)
+    sums, arrived = call(
         sums_kernel,
-        [jax.ShapeDtypeStruct((devices, 1, LANES), F32)],
+        [jax.ShapeDtypeStruct((devices, 1, LANES), F32), shape(faces)],
         [
             (value, VMEM)
-            for value in (product, weights_west, west, from_last, jump, padded, image)
+            for value in (product, weights_west, west, last_rows, from_last, jump, padded, image)
         ],
     )
     (second,) = call(
@@ -504,9 +523,18 @@
         [
             (value, VMEM)
             for value in (
-                aligned, product, weights_east, weights_west, east, west, from_next, from_last
+                aligned,
+                product,
+                weights_east,
+                weights_west,
+                east,
+                west,
+                next_rows,
+                from_next,
+                arrived,
             )
         ],
+        scratch=[pltpu.VMEM((faces, LANES), F32)],
         flops=1_000_000_000,
     )
     sums = lax.all_to_all(sums, ("sub", "blk"), split_axis=0, concat_axis=0, tiled=True)

time: 33.2 us -> 32.8 us (0.988)
  waiting for transfers between devices: 6.87 us -> 6.51 us
  transfers between devices with their start and end apart: 9 -> 9, of which waited for: 3 -> 3; matrix products, arithmetic and copies ran while one was open for 7% -> 7% of each run, Pallas kernels for 16% -> 18%
where the time goes in v19:
time: 32.8 us; the launch traced here: 32.6 us
  starting transfers between devices  15.4 us (47%)
  Pallas kernels  7.81 us (24%)
  waiting for transfers between devices  6.51 us (20%)
  other arithmetic  2.2 us (7%)
  between operations  0.72 us (2%)
    ppermute x3, starting transfers between devices, from_behind(): return lax.ppermute(value, axis, pairs)  7.83 us
    pallas_call x8, Pallas kernels, call(): pl.pallas_call(body, out_shape=outs, in_specs=[spec for _, spec in inputs...  7.81 us
    all_to_all x1, waiting for transfers between devices, on_device(): lax.all_to_all(sums, ('sub', 'blk'), split_axis=0, concat_axis=0, tiled=T...  5.95 us
    ppermute x2, starting transfers between devices, swap(): return lax.ppermute(value, 'sub', pairs)  3.12 us
    all_to_all x1, starting transfers between devices, on_device(): lax.all_to_all(sums, ('sub', 'blk'), split_axis=0, concat_axis=0, tiled=T...  2.54 us
    ppermute x3, starting transfers between devices, swap_slots(): lax.ppermute(value, 'blk', [(slot, slot ^ k) for slot in range(count)])  1.88 us
    convert_element_type x1, other arithmetic, on_device(): blocks = stiffness[0, 0].astype(F32)  1.28 us
    add x1, other arithmetic, on_device(): indices.astype(F32) + placed(field, 2 * faces)  0.92 us
  transfers between devices with their start and end apart: 9, of which 3 were waited for; matrix products, arithmetic and copies ran while one was open for 7% of the time, Pallas kernels for 18%

profile of v19, /device:TPU:0, one launch (start us, length us, event | category | flops | bytes accessed | tf_op | source)
XLA Modules:
  0.0 32.6 jit_solution(4902593656535084173)
XLA Ops:
  0.6 3.0 %collective-permute-start = (f32[4,16,128]{2,1,0:T(8,128)}, f32[4,16,128]{2,1,0:T(8,128)S(1)}, u32[]{:S(2)}, u32[]{:S(2)}) collective-permute-start(f32[4,16,128]{2,1,0:T(8,128)} %bitcast.21), channel_id=1, source_target_pairs={{0,4},{4,8},{8,12},{12,16},{16,20},{20,24},{24,28},{28,0},{1,5},{5... | collective-permute-start | bytes 98312 | tf_op jit(solution)/shard_map/ppermute | solution.py:420
  3.7 0.9 %pad_add_fusion.packed_ref = f32[232,128]{1,0:T(8,128)S(1)} fusion(f32[64,128]{1,0:T(8,128)} %bitcast.22, f32[32,96]{1,0:T(8,128)} %bitcast.23, s32[1,4]{1,0:T(1,128)} %bitcast.24, s32[1,64]{1,0:T(1,128)} %bitcast.25, s32[128,128]{1,0:T(8,128)} %bitcast.20), kind=kLoop, calls=%fused_computation.1 | loop fusion | flops 148480 | bytes 229648 | tf_op jit(solution)/shard_map/add | solution.py:451
  4.6 0.8 %shard_map.86 = (s32[128,128]{1,0:T(8,128)S(1)}, f32[32,128]{1,0:T(8,128)S(1)}, f32[8,128]{1,0:T(8,128)S(1)}, f32[64,128]{1,0:T(8,128)S(1)}, f32[64,128]{1,0:T(8...) custom-call(f32[232,128]{1,0:T(8,128)S(1)} %pad_add_fusion.packed_ref), custom_call_target="tpu_custom_call" | custom-call | flops 1000000 | bytes 1000000 | tf_op jit(solution)/shard_map/pallas_call | solution.py:19
  5.4 3.1 %collective-permute-start.1 = (f32[136,128]{1,0:T(8,128)S(1)}, f32[136,128]{1,0:T(8,128)S(1)}, u32[]{:S(2)}, u32[]{:S(2)}) collective-permute-start(f32[136,128]{1,0:T(8,128)S(1)} %get-tuple-element.31), channel_id=1, source_target_pairs={{4,8},{8,4},{12,16},{16,12},{20,24},{24,20},{28,0},{0,28},{5,9},{9... | collective-permute-start | bytes 208904 | tf_op jit(solution)/shard_map/ppermute | solution.py:414
  8.5 0.0 collective-permute-start.2
  8.5 0.3 collective-permute-done.last_ref
  8.8 0.5 %collective-permute-start.3 = (f32[32,128]{1,0:T(8,128)S(1)}, f32[32,128]{1,0:T(8,128)S(1)}, u32[]{:S(2)}, u32[]{:S(2)}) collective-permute-start(f32[32,128]{1,0:T(8,128)S(1)} %get-tuple-element.33), channel_id=1, source_target_pairs={{0,3},{1,2},{2,1},{3,0},{4,7},{5,6},{6,5},{7,4},{8,11},{9,10},{10,... | collective-permute-start | bytes 49160 | tf_op jit(solution)/shard_map/ppermute | solution.py:425
  9.3 1.3 %collective-permute-start.4 = (f32[32,128]{1,0:T(8,128)S(1)}, f32[32,128]{1,0:T(8,128)S(1)}, u32[]{:S(2)}, u32[]{:S(2)}) collective-permute-start(f32[32,128]{1,0:T(8,128)S(1)} %get-tuple-element.34), channel_id=1, source_target_pairs={{0,2},{1,3},{2,0},{3,1},{4,6},{5,7},{6,4},{7,5},{8,10},{9,11},{10,... | collective-permute-start | bytes 49160 | tf_op jit(solution)/shard_map/ppermute | solution.py:425
  10.5 0.2 collective-permute-start.5
  10.7 1.3 %bitcast_convert_fusion.blocks_ref = f32[48,9216]{1,0:T(8,128)S(1)} fusion(bf16[1,1,48,9216]{3,2,1,0:T(8,128)(2,1)} %param.8), kind=kLoop, calls=%fused_computation | loop fusion | flops 442368 | bytes 2654208 | tf_op jit(solution)/shard_map/convert_element_type | solution.py:433
  12.0 1.4 %shard_map.87.product_ref = f32[32,128]{1,0:T(8,128)S(1)} custom-call(s32[2,16]{1,0:T(2,128)S(1)} %bitcast.18, f32[48,9216]{1,0:T(8,128)S(1)} %bitcast_convert_fusion.blocks_ref, f32[32,128]{1,0:T(8,128)S(1)} %get-tuple-element.26.field_ref), custom_call_target="tpu_custom_call" | custom-call | flops 1000000 | bytes 1000000 | tf_op jit(solution)/shard_map/pallas_call | solution.py:19
  13.4 0.0 collective-permute-done.4.refs_1_
  13.4 0.0 collective-permute-done.5.refs_2_
  13.4 0.0 collective-permute-done.2.from_b_ref
  13.4 1.2 %shard_map.89 = (f32[32,128]{1,0:T(8,128)S(1)}, f32[64,128]{1,0:T(8,128)S(1)}, f32[64,128]{1,0:T(8,128)S(1)}, f32[64,128]{1,0:T(8,128)S(1)}, s32[64,128]{1,0:T(8,128)S(1)}, /*index=5*/s32[64,128]{1,0:T(8,128)S(1)}) custom-call(f32[232,128]{1,0:T(8,128)S(1)} %pad_add_fusion.packed_ref, f32[4,16,128]{2,1,0:T(8,128)S(1)} %collective-permute-done.last_ref, ...), custom_call_target="tpu_custom_call" | custom-call | flops 1000000 | bytes 1000000 | tf_op jit(solution)/shard_map/pallas_call | solution.py:19
  14.7 1.9 %collective-permute-start.7 = (f32[32,128]{1,0:T(8,128)S(1)}, f32[32,128]{1,0:T(8,128)S(1)}, u32[]{:S(2)}, u32[]{:S(2)}) collective-permute-start(f32[32,128]{1,0:T(8,128)S(1)} %get-tuple-element.36.field_ref.image_ref), channel_id=1, source_target_pairs={{0,4},{4,8},{8,12},{12,16},{16,20},{20,24},{24,28},{28,0},{1,5},{5... | collective-permute-start | bytes 49160 | tf_op jit(solution)/shard_map/ppermute | solution.py:420
  16.5 1.4 %shard_map.90 = (f32[32,128]{1,0:T(8,128)S(1)}, f32[32,128]{1,0:T(8,128)S(1)}, f32[64,128]{1,0:T(8,128)S(1)}, f32[64,128]{1,0:T(8,128)S(1)}) custom-call(s32[2,16]{1,0:T(2,128)S(1)} %bitcast.19, f32[48,9216]{1,0:T(8,128)S(1)} %bitcast_convert_fusion.blocks_ref, f32[32,128]{1,0:T(8,128)S(1)} %get-tuple-element.36.field_ref.image_ref, ...), custom_call_target="tpu_custom_call" | custom-call | flops 1000000 | bytes 1000000 | tf_op jit(solution)/shard_map/pallas_call | solution.py:19
  18.0 2.9 %collective-permute-start.6 = (f32[32,128]{1,0:T(8,128)S(1)}, f32[32,128]{1,0:T(8,128)S(1)}, u32[]{:S(2)}, u32[]{:S(2)}) collective-permute-start(f32[32,128]{1,0:T(8,128)S(1)} %get-tuple-element.43), channel_id=1, source_target_pairs={{0,28},{4,0},{8,4},{12,8},{16,12},{20,16},{24,20},{28,24},{1,29},{... | collective-permute-start | bytes 49160 | tf_op jit(solution)/shard_map/ppermute | solution.py:420
  20.9 0.2 collective-permute-done.7.last_ref
  21.2 1.1 %shard_map.91 = (f32[32,1,128]{2,1,0:T(1,128)}, f32[64,128]{1,0:T(8,128)S(1)}) custom-call(f32[32,128]{1,0:T(8,128)S(1)} %get-tuple-element.37.product_ref, f32[64,128]{1,0:T(8,128)S(1)} %get-tuple-element.39.weights_ref.weights_west_ref, f32[64,128]{1,0:T(8,128)S(1)} %get-tuple-element.41.own_ref.west_ref, s32[64,128]{1,0:T(8,128)S(1)} %get-tuple-element.44.rows_ref, ...), custom_call_target="tpu_custom_call" | custom-call | flops 1000000 | bytes 1000000 | tf_op jit(solution)/shard_map/pallas_call | solution.py:19
  22.2 2.5 %all-to-all-start = ((f32[32,1,128]{2,1,0:T(1,128)}), f32[32,1,128]{2,1,0:T(1,128)S(1)}, u32[]{:S(2)}, u32[]{:S(2)}) async-start(f32[32,1,128]{2,1,0:T(1,128)} %get-tuple-element.47), calls=%async_computation | async-start | bytes 32768 | tf_op jit(solution)/shard_map/all_to_all | solution.py:540
  24.8 1.1 %shard_map.92.second_ref = f32[32,128]{1,0:T(8,128)S(1)} custom-call(s32[128,128]{1,0:T(8,128)S(1)} %get-tuple-element.28.aligned_ref.refs_0_, f32[32,128]{1,0:T(8,128)S(1)} %get-tuple-element.37.product_ref, f32[64,128]{1,0:T(8,128)S(1)} %get-tuple-element.38.weights_east_ref, f32[64,128]{1,0:T(8,128)S(1)} %get-tuple-element.39.weights_ref.weights_west_ref, ...), custom_call_target="tpu_custom_call" | custom-call | flops 1000000000 | bytes 1000000 | tf_op jit(solution)/shard_map/pallas_call | solution.py:19
  25.9 6.0 %all-to-all-done.sums_ref = f32[32,1,128]{2,1,0:T(1,128)S(1)} async-done(((f32[32,1,128]{2,1,0:T(1,128)}), f32[32,1,128]{2,1,0:T(1,128)S(1)}, u32[]{:S(2)}, u32[]{:S(2)}) %all-to-all-start) | async-done | bytes 16416 | tf_op jit(solution)/shard_map/all_to_all | solution.py:540
  31.9 0.7 %shard_map.93 = (f32[32,96]{1,0:T(8,128)}, f32[32,96]{1,0:T(8,128)}) custom-call(f32[32,128]{1,0:T(8,128)S(1)} %get-tuple-element.26.field_ref, f32[32,128]{1,0:T(8,128)S(1)} %get-tuple-element.36.field_ref.image_ref, f32[32,128]{1,0:T(8,128)S(1)} %shard_map.92.second_ref, f32[32,1,128]{2,1,0:T(1,128)S(1)} %all-to-all-done.sums_ref), custom_call_target="tpu_custom_call" | custom-call | flops 1000000 | bytes 1000000 | tf_op jit(solution)/shard_map/pallas_call | solution.py:19
  (6 shorter events, 0.0 us)
Async XLA Ops:
  0.6 11.3 %copy-start = (s32[1,1,2,16]{3,2,1,0:T(2,128)S(1)}, s32[1,1,2,16]{3,2,1,0:T(2,128)}, u32[]{:S(2)}) copy-start(s32[1,1,2,16]{3,2,1,0:T(2,128)} %param.9) | copy-start | bytes 388
  0.6 8.2 %collective-permute-start = (f32[4,16,128]{2,1,0:T(8,128)}, f32[4,16,128]{2,1,0:T(8,128)S(1)}, u32[]{:S(2)}, u32[]{:S(2)}) collective-permute-start(f32[4,16,128]{2,1,0:T(8,128)} %bitcast.21), channel_id=1, source_target_pairs={{0,4},{4,8},{8,12},{12,16},{16,20},{20,24},{24,28},{28,0},{1,5},{5... | collective-permute-start | bytes 98312 | tf_op jit(solution)/shard_map/ppermute | solution.py:420
  5.4 8.0 %collective-permute-start.1 = (f32[136,128]{1,0:T(8,128)S(1)}, f32[136,128]{1,0:T(8,128)S(1)}, u32[]{:S(2)}, u32[]{:S(2)}) collective-permute-start(f32[136,128]{1,0:T(8,128)S(1)} %get-tuple-element.31), channel_id=1, source_target_pairs={{4,8},{8,4},{12,16},{16,12},{20,24},{24,20},{28,0},{0,28},{5,9},{9... | collective-permute-start | bytes 208904 | tf_op jit(solution)/shard_map/ppermute | solution.py:414
  8.5 4.9 %collective-permute-start.2 = (f32[136,128]{1,0:T(8,128)S(1)}, f32[136,128]{1,0:T(8,128)S(1)}, u32[]{:S(2)}, u32[]{:S(2)}) collective-permute-start(f32[136,128]{1,0:T(8,128)S(1)} %get-tuple-element.32), channel_id=1, source_target_pairs={{0,4},{4,0},{8,12},{12,8},{16,20},{20,16},{24,28},{28,24},{1,5},{5... | collective-permute-start | bytes 208904 | tf_op jit(solution)/shard_map/ppermute | solution.py:414
  8.8 4.6 %collective-permute-start.3 = (f32[32,128]{1,0:T(8,128)S(1)}, f32[32,128]{1,0:T(8,128)S(1)}, u32[]{:S(2)}, u32[]{:S(2)}) collective-permute-start(f32[32,128]{1,0:T(8,128)S(1)} %get-tuple-element.33), channel_id=1, source_target_pairs={{0,3},{1,2},{2,1},{3,0},{4,7},{5,6},{6,5},{7,4},{8,11},{9,10},{10,... | collective-permute-start | bytes 49160 | tf_op jit(solution)/shard_map/ppermute | solution.py:425
  9.3 4.1 %collective-permute-start.4 = (f32[32,128]{1,0:T(8,128)S(1)}, f32[32,128]{1,0:T(8,128)S(1)}, u32[]{:S(2)}, u32[]{:S(2)}) collective-permute-start(f32[32,128]{1,0:T(8,128)S(1)} %get-tuple-element.34), channel_id=1, source_target_pairs={{0,2},{1,3},{2,0},{3,1},{4,6},{5,7},{6,4},{7,5},{8,10},{9,11},{10,... | collective-permute-start | bytes 49160 | tf_op jit(solution)/shard_map/ppermute | solution.py:425
  10.5 2.9 %collective-permute-start.5 = (f32[32,128]{1,0:T(8,128)S(1)}, f32[32,128]{1,0:T(8,128)S(1)}, u32[]{:S(2)}, u32[]{:S(2)}) collective-permute-start(f32[32,128]{1,0:T(8,128)S(1)} %get-tuple-element.35), channel_id=1, source_target_pairs={{0,1},{1,0},{2,3},{3,2},{4,5},{5,4},{6,7},{7,6},{8,9},{9,8},{10,11... | collective-permute-start | bytes 49160 | tf_op jit(solution)/shard_map/ppermute | solution.py:425
  14.7 6.5 %collective-permute-start.7 = (f32[32,128]{1,0:T(8,128)S(1)}, f32[32,128]{1,0:T(8,128)S(1)}, u32[]{:S(2)}, u32[]{:S(2)}) collective-permute-start(f32[32,128]{1,0:T(8,128)S(1)} %get-tuple-element.36.field_ref.image_ref), channel_id=1, source_target_pairs={{0,4},{4,8},{8,12},{12,16},{16,20},{20,24},{24,28},{28,0},{1,5},{5... | collective-permute-start | bytes 49160 | tf_op jit(solution)/shard_map/ppermute | solution.py:420
  18.0 6.8 %collective-permute-start.6 = (f32[32,128]{1,0:T(8,128)S(1)}, f32[32,128]{1,0:T(8,128)S(1)}, u32[]{:S(2)}, u32[]{:S(2)}) collective-permute-start(f32[32,128]{1,0:T(8,128)S(1)} %get-tuple-element.43), channel_id=1, source_target_pairs={{0,28},{4,0},{8,4},{12,8},{16,12},{20,16},{24,20},{28,24},{1,29},{... | collective-permute-start | bytes 49160 | tf_op jit(solution)/shard_map/ppermute | solution.py:420
  22.2 9.6 %all-to-all-start = ((f32[32,1,128]{2,1,0:T(1,128)}), f32[32,1,128]{2,1,0:T(1,128)S(1)}, u32[]{:S(2)}, u32[]{:S(2)}) async-start(f32[32,1,128]{2,1,0:T(1,128)} %get-tuple-element.47), calls=%async_computation | async-start | bytes 32768 | tf_op jit(solution)/shard_map/all_to_all | solution.py:540

commit v20 on v19

--- a/solution.py
+++ b/solution.py
@@ -134,6 +134,35 @@
         block_ref[per_group:, :] = last_ref[k]
 
 
+def thirds(value, axis):
+    high, rest = halves(value)
+    middle, low = halves(rest)
+    return jnp.concatenate([high, middle, low], axis=axis).astype(BF16)
+
+
+def sum_thirds(value, axis):
+    size = value.shape[axis] // 3
+    parts = [lax.slice_in_dim(value, k * size, (k + 1) * size, axis=axis) for k in range(3)]
+    return (parts[0] + parts[1]) + parts[2]
+
+
+def pick_rows(choice, value):
+    picked = lax.dot_general(
+        one_hot(choice, value.shape[0]).astype(BF16),
+        thirds(value, 1),
+        (((0,), (0,)), ((), ())),
+        preferred_element_type=F32,
+    )
+    return sum_thirds(picked, 1)
+
+
+def put_rows(choice, value, rows):
+    put = jnp.dot(
+        one_hot(choice, rows).astype(BF16), thirds(value, 1), preferred_element_type=F32
+    )
+    return sum_thirds(put, 1)
+
+
 def stiffness_kernel(size, pairs_ref, blocks_ref, field_ref, *refs):
     out_ref = refs[min(1, len(refs) - 1)]
     block_rows = field_ref.shape[0]
@@ -159,25 +188,17 @@
         return jnp.concatenate(slabs, axis=0)
 
     field = field_ref[...]
-    first_of, other_of = (one_hot(pairs_ref[k : k + 1, :], block_rows) for k in (0, 1))
-    left, other = (
-        lax.dot_general(
-            ends,
-            field,
-            (((0,), (0,)), ((), ())),
-            precision=lax.Precision.HIGHEST,
-            preferred_element_type=F32,
-        )
-        for ends in (first_of, other_of)
-    )
-    right = jnp.concatenate([field, other], axis=0)
+    ends = jnp.concatenate([pairs_ref[:1, :], pairs_ref[1:, :]], axis=1)
+    both = pick_rows(ends, field)
+    left = both[:count]
+    right = jnp.concatenate([field, both[count:]], axis=0)
     lane = lax.broadcasted_iota(jnp.int32, (SUBLANES, LANES), 1)
     places = [place(lane + t * LANES) for t in range(tiles)]
     repeated = jnp.concatenate([lanes_of(right, inside) for _, inside in places], axis=1)
     segment, inside = place(lax.broadcasted_iota(jnp.int32, (width, LANES), 0))
     column = lax.broadcasted_iota(jnp.int32, (width, LANES), 1)
     add_segments = jnp.where(segment == column % segments, 1.0, 0.0).astype(BF16)
-    fold = jnp.where(inside == column, 1.0, 0.0)
+    fold = jnp.where(inside == column, 1.0, 0.0).astype(BF16)
     dof_group = lax.broadcasted_iota(jnp.int32, (rows, LANES), 1) // segments
     total = jnp.zeros((rows, LANES), F32)
     turned = jnp.zeros((count, width), F32)
@@ -194,12 +215,13 @@
             jnp.concatenate(stack, axis=0), add_segments, preferred_element_type=F32
         )
         for n in range(batch):
-            both = sums[2 * n * rows : 2 * (n + 1) * rows]
-            total = jnp.where(dof_group == base + n, both[:rows] + both[rows:], total)
-    out_ref[...] = (
-        total[:block_rows]
-        + exact_dot(first_of, total[block_rows:])
-        + exact_dot(other_of, exact_dot(turned, fold))
+            part = sums[2 * n * rows : 2 * (n + 1) * rows]
+            total = jnp.where(dof_group == base + n, part[:rows] + part[rows:], total)
+    folded = sum_thirds(
+        jnp.dot(thirds(turned, 0), fold, preferred_element_type=F32), 0
+    )
+    out_ref[...] = total[:block_rows] + put_rows(
+        ends, jnp.concatenate([total[block_rows:], folded], axis=0), block_rows
     )
     if len(refs) > 1:
         aligned_ref, _, copy_ref, east_ref, west_ref = refs
@@ -248,21 +270,6 @@
             )
     total = total.T
     return total[:block_rows] + total[block_rows:]
-
-
-def pick_rows(choice, value):
-    high, rest = halves(value)
-    middle, low = halves(rest)
-    pieces = jnp.concatenate([high, middle, low], axis=1).astype(BF16)
-    picked = lax.dot_general(
-        one_hot(choice, value.shape[0]).astype(BF16),
-        pieces,
-        (((0,), (0,)), ((), ())),
-        preferred_element_type=F32,
-    )
-    return (
-        picked[:, :LANES] + picked[:, LANES : 2 * LANES]
-    ) + picked[:, 2 * LANES :]
 
 
 def image_kernel(

time: 32.8 us -> 32.7 us (level)
  transfers between devices with their start and end apart: 9 -> 9, of which waited for: 3 -> 4; matrix products, arithmetic and copies ran while one was open for 7% -> 7% of each run, Pallas kernels for 18% -> 17%
where the time goes in v20:
time: 32.7 us; the launch traced here: 32.5 us
  starting transfers between devices  15.4 us (47%)
  Pallas kernels  7.49 us (23%)
  waiting for transfers between devices  6.65 us (20%)
  other arithmetic  2.2 us (7%)
  between operations  0.73 us (2%)
    ppermute x3, starting transfers between devices, from_behind(): return lax.ppermute(value, axis, pairs)  7.84 us
    pallas_call x8, Pallas kernels, call(): pl.pallas_call(body, out_shape=outs, in_specs=[spec for _, spec in inputs...  7.49 us
    all_to_all x1, waiting for transfers between devices, on_device(): lax.all_to_all(sums, ('sub', 'blk'), split_axis=0, concat_axis=0, tiled=T...  5.96 us
    ppermute x2, starting transfers between devices, swap(): return lax.ppermute(value, 'sub', pairs)  3.12 us
    all_to_all x1, starting transfers between devices, on_device(): lax.all_to_all(sums, ('sub', 'blk'), split_axis=0, concat_axis=0, tiled=T...  2.54 us
    ppermute x3, starting transfers between devices, swap_slots(): lax.ppermute(value, 'blk', [(slot, slot ^ k) for slot in range(count)])  1.88 us
    convert_element_type x1, other arithmetic, on_device(): blocks = stiffness[0, 0].astype(F32)  1.28 us
    add x1, other arithmetic, on_device(): indices.astype(F32) + placed(field, 2 * faces)  0.92 us
  transfers between devices with their start and end apart: 9, of which 4 were waited for; matrix products, arithmetic and copies ran while one was open for 7% of the time, Pallas kernels for 17%

profile of v20, /device:TPU:0, one launch (start us, length us, event | category | flops | bytes accessed | tf_op | source)
XLA Modules:
  0.0 32.5 jit_solution(4155061026611210352)
XLA Ops:
  0.6 3.0 %collective-permute-start = (f32[4,16,128]{2,1,0:T(8,128)}, f32[4,16,128]{2,1,0:T(8,128)S(1)}, u32[]{:S(2)}, u32[]{:S(2)}) collective-permute-start(f32[4,16,128]{2,1,0:T(8,128)} %bitcast.21), channel_id=1, source_target_pairs={{0,4},{4,8},{8,12},{12,16},{16,20},{20,24},{24,28},{28,0},{1,5},{5... | collective-permute-start | bytes 98312 | tf_op jit(solution)/shard_map/ppermute | solution.py:427
  3.7 0.9 %pad_add_fusion.packed_ref = f32[232,128]{1,0:T(8,128)S(1)} fusion(f32[64,128]{1,0:T(8,128)} %bitcast.22, f32[32,96]{1,0:T(8,128)} %bitcast.23, s32[1,4]{1,0:T(1,128)} %bitcast.24, s32[1,64]{1,0:T(1,128)} %bitcast.25, s32[128,128]{1,0:T(8,128)} %bitcast.20), kind=kLoop, calls=%fused_computation.1 | loop fusion | flops 148480 | bytes 229648 | tf_op jit(solution)/shard_map/add | solution.py:458
  4.6 0.8 %shard_map.86 = (s32[128,128]{1,0:T(8,128)S(1)}, f32[32,128]{1,0:T(8,128)S(1)}, f32[8,128]{1,0:T(8,128)S(1)}, f32[64,128]{1,0:T(8,128)S(1)}, f32[64,128]{1,0:T(8...) custom-call(f32[232,128]{1,0:T(8,128)S(1)} %pad_add_fusion.packed_ref), custom_call_target="tpu_custom_call" | custom-call | flops 1000000 | bytes 1000000 | tf_op jit(solution)/shard_map/pallas_call | solution.py:19
  5.4 3.1 %collective-permute-start.1 = (f32[136,128]{1,0:T(8,128)S(1)}, f32[136,128]{1,0:T(8,128)S(1)}, u32[]{:S(2)}, u32[]{:S(2)}) collective-permute-start(f32[136,128]{1,0:T(8,128)S(1)} %get-tuple-element.31), channel_id=1, source_target_pairs={{4,8},{8,4},{12,16},{16,12},{20,24},{24,20},{28,0},{0,28},{5,9},{9... | collective-permute-start | bytes 208904 | tf_op jit(solution)/shard_map/ppermute | solution.py:421
  8.5 0.0 collective-permute-start.2
  8.5 0.3 collective-permute-done.last_ref
  8.8 0.5 %collective-permute-start.3 = (f32[32,128]{1,0:T(8,128)S(1)}, f32[32,128]{1,0:T(8,128)S(1)}, u32[]{:S(2)}, u32[]{:S(2)}) collective-permute-start(f32[32,128]{1,0:T(8,128)S(1)} %get-tuple-element.33), channel_id=1, source_target_pairs={{0,3},{1,2},{2,1},{3,0},{4,7},{5,6},{6,5},{7,4},{8,11},{9,10},{10,... | collective-permute-start | bytes 49160 | tf_op jit(solution)/shard_map/ppermute | solution.py:432
  9.3 1.3 %collective-permute-start.4 = (f32[32,128]{1,0:T(8,128)S(1)}, f32[32,128]{1,0:T(8,128)S(1)}, u32[]{:S(2)}, u32[]{:S(2)}) collective-permute-start(f32[32,128]{1,0:T(8,128)S(1)} %get-tuple-element.34), channel_id=1, source_target_pairs={{0,2},{1,3},{2,0},{3,1},{4,6},{5,7},{6,4},{7,5},{8,10},{9,11},{10,... | collective-permute-start | bytes 49160 | tf_op jit(solution)/shard_map/ppermute | solution.py:432
  10.5 0.2 collective-permute-start.5
  10.7 1.3 %bitcast_convert_fusion.blocks_ref = f32[48,9216]{1,0:T(8,128)S(1)} fusion(bf16[1,1,48,9216]{3,2,1,0:T(8,128)(2,1)} %param.8), kind=kLoop, calls=%fused_computation | loop fusion | flops 442368 | bytes 2654208 | tf_op jit(solution)/shard_map/convert_element_type | solution.py:440
  12.0 1.1 %shard_map.87.product_ref = f32[32,128]{1,0:T(8,128)S(1)} custom-call(s32[2,16]{1,0:T(2,128)S(1)} %bitcast.18, f32[48,9216]{1,0:T(8,128)S(1)} %bitcast_convert_fusion.blocks_ref, f32[32,128]{1,0:T(8,128)S(1)} %get-tuple-element.26.field_ref), custom_call_target="tpu_custom_call" | custom-call | flops 1000000 | bytes 1000000 | tf_op jit(solution)/shard_map/pallas_call | solution.py:19
  13.1 0.0 collective-permute-done.4.refs_1_
  13.1 0.0 collective-permute-done.5.refs_2_
  13.1 0.2 collective-permute-done.2.from_b_ref
  13.3 1.2 %shard_map.89 = (f32[32,128]{1,0:T(8,128)S(1)}, f32[64,128]{1,0:T(8,128)S(1)}, f32[64,128]{1,0:T(8,128)S(1)}, f32[64,128]{1,0:T(8,128)S(1)}, s32[64,128]{1,0:T(8,128)S(1)}, /*index=5*/s32[64,128]{1,0:T(8,128)S(1)}) custom-call(f32[232,128]{1,0:T(8,128)S(1)} %pad_add_fusion.packed_ref, f32[4,16,128]{2,1,0:T(8,128)S(1)} %collective-permute-done.last_ref, ...), custom_call_target="tpu_custom_call" | custom-call | flops 1000000 | bytes 1000000 | tf_op jit(solution)/shard_map/pallas_call | solution.py:19
  14.5 1.7 %collective-permute-start.7 = (f32[32,128]{1,0:T(8,128)S(1)}, f32[32,128]{1,0:T(8,128)S(1)}, u32[]{:S(2)}, u32[]{:S(2)}) collective-permute-start(f32[32,128]{1,0:T(8,128)S(1)} %get-tuple-element.36.field_ref.image_ref), channel_id=1, source_target_pairs={{0,4},{4,8},{8,12},{12,16},{16,20},{20,24},{24,28},{28,0},{1,5},{5... | collective-permute-start | bytes 49160 | tf_op jit(solution)/shard_map/ppermute | solution.py:427
  16.2 1.4 %shard_map.90 = (f32[32,128]{1,0:T(8,128)S(1)}, f32[32,128]{1,0:T(8,128)S(1)}, f32[64,128]{1,0:T(8,128)S(1)}, f32[64,128]{1,0:T(8,128)S(1)}) custom-call(s32[2,16]{1,0:T(2,128)S(1)} %bitcast.19, f32[48,9216]{1,0:T(8,128)S(1)} %bitcast_convert_fusion.blocks_ref, f32[32,128]{1,0:T(8,128)S(1)} %get-tuple-element.36.field_ref.image_ref, ...), custom_call_target="tpu_custom_call" | custom-call | flops 1000000 | bytes 1000000 | tf_op jit(solution)/shard_map/pallas_call | solution.py:19
  17.7 3.1 %collective-permute-start.6 = (f32[32,128]{1,0:T(8,128)S(1)}, f32[32,128]{1,0:T(8,128)S(1)}, u32[]{:S(2)}, u32[]{:S(2)}) collective-permute-start(f32[32,128]{1,0:T(8,128)S(1)} %get-tuple-element.43), channel_id=1, source_target_pairs={{0,28},{4,0},{8,4},{12,8},{16,12},{20,16},{24,20},{28,24},{1,29},{... | collective-permute-start | bytes 49160 | tf_op jit(solution)/shard_map/ppermute | solution.py:427
  20.8 0.2 collective-permute-done.7.last_ref
  21.0 1.1 %shard_map.91 = (f32[32,1,128]{2,1,0:T(1,128)}, f32[64,128]{1,0:T(8,128)S(1)}) custom-call(f32[32,128]{1,0:T(8,128)S(1)} %get-tuple-element.37.product_ref, f32[64,128]{1,0:T(8,128)S(1)} %get-tuple-element.39.weights_ref.weights_west_ref, f32[64,128]{1,0:T(8,128)S(1)} %get-tuple-element.41.own_ref.west_ref, s32[64,128]{1,0:T(8,128)S(1)} %get-tuple-element.44.rows_ref, ...), custom_call_target="tpu_custom_call" | custom-call | flops 1000000 | bytes 1000000 | tf_op jit(solution)/shard_map/pallas_call | solution.py:19
  22.1 2.5 %all-to-all-start = ((f32[32,1,128]{2,1,0:T(1,128)}), f32[32,1,128]{2,1,0:T(1,128)S(1)}, u32[]{:S(2)}, u32[]{:S(2)}) async-start(f32[32,1,128]{2,1,0:T(1,128)} %get-tuple-element.47), calls=%async_computation | async-start | bytes 32768 | tf_op jit(solution)/shard_map/all_to_all | solution.py:547
  24.6 1.1 %shard_map.92.second_ref = f32[32,128]{1,0:T(8,128)S(1)} custom-call(s32[128,128]{1,0:T(8,128)S(1)} %get-tuple-element.28.aligned_ref.refs_0_, f32[32,128]{1,0:T(8,128)S(1)} %get-tuple-element.37.product_ref, f32[64,128]{1,0:T(8,128)S(1)} %get-tuple-element.38.weights_east_ref, f32[64,128]{1,0:T(8,128)S(1)} %get-tuple-element.39.weights_ref.weights_west_ref, ...), custom_call_target="tpu_custom_call" | custom-call | flops 1000000000 | bytes 1000000 | tf_op jit(solution)/shard_map/pallas_call | solution.py:19
  25.7 6.0 %all-to-all-done.sums_ref = f32[32,1,128]{2,1,0:T(1,128)S(1)} async-done(((f32[32,1,128]{2,1,0:T(1,128)}), f32[32,1,128]{2,1,0:T(1,128)S(1)}, u32[]{:S(2)}, u32[]{:S(2)}) %all-to-all-start) | async-done | bytes 16416 | tf_op jit(solution)/shard_map/all_to_all | solution.py:547
  31.7 0.7 %shard_map.93 = (f32[32,96]{1,0:T(8,128)}, f32[32,96]{1,0:T(8,128)}) custom-call(f32[32,128]{1,0:T(8,128)S(1)} %get-tuple-element.26.field_ref, f32[32,128]{1,0:T(8,128)S(1)} %get-tuple-element.36.field_ref.image_ref, f32[32,128]{1,0:T(8,128)S(1)} %shard_map.92.second_ref, f32[32,1,128]{2,1,0:T(1,128)S(1)} %all-to-all-done.sums_ref), custom_call_target="tpu_custom_call" | custom-call | flops 1000000 | bytes 1000000 | tf_op jit(solution)/shard_map/pallas_call | solution.py:19
  (6 shorter events, 0.0 us)
Async XLA Ops:
  0.6 11.3 %copy-start = (s32[1,1,2,16]{3,2,1,0:T(2,128)S(1)}, s32[1,1,2,16]{3,2,1,0:T(2,128)}, u32[]{:S(2)}) copy-start(s32[1,1,2,16]{3,2,1,0:T(2,128)} %param.9) | copy-start | bytes 388
  0.6 8.2 %collective-permute-start = (f32[4,16,128]{2,1,0:T(8,128)}, f32[4,16,128]{2,1,0:T(8,128)S(1)}, u32[]{:S(2)}, u32[]{:S(2)}) collective-permute-start(f32[4,16,128]{2,1,0:T(8,128)} %bitcast.21), channel_id=1, source_target_pairs={{0,4},{4,8},{8,12},{12,16},{16,20},{20,24},{24,28},{28,0},{1,5},{5... | collective-permute-start | bytes 98312 | tf_op jit(solution)/shard_map/ppermute | solution.py:427
  5.4 7.7 %collective-permute-start.1 = (f32[136,128]{1,0:T(8,128)S(1)}, f32[136,128]{1,0:T(8,128)S(1)}, u32[]{:S(2)}, u32[]{:S(2)}) collective-permute-start(f32[136,128]{1,0:T(8,128)S(1)} %get-tuple-element.31), channel_id=1, source_target_pairs={{4,8},{8,4},{12,16},{16,12},{20,24},{24,20},{28,0},{0,28},{5,9},{9... | collective-permute-start | bytes 208904 | tf_op jit(solution)/shard_map/ppermute | solution.py:421
  8.5 4.8 %collective-permute-start.2 = (f32[136,128]{1,0:T(8,128)S(1)}, f32[136,128]{1,0:T(8,128)S(1)}, u32[]{:S(2)}, u32[]{:S(2)}) collective-permute-start(f32[136,128]{1,0:T(8,128)S(1)} %get-tuple-element.32), channel_id=1, source_target_pairs={{0,4},{4,0},{8,12},{12,8},{16,20},{20,16},{24,28},{28,24},{1,5},{5... | collective-permute-start | bytes 208904 | tf_op jit(solution)/shard_map/ppermute | solution.py:421
  8.8 4.3 %collective-permute-start.3 = (f32[32,128]{1,0:T(8,128)S(1)}, f32[32,128]{1,0:T(8,128)S(1)}, u32[]{:S(2)}, u32[]{:S(2)}) collective-permute-start(f32[32,128]{1,0:T(8,128)S(1)} %get-tuple-element.33), channel_id=1, source_target_pairs={{0,3},{1,2},{2,1},{3,0},{4,7},{5,6},{6,5},{7,4},{8,11},{9,10},{10,... | collective-permute-start | bytes 49160 | tf_op jit(solution)/shard_map/ppermute | solution.py:432
  9.3 3.9 %collective-permute-start.4 = (f32[32,128]{1,0:T(8,128)S(1)}, f32[32,128]{1,0:T(8,128)S(1)}, u32[]{:S(2)}, u32[]{:S(2)}) collective-permute-start(f32[32,128]{1,0:T(8,128)S(1)} %get-tuple-element.34), channel_id=1, source_target_pairs={{0,2},{1,3},{2,0},{3,1},{4,6},{5,7},{6,4},{7,5},{8,10},{9,11},{10,... | collective-permute-start | bytes 49160 | tf_op jit(solution)/shard_map/ppermute | solution.py:432
  10.5 2.6 %collective-permute-start.5 = (f32[32,128]{1,0:T(8,128)S(1)}, f32[32,128]{1,0:T(8,128)S(1)}, u32[]{:S(2)}, u32[]{:S(2)}) collective-permute-start(f32[32,128]{1,0:T(8,128)S(1)} %get-tuple-element.35), channel_id=1, source_target_pairs={{0,1},{1,0},{2,3},{3,2},{4,5},{5,4},{6,7},{7,6},{8,9},{9,8},{10,11... | collective-permute-start | bytes 49160 | tf_op jit(solution)/shard_map/ppermute | solution.py:432
  14.5 6.5 %collective-permute-start.7 = (f32[32,128]{1,0:T(8,128)S(1)}, f32[32,128]{1,0:T(8,128)S(1)}, u32[]{:S(2)}, u32[]{:S(2)}) collective-permute-start(f32[32,128]{1,0:T(8,128)S(1)} %get-tuple-element.36.field_ref.image_ref), channel_id=1, source_target_pairs={{0,4},{4,8},{8,12},{12,16},{16,20},{20,24},{24,28},{28,0},{1,5},{5... | collective-permute-start | bytes 49160 | tf_op jit(solution)/shard_map/ppermute | solution.py:427
  17.7 7.0 %collective-permute-start.6 = (f32[32,128]{1,0:T(8,128)S(1)}, f32[32,128]{1,0:T(8,128)S(1)}, u32[]{:S(2)}, u32[]{:S(2)}) collective-permute-start(f32[32,128]{1,0:T(8,128)S(1)} %get-tuple-element.43), channel_id=1, source_target_pairs={{0,28},{4,0},{8,4},{12,8},{16,12},{20,16},{24,20},{28,24},{1,29},{... | collective-permute-start | bytes 49160 | tf_op jit(solution)/shard_map/ppermute | solution.py:427
  22.1 9.6 %all-to-all-start = ((f32[32,1,128]{2,1,0:T(1,128)}), f32[32,1,128]{2,1,0:T(1,128)S(1)}, u32[]{:S(2)}, u32[]{:S(2)}) async-start(f32[32,1,128]{2,1,0:T(1,128)} %get-tuple-element.47), calls=%async_computation | async-start | bytes 32768 | tf_op jit(solution)/shard_map/all_to_all | solution.py:547

commit v21 on v20

--- a/solution.py
+++ b/solution.py
@@ -224,9 +224,8 @@
         ends, jnp.concatenate([total[block_rows:], folded], axis=0), block_rows
     )
     if len(refs) > 1:
-        aligned_ref, _, copy_ref, east_ref, west_ref = refs
+        aligned_ref, _, copy_ref, west_ref = refs
         copy_ref[...] = field
-        gather_traces(field, aligned_ref, 0, east_ref)
         gather_traces(field, aligned_ref, west_ref.shape[0], west_ref)
 
 
@@ -362,15 +361,17 @@
     product_ref,
     weights_east_ref,
     weights_west_ref,
-    east_ref,
+    image_ref,
     west_ref,
     rows_ref,
     next_ref,
     from_last_ref,
     second_ref,
+    east_ref,
     from_next_ref,
 ):
     block_rows = product_ref.shape[0]
+    gather_traces(image_ref[...], aligned_ref, 0, east_ref)
     gather_traces(next_ref[...], rows_ref, 0, from_next_ref)
     second_ref[...] = product_ref[...]
     second_ref[:, :size] = second_ref[:, :size] + spread_jumps(
@@ -389,11 +390,11 @@
 
 def final_kernel(field_ref, image_ref, second_ref, sums_ref, solution_ref, residual_ref):
     size = solution_ref.shape[1]
-    row = jnp.sum(sums_ref[...], axis=0)
-    lane = lax.broadcasted_iota(jnp.int32, (1, LANES), 1)
+    row = jnp.broadcast_to(jnp.sum(sums_ref[...], axis=0), (SUBLANES, LANES))
 
     def entry(k):
-        return jnp.sum(jnp.where(lane == k, row, 0.0), axis=1, keepdims=True)
+        place = jnp.full((SUBLANES, LANES), k, jnp.int32)
+        return jnp.take_along_axis(row, place, axis=1, mode="promise_in_bounds")[:1, :size]
 
     bb, bq, qq, bw, qw = (entry(k) for k in range(5))
     field = field_ref[:, :size]
@@ -489,7 +490,7 @@
     def stiff(vector, *ordered):
         return call(
             functools.partial(stiffness_kernel, size),
-            [shape(block_rows)] * (1 + len(ordered)) + [shape(faces)] * (2 * len(ordered)),
+            [shape(block_rows)] * (1 + len(ordered)) + [shape(faces)] * len(ordered),
             [(value, VMEM) for value in (pairs, blocks, vector, *ordered)],
         )
 
@@ -514,7 +515,7 @@
         ],
     )
     from_last = from_behind(image, "sub", 1)
-    product, copied, east, west = stiff(image, aligned)
+    product, copied, west = stiff(image, aligned)
     from_next = from_behind(copied, "sub", -1)
     sums, arrived = call(
         sums_kernel,
@@ -534,14 +535,14 @@
                 product,
                 weights_east,
                 weights_west,
-                east,
+                image,
                 west,
                 next_rows,
                 from_next,
                 arrived,
             )
         ],
-        scratch=[pltpu.VMEM((faces, LANES), F32)],
+        scratch=[pltpu.VMEM((faces, LANES), F32)] * 2,
         flops=1_000_000_000,
     )
     sums = lax.all_to_all(sums, ("sub", "blk"), split_axis=0, concat_axis=0, tiled=True)

time: 32.7 us -> 32.7 us (level)
  no operation moved by 1% of the time
where the time goes in v21:
time: 32.7 us; the launch traced here: 32.4 us
  starting transfers between devices  15.4 us (47%)
  Pallas kernels  7.47 us (23%)
  waiting for transfers between devices  6.65 us (20%)
  other arithmetic  2.2 us (7%)
  between operations  0.73 us (2%)
    ppermute x3, starting transfers between devices, from_behind(): return lax.ppermute(value, axis, pairs)  7.85 us
    pallas_call x8, Pallas kernels, call(): pl.pallas_call(body, out_shape=outs, in_specs=[spec for _, spec in inputs...  7.47 us
    all_to_all x1, waiting for transfers between devices, on_device(): lax.all_to_all(sums, ('sub', 'blk'), split_axis=0, concat_axis=0, tiled=T...  5.74 us
    ppermute x2, starting transfers between devices, swap(): return lax.ppermute(value, 'sub', pairs)  3.12 us
    all_to_all x1, starting transfers between devices, on_device(): lax.all_to_all(sums, ('sub', 'blk'), split_axis=0, concat_axis=0, tiled=T...  2.54 us
    ppermute x3, starting transfers between devices, swap_slots(): lax.ppermute(value, 'blk', [(slot, slot ^ k) for slot in range(count)])  1.88 us
    convert_element_type x1, other arithmetic, on_device(): blocks = stiffness[0, 0].astype(F32)  1.28 us
    add x1, other arithmetic, on_device(): indices.astype(F32) + placed(field, 2 * faces)  0.92 us
  transfers between devices with their start and end apart: 9, of which 4 were waited for; matrix products, arithmetic and copies ran while one was open for 7% of the time, Pallas kernels for 17%

profile of v21, /device:TPU:0, one launch (start us, length us, event | category | flops | bytes accessed | tf_op | source)
XLA Modules:
  0.0 32.4 jit_solution(2790654326894668780)
XLA Ops:
  0.6 3.0 %collective-permute-start = (f32[4,16,128]{2,1,0:T(8,128)}, f32[4,16,128]{2,1,0:T(8,128)S(1)}, u32[]{:S(2)}, u32[]{:S(2)}) collective-permute-start(f32[4,16,128]{2,1,0:T(8,128)} %bitcast.21), channel_id=1, source_target_pairs={{0,4},{4,8},{8,12},{12,16},{16,20},{20,24},{24,28},{28,0},{1,5},{5... | collective-permute-start | bytes 98312 | tf_op jit(solution)/shard_map/ppermute | solution.py:428
  3.7 0.9 %pad_add_fusion.packed_ref = f32[232,128]{1,0:T(8,128)S(1)} fusion(f32[64,128]{1,0:T(8,128)} %bitcast.22, f32[32,96]{1,0:T(8,128)} %bitcast.23, s32[1,4]{1,0:T(1,128)} %bitcast.24, s32[1,64]{1,0:T(1,128)} %bitcast.25, s32[128,128]{1,0:T(8,128)} %bitcast.20), kind=kLoop, calls=%fused_computation.1 | loop fusion | flops 148480 | bytes 229648 | tf_op jit(solution)/shard_map/add | solution.py:459
  4.6 0.8 %shard_map.86 = (s32[128,128]{1,0:T(8,128)S(1)}, f32[32,128]{1,0:T(8,128)S(1)}, f32[8,128]{1,0:T(8,128)S(1)}, f32[64,128]{1,0:T(8,128)S(1)}, f32[64,128]{1,0:T(8...) custom-call(f32[232,128]{1,0:T(8,128)S(1)} %pad_add_fusion.packed_ref), custom_call_target="tpu_custom_call" | custom-call | flops 1000000 | bytes 1000000 | tf_op jit(solution)/shard_map/pallas_call | solution.py:19
  5.4 3.1 %collective-permute-start.1 = (f32[136,128]{1,0:T(8,128)S(1)}, f32[136,128]{1,0:T(8,128)S(1)}, u32[]{:S(2)}, u32[]{:S(2)}) collective-permute-start(f32[136,128]{1,0:T(8,128)S(1)} %get-tuple-element.30), channel_id=1, source_target_pairs={{4,8},{8,4},{12,16},{16,12},{20,24},{24,20},{28,0},{0,28},{5,9},{9... | collective-permute-start | bytes 208904 | tf_op jit(solution)/shard_map/ppermute | solution.py:422
  8.5 0.0 collective-permute-start.2
  8.5 0.3 collective-permute-done.last_ref
  8.8 0.5 %collective-permute-start.3 = (f32[32,128]{1,0:T(8,128)S(1)}, f32[32,128]{1,0:T(8,128)S(1)}, u32[]{:S(2)}, u32[]{:S(2)}) collective-permute-start(f32[32,128]{1,0:T(8,128)S(1)} %get-tuple-element.32), channel_id=1, source_target_pairs={{0,3},{1,2},{2,1},{3,0},{4,7},{5,6},{6,5},{7,4},{8,11},{9,10},{10,... | collective-permute-start | bytes 49160 | tf_op jit(solution)/shard_map/ppermute | solution.py:433
  9.3 1.3 %collective-permute-start.4 = (f32[32,128]{1,0:T(8,128)S(1)}, f32[32,128]{1,0:T(8,128)S(1)}, u32[]{:S(2)}, u32[]{:S(2)}) collective-permute-start(f32[32,128]{1,0:T(8,128)S(1)} %get-tuple-element.33), channel_id=1, source_target_pairs={{0,2},{1,3},{2,0},{3,1},{4,6},{5,7},{6,4},{7,5},{8,10},{9,11},{10,... | collective-permute-start | bytes 49160 | tf_op jit(solution)/shard_map/ppermute | solution.py:433
  10.5 0.2 collective-permute-start.5
  10.7 1.3 %bitcast_convert_fusion.blocks_ref = f32[48,9216]{1,0:T(8,128)S(1)} fusion(bf16[1,1,48,9216]{3,2,1,0:T(8,128)(2,1)} %param.8), kind=kLoop, calls=%fused_computation | loop fusion | flops 442368 | bytes 2654208 | tf_op jit(solution)/shard_map/convert_element_type | solution.py:441
  12.0 1.1 %shard_map.87.product_ref = f32[32,128]{1,0:T(8,128)S(1)} custom-call(s32[2,16]{1,0:T(2,128)S(1)} %bitcast.18, f32[48,9216]{1,0:T(8,128)S(1)} %bitcast_convert_fusion.blocks_ref, f32[32,128]{1,0:T(8,128)S(1)} %get-tuple-element.25.field_ref), custom_call_target="tpu_custom_call" | custom-call | flops 1000000 | bytes 1000000 | tf_op jit(solution)/shard_map/pallas_call | solution.py:19
  13.1 0.0 collective-permute-done.3.refs_0_
  13.1 0.0 collective-permute-done.5.refs_2_
  13.1 0.2 collective-permute-done.2.from_b_ref
  13.3 1.2 %shard_map.89 = (f32[32,128]{1,0:T(8,128)S(1)}, f32[64,128]{1,0:T(8,128)S(1)}, f32[64,128]{1,0:T(8,128)S(1)}, f32[64,128]{1,0:T(8,128)S(1)}, s32[64,128]{1,0:T(8,128)S(1)}, /*index=5*/s32[64,128]{1,0:T(8,128)S(1)}) custom-call(f32[232,128]{1,0:T(8,128)S(1)} %pad_add_fusion.packed_ref, f32[4,16,128]{2,1,0:T(8,128)S(1)} %collective-permute-done.last_ref, ...), custom_call_target="tpu_custom_call" | custom-call | flops 1000000 | bytes 1000000 | tf_op jit(solution)/shard_map/pallas_call | solution.py:19
  14.5 1.7 %collective-permute-start.7 = (f32[32,128]{1,0:T(8,128)S(1)}, f32[32,128]{1,0:T(8,128)S(1)}, u32[]{:S(2)}, u32[]{:S(2)}) collective-permute-start(f32[32,128]{1,0:T(8,128)S(1)} %get-tuple-element.35.field_ref.image_ref), channel_id=1, source_target_pairs={{0,4},{4,8},{8,12},{12,16},{16,20},{20,24},{24,28},{28,0},{1,5},{5... | collective-permute-start | bytes 49160 | tf_op jit(solution)/shard_map/ppermute | solution.py:428
  16.2 1.2 %shard_map.90 = (f32[32,128]{1,0:T(8,128)S(1)}, f32[32,128]{1,0:T(8,128)S(1)}, f32[64,128]{1,0:T(8,128)S(1)}) custom-call(s32[2,16]{1,0:T(2,128)S(1)} %bitcast.19, f32[48,9216]{1,0:T(8,128)S(1)} %bitcast_convert_fusion.blocks_ref, f32[32,128]{1,0:T(8,128)S(1)} %get-tuple-element.35.field_ref.image_ref, s32[128,128]{1,0:T(8,128)S(1)} %get-tuple-element.27.aligned_ref.refs_0_), custom_call_target="tpu_custom_call" | custom-call | flops 1000000 | bytes 1000000 | tf_op jit(solution)/shard_map/pallas_call | solution.py:19
  17.4 3.1 %collective-permute-start.6 = (f32[32,128]{1,0:T(8,128)S(1)}, f32[32,128]{1,0:T(8,128)S(1)}, u32[]{:S(2)}, u32[]{:S(2)}) collective-permute-start(f32[32,128]{1,0:T(8,128)S(1)} %get-tuple-element.41), channel_id=1, source_target_pairs={{0,28},{4,0},{8,4},{12,8},{16,12},{20,16},{24,20},{28,24},{1,29},{... | collective-permute-start | bytes 49160 | tf_op jit(solution)/shard_map/ppermute | solution.py:428
  20.5 0.5 %collective-permute-done.7.last_ref = f32[32,128]{1,0:T(8,128)S(1)} collective-permute-done((f32[32,128]{1,0:T(8,128)S(1)}, f32[32,128]{1,0:T(8,128)S(1)}, u32[]{:S(2)}, u32[]{:S(2)}) %collective-permute-start.7) | collective-permute-done | bytes 16416 | tf_op jit(solution)/shard_map/ppermute | solution.py:428
  21.0 1.1 %shard_map.91 = (f32[32,1,128]{2,1,0:T(1,128)}, f32[64,128]{1,0:T(8,128)S(1)}) custom-call(f32[32,128]{1,0:T(8,128)S(1)} %get-tuple-element.36.product_ref, f32[64,128]{1,0:T(8,128)S(1)} %get-tuple-element.38.weights_ref.weights_west_ref, f32[64,128]{1,0:T(8,128)S(1)} %get-tuple-element.39.own_ref.west_ref, s32[64,128]{1,0:T(8,128)S(1)} %get-tuple-element.42.rows_ref, ...), custom_call_target="tpu_custom_call" | custom-call | flops 1000000 | bytes 1000000 | tf_op jit(solution)/shard_map/pallas_call | solution.py:19
  22.1 2.5 %all-to-all-start = ((f32[32,1,128]{2,1,0:T(1,128)}), f32[32,1,128]{2,1,0:T(1,128)S(1)}, u32[]{:S(2)}, u32[]{:S(2)}) async-start(f32[32,1,128]{2,1,0:T(1,128)} %get-tuple-element.45), calls=%async_computation | async-start | bytes 32768 | tf_op jit(solution)/shard_map/all_to_all | solution.py:548
  24.6 1.3 %shard_map.92.second_ref = f32[32,128]{1,0:T(8,128)S(1)} custom-call(s32[128,128]{1,0:T(8,128)S(1)} %get-tuple-element.27.aligned_ref.refs_0_, f32[32,128]{1,0:T(8,128)S(1)} %get-tuple-element.36.product_ref, f32[64,128]{1,0:T(8,128)S(1)} %get-tuple-element.37.weights_east_ref, f32[64,128]{1,0:T(8,128)S(1)} %get-tuple-element.38.weights_ref.weights_west_ref, ...), custom_call_target="tpu_custom_call" | custom-call | flops 1000000000 | bytes 1000000 | tf_op jit(solution)/shard_map/pallas_call | solution.py:19
  26.0 5.7 %all-to-all-done.sums_ref = f32[32,1,128]{2,1,0:T(1,128)S(1)} async-done(((f32[32,1,128]{2,1,0:T(1,128)}), f32[32,1,128]{2,1,0:T(1,128)S(1)}, u32[]{:S(2)}, u32[]{:S(2)}) %all-to-all-start) | async-done | bytes 16416 | tf_op jit(solution)/shard_map/all_to_all | solution.py:548
  31.7 0.7 %shard_map.93 = (f32[32,96]{1,0:T(8,128)}, f32[32,96]{1,0:T(8,128)}) custom-call(f32[32,128]{1,0:T(8,128)S(1)} %get-tuple-element.25.field_ref, f32[32,128]{1,0:T(8,128)S(1)} %get-tuple-element.35.field_ref.image_ref, f32[32,128]{1,0:T(8,128)S(1)} %shard_map.92.second_ref, f32[32,1,128]{2,1,0:T(1,128)S(1)} %all-to-all-done.sums_ref), custom_call_target="tpu_custom_call" | custom-call | flops 1000000 | bytes 1000000 | tf_op jit(solution)/shard_map/pallas_call | solution.py:19
  (6 shorter events, 0.0 us)
Async XLA Ops:
  0.6 11.3 %copy-start = (s32[1,1,2,16]{3,2,1,0:T(2,128)S(1)}, s32[1,1,2,16]{3,2,1,0:T(2,128)}, u32[]{:S(2)}) copy-start(s32[1,1,2,16]{3,2,1,0:T(2,128)} %param.9) | copy-start | bytes 388
  0.6 8.2 %collective-permute-start = (f32[4,16,128]{2,1,0:T(8,128)}, f32[4,16,128]{2,1,0:T(8,128)S(1)}, u32[]{:S(2)}, u32[]{:S(2)}) collective-permute-start(f32[4,16,128]{2,1,0:T(8,128)} %bitcast.21), channel_id=1, source_target_pairs={{0,4},{4,8},{8,12},{12,16},{16,20},{20,24},{24,28},{28,0},{1,5},{5... | collective-permute-start | bytes 98312 | tf_op jit(solution)/shard_map/ppermute | solution.py:428
  5.4 7.7 %collective-permute-start.1 = (f32[136,128]{1,0:T(8,128)S(1)}, f32[136,128]{1,0:T(8,128)S(1)}, u32[]{:S(2)}, u32[]{:S(2)}) collective-permute-start(f32[136,128]{1,0:T(8,128)S(1)} %get-tuple-element.30), channel_id=1, source_target_pairs={{4,8},{8,4},{12,16},{16,12},{20,24},{24,20},{28,0},{0,28},{5,9},{9... | collective-permute-start | bytes 208904 | tf_op jit(solution)/shard_map/ppermute | solution.py:422
  8.5 4.8 %collective-permute-start.2 = (f32[136,128]{1,0:T(8,128)S(1)}, f32[136,128]{1,0:T(8,128)S(1)}, u32[]{:S(2)}, u32[]{:S(2)}) collective-permute-start(f32[136,128]{1,0:T(8,128)S(1)} %get-tuple-element.31), channel_id=1, source_target_pairs={{0,4},{4,0},{8,12},{12,8},{16,20},{20,16},{24,28},{28,24},{1,5},{5... | collective-permute-start | bytes 208904 | tf_op jit(solution)/shard_map/ppermute | solution.py:422
  8.8 4.3 %collective-permute-start.3 = (f32[32,128]{1,0:T(8,128)S(1)}, f32[32,128]{1,0:T(8,128)S(1)}, u32[]{:S(2)}, u32[]{:S(2)}) collective-permute-start(f32[32,128]{1,0:T(8,128)S(1)} %get-tuple-element.32), channel_id=1, source_target_pairs={{0,3},{1,2},{2,1},{3,0},{4,7},{5,6},{6,5},{7,4},{8,11},{9,10},{10,... | collective-permute-start | bytes 49160 | tf_op jit(solution)/shard_map/ppermute | solution.py:433
  9.3 3.9 %collective-permute-start.4 = (f32[32,128]{1,0:T(8,128)S(1)}, f32[32,128]{1,0:T(8,128)S(1)}, u32[]{:S(2)}, u32[]{:S(2)}) collective-permute-start(f32[32,128]{1,0:T(8,128)S(1)} %get-tuple-element.33), channel_id=1, source_target_pairs={{0,2},{1,3},{2,0},{3,1},{4,6},{5,7},{6,4},{7,5},{8,10},{9,11},{10,... | collective-permute-start | bytes 49160 | tf_op jit(solution)/shard_map/ppermute | solution.py:433
  10.5 2.6 %collective-permute-start.5 = (f32[32,128]{1,0:T(8,128)S(1)}, f32[32,128]{1,0:T(8,128)S(1)}, u32[]{:S(2)}, u32[]{:S(2)}) collective-permute-start(f32[32,128]{1,0:T(8,128)S(1)} %get-tuple-element.34), channel_id=1, source_target_pairs={{0,1},{1,0},{2,3},{3,2},{4,5},{5,4},{6,7},{7,6},{8,9},{9,8},{10,11... | collective-permute-start | bytes 49160 | tf_op jit(solution)/shard_map/ppermute | solution.py:433
  14.5 6.5 %collective-permute-start.7 = (f32[32,128]{1,0:T(8,128)S(1)}, f32[32,128]{1,0:T(8,128)S(1)}, u32[]{:S(2)}, u32[]{:S(2)}) collective-permute-start(f32[32,128]{1,0:T(8,128)S(1)} %get-tuple-element.35.field_ref.image_ref), channel_id=1, source_target_pairs={{0,4},{4,8},{8,12},{12,16},{16,20},{20,24},{24,28},{28,0},{1,5},{5... | collective-permute-start | bytes 49160 | tf_op jit(solution)/shard_map/ppermute | solution.py:428
  17.4 7.2 %collective-permute-start.6 = (f32[32,128]{1,0:T(8,128)S(1)}, f32[32,128]{1,0:T(8,128)S(1)}, u32[]{:S(2)}, u32[]{:S(2)}) collective-permute-start(f32[32,128]{1,0:T(8,128)S(1)} %get-tuple-element.41), channel_id=1, source_target_pairs={{0,28},{4,0},{8,4},{12,8},{16,12},{20,16},{24,20},{28,24},{1,29},{... | collective-permute-start | bytes 49160 | tf_op jit(solution)/shard_map/ppermute | solution.py:428
  22.1 9.6 %all-to-all-start = ((f32[32,1,128]{2,1,0:T(1,128)}), f32[32,1,128]{2,1,0:T(1,128)S(1)}, u32[]{:S(2)}, u32[]{:S(2)}) async-start(f32[32,1,128]{2,1,0:T(1,128)} %get-tuple-element.45), calls=%async_computation | async-start | bytes 32768 | tf_op jit(solution)/shard_map/all_to_all | solution.py:548

commit v22 on v21

--- a/solution.py
+++ b/solution.py
@@ -11,6 +11,10 @@
 LANES = 128
 SUBLANES = 8
 VMEM = pl.BlockSpec(memory_space=pltpu.VMEM)
+MARK = 5
+LARGE = 2.0**40
+SMALL = 2.0**-40
+SHRINK = 2.0**-60
 F32 = jnp.float32
 BF16 = jnp.bfloat16
 
@@ -334,24 +338,33 @@
     sums_ref,
     arrived_ref,
 ):
-    field = field_ref[...]
-    image = image_ref[...]
-    product = product_ref[...]
     gather_traces(last_ref[...], rows_ref, 0, arrived_ref)
-    jump = own_ref[...] - arrived_ref[...]
+    largest = jnp.maximum(jnp.abs(field_ref[...]), jnp.abs(image_ref[...]))
+    for value in (arrived_ref[...], jump_ref[...]):
+        value = jnp.abs(value)
+        for k in range(0, value.shape[0], largest.shape[0]):
+            largest = jnp.maximum(largest, value[k : k + largest.shape[0]])
+    largest = jnp.max(jnp.max(largest, axis=0, keepdims=True), axis=1, keepdims=True)
+    level = jnp.where(largest > LARGE, 0, jnp.where(largest < SMALL, 2, 1))
+    scale = jnp.where(largest > LARGE, SHRINK, jnp.where(largest < SMALL, 1.0 / SHRINK, 1.0))
+    field = field_ref[...] * scale
+    image = image_ref[...] * scale
+    product = product_ref[...] * scale
+    jump = own_ref[...] * scale - arrived_ref[...] * scale
     lam = weights_ref[...] * jump
     parts = [
         column_sums(field * field),
         column_sums(field * image),
         column_sums(image * image),
-        column_sums(field * product) + column_sums(lam * jump_ref[...]),
+        column_sums(field * product) + column_sums(lam * (jump_ref[...] * scale)),
         column_sums(image * product) + column_sums(lam * jump),
     ]
     parts += [jnp.zeros_like(parts[0])] * (SUBLANES - len(parts))
     whole = jnp.sum(jnp.concatenate(parts, axis=0), axis=1, keepdims=True)
     row = lax.broadcasted_iota(jnp.int32, (SUBLANES, LANES), 0)
     lane = lax.broadcasted_iota(jnp.int32, (SUBLANES, LANES), 1)
-    packed = column_sums(jnp.where(lane == row, whole, 0.0))
+    whole = jnp.where(row == MARK, 1.0, whole)
+    packed = column_sums(jnp.where(lane == row + SUBLANES * level, whole, 0.0))
     sums_ref[...] = jnp.broadcast_to(packed[None], sums_ref.shape)
 
 
@@ -392,9 +405,20 @@
     size = solution_ref.shape[1]
     row = jnp.broadcast_to(jnp.sum(sums_ref[...], axis=0), (SUBLANES, LANES))
 
-    def entry(k):
+    def lane(k):
         place = jnp.full((SUBLANES, LANES), k, jnp.int32)
         return jnp.take_along_axis(row, place, axis=1, mode="promise_in_bounds")[:1, :size]
+
+    large, plain = (lane(SUBLANES * level + MARK) > 0.0 for level in (0, 1))
+
+    def entry(k):
+        sums = [lane(SUBLANES * level + k) for level in range(3)]
+        lower = SHRINK * SHRINK
+        return jnp.where(
+            large,
+            sums[0] + sums[1] * lower,
+            jnp.where(plain, sums[1] + sums[2] * lower, sums[2]),
+        )
 
     bb, bq, qq, bw, qw = (entry(k) for k in range(5))
     field = field_ref[:, :size]

time: 32.7 us -> 32.9 us (level)
  transfers between devices with their start and end apart: 9 -> 9, of which waited for: 4 -> 4; matrix products, arithmetic and copies ran while one was open for 7% -> 7% of each run, Pallas kernels for 17% -> 18%
where the time goes in v22:
time: 32.9 us; the launch traced here: 32.6 us
  starting transfers between devices  15.4 us (47%)
  Pallas kernels  7.68 us (23%)
  waiting for transfers between devices  6.65 us (20%)
  other arithmetic  2.2 us (7%)
  between operations  0.73 us (2%)
    ppermute x3, starting transfers between devices, from_behind(): return lax.ppermute(value, axis, pairs)  7.85 us
    pallas_call x8, Pallas kernels, call(): pl.pallas_call(body, out_shape=outs, in_specs=[spec for _, spec in inputs...  7.68 us
    all_to_all x1, waiting for transfers between devices, on_device(): lax.all_to_all(sums, ('sub', 'blk'), split_axis=0, concat_axis=0, tiled=T...  5.74 us
    ppermute x2, starting transfers between devices, swap(): return lax.ppermute(value, 'sub', pairs)  3.12 us
    all_to_all x1, starting transfers between devices, on_device(): lax.all_to_all(sums, ('sub', 'blk'), split_axis=0, concat_axis=0, tiled=T...  2.54 us
    ppermute x3, starting transfers between devices, swap_slots(): lax.ppermute(value, 'blk', [(slot, slot ^ k) for slot in range(count)])  1.88 us
    convert_element_type x1, other arithmetic, on_device(): blocks = stiffness[0, 0].astype(F32)  1.28 us
    add x1, other arithmetic, on_device(): indices.astype(F32) + placed(field, 2 * faces)  0.92 us
  transfers between devices with their start and end apart: 9, of which 4 were waited for; matrix products, arithmetic and copies ran while one was open for 7% of the time, Pallas kernels for 18%

profile of v22, /device:TPU:0, one launch (start us, length us, event | category | flops | bytes accessed | tf_op | source)
XLA Modules:
  0.0 32.6 jit_solution(12099761769348725139)
XLA Ops:
  0.6 3.0 %collective-permute-start = (f32[4,16,128]{2,1,0:T(8,128)}, f32[4,16,128]{2,1,0:T(8,128)S(1)}, u32[]{:S(2)}, u32[]{:S(2)}) collective-permute-start(f32[4,16,128]{2,1,0:T(8,128)} %bitcast.21), channel_id=1, source_target_pairs={{0,4},{4,8},{8,12},{12,16},{16,20},{20,24},{24,28},{28,0},{1,5},{5... | collective-permute-start | bytes 98312 | tf_op jit(solution)/shard_map/ppermute | solution.py:452
  3.7 0.9 %pad_add_fusion.packed_ref = f32[232,128]{1,0:T(8,128)S(1)} fusion(f32[64,128]{1,0:T(8,128)} %bitcast.22, f32[32,96]{1,0:T(8,128)} %bitcast.23, s32[1,4]{1,0:T(1,128)} %bitcast.24, s32[1,64]{1,0:T(1,128)} %bitcast.25, s32[128,128]{1,0:T(8,128)} %bitcast.20), kind=kLoop, calls=%fused_computation.1 | loop fusion | flops 148480 | bytes 229648 | tf_op jit(solution)/shard_map/add | solution.py:483
  4.6 0.8 %shard_map.86 = (s32[128,128]{1,0:T(8,128)S(1)}, f32[32,128]{1,0:T(8,128)S(1)}, f32[8,128]{1,0:T(8,128)S(1)}, f32[64,128]{1,0:T(8,128)S(1)}, f32[64,128]{1,0:T(8...) custom-call(f32[232,128]{1,0:T(8,128)S(1)} %pad_add_fusion.packed_ref), custom_call_target="tpu_custom_call" | custom-call | flops 1000000 | bytes 1000000 | tf_op jit(solution)/shard_map/pallas_call | solution.py:23
  5.4 3.1 %collective-permute-start.1 = (f32[136,128]{1,0:T(8,128)S(1)}, f32[136,128]{1,0:T(8,128)S(1)}, u32[]{:S(2)}, u32[]{:S(2)}) collective-permute-start(f32[136,128]{1,0:T(8,128)S(1)} %get-tuple-element.30), channel_id=1, source_target_pairs={{4,8},{8,4},{12,16},{16,12},{20,24},{24,20},{28,0},{0,28},{5,9},{9... | collective-permute-start | bytes 208904 | tf_op jit(solution)/shard_map/ppermute | solution.py:446
  8.5 0.0 collective-permute-start.2
  8.5 0.3 collective-permute-done.last_ref
  8.8 0.5 %collective-permute-start.3 = (f32[32,128]{1,0:T(8,128)S(1)}, f32[32,128]{1,0:T(8,128)S(1)}, u32[]{:S(2)}, u32[]{:S(2)}) collective-permute-start(f32[32,128]{1,0:T(8,128)S(1)} %get-tuple-element.32), channel_id=1, source_target_pairs={{0,3},{1,2},{2,1},{3,0},{4,7},{5,6},{6,5},{7,4},{8,11},{9,10},{10,... | collective-permute-start | bytes 49160 | tf_op jit(solution)/shard_map/ppermute | solution.py:457
  9.3 1.3 %collective-permute-start.4 = (f32[32,128]{1,0:T(8,128)S(1)}, f32[32,128]{1,0:T(8,128)S(1)}, u32[]{:S(2)}, u32[]{:S(2)}) collective-permute-start(f32[32,128]{1,0:T(8,128)S(1)} %get-tuple-element.33), channel_id=1, source_target_pairs={{0,2},{1,3},{2,0},{3,1},{4,6},{5,7},{6,4},{7,5},{8,10},{9,11},{10,... | collective-permute-start | bytes 49160 | tf_op jit(solution)/shard_map/ppermute | solution.py:457
  10.5 0.2 collective-permute-start.5
  10.7 1.3 %bitcast_convert_fusion.blocks_ref = f32[48,9216]{1,0:T(8,128)S(1)} fusion(bf16[1,1,48,9216]{3,2,1,0:T(8,128)(2,1)} %param.8), kind=kLoop, calls=%fused_computation | loop fusion | flops 442368 | bytes 2654208 | tf_op jit(solution)/shard_map/convert_element_type | solution.py:465
  12.0 1.1 %shard_map.87.product_ref = f32[32,128]{1,0:T(8,128)S(1)} custom-call(s32[2,16]{1,0:T(2,128)S(1)} %bitcast.18, f32[48,9216]{1,0:T(8,128)S(1)} %bitcast_convert_fusion.blocks_ref, f32[32,128]{1,0:T(8,128)S(1)} %get-tuple-element.25.field_ref), custom_call_target="tpu_custom_call" | custom-call | flops 1000000 | bytes 1000000 | tf_op jit(solution)/shard_map/pallas_call | solution.py:23
  13.1 0.0 collective-permute-done.3.refs_0_
  13.1 0.0 collective-permute-done.5.refs_2_
  13.1 0.2 collective-permute-done.2.from_b_ref
  13.3 1.2 %shard_map.89 = (f32[32,128]{1,0:T(8,128)S(1)}, f32[64,128]{1,0:T(8,128)S(1)}, f32[64,128]{1,0:T(8,128)S(1)}, f32[64,128]{1,0:T(8,128)S(1)}, s32[64,128]{1,0:T(8,128)S(1)}, /*index=5*/s32[64,128]{1,0:T(8,128)S(1)}) custom-call(f32[232,128]{1,0:T(8,128)S(1)} %pad_add_fusion.packed_ref, f32[4,16,128]{2,1,0:T(8,128)S(1)} %collective-permute-done.last_ref, ...), custom_call_target="tpu_custom_call" | custom-call | flops 1000000 | bytes 1000000 | tf_op jit(solution)/shard_map/pallas_call | solution.py:23
  14.5 1.7 %collective-permute-start.7 = (f32[32,128]{1,0:T(8,128)S(1)}, f32[32,128]{1,0:T(8,128)S(1)}, u32[]{:S(2)}, u32[]{:S(2)}) collective-permute-start(f32[32,128]{1,0:T(8,128)S(1)} %get-tuple-element.35.field_ref.image_ref), channel_id=1, source_target_pairs={{0,4},{4,8},{8,12},{12,16},{16,20},{20,24},{24,28},{28,0},{1,5},{5... | collective-permute-start | bytes 49160 | tf_op jit(solution)/shard_map/ppermute | solution.py:452
  16.2 1.2 %shard_map.90 = (f32[32,128]{1,0:T(8,128)S(1)}, f32[32,128]{1,0:T(8,128)S(1)}, f32[64,128]{1,0:T(8,128)S(1)}) custom-call(s32[2,16]{1,0:T(2,128)S(1)} %bitcast.19, f32[48,9216]{1,0:T(8,128)S(1)} %bitcast_convert_fusion.blocks_ref, f32[32,128]{1,0:T(8,128)S(1)} %get-tuple-element.35.field_ref.image_ref, s32[128,128]{1,0:T(8,128)S(1)} %get-tuple-element.27.aligned_ref.refs_0_), custom_call_target="tpu_custom_call" | custom-call | flops 1000000 | bytes 1000000 | tf_op jit(solution)/shard_map/pallas_call | solution.py:23
  17.4 3.1 %collective-permute-start.6 = (f32[32,128]{1,0:T(8,128)S(1)}, f32[32,128]{1,0:T(8,128)S(1)}, u32[]{:S(2)}, u32[]{:S(2)}) collective-permute-start(f32[32,128]{1,0:T(8,128)S(1)} %get-tuple-element.41), channel_id=1, source_target_pairs={{0,28},{4,0},{8,4},{12,8},{16,12},{20,16},{24,20},{28,24},{1,29},{... | collective-permute-start | bytes 49160 | tf_op jit(solution)/shard_map/ppermute | solution.py:452
  20.5 0.5 %collective-permute-done.7.last_ref = f32[32,128]{1,0:T(8,128)S(1)} collective-permute-done((f32[32,128]{1,0:T(8,128)S(1)}, f32[32,128]{1,0:T(8,128)S(1)}, u32[]{:S(2)}, u32[]{:S(2)}) %collective-permute-start.7) | collective-permute-done | bytes 16416 | tf_op jit(solution)/shard_map/ppermute | solution.py:452
  21.0 1.3 %shard_map.91 = (f32[32,1,128]{2,1,0:T(1,128)}, f32[64,128]{1,0:T(8,128)S(1)}) custom-call(f32[32,128]{1,0:T(8,128)S(1)} %get-tuple-element.36.product_ref, f32[64,128]{1,0:T(8,128)S(1)} %get-tuple-element.38.weights_ref.weights_west_ref, f32[64,128]{1,0:T(8,128)S(1)} %get-tuple-element.39.own_ref.west_ref, s32[64,128]{1,0:T(8,128)S(1)} %get-tuple-element.42.rows_ref, ...), custom_call_target="tpu_custom_call" | custom-call | flops 1000000 | bytes 1000000 | tf_op jit(solution)/shard_map/pallas_call | solution.py:23
  22.3 2.5 %all-to-all-start = ((f32[32,1,128]{2,1,0:T(1,128)}), f32[32,1,128]{2,1,0:T(1,128)S(1)}, u32[]{:S(2)}, u32[]{:S(2)}) async-start(f32[32,1,128]{2,1,0:T(1,128)} %get-tuple-element.45), calls=%async_computation | async-start | bytes 32768 | tf_op jit(solution)/shard_map/all_to_all | solution.py:572
  24.8 1.3 %shard_map.92.second_ref = f32[32,128]{1,0:T(8,128)S(1)} custom-call(s32[128,128]{1,0:T(8,128)S(1)} %get-tuple-element.27.aligned_ref.refs_0_, f32[32,128]{1,0:T(8,128)S(1)} %get-tuple-element.36.product_ref, f32[64,128]{1,0:T(8,128)S(1)} %get-tuple-element.37.weights_east_ref, f32[64,128]{1,0:T(8,128)S(1)} %get-tuple-element.38.weights_ref.weights_west_ref, ...), custom_call_target="tpu_custom_call" | custom-call | flops 1000000000 | bytes 1000000 | tf_op jit(solution)/shard_map/pallas_call | solution.py:23
  26.2 5.7 %all-to-all-done.sums_ref = f32[32,1,128]{2,1,0:T(1,128)S(1)} async-done(((f32[32,1,128]{2,1,0:T(1,128)}), f32[32,1,128]{2,1,0:T(1,128)S(1)}, u32[]{:S(2)}, u32[]{:S(2)}) %all-to-all-start) | async-done | bytes 16416 | tf_op jit(solution)/shard_map/all_to_all | solution.py:572
  31.9 0.8 %shard_map.93 = (f32[32,96]{1,0:T(8,128)}, f32[32,96]{1,0:T(8,128)}) custom-call(f32[32,128]{1,0:T(8,128)S(1)} %get-tuple-element.25.field_ref, f32[32,128]{1,0:T(8,128)S(1)} %get-tuple-element.35.field_ref.image_ref, f32[32,128]{1,0:T(8,128)S(1)} %shard_map.92.second_ref, f32[32,1,128]{2,1,0:T(1,128)S(1)} %all-to-all-done.sums_ref), custom_call_target="tpu_custom_call" | custom-call | flops 1000000 | bytes 1000000 | tf_op jit(solution)/shard_map/pallas_call | solution.py:23
  (6 shorter events, 0.0 us)
Async XLA Ops:
  0.6 11.3 %copy-start = (s32[1,1,2,16]{3,2,1,0:T(2,128)S(1)}, s32[1,1,2,16]{3,2,1,0:T(2,128)}, u32[]{:S(2)}) copy-start(s32[1,1,2,16]{3,2,1,0:T(2,128)} %param.9) | copy-start | bytes 388
  0.6 8.2 %collective-permute-start = (f32[4,16,128]{2,1,0:T(8,128)}, f32[4,16,128]{2,1,0:T(8,128)S(1)}, u32[]{:S(2)}, u32[]{:S(2)}) collective-permute-start(f32[4,16,128]{2,1,0:T(8,128)} %bitcast.21), channel_id=1, source_target_pairs={{0,4},{4,8},{8,12},{12,16},{16,20},{20,24},{24,28},{28,0},{1,5},{5... | collective-permute-start | bytes 98312 | tf_op jit(solution)/shard_map/ppermute | solution.py:452
  5.4 7.7 %collective-permute-start.1 = (f32[136,128]{1,0:T(8,128)S(1)}, f32[136,128]{1,0:T(8,128)S(1)}, u32[]{:S(2)}, u32[]{:S(2)}) collective-permute-start(f32[136,128]{1,0:T(8,128)S(1)} %get-tuple-element.30), channel_id=1, source_target_pairs={{4,8},{8,4},{12,16},{16,12},{20,24},{24,20},{28,0},{0,28},{5,9},{9... | collective-permute-start | bytes 208904 | tf_op jit(solution)/shard_map/ppermute | solution.py:446
  8.5 4.8 %collective-permute-start.2 = (f32[136,128]{1,0:T(8,128)S(1)}, f32[136,128]{1,0:T(8,128)S(1)}, u32[]{:S(2)}, u32[]{:S(2)}) collective-permute-start(f32[136,128]{1,0:T(8,128)S(1)} %get-tuple-element.31), channel_id=1, source_target_pairs={{0,4},{4,0},{8,12},{12,8},{16,20},{20,16},{24,28},{28,24},{1,5},{5... | collective-permute-start | bytes 208904 | tf_op jit(solution)/shard_map/ppermute | solution.py:446
  8.8 4.3 %collective-permute-start.3 = (f32[32,128]{1,0:T(8,128)S(1)}, f32[32,128]{1,0:T(8,128)S(1)}, u32[]{:S(2)}, u32[]{:S(2)}) collective-permute-start(f32[32,128]{1,0:T(8,128)S(1)} %get-tuple-element.32), channel_id=1, source_target_pairs={{0,3},{1,2},{2,1},{3,0},{4,7},{5,6},{6,5},{7,4},{8,11},{9,10},{10,... | collective-permute-start | bytes 49160 | tf_op jit(solution)/shard_map/ppermute | solution.py:457
  9.3 3.9 %collective-permute-start.4 = (f32[32,128]{1,0:T(8,128)S(1)}, f32[32,128]{1,0:T(8,128)S(1)}, u32[]{:S(2)}, u32[]{:S(2)}) collective-permute-start(f32[32,128]{1,0:T(8,128)S(1)} %get-tuple-element.33), channel_id=1, source_target_pairs={{0,2},{1,3},{2,0},{3,1},{4,6},{5,7},{6,4},{7,5},{8,10},{9,11},{10,... | collective-permute-start | bytes 49160 | tf_op jit(solution)/shard_map/ppermute | solution.py:457
  10.5 2.6 %collective-permute-start.5 = (f32[32,128]{1,0:T(8,128)S(1)}, f32[32,128]{1,0:T(8,128)S(1)}, u32[]{:S(2)}, u32[]{:S(2)}) collective-permute-start(f32[32,128]{1,0:T(8,128)S(1)} %get-tuple-element.34), channel_id=1, source_target_pairs={{0,1},{1,0},{2,3},{3,2},{4,5},{5,4},{6,7},{7,6},{8,9},{9,8},{10,11... | collective-permute-start | bytes 49160 | tf_op jit(solution)/shard_map/ppermute | solution.py:457
  14.5 6.5 %collective-permute-start.7 = (f32[32,128]{1,0:T(8,128)S(1)}, f32[32,128]{1,0:T(8,128)S(1)}, u32[]{:S(2)}, u32[]{:S(2)}) collective-permute-start(f32[32,128]{1,0:T(8,128)S(1)} %get-tuple-element.35.field_ref.image_ref), channel_id=1, source_target_pairs={{0,4},{4,8},{8,12},{12,16},{16,20},{20,24},{24,28},{28,0},{1,5},{5... | collective-permute-start | bytes 49160 | tf_op jit(solution)/shard_map/ppermute | solution.py:452
  17.4 7.4 %collective-permute-start.6 = (f32[32,128]{1,0:T(8,128)S(1)}, f32[32,128]{1,0:T(8,128)S(1)}, u32[]{:S(2)}, u32[]{:S(2)}) collective-permute-start(f32[32,128]{1,0:T(8,128)S(1)} %get-tuple-element.41), channel_id=1, source_target_pairs={{0,28},{4,0},{8,4},{12,8},{16,12},{20,16},{24,20},{28,24},{1,29},{... | collective-permute-start | bytes 49160 | tf_op jit(solution)/shard_map/ppermute | solution.py:452
  22.3 9.6 %all-to-all-start = ((f32[32,1,128]{2,1,0:T(1,128)}), f32[32,1,128]{2,1,0:T(1,128)S(1)}, u32[]{:S(2)}, u32[]{:S(2)}) async-start(f32[32,1,128]{2,1,0:T(1,128)} %get-tuple-element.45), calls=%async_computation | async-start | bytes 32768 | tf_op jit(solution)/shard_map/all_to_all | solution.py:572

commit v23 on v22

--- a/solution.py
+++ b/solution.py
@@ -346,25 +346,28 @@
             largest = jnp.maximum(largest, value[k : k + largest.shape[0]])
     largest = jnp.max(jnp.max(largest, axis=0, keepdims=True), axis=1, keepdims=True)
     level = jnp.where(largest > LARGE, 0, jnp.where(largest < SMALL, 2, 1))
-    scale = jnp.where(largest > LARGE, SHRINK, jnp.where(largest < SMALL, 1.0 / SHRINK, 1.0))
-    field = field_ref[...] * scale
-    image = image_ref[...] * scale
-    product = product_ref[...] * scale
-    jump = own_ref[...] * scale - arrived_ref[...] * scale
-    lam = weights_ref[...] * jump
-    parts = [
-        column_sums(field * field),
-        column_sums(field * image),
-        column_sums(image * image),
-        column_sums(field * product) + column_sums(lam * (jump_ref[...] * scale)),
-        column_sums(image * product) + column_sums(lam * jump),
-    ]
-    parts += [jnp.zeros_like(parts[0])] * (SUBLANES - len(parts))
+    parts = []
+    for scale in (SHRINK, 1.0, 1.0 / SHRINK):
+        field = field_ref[...] * scale
+        image = image_ref[...] * scale
+        product = product_ref[...] * scale
+        jump = own_ref[...] * scale - arrived_ref[...] * scale
+        lam = weights_ref[...] * jump
+        parts += [
+            column_sums(field * field),
+            column_sums(field * image),
+            column_sums(image * image),
+            column_sums(field * product) + column_sums(lam * (jump_ref[...] * scale)),
+            column_sums(image * product) + column_sums(lam * jump),
+        ]
+        parts += [jnp.zeros_like(parts[0])] * (SUBLANES - MARK)
     whole = jnp.sum(jnp.concatenate(parts, axis=0), axis=1, keepdims=True)
-    row = lax.broadcasted_iota(jnp.int32, (SUBLANES, LANES), 0)
-    lane = lax.broadcasted_iota(jnp.int32, (SUBLANES, LANES), 1)
-    whole = jnp.where(row == MARK, 1.0, whole)
-    packed = column_sums(jnp.where(lane == row + SUBLANES * level, whole, 0.0))
+    row = lax.broadcasted_iota(jnp.int32, (len(parts), LANES), 0)
+    lane = lax.broadcasted_iota(jnp.int32, (len(parts), LANES), 1)
+    first = SUBLANES * level
+    whole = jnp.where(row == first + MARK, 1.0, whole)
+    chosen = (lane == row) & (row >= first) & (row < first + SUBLANES)
+    packed = column_sums(jnp.where(chosen, whole, 0.0))
     sums_ref[...] = jnp.broadcast_to(packed[None], sums_ref.shape)
 
 

time: 32.9 us -> 32.7 us (level)
  transfers between devices with their start and end apart: 9 -> 9, of which waited for: 4 -> 4; matrix products, arithmetic and copies ran while one was open for 7% -> 7% of each run, Pallas kernels for 18% -> 17%
where the time goes in v23:
time: 32.7 us; the launch traced here: 32.5 us
  starting transfers between devices  15.4 us (47%)
  Pallas kernels  7.49 us (23%)
  waiting for transfers between devices  6.65 us (20%)
  other arithmetic  2.2 us (7%)
  between operations  0.73 us (2%)
    ppermute x3, starting transfers between devices, from_behind(): return lax.ppermute(value, axis, pairs)  7.85 us
    pallas_call x8, Pallas kernels, call(): pl.pallas_call(body, out_shape=outs, in_specs=[spec for _, spec in inputs...  7.49 us
    all_to_all x1, waiting for transfers between devices, on_device(): lax.all_to_all(sums, ('sub', 'blk'), split_axis=0, concat_axis=0, tiled=T...  5.74 us
    ppermute x2, starting transfers between devices, swap(): return lax.ppermute(value, 'sub', pairs)  3.12 us
    all_to_all x1, starting transfers between devices, on_device(): lax.all_to_all(sums, ('sub', 'blk'), split_axis=0, concat_axis=0, tiled=T...  2.54 us
    ppermute x3, starting transfers between devices, swap_slots(): lax.ppermute(value, 'blk', [(slot, slot ^ k) for slot in range(count)])  1.88 us
    convert_element_type x1, other arithmetic, on_device(): blocks = stiffness[0, 0].astype(F32)  1.28 us
    add x1, other arithmetic, on_device(): indices.astype(F32) + placed(field, 2 * faces)  0.92 us
  transfers between devices with their start and end apart: 9, of which 4 were waited for; matrix products, arithmetic and copies ran while one was open for 7% of the time, Pallas kernels for 17%

profile of v23, /device:TPU:0, one launch (start us, length us, event | category | flops | bytes accessed | tf_op | source)
XLA Modules:
  0.0 32.5 jit_solution(13628425102217431859)
XLA Ops:
  0.6 3.0 %collective-permute-start = (f32[4,16,128]{2,1,0:T(8,128)}, f32[4,16,128]{2,1,0:T(8,128)S(1)}, u32[]{:S(2)}, u32[]{:S(2)}) collective-permute-start(f32[4,16,128]{2,1,0:T(8,128)} %bitcast.21), channel_id=1, source_target_pairs={{0,4},{4,8},{8,12},{12,16},{16,20},{20,24},{24,28},{28,0},{1,5},{5... | collective-permute-start | bytes 98312 | tf_op jit(solution)/shard_map/ppermute | solution.py:455
  3.7 0.9 %pad_add_fusion.packed_ref = f32[232,128]{1,0:T(8,128)S(1)} fusion(f32[64,128]{1,0:T(8,128)} %bitcast.22, f32[32,96]{1,0:T(8,128)} %bitcast.23, s32[1,4]{1,0:T(1,128)} %bitcast.24, s32[1,64]{1,0:T(1,128)} %bitcast.25, s32[128,128]{1,0:T(8,128)} %bitcast.20), kind=kLoop, calls=%fused_computation.1 | loop fusion | flops 148480 | bytes 229648 | tf_op jit(solution)/shard_map/add | solution.py:486
  4.6 0.8 %shard_map.86 = (s32[128,128]{1,0:T(8,128)S(1)}, f32[32,128]{1,0:T(8,128)S(1)}, f32[8,128]{1,0:T(8,128)S(1)}, f32[64,128]{1,0:T(8,128)S(1)}, f32[64,128]{1,0:T(8...) custom-call(f32[232,128]{1,0:T(8,128)S(1)} %pad_add_fusion.packed_ref), custom_call_target="tpu_custom_call" | custom-call | flops 1000000 | bytes 1000000 | tf_op jit(solution)/shard_map/pallas_call | solution.py:23
  5.4 3.1 %collective-permute-start.1 = (f32[136,128]{1,0:T(8,128)S(1)}, f32[136,128]{1,0:T(8,128)S(1)}, u32[]{:S(2)}, u32[]{:S(2)}) collective-permute-start(f32[136,128]{1,0:T(8,128)S(1)} %get-tuple-element.30), channel_id=1, source_target_pairs={{4,8},{8,4},{12,16},{16,12},{20,24},{24,20},{28,0},{0,28},{5,9},{9... | collective-permute-start | bytes 208904 | tf_op jit(solution)/shard_map/ppermute | solution.py:449
  8.5 0.0 collective-permute-start.2
  8.5 0.3 collective-permute-done.last_ref
  8.8 0.5 %collective-permute-start.3 = (f32[32,128]{1,0:T(8,128)S(1)}, f32[32,128]{1,0:T(8,128)S(1)}, u32[]{:S(2)}, u32[]{:S(2)}) collective-permute-start(f32[32,128]{1,0:T(8,128)S(1)} %get-tuple-element.32), channel_id=1, source_target_pairs={{0,3},{1,2},{2,1},{3,0},{4,7},{5,6},{6,5},{7,4},{8,11},{9,10},{10,... | collective-permute-start | bytes 49160 | tf_op jit(solution)/shard_map/ppermute | solution.py:460
  9.3 1.3 %collective-permute-start.4 = (f32[32,128]{1,0:T(8,128)S(1)}, f32[32,128]{1,0:T(8,128)S(1)}, u32[]{:S(2)}, u32[]{:S(2)}) collective-permute-start(f32[32,128]{1,0:T(8,128)S(1)} %get-tuple-element.33), channel_id=1, source_target_pairs={{0,2},{1,3},{2,0},{3,1},{4,6},{5,7},{6,4},{7,5},{8,10},{9,11},{10,... | collective-permute-start | bytes 49160 | tf_op jit(solution)/shard_map/ppermute | solution.py:460
  10.5 0.2 collective-permute-start.5
  10.7 1.3 %bitcast_convert_fusion.blocks_ref = f32[48,9216]{1,0:T(8,128)S(1)} fusion(bf16[1,1,48,9216]{3,2,1,0:T(8,128)(2,1)} %param.8), kind=kLoop, calls=%fused_computation | loop fusion | flops 442368 | bytes 2654208 | tf_op jit(solution)/shard_map/convert_element_type | solution.py:468
  12.0 1.1 %shard_map.87.product_ref = f32[32,128]{1,0:T(8,128)S(1)} custom-call(s32[2,16]{1,0:T(2,128)S(1)} %bitcast.18, f32[48,9216]{1,0:T(8,128)S(1)} %bitcast_convert_fusion.blocks_ref, f32[32,128]{1,0:T(8,128)S(1)} %get-tuple-element.25.field_ref), custom_call_target="tpu_custom_call" | custom-call | flops 1000000 | bytes 1000000 | tf_op jit(solution)/shard_map/pallas_call | solution.py:23
  13.1 0.0 collective-permute-done.3.refs_0_
  13.1 0.0 collective-permute-done.5.refs_2_
  13.1 0.2 collective-permute-done.2.from_b_ref
  13.3 1.2 %shard_map.89 = (f32[32,128]{1,0:T(8,128)S(1)}, f32[64,128]{1,0:T(8,128)S(1)}, f32[64,128]{1,0:T(8,128)S(1)}, f32[64,128]{1,0:T(8,128)S(1)}, s32[64,128]{1,0:T(8,128)S(1)}, /*index=5*/s32[64,128]{1,0:T(8,128)S(1)}) custom-call(f32[232,128]{1,0:T(8,128)S(1)} %pad_add_fusion.packed_ref, f32[4,16,128]{2,1,0:T(8,128)S(1)} %collective-permute-done.last_ref, ...), custom_call_target="tpu_custom_call" | custom-call | flops 1000000 | bytes 1000000 | tf_op jit(solution)/shard_map/pallas_call | solution.py:23
  14.5 1.7 %collective-permute-start.7 = (f32[32,128]{1,0:T(8,128)S(1)}, f32[32,128]{1,0:T(8,128)S(1)}, u32[]{:S(2)}, u32[]{:S(2)}) collective-permute-start(f32[32,128]{1,0:T(8,128)S(1)} %get-tuple-element.35.field_ref.image_ref), channel_id=1, source_target_pairs={{0,4},{4,8},{8,12},{12,16},{16,20},{20,24},{24,28},{28,0},{1,5},{5... | collective-permute-start | bytes 49160 | tf_op jit(solution)/shard_map/ppermute | solution.py:455
  16.2 1.2 %shard_map.90 = (f32[32,128]{1,0:T(8,128)S(1)}, f32[32,128]{1,0:T(8,128)S(1)}, f32[64,128]{1,0:T(8,128)S(1)}) custom-call(s32[2,16]{1,0:T(2,128)S(1)} %bitcast.19, f32[48,9216]{1,0:T(8,128)S(1)} %bitcast_convert_fusion.blocks_ref, f32[32,128]{1,0:T(8,128)S(1)} %get-tuple-element.35.field_ref.image_ref, s32[128,128]{1,0:T(8,128)S(1)} %get-tuple-element.27.aligned_ref.refs_0_), custom_call_target="tpu_custom_call" | custom-call | flops 1000000 | bytes 1000000 | tf_op jit(solution)/shard_map/pallas_call | solution.py:23
  17.4 3.1 %collective-permute-start.6 = (f32[32,128]{1,0:T(8,128)S(1)}, f32[32,128]{1,0:T(8,128)S(1)}, u32[]{:S(2)}, u32[]{:S(2)}) collective-permute-start(f32[32,128]{1,0:T(8,128)S(1)} %get-tuple-element.41), channel_id=1, source_target_pairs={{0,28},{4,0},{8,4},{12,8},{16,12},{20,16},{24,20},{28,24},{1,29},{... | collective-permute-start | bytes 49160 | tf_op jit(solution)/shard_map/ppermute | solution.py:455
  20.5 0.5 %collective-permute-done.7.last_ref = f32[32,128]{1,0:T(8,128)S(1)} collective-permute-done((f32[32,128]{1,0:T(8,128)S(1)}, f32[32,128]{1,0:T(8,128)S(1)}, u32[]{:S(2)}, u32[]{:S(2)}) %collective-permute-start.7) | collective-permute-done | bytes 16416 | tf_op jit(solution)/shard_map/ppermute | solution.py:455
  21.0 1.1 %shard_map.91 = (f32[32,1,128]{2,1,0:T(1,128)}, f32[64,128]{1,0:T(8,128)S(1)}) custom-call(f32[32,128]{1,0:T(8,128)S(1)} %get-tuple-element.36.product_ref, f32[64,128]{1,0:T(8,128)S(1)} %get-tuple-element.38.weights_ref.weights_west_ref, f32[64,128]{1,0:T(8,128)S(1)} %get-tuple-element.39.own_ref.west_ref, s32[64,128]{1,0:T(8,128)S(1)} %get-tuple-element.42.rows_ref, ...), custom_call_target="tpu_custom_call" | custom-call | flops 1000000 | bytes 1000000 | tf_op jit(solution)/shard_map/pallas_call | solution.py:23
  22.1 2.5 %all-to-all-start = ((f32[32,1,128]{2,1,0:T(1,128)}), f32[32,1,128]{2,1,0:T(1,128)S(1)}, u32[]{:S(2)}, u32[]{:S(2)}) async-start(f32[32,1,128]{2,1,0:T(1,128)} %get-tuple-element.45), calls=%async_computation | async-start | bytes 32768 | tf_op jit(solution)/shard_map/all_to_all | solution.py:575
  24.6 1.3 %shard_map.92.second_ref = f32[32,128]{1,0:T(8,128)S(1)} custom-call(s32[128,128]{1,0:T(8,128)S(1)} %get-tuple-element.27.aligned_ref.refs_0_, f32[32,128]{1,0:T(8,128)S(1)} %get-tuple-element.36.product_ref, f32[64,128]{1,0:T(8,128)S(1)} %get-tuple-element.37.weights_east_ref, f32[64,128]{1,0:T(8,128)S(1)} %get-tuple-element.38.weights_ref.weights_west_ref, ...), custom_call_target="tpu_custom_call" | custom-call | flops 1000000000 | bytes 1000000 | tf_op jit(solution)/shard_map/pallas_call | solution.py:23
  26.0 5.7 %all-to-all-done.sums_ref = f32[32,1,128]{2,1,0:T(1,128)S(1)} async-done(((f32[32,1,128]{2,1,0:T(1,128)}), f32[32,1,128]{2,1,0:T(1,128)S(1)}, u32[]{:S(2)}, u32[]{:S(2)}) %all-to-all-start) | async-done | bytes 16416 | tf_op jit(solution)/shard_map/all_to_all | solution.py:575
  31.7 0.8 %shard_map.93 = (f32[32,96]{1,0:T(8,128)}, f32[32,96]{1,0:T(8,128)}) custom-call(f32[32,128]{1,0:T(8,128)S(1)} %get-tuple-element.25.field_ref, f32[32,128]{1,0:T(8,128)S(1)} %get-tuple-element.35.field_ref.image_ref, f32[32,128]{1,0:T(8,128)S(1)} %shard_map.92.second_ref, f32[32,1,128]{2,1,0:T(1,128)S(1)} %all-to-all-done.sums_ref), custom_call_target="tpu_custom_call" | custom-call | flops 1000000 | bytes 1000000 | tf_op jit(solution)/shard_map/pallas_call | solution.py:23
  (6 shorter events, 0.0 us)
Async XLA Ops:
  0.6 11.3 %copy-start = (s32[1,1,2,16]{3,2,1,0:T(2,128)S(1)}, s32[1,1,2,16]{3,2,1,0:T(2,128)}, u32[]{:S(2)}) copy-start(s32[1,1,2,16]{3,2,1,0:T(2,128)} %param.9) | copy-start | bytes 388
  0.6 8.2 %collective-permute-start = (f32[4,16,128]{2,1,0:T(8,128)}, f32[4,16,128]{2,1,0:T(8,128)S(1)}, u32[]{:S(2)}, u32[]{:S(2)}) collective-permute-start(f32[4,16,128]{2,1,0:T(8,128)} %bitcast.21), channel_id=1, source_target_pairs={{0,4},{4,8},{8,12},{12,16},{16,20},{20,24},{24,28},{28,0},{1,5},{5... | collective-permute-start | bytes 98312 | tf_op jit(solution)/shard_map/ppermute | solution.py:455
  5.4 7.7 %collective-permute-start.1 = (f32[136,128]{1,0:T(8,128)S(1)}, f32[136,128]{1,0:T(8,128)S(1)}, u32[]{:S(2)}, u32[]{:S(2)}) collective-permute-start(f32[136,128]{1,0:T(8,128)S(1)} %get-tuple-element.30), channel_id=1, source_target_pairs={{4,8},{8,4},{12,16},{16,12},{20,24},{24,20},{28,0},{0,28},{5,9},{9... | collective-permute-start | bytes 208904 | tf_op jit(solution)/shard_map/ppermute | solution.py:449
  8.5 4.8 %collective-permute-start.2 = (f32[136,128]{1,0:T(8,128)S(1)}, f32[136,128]{1,0:T(8,128)S(1)}, u32[]{:S(2)}, u32[]{:S(2)}) collective-permute-start(f32[136,128]{1,0:T(8,128)S(1)} %get-tuple-element.31), channel_id=1, source_target_pairs={{0,4},{4,0},{8,12},{12,8},{16,20},{20,16},{24,28},{28,24},{1,5},{5... | collective-permute-start | bytes 208904 | tf_op jit(solution)/shard_map/ppermute | solution.py:449
  8.8 4.3 %collective-permute-start.3 = (f32[32,128]{1,0:T(8,128)S(1)}, f32[32,128]{1,0:T(8,128)S(1)}, u32[]{:S(2)}, u32[]{:S(2)}) collective-permute-start(f32[32,128]{1,0:T(8,128)S(1)} %get-tuple-element.32), channel_id=1, source_target_pairs={{0,3},{1,2},{2,1},{3,0},{4,7},{5,6},{6,5},{7,4},{8,11},{9,10},{10,... | collective-permute-start | bytes 49160 | tf_op jit(solution)/shard_map/ppermute | solution.py:460
  9.3 3.9 %collective-permute-start.4 = (f32[32,128]{1,0:T(8,128)S(1)}, f32[32,128]{1,0:T(8,128)S(1)}, u32[]{:S(2)}, u32[]{:S(2)}) collective-permute-start(f32[32,128]{1,0:T(8,128)S(1)} %get-tuple-element.33), channel_id=1, source_target_pairs={{0,2},{1,3},{2,0},{3,1},{4,6},{5,7},{6,4},{7,5},{8,10},{9,11},{10,... | collective-permute-start | bytes 49160 | tf_op jit(solution)/shard_map/ppermute | solution.py:460
  10.5 2.6 %collective-permute-start.5 = (f32[32,128]{1,0:T(8,128)S(1)}, f32[32,128]{1,0:T(8,128)S(1)}, u32[]{:S(2)}, u32[]{:S(2)}) collective-permute-start(f32[32,128]{1,0:T(8,128)S(1)} %get-tuple-element.34), channel_id=1, source_target_pairs={{0,1},{1,0},{2,3},{3,2},{4,5},{5,4},{6,7},{7,6},{8,9},{9,8},{10,11... | collective-permute-start | bytes 49160 | tf_op jit(solution)/shard_map/ppermute | solution.py:460
  14.5 6.5 %collective-permute-start.7 = (f32[32,128]{1,0:T(8,128)S(1)}, f32[32,128]{1,0:T(8,128)S(1)}, u32[]{:S(2)}, u32[]{:S(2)}) collective-permute-start(f32[32,128]{1,0:T(8,128)S(1)} %get-tuple-element.35.field_ref.image_ref), channel_id=1, source_target_pairs={{0,4},{4,8},{8,12},{12,16},{16,20},{20,24},{24,28},{28,0},{1,5},{5... | collective-permute-start | bytes 49160 | tf_op jit(solution)/shard_map/ppermute | solution.py:455
  17.4 7.2 %collective-permute-start.6 = (f32[32,128]{1,0:T(8,128)S(1)}, f32[32,128]{1,0:T(8,128)S(1)}, u32[]{:S(2)}, u32[]{:S(2)}) collective-permute-start(f32[32,128]{1,0:T(8,128)S(1)} %get-tuple-element.41), channel_id=1, source_target_pairs={{0,28},{4,0},{8,4},{12,8},{16,12},{20,16},{24,20},{28,24},{1,29},{... | collective-permute-start | bytes 49160 | tf_op jit(solution)/shard_map/ppermute | solution.py:455
  22.1 9.6 %all-to-all-start = ((f32[32,1,128]{2,1,0:T(1,128)}), f32[32,1,128]{2,1,0:T(1,128)S(1)}, u32[]{:S(2)}, u32[]{:S(2)}) async-start(f32[32,1,128]{2,1,0:T(1,128)} %get-tuple-element.45), calls=%async_computation | async-start | bytes 32768 | tf_op jit(solution)/shard_map/all_to_all | solution.py:575

commit v24 on v23

--- a/solution.py
+++ b/solution.py
@@ -50,11 +50,18 @@
     for k in range(target.shape[0] // SUBLANES):
         index = rows_ref[rows_first + k * SUBLANES : rows_first + (k + 1) * SUBLANES, :]
         dof, row = split(index, block_rows)
-        taken = jnp.zeros((SUBLANES, LANES), F32)
-        for i in range(block_rows):
-            here = jnp.take_along_axis(spread[i], dof, axis=1, mode="promise_in_bounds")
-            taken = jnp.where(row == i, here, taken)
-        target[k * SUBLANES : (k + 1) * SUBLANES, :] = taken
+        bits = {}
+
+        def pick(first, count):
+            if count == 1:
+                return jnp.take_along_axis(spread[first], dof, axis=1, mode="promise_in_bounds")
+            half = 1 << ((count - 1).bit_length() - 1)
+            if half not in bits:
+                bits[half] = (row & half) != 0
+            lower = pick(first, half)
+            return jnp.where(bits[half], pick(first + half, count - half), lower)
+
+        target[k * SUBLANES : (k + 1) * SUBLANES, :] = pick(0, block_rows)
 
 
 def tile(k):

time: 32.7 us -> 32.7 us (level)
  no operation moved by 1% of the time
where the time goes in v24:
time: 32.7 us; the launch traced here: 32.5 us
  starting transfers between devices  15.4 us (47%)
  Pallas kernels  7.35 us (22%)
  waiting for transfers between devices  6.81 us (21%)
  other arithmetic  2.2 us (7%)
  between operations  0.73 us (2%)
    ppermute x3, starting transfers between devices, from_behind(): return lax.ppermute(value, axis, pairs)  7.85 us
    pallas_call x8, Pallas kernels, call(): pl.pallas_call(body, out_shape=outs, in_specs=[spec for _, spec in inputs...  7.35 us
    all_to_all x1, waiting for transfers between devices, on_device(): lax.all_to_all(sums, ('sub', 'blk'), split_axis=0, concat_axis=0, tiled=T...  5.88 us
    ppermute x2, starting transfers between devices, swap(): return lax.ppermute(value, 'sub', pairs)  3.12 us
    all_to_all x1, starting transfers between devices, on_device(): lax.all_to_all(sums, ('sub', 'blk'), split_axis=0, concat_axis=0, tiled=T...  2.54 us
    ppermute x3, starting transfers between devices, swap_slots(): lax.ppermute(value, 'blk', [(slot, slot ^ k) for slot in range(count)])  1.88 us
    convert_element_type x1, other arithmetic, on_device(): blocks = stiffness[0, 0].astype(F32)  1.28 us
    add x1, other arithmetic, on_device(): indices.astype(F32) + placed(field, 2 * faces)  0.92 us
  transfers between devices with their start and end apart: 9, of which 4 were waited for; matrix products, arithmetic and copies ran while one was open for 7% of the time, Pallas kernels for 17%

profile of v24, /device:TPU:0, one launch (start us, length us, event | category | flops | bytes accessed | tf_op | source)
XLA Modules:
  0.0 32.5 jit_solution(7074145280243448292)
XLA Ops:
  0.6 3.0 %collective-permute-start = (f32[4,16,128]{2,1,0:T(8,128)}, f32[4,16,128]{2,1,0:T(8,128)S(1)}, u32[]{:S(2)}, u32[]{:S(2)}) collective-permute-start(f32[4,16,128]{2,1,0:T(8,128)} %bitcast.21), channel_id=1, source_target_pairs={{0,4},{4,8},{8,12},{12,16},{16,20},{20,24},{24,28},{28,0},{1,5},{5... | collective-permute-start | bytes 98312 | tf_op jit(solution)/shard_map/ppermute | solution.py:462
  3.7 0.9 %pad_add_fusion.packed_ref = f32[232,128]{1,0:T(8,128)S(1)} fusion(f32[64,128]{1,0:T(8,128)} %bitcast.22, f32[32,96]{1,0:T(8,128)} %bitcast.23, s32[1,4]{1,0:T(1,128)} %bitcast.24, s32[1,64]{1,0:T(1,128)} %bitcast.25, s32[128,128]{1,0:T(8,128)} %bitcast.20), kind=kLoop, calls=%fused_computation.1 | loop fusion | flops 148480 | bytes 229648 | tf_op jit(solution)/shard_map/add | solution.py:493
  4.6 0.8 %shard_map.86 = (s32[128,128]{1,0:T(8,128)S(1)}, f32[32,128]{1,0:T(8,128)S(1)}, f32[8,128]{1,0:T(8,128)S(1)}, f32[64,128]{1,0:T(8,128)S(1)}, f32[64,128]{1,0:T(8...) custom-call(f32[232,128]{1,0:T(8,128)S(1)} %pad_add_fusion.packed_ref), custom_call_target="tpu_custom_call" | custom-call | flops 1000000 | bytes 1000000 | tf_op jit(solution)/shard_map/pallas_call | solution.py:23
  5.4 3.1 %collective-permute-start.1 = (f32[136,128]{1,0:T(8,128)S(1)}, f32[136,128]{1,0:T(8,128)S(1)}, u32[]{:S(2)}, u32[]{:S(2)}) collective-permute-start(f32[136,128]{1,0:T(8,128)S(1)} %get-tuple-element.30), channel_id=1, source_target_pairs={{4,8},{8,4},{12,16},{16,12},{20,24},{24,20},{28,0},{0,28},{5,9},{9... | collective-permute-start | bytes 208904 | tf_op jit(solution)/shard_map/ppermute | solution.py:456
  8.5 0.0 collective-permute-start.2
  8.5 0.3 collective-permute-done.last_ref
  8.8 0.5 %collective-permute-start.3 = (f32[32,128]{1,0:T(8,128)S(1)}, f32[32,128]{1,0:T(8,128)S(1)}, u32[]{:S(2)}, u32[]{:S(2)}) collective-permute-start(f32[32,128]{1,0:T(8,128)S(1)} %get-tuple-element.32), channel_id=1, source_target_pairs={{0,3},{1,2},{2,1},{3,0},{4,7},{5,6},{6,5},{7,4},{8,11},{9,10},{10,... | collective-permute-start | bytes 49160 | tf_op jit(solution)/shard_map/ppermute | solution.py:467
  9.3 1.3 %collective-permute-start.4 = (f32[32,128]{1,0:T(8,128)S(1)}, f32[32,128]{1,0:T(8,128)S(1)}, u32[]{:S(2)}, u32[]{:S(2)}) collective-permute-start(f32[32,128]{1,0:T(8,128)S(1)} %get-tuple-element.33), channel_id=1, source_target_pairs={{0,2},{1,3},{2,0},{3,1},{4,6},{5,7},{6,4},{7,5},{8,10},{9,11},{10,... | collective-permute-start | bytes 49160 | tf_op jit(solution)/shard_map/ppermute | solution.py:467
  10.5 0.2 collective-permute-start.5
  10.7 1.3 %bitcast_convert_fusion.blocks_ref = f32[48,9216]{1,0:T(8,128)S(1)} fusion(bf16[1,1,48,9216]{3,2,1,0:T(8,128)(2,1)} %param.8), kind=kLoop, calls=%fused_computation | loop fusion | flops 442368 | bytes 2654208 | tf_op jit(solution)/shard_map/convert_element_type | solution.py:475
  12.0 1.1 %shard_map.87.product_ref = f32[32,128]{1,0:T(8,128)S(1)} custom-call(s32[2,16]{1,0:T(2,128)S(1)} %bitcast.18, f32[48,9216]{1,0:T(8,128)S(1)} %bitcast_convert_fusion.blocks_ref, f32[32,128]{1,0:T(8,128)S(1)} %get-tuple-element.25.field_ref), custom_call_target="tpu_custom_call" | custom-call | flops 1000000 | bytes 1000000 | tf_op jit(solution)/shard_map/pallas_call | solution.py:23
  13.1 0.0 collective-permute-done.3.refs_0_
  13.1 0.0 collective-permute-done.5.refs_2_
  13.1 0.2 collective-permute-done.2.from_b_ref
  13.3 1.2 %shard_map.89 = (f32[32,128]{1,0:T(8,128)S(1)}, f32[64,128]{1,0:T(8,128)S(1)}, f32[64,128]{1,0:T(8,128)S(1)}, f32[64,128]{1,0:T(8,128)S(1)}, s32[64,128]{1,0:T(8,128)S(1)}, /*index=5*/s32[64,128]{1,0:T(8,128)S(1)}) custom-call(f32[232,128]{1,0:T(8,128)S(1)} %pad_add_fusion.packed_ref, f32[4,16,128]{2,1,0:T(8,128)S(1)} %collective-permute-done.last_ref, ...), custom_call_target="tpu_custom_call" | custom-call | flops 1000000 | bytes 1000000 | tf_op jit(solution)/shard_map/pallas_call | solution.py:23
  14.5 1.7 %collective-permute-start.7 = (f32[32,128]{1,0:T(8,128)S(1)}, f32[32,128]{1,0:T(8,128)S(1)}, u32[]{:S(2)}, u32[]{:S(2)}) collective-permute-start(f32[32,128]{1,0:T(8,128)S(1)} %get-tuple-element.35.field_ref.image_ref), channel_id=1, source_target_pairs={{0,4},{4,8},{8,12},{12,16},{16,20},{20,24},{24,28},{28,0},{1,5},{5... | collective-permute-start | bytes 49160 | tf_op jit(solution)/shard_map/ppermute | solution.py:462
  16.2 1.2 %shard_map.90 = (f32[32,128]{1,0:T(8,128)S(1)}, f32[32,128]{1,0:T(8,128)S(1)}, f32[64,128]{1,0:T(8,128)S(1)}) custom-call(s32[2,16]{1,0:T(2,128)S(1)} %bitcast.19, f32[48,9216]{1,0:T(8,128)S(1)} %bitcast_convert_fusion.blocks_ref, f32[32,128]{1,0:T(8,128)S(1)} %get-tuple-element.35.field_ref.image_ref, s32[128,128]{1,0:T(8,128)S(1)} %get-tuple-element.27.aligned_ref.refs_0_), custom_call_target="tpu_custom_call" | custom-call | flops 1000000 | bytes 1000000 | tf_op jit(solution)/shard_map/pallas_call | solution.py:23
  17.4 3.1 %collective-permute-start.6 = (f32[32,128]{1,0:T(8,128)S(1)}, f32[32,128]{1,0:T(8,128)S(1)}, u32[]{:S(2)}, u32[]{:S(2)}) collective-permute-start(f32[32,128]{1,0:T(8,128)S(1)} %get-tuple-element.41), channel_id=1, source_target_pairs={{0,28},{4,0},{8,4},{12,8},{16,12},{20,16},{24,20},{28,24},{1,29},{... | collective-permute-start | bytes 49160 | tf_op jit(solution)/shard_map/ppermute | solution.py:462
  20.5 0.5 %collective-permute-done.7.last_ref = f32[32,128]{1,0:T(8,128)S(1)} collective-permute-done((f32[32,128]{1,0:T(8,128)S(1)}, f32[32,128]{1,0:T(8,128)S(1)}, u32[]{:S(2)}, u32[]{:S(2)}) %collective-permute-start.7) | collective-permute-done | bytes 16416 | tf_op jit(solution)/shard_map/ppermute | solution.py:462
  21.0 1.1 %shard_map.91 = (f32[32,1,128]{2,1,0:T(1,128)}, f32[64,128]{1,0:T(8,128)S(1)}) custom-call(f32[32,128]{1,0:T(8,128)S(1)} %get-tuple-element.36.product_ref, f32[64,128]{1,0:T(8,128)S(1)} %get-tuple-element.38.weights_ref.weights_west_ref, f32[64,128]{1,0:T(8,128)S(1)} %get-tuple-element.39.own_ref.west_ref, s32[64,128]{1,0:T(8,128)S(1)} %get-tuple-element.42.rows_ref, ...), custom_call_target="tpu_custom_call" | custom-call | flops 1000000 | bytes 1000000 | tf_op jit(solution)/shard_map/pallas_call | solution.py:23
  22.1 2.5 %all-to-all-start = ((f32[32,1,128]{2,1,0:T(1,128)}), f32[32,1,128]{2,1,0:T(1,128)S(1)}, u32[]{:S(2)}, u32[]{:S(2)}) async-start(f32[32,1,128]{2,1,0:T(1,128)} %get-tuple-element.45), calls=%async_computation | async-start | bytes 32768 | tf_op jit(solution)/shard_map/all_to_all | solution.py:582
  24.7 1.2 %shard_map.92.second_ref = f32[32,128]{1,0:T(8,128)S(1)} custom-call(s32[128,128]{1,0:T(8,128)S(1)} %get-tuple-element.27.aligned_ref.refs_0_, f32[32,128]{1,0:T(8,128)S(1)} %get-tuple-element.36.product_ref, f32[64,128]{1,0:T(8,128)S(1)} %get-tuple-element.37.weights_east_ref, f32[64,128]{1,0:T(8,128)S(1)} %get-tuple-element.38.weights_ref.weights_west_ref, ...), custom_call_target="tpu_custom_call" | custom-call | flops 1000000000 | bytes 1000000 | tf_op jit(solution)/shard_map/pallas_call | solution.py:23
  25.8 5.9 %all-to-all-done.sums_ref = f32[32,1,128]{2,1,0:T(1,128)S(1)} async-done(((f32[32,1,128]{2,1,0:T(1,128)}), f32[32,1,128]{2,1,0:T(1,128)S(1)}, u32[]{:S(2)}, u32[]{:S(2)}) %all-to-all-start) | async-done | bytes 16416 | tf_op jit(solution)/shard_map/all_to_all | solution.py:582
  31.7 0.8 %shard_map.93 = (f32[32,96]{1,0:T(8,128)}, f32[32,96]{1,0:T(8,128)}) custom-call(f32[32,128]{1,0:T(8,128)S(1)} %get-tuple-element.25.field_ref, f32[32,128]{1,0:T(8,128)S(1)} %get-tuple-element.35.field_ref.image_ref, f32[32,128]{1,0:T(8,128)S(1)} %shard_map.92.second_ref, f32[32,1,128]{2,1,0:T(1,128)S(1)} %all-to-all-done.sums_ref), custom_call_target="tpu_custom_call" | custom-call | flops 1000000 | bytes 1000000 | tf_op jit(solution)/shard_map/pallas_call | solution.py:23
  (6 shorter events, 0.0 us)
Async XLA Ops:
  0.6 11.3 %copy-start = (s32[1,1,2,16]{3,2,1,0:T(2,128)S(1)}, s32[1,1,2,16]{3,2,1,0:T(2,128)}, u32[]{:S(2)}) copy-start(s32[1,1,2,16]{3,2,1,0:T(2,128)} %param.9) | copy-start | bytes 388
  0.6 8.2 %collective-permute-start = (f32[4,16,128]{2,1,0:T(8,128)}, f32[4,16,128]{2,1,0:T(8,128)S(1)}, u32[]{:S(2)}, u32[]{:S(2)}) collective-permute-start(f32[4,16,128]{2,1,0:T(8,128)} %bitcast.21), channel_id=1, source_target_pairs={{0,4},{4,8},{8,12},{12,16},{16,20},{20,24},{24,28},{28,0},{1,5},{5... | collective-permute-start | bytes 98312 | tf_op jit(solution)/shard_map/ppermute | solution.py:462
  5.4 7.7 %collective-permute-start.1 = (f32[136,128]{1,0:T(8,128)S(1)}, f32[136,128]{1,0:T(8,128)S(1)}, u32[]{:S(2)}, u32[]{:S(2)}) collective-permute-start(f32[136,128]{1,0:T(8,128)S(1)} %get-tuple-element.30), channel_id=1, source_target_pairs={{4,8},{8,4},{12,16},{16,12},{20,24},{24,20},{28,0},{0,28},{5,9},{9... | collective-permute-start | bytes 208904 | tf_op jit(solution)/shard_map/ppermute | solution.py:456
  8.5 4.8 %collective-permute-start.2 = (f32[136,128]{1,0:T(8,128)S(1)}, f32[136,128]{1,0:T(8,128)S(1)}, u32[]{:S(2)}, u32[]{:S(2)}) collective-permute-start(f32[136,128]{1,0:T(8,128)S(1)} %get-tuple-element.31), channel_id=1, source_target_pairs={{0,4},{4,0},{8,12},{12,8},{16,20},{20,16},{24,28},{28,24},{1,5},{5... | collective-permute-start | bytes 208904 | tf_op jit(solution)/shard_map/ppermute | solution.py:456
  8.8 4.3 %collective-permute-start.3 = (f32[32,128]{1,0:T(8,128)S(1)}, f32[32,128]{1,0:T(8,128)S(1)}, u32[]{:S(2)}, u32[]{:S(2)}) collective-permute-start(f32[32,128]{1,0:T(8,128)S(1)} %get-tuple-element.32), channel_id=1, source_target_pairs={{0,3},{1,2},{2,1},{3,0},{4,7},{5,6},{6,5},{7,4},{8,11},{9,10},{10,... | collective-permute-start | bytes 49160 | tf_op jit(solution)/shard_map/ppermute | solution.py:467
  9.3 3.9 %collective-permute-start.4 = (f32[32,128]{1,0:T(8,128)S(1)}, f32[32,128]{1,0:T(8,128)S(1)}, u32[]{:S(2)}, u32[]{:S(2)}) collective-permute-start(f32[32,128]{1,0:T(8,128)S(1)} %get-tuple-element.33), channel_id=1, source_target_pairs={{0,2},{1,3},{2,0},{3,1},{4,6},{5,7},{6,4},{7,5},{8,10},{9,11},{10,... | collective-permute-start | bytes 49160 | tf_op jit(solution)/shard_map/ppermute | solution.py:467
  10.5 2.6 %collective-permute-start.5 = (f32[32,128]{1,0:T(8,128)S(1)}, f32[32,128]{1,0:T(8,128)S(1)}, u32[]{:S(2)}, u32[]{:S(2)}) collective-permute-start(f32[32,128]{1,0:T(8,128)S(1)} %get-tuple-element.34), channel_id=1, source_target_pairs={{0,1},{1,0},{2,3},{3,2},{4,5},{5,4},{6,7},{7,6},{8,9},{9,8},{10,11... | collective-permute-start | bytes 49160 | tf_op jit(solution)/shard_map/ppermute | solution.py:467
  14.5 6.5 %collective-permute-start.7 = (f32[32,128]{1,0:T(8,128)S(1)}, f32[32,128]{1,0:T(8,128)S(1)}, u32[]{:S(2)}, u32[]{:S(2)}) collective-permute-start(f32[32,128]{1,0:T(8,128)S(1)} %get-tuple-element.35.field_ref.image_ref), channel_id=1, source_target_pairs={{0,4},{4,8},{8,12},{12,16},{16,20},{20,24},{24,28},{28,0},{1,5},{5... | collective-permute-start | bytes 49160 | tf_op jit(solution)/shard_map/ppermute | solution.py:462
  17.4 7.2 %collective-permute-start.6 = (f32[32,128]{1,0:T(8,128)S(1)}, f32[32,128]{1,0:T(8,128)S(1)}, u32[]{:S(2)}, u32[]{:S(2)}) collective-permute-start(f32[32,128]{1,0:T(8,128)S(1)} %get-tuple-element.41), channel_id=1, source_target_pairs={{0,28},{4,0},{8,4},{12,8},{16,12},{20,16},{24,20},{28,24},{1,29},{... | collective-permute-start | bytes 49160 | tf_op jit(solution)/shard_map/ppermute | solution.py:462
  22.1 9.6 %all-to-all-start = ((f32[32,1,128]{2,1,0:T(1,128)}), f32[32,1,128]{2,1,0:T(1,128)S(1)}, u32[]{:S(2)}, u32[]{:S(2)}) async-start(f32[32,1,128]{2,1,0:T(1,128)} %get-tuple-element.45), calls=%async_computation | async-start | bytes 32768 | tf_op jit(solution)/shard_map/all_to_all | solution.py:582

commit v25 on v24

--- a/solution.py
+++ b/solution.py
@@ -11,6 +11,7 @@
 LANES = 128
 SUBLANES = 8
 VMEM = pl.BlockSpec(memory_space=pltpu.VMEM)
+BATCH = 4
 MARK = 5
 LARGE = 2.0**40
 SMALL = 2.0**-40
@@ -258,26 +259,27 @@
             dof, row = split(rows_ref[first : first + SUBLANES, :], block_rows)
             dof = dof.astype(F32)
             row = row.astype(F32)
-            left = []
-            right = []
-            for f in range(SUBLANES):
-                here = row_of == widened(row, f, block_rows)
-                left.append(
-                    jnp.concatenate(
-                        [
-                            jnp.where(here, widened(high, f, block_rows), none),
-                            jnp.where(here, widened(low, f, block_rows), none),
-                        ],
-                        axis=0,
+            for start in range(0, SUBLANES, BATCH):
+                left = []
+                right = []
+                for f in range(start, start + BATCH):
+                    here = row_of == widened(row, f, block_rows)
+                    left.append(
+                        jnp.concatenate(
+                            [
+                                jnp.where(here, widened(high, f, block_rows), none),
+                                jnp.where(here, widened(low, f, block_rows), none),
+                            ],
+                            axis=0,
+                        )
                     )
+                    right.append(jnp.where(dof_of == widened(dof, f, size), one, none))
+                total = total + lax.dot_general(
+                    jnp.concatenate(right, axis=1),
+                    jnp.concatenate(left, axis=1),
+                    (((1,), (1,)), ((), ())),
+                    preferred_element_type=F32,
                 )
-                right.append(jnp.where(dof_of == widened(dof, f, size), one, none))
-            total = total + lax.dot_general(
-                jnp.concatenate(right, axis=1),
-                jnp.concatenate(left, axis=1),
-                (((1,), (1,)), ((), ())),
-                preferred_element_type=F32,
-            )
     total = total.T
     return total[:block_rows] + total[block_rows:]
 

time: 32.7 us -> 32.7 us (level)
  transfers between devices with their start and end apart: 9 -> 9, of which waited for: 4 -> 4; matrix products, arithmetic and copies ran while one was open for 7% -> 7% of each run, Pallas kernels for 17% -> 16%
where the time goes in v25:
time: 32.7 us; the launch traced here: 32.5 us
  starting transfers between devices  15.4 us (47%)
  Pallas kernels  7.33 us (22%)
  waiting for transfers between devices  6.83 us (21%)
  other arithmetic  2.2 us (7%)
  between operations  0.73 us (2%)
    ppermute x3, starting transfers between devices, from_behind(): return lax.ppermute(value, axis, pairs)  7.85 us
    pallas_call x8, Pallas kernels, call(): pl.pallas_call(body, out_shape=outs, in_specs=[spec for _, spec in inputs...  7.33 us
    all_to_all x1, waiting for transfers between devices, on_device(): lax.all_to_all(sums, ('sub', 'blk'), split_axis=0, concat_axis=0, tiled=T...  5.9 us
    ppermute x2, starting transfers between devices, swap(): return lax.ppermute(value, 'sub', pairs)  3.12 us
    all_to_all x1, starting transfers between devices, on_device(): lax.all_to_all(sums, ('sub', 'blk'), split_axis=0, concat_axis=0, tiled=T...  2.54 us
    ppermute x3, starting transfers between devices, swap_slots(): lax.ppermute(value, 'blk', [(slot, slot ^ k) for slot in range(count)])  1.88 us
    convert_element_type x1, other arithmetic, on_device(): blocks = stiffness[0, 0].astype(F32)  1.28 us
    add x1, other arithmetic, on_device(): indices.astype(F32) + placed(field, 2 * faces)  0.92 us
  transfers between devices with their start and end apart: 9, of which 4 were waited for; matrix products, arithmetic and copies ran while one was open for 7% of the time, Pallas kernels for 16%

profile of v25, /device:TPU:0, one launch (start us, length us, event | category | flops | bytes accessed | tf_op | source)
XLA Modules:
  0.0 32.5 jit_solution(4044204797029224605)
XLA Ops:
  0.6 3.0 %collective-permute-start = (f32[4,16,128]{2,1,0:T(8,128)}, f32[4,16,128]{2,1,0:T(8,128)S(1)}, u32[]{:S(2)}, u32[]{:S(2)}) collective-permute-start(f32[4,16,128]{2,1,0:T(8,128)} %bitcast.21), channel_id=1, source_target_pairs={{0,4},{4,8},{8,12},{12,16},{16,20},{20,24},{24,28},{28,0},{1,5},{5... | collective-permute-start | bytes 98312 | tf_op jit(solution)/shard_map/ppermute | solution.py:464
  3.7 0.9 %pad_add_fusion.packed_ref = f32[232,128]{1,0:T(8,128)S(1)} fusion(f32[64,128]{1,0:T(8,128)} %bitcast.22, f32[32,96]{1,0:T(8,128)} %bitcast.23, s32[1,4]{1,0:T(1,128)} %bitcast.24, s32[1,64]{1,0:T(1,128)} %bitcast.25, s32[128,128]{1,0:T(8,128)} %bitcast.20), kind=kLoop, calls=%fused_computation.1 | loop fusion | flops 148480 | bytes 229648 | tf_op jit(solution)/shard_map/add | solution.py:495
  4.6 0.8 %shard_map.86 = (s32[128,128]{1,0:T(8,128)S(1)}, f32[32,128]{1,0:T(8,128)S(1)}, f32[8,128]{1,0:T(8,128)S(1)}, f32[64,128]{1,0:T(8,128)S(1)}, f32[64,128]{1,0:T(8...) custom-call(f32[232,128]{1,0:T(8,128)S(1)} %pad_add_fusion.packed_ref), custom_call_target="tpu_custom_call" | custom-call | flops 1000000 | bytes 1000000 | tf_op jit(solution)/shard_map/pallas_call | solution.py:24
  5.4 3.1 %collective-permute-start.1 = (f32[136,128]{1,0:T(8,128)S(1)}, f32[136,128]{1,0:T(8,128)S(1)}, u32[]{:S(2)}, u32[]{:S(2)}) collective-permute-start(f32[136,128]{1,0:T(8,128)S(1)} %get-tuple-element.30), channel_id=1, source_target_pairs={{4,8},{8,4},{12,16},{16,12},{20,24},{24,20},{28,0},{0,28},{5,9},{9... | collective-permute-start | bytes 208904 | tf_op jit(solution)/shard_map/ppermute | solution.py:458
  8.5 0.0 collective-permute-start.2
  8.5 0.3 collective-permute-done.last_ref
  8.8 0.5 %collective-permute-start.3 = (f32[32,128]{1,0:T(8,128)S(1)}, f32[32,128]{1,0:T(8,128)S(1)}, u32[]{:S(2)}, u32[]{:S(2)}) collective-permute-start(f32[32,128]{1,0:T(8,128)S(1)} %get-tuple-element.32), channel_id=1, source_target_pairs={{0,3},{1,2},{2,1},{3,0},{4,7},{5,6},{6,5},{7,4},{8,11},{9,10},{10,... | collective-permute-start | bytes 49160 | tf_op jit(solution)/shard_map/ppermute | solution.py:469
  9.3 1.3 %collective-permute-start.4 = (f32[32,128]{1,0:T(8,128)S(1)}, f32[32,128]{1,0:T(8,128)S(1)}, u32[]{:S(2)}, u32[]{:S(2)}) collective-permute-start(f32[32,128]{1,0:T(8,128)S(1)} %get-tuple-element.33), channel_id=1, source_target_pairs={{0,2},{1,3},{2,0},{3,1},{4,6},{5,7},{6,4},{7,5},{8,10},{9,11},{10,... | collective-permute-start | bytes 49160 | tf_op jit(solution)/shard_map/ppermute | solution.py:469
  10.5 0.2 collective-permute-start.5
  10.7 1.3 %bitcast_convert_fusion.blocks_ref = f32[48,9216]{1,0:T(8,128)S(1)} fusion(bf16[1,1,48,9216]{3,2,1,0:T(8,128)(2,1)} %param.8), kind=kLoop, calls=%fused_computation | loop fusion | flops 442368 | bytes 2654208 | tf_op jit(solution)/shard_map/convert_element_type | solution.py:477
  12.0 1.1 %shard_map.87.product_ref = f32[32,128]{1,0:T(8,128)S(1)} custom-call(s32[2,16]{1,0:T(2,128)S(1)} %bitcast.18, f32[48,9216]{1,0:T(8,128)S(1)} %bitcast_convert_fusion.blocks_ref, f32[32,128]{1,0:T(8,128)S(1)} %get-tuple-element.25.field_ref), custom_call_target="tpu_custom_call" | custom-call | flops 1000000 | bytes 1000000 | tf_op jit(solution)/shard_map/pallas_call | solution.py:24
  13.1 0.0 collective-permute-done.3.refs_0_
  13.1 0.0 collective-permute-done.5.refs_2_
  13.1 0.2 collective-permute-done.2.from_b_ref
  13.3 1.2 %shard_map.89 = (f32[32,128]{1,0:T(8,128)S(1)}, f32[64,128]{1,0:T(8,128)S(1)}, f32[64,128]{1,0:T(8,128)S(1)}, f32[64,128]{1,0:T(8,128)S(1)}, s32[64,128]{1,0:T(8,128)S(1)}, /*index=5*/s32[64,128]{1,0:T(8,128)S(1)}) custom-call(f32[232,128]{1,0:T(8,128)S(1)} %pad_add_fusion.packed_ref, f32[4,16,128]{2,1,0:T(8,128)S(1)} %collective-permute-done.last_ref, ...), custom_call_target="tpu_custom_call" | custom-call | flops 1000000 | bytes 1000000 | tf_op jit(solution)/shard_map/pallas_call | solution.py:24
  14.5 1.7 %collective-permute-start.7 = (f32[32,128]{1,0:T(8,128)S(1)}, f32[32,128]{1,0:T(8,128)S(1)}, u32[]{:S(2)}, u32[]{:S(2)}) collective-permute-start(f32[32,128]{1,0:T(8,128)S(1)} %get-tuple-element.35.field_ref.image_ref), channel_id=1, source_target_pairs={{0,4},{4,8},{8,12},{12,16},{16,20},{20,24},{24,28},{28,0},{1,5},{5... | collective-permute-start | bytes 49160 | tf_op jit(solution)/shard_map/ppermute | solution.py:464
  16.3 1.2 %shard_map.90 = (f32[32,128]{1,0:T(8,128)S(1)}, f32[32,128]{1,0:T(8,128)S(1)}, f32[64,128]{1,0:T(8,128)S(1)}) custom-call(s32[2,16]{1,0:T(2,128)S(1)} %bitcast.19, f32[48,9216]{1,0:T(8,128)S(1)} %bitcast_convert_fusion.blocks_ref, f32[32,128]{1,0:T(8,128)S(1)} %get-tuple-element.35.field_ref.image_ref, s32[128,128]{1,0:T(8,128)S(1)} %get-tuple-element.27.aligned_ref.refs_0_), custom_call_target="tpu_custom_call" | custom-call | flops 1000000 | bytes 1000000 | tf_op jit(solution)/shard_map/pallas_call | solution.py:24
  17.4 3.1 %collective-permute-start.6 = (f32[32,128]{1,0:T(8,128)S(1)}, f32[32,128]{1,0:T(8,128)S(1)}, u32[]{:S(2)}, u32[]{:S(2)}) collective-permute-start(f32[32,128]{1,0:T(8,128)S(1)} %get-tuple-element.41), channel_id=1, source_target_pairs={{0,28},{4,0},{8,4},{12,8},{16,12},{20,16},{24,20},{28,24},{1,29},{... | collective-permute-start | bytes 49160 | tf_op jit(solution)/shard_map/ppermute | solution.py:464
  20.5 0.5 %collective-permute-done.7.last_ref = f32[32,128]{1,0:T(8,128)S(1)} collective-permute-done((f32[32,128]{1,0:T(8,128)S(1)}, f32[32,128]{1,0:T(8,128)S(1)}, u32[]{:S(2)}, u32[]{:S(2)}) %collective-permute-start.7) | collective-permute-done | bytes 16416 | tf_op jit(solution)/shard_map/ppermute | solution.py:464
  21.0 1.1 %shard_map.91 = (f32[32,1,128]{2,1,0:T(1,128)}, f32[64,128]{1,0:T(8,128)S(1)}) custom-call(f32[32,128]{1,0:T(8,128)S(1)} %get-tuple-element.36.product_ref, f32[64,128]{1,0:T(8,128)S(1)} %get-tuple-element.38.weights_ref.weights_west_ref, f32[64,128]{1,0:T(8,128)S(1)} %get-tuple-element.39.own_ref.west_ref, s32[64,128]{1,0:T(8,128)S(1)} %get-tuple-element.42.rows_ref, ...), custom_call_target="tpu_custom_call" | custom-call | flops 1000000 | bytes 1000000 | tf_op jit(solution)/shard_map/pallas_call | solution.py:24
  22.1 2.5 %all-to-all-start = ((f32[32,1,128]{2,1,0:T(1,128)}), f32[32,1,128]{2,1,0:T(1,128)S(1)}, u32[]{:S(2)}, u32[]{:S(2)}) async-start(f32[32,1,128]{2,1,0:T(1,128)} %get-tuple-element.45), calls=%async_computation | async-start | bytes 32768 | tf_op jit(solution)/shard_map/all_to_all | solution.py:584
  24.7 1.2 %shard_map.92.second_ref = f32[32,128]{1,0:T(8,128)S(1)} custom-call(s32[128,128]{1,0:T(8,128)S(1)} %get-tuple-element.27.aligned_ref.refs_0_, f32[32,128]{1,0:T(8,128)S(1)} %get-tuple-element.36.product_ref, f32[64,128]{1,0:T(8,128)S(1)} %get-tuple-element.37.weights_east_ref, f32[64,128]{1,0:T(8,128)S(1)} %get-tuple-element.38.weights_ref.weights_west_ref, ...), custom_call_target="tpu_custom_call" | custom-call | flops 1000000000 | bytes 1000000 | tf_op jit(solution)/shard_map/pallas_call | solution.py:24
  25.8 5.9 %all-to-all-done.sums_ref = f32[32,1,128]{2,1,0:T(1,128)S(1)} async-done(((f32[32,1,128]{2,1,0:T(1,128)}), f32[32,1,128]{2,1,0:T(1,128)S(1)}, u32[]{:S(2)}, u32[]{:S(2)}) %all-to-all-start) | async-done | bytes 16416 | tf_op jit(solution)/shard_map/all_to_all | solution.py:584
  31.7 0.8 %shard_map.93 = (f32[32,96]{1,0:T(8,128)}, f32[32,96]{1,0:T(8,128)}) custom-call(f32[32,128]{1,0:T(8,128)S(1)} %get-tuple-element.25.field_ref, f32[32,128]{1,0:T(8,128)S(1)} %get-tuple-element.35.field_ref.image_ref, f32[32,128]{1,0:T(8,128)S(1)} %shard_map.92.second_ref, f32[32,1,128]{2,1,0:T(1,128)S(1)} %all-to-all-done.sums_ref), custom_call_target="tpu_custom_call" | custom-call | flops 1000000 | bytes 1000000 | tf_op jit(solution)/shard_map/pallas_call | solution.py:24
  (6 shorter events, 0.0 us)
Async XLA Ops:
  0.6 11.3 %copy-start = (s32[1,1,2,16]{3,2,1,0:T(2,128)S(1)}, s32[1,1,2,16]{3,2,1,0:T(2,128)}, u32[]{:S(2)}) copy-start(s32[1,1,2,16]{3,2,1,0:T(2,128)} %param.9) | copy-start | bytes 388
  0.6 8.2 %collective-permute-start = (f32[4,16,128]{2,1,0:T(8,128)}, f32[4,16,128]{2,1,0:T(8,128)S(1)}, u32[]{:S(2)}, u32[]{:S(2)}) collective-permute-start(f32[4,16,128]{2,1,0:T(8,128)} %bitcast.21), channel_id=1, source_target_pairs={{0,4},{4,8},{8,12},{12,16},{16,20},{20,24},{24,28},{28,0},{1,5},{5... | collective-permute-start | bytes 98312 | tf_op jit(solution)/shard_map/ppermute | solution.py:464
  5.4 7.7 %collective-permute-start.1 = (f32[136,128]{1,0:T(8,128)S(1)}, f32[136,128]{1,0:T(8,128)S(1)}, u32[]{:S(2)}, u32[]{:S(2)}) collective-permute-start(f32[136,128]{1,0:T(8,128)S(1)} %get-tuple-element.30), channel_id=1, source_target_pairs={{4,8},{8,4},{12,16},{16,12},{20,24},{24,20},{28,0},{0,28},{5,9},{9... | collective-permute-start | bytes 208904 | tf_op jit(solution)/shard_map/ppermute | solution.py:458
  8.5 4.8 %collective-permute-start.2 = (f32[136,128]{1,0:T(8,128)S(1)}, f32[136,128]{1,0:T(8,128)S(1)}, u32[]{:S(2)}, u32[]{:S(2)}) collective-permute-start(f32[136,128]{1,0:T(8,128)S(1)} %get-tuple-element.31), channel_id=1, source_target_pairs={{0,4},{4,0},{8,12},{12,8},{16,20},{20,16},{24,28},{28,24},{1,5},{5... | collective-permute-start | bytes 208904 | tf_op jit(solution)/shard_map/ppermute | solution.py:458
  8.8 4.3 %collective-permute-start.3 = (f32[32,128]{1,0:T(8,128)S(1)}, f32[32,128]{1,0:T(8,128)S(1)}, u32[]{:S(2)}, u32[]{:S(2)}) collective-permute-start(f32[32,128]{1,0:T(8,128)S(1)} %get-tuple-element.32), channel_id=1, source_target_pairs={{0,3},{1,2},{2,1},{3,0},{4,7},{5,6},{6,5},{7,4},{8,11},{9,10},{10,... | collective-permute-start | bytes 49160 | tf_op jit(solution)/shard_map/ppermute | solution.py:469
  9.3 3.9 %collective-permute-start.4 = (f32[32,128]{1,0:T(8,128)S(1)}, f32[32,128]{1,0:T(8,128)S(1)}, u32[]{:S(2)}, u32[]{:S(2)}) collective-permute-start(f32[32,128]{1,0:T(8,128)S(1)} %get-tuple-element.33), channel_id=1, source_target_pairs={{0,2},{1,3},{2,0},{3,1},{4,6},{5,7},{6,4},{7,5},{8,10},{9,11},{10,... | collective-permute-start | bytes 49160 | tf_op jit(solution)/shard_map/ppermute | solution.py:469
  10.5 2.6 %collective-permute-start.5 = (f32[32,128]{1,0:T(8,128)S(1)}, f32[32,128]{1,0:T(8,128)S(1)}, u32[]{:S(2)}, u32[]{:S(2)}) collective-permute-start(f32[32,128]{1,0:T(8,128)S(1)} %get-tuple-element.34), channel_id=1, source_target_pairs={{0,1},{1,0},{2,3},{3,2},{4,5},{5,4},{6,7},{7,6},{8,9},{9,8},{10,11... | collective-permute-start | bytes 49160 | tf_op jit(solution)/shard_map/ppermute | solution.py:469
  14.5 6.5 %collective-permute-start.7 = (f32[32,128]{1,0:T(8,128)S(1)}, f32[32,128]{1,0:T(8,128)S(1)}, u32[]{:S(2)}, u32[]{:S(2)}) collective-permute-start(f32[32,128]{1,0:T(8,128)S(1)} %get-tuple-element.35.field_ref.image_ref), channel_id=1, source_target_pairs={{0,4},{4,8},{8,12},{12,16},{16,20},{20,24},{24,28},{28,0},{1,5},{5... | collective-permute-start | bytes 49160 | tf_op jit(solution)/shard_map/ppermute | solution.py:464
  17.4 7.2 %collective-permute-start.6 = (f32[32,128]{1,0:T(8,128)S(1)}, f32[32,128]{1,0:T(8,128)S(1)}, u32[]{:S(2)}, u32[]{:S(2)}) collective-permute-start(f32[32,128]{1,0:T(8,128)S(1)} %get-tuple-element.41), channel_id=1, source_target_pairs={{0,28},{4,0},{8,4},{12,8},{16,12},{20,16},{24,20},{28,24},{1,29},{... | collective-permute-start | bytes 49160 | tf_op jit(solution)/shard_map/ppermute | solution.py:464
  22.1 9.6 %all-to-all-start = ((f32[32,1,128]{2,1,0:T(1,128)}), f32[32,1,128]{2,1,0:T(1,128)S(1)}, u32[]{:S(2)}, u32[]{:S(2)}) async-start(f32[32,1,128]{2,1,0:T(1,128)} %get-tuple-element.45), calls=%async_computation | async-start | bytes 32768 | tf_op jit(solution)/shard_map/all_to_all | solution.py:584

commit v26 on v24

--- a/solution.py
+++ b/solution.py
@@ -11,6 +11,7 @@
 LANES = 128
 SUBLANES = 8
 VMEM = pl.BlockSpec(memory_space=pltpu.VMEM)
+BATCH = 16
 MARK = 5
 LARGE = 2.0**40
 SMALL = 2.0**-40
@@ -251,6 +252,7 @@
         return jnp.concatenate([slab] * (rows // (2 * SUBLANES)), axis=0)
 
     total = jnp.zeros((size, 2 * block_rows), F32)
+    left, right = [], []
     for side, weighted in enumerate(sides):
         for k in range(0, weighted.shape[0], SUBLANES):
             high, low = halves(weighted[k : k + SUBLANES])
@@ -258,8 +260,6 @@
             dof, row = split(rows_ref[first : first + SUBLANES, :], block_rows)
             dof = dof.astype(F32)
             row = row.astype(F32)
-            left = []
-            right = []
             for f in range(SUBLANES):
                 here = row_of == widened(row, f, block_rows)
                 left.append(
@@ -272,12 +272,15 @@
                     )
                 )
                 right.append(jnp.where(dof_of == widened(dof, f, size), one, none))
+            if len(left) < BATCH:
+                continue
             total = total + lax.dot_general(
                 jnp.concatenate(right, axis=1),
                 jnp.concatenate(left, axis=1),
                 (((1,), (1,)), ((), ())),
                 preferred_element_type=F32,
             )
+            left, right = [], []
     total = total.T
     return total[:block_rows] + total[block_rows:]
 

time: 32.7 us -> 32.7 us (level)
  no operation moved by 1% of the time
where the time goes in v26:
time: 32.7 us; the launch traced here: 32.5 us
  starting transfers between devices  15.4 us (47%)
  Pallas kernels  7.36 us (23%)
  waiting for transfers between devices  6.79 us (21%)
  other arithmetic  2.2 us (7%)
  between operations  0.73 us (2%)
    ppermute x3, starting transfers between devices, from_behind(): return lax.ppermute(value, axis, pairs)  7.84 us
    pallas_call x8, Pallas kernels, call(): pl.pallas_call(body, out_shape=outs, in_specs=[spec for _, spec in inputs...  7.36 us
    all_to_all x1, waiting for transfers between devices, on_device(): lax.all_to_all(sums, ('sub', 'blk'), split_axis=0, concat_axis=0, tiled=T...  5.87 us
    ppermute x2, starting transfers between devices, swap(): return lax.ppermute(value, 'sub', pairs)  3.12 us
    all_to_all x1, starting transfers between devices, on_device(): lax.all_to_all(sums, ('sub', 'blk'), split_axis=0, concat_axis=0, tiled=T...  2.54 us
    ppermute x3, starting transfers between devices, swap_slots(): lax.ppermute(value, 'blk', [(slot, slot ^ k) for slot in range(count)])  1.88 us
    convert_element_type x1, other arithmetic, on_device(): blocks = stiffness[0, 0].astype(F32)  1.28 us
    add x1, other arithmetic, on_device(): indices.astype(F32) + placed(field, 2 * faces)  0.92 us
  transfers between devices with their start and end apart: 9, of which 4 were waited for; matrix products, arithmetic and copies ran while one was open for 7% of the time, Pallas kernels for 17%

profile of v26, /device:TPU:0, one launch (start us, length us, event | category | flops | bytes accessed | tf_op | source)
XLA Modules:
  0.0 32.5 jit_solution(10906549745073286509)
XLA Ops:
  0.6 3.0 %collective-permute-start = (f32[4,16,128]{2,1,0:T(8,128)}, f32[4,16,128]{2,1,0:T(8,128)S(1)}, u32[]{:S(2)}, u32[]{:S(2)}) collective-permute-start(f32[4,16,128]{2,1,0:T(8,128)} %bitcast.21), channel_id=1, source_target_pairs={{0,4},{4,8},{8,12},{12,16},{16,20},{20,24},{24,28},{28,0},{1,5},{5... | collective-permute-start | bytes 98312 | tf_op jit(solution)/shard_map/ppermute | solution.py:465
  3.7 0.9 %pad_add_fusion.packed_ref = f32[232,128]{1,0:T(8,128)S(1)} fusion(f32[64,128]{1,0:T(8,128)} %bitcast.22, f32[32,96]{1,0:T(8,128)} %bitcast.23, s32[1,4]{1,0:T(1,128)} %bitcast.24, s32[1,64]{1,0:T(1,128)} %bitcast.25, s32[128,128]{1,0:T(8,128)} %bitcast.20), kind=kLoop, calls=%fused_computation.1 | loop fusion | flops 148480 | bytes 229648 | tf_op jit(solution)/shard_map/add | solution.py:496
  4.6 0.8 %shard_map.86 = (s32[128,128]{1,0:T(8,128)S(1)}, f32[32,128]{1,0:T(8,128)S(1)}, f32[8,128]{1,0:T(8,128)S(1)}, f32[64,128]{1,0:T(8,128)S(1)}, f32[64,128]{1,0:T(8...) custom-call(f32[232,128]{1,0:T(8,128)S(1)} %pad_add_fusion.packed_ref), custom_call_target="tpu_custom_call" | custom-call | flops 1000000 | bytes 1000000 | tf_op jit(solution)/shard_map/pallas_call | solution.py:24
  5.4 3.1 %collective-permute-start.1 = (f32[136,128]{1,0:T(8,128)S(1)}, f32[136,128]{1,0:T(8,128)S(1)}, u32[]{:S(2)}, u32[]{:S(2)}) collective-permute-start(f32[136,128]{1,0:T(8,128)S(1)} %get-tuple-element.30), channel_id=1, source_target_pairs={{4,8},{8,4},{12,16},{16,12},{20,24},{24,20},{28,0},{0,28},{5,9},{9... | collective-permute-start | bytes 208904 | tf_op jit(solution)/shard_map/ppermute | solution.py:459
  8.5 0.0 collective-permute-start.2
  8.5 0.3 collective-permute-done.last_ref
  8.8 0.5 %collective-permute-start.3 = (f32[32,128]{1,0:T(8,128)S(1)}, f32[32,128]{1,0:T(8,128)S(1)}, u32[]{:S(2)}, u32[]{:S(2)}) collective-permute-start(f32[32,128]{1,0:T(8,128)S(1)} %get-tuple-element.32), channel_id=1, source_target_pairs={{0,3},{1,2},{2,1},{3,0},{4,7},{5,6},{6,5},{7,4},{8,11},{9,10},{10,... | collective-permute-start | bytes 49160 | tf_op jit(solution)/shard_map/ppermute | solution.py:470
  9.3 1.3 %collective-permute-start.4 = (f32[32,128]{1,0:T(8,128)S(1)}, f32[32,128]{1,0:T(8,128)S(1)}, u32[]{:S(2)}, u32[]{:S(2)}) collective-permute-start(f32[32,128]{1,0:T(8,128)S(1)} %get-tuple-element.33), channel_id=1, source_target_pairs={{0,2},{1,3},{2,0},{3,1},{4,6},{5,7},{6,4},{7,5},{8,10},{9,11},{10,... | collective-permute-start | bytes 49160 | tf_op jit(solution)/shard_map/ppermute | solution.py:470
  10.5 0.2 collective-permute-start.5
  10.7 1.3 %bitcast_convert_fusion.blocks_ref = f32[48,9216]{1,0:T(8,128)S(1)} fusion(bf16[1,1,48,9216]{3,2,1,0:T(8,128)(2,1)} %param.8), kind=kLoop, calls=%fused_computation | loop fusion | flops 442368 | bytes 2654208 | tf_op jit(solution)/shard_map/convert_element_type | solution.py:478
  12.0 1.1 %shard_map.87.product_ref = f32[32,128]{1,0:T(8,128)S(1)} custom-call(s32[2,16]{1,0:T(2,128)S(1)} %bitcast.18, f32[48,9216]{1,0:T(8,128)S(1)} %bitcast_convert_fusion.blocks_ref, f32[32,128]{1,0:T(8,128)S(1)} %get-tuple-element.25.field_ref), custom_call_target="tpu_custom_call" | custom-call | flops 1000000 | bytes 1000000 | tf_op jit(solution)/shard_map/pallas_call | solution.py:24
  13.1 0.0 collective-permute-done.3.refs_0_
  13.1 0.0 collective-permute-done.5.refs_2_
  13.1 0.2 collective-permute-done.2.from_b_ref
  13.3 1.2 %shard_map.89 = (f32[32,128]{1,0:T(8,128)S(1)}, f32[64,128]{1,0:T(8,128)S(1)}, f32[64,128]{1,0:T(8,128)S(1)}, f32[64,128]{1,0:T(8,128)S(1)}, s32[64,128]{1,0:T(8,128)S(1)}, /*index=5*/s32[64,128]{1,0:T(8,128)S(1)}) custom-call(f32[232,128]{1,0:T(8,128)S(1)} %pad_add_fusion.packed_ref, f32[4,16,128]{2,1,0:T(8,128)S(1)} %collective-permute-done.last_ref, ...), custom_call_target="tpu_custom_call" | custom-call | flops 1000000 | bytes 1000000 | tf_op jit(solution)/shard_map/pallas_call | solution.py:24
  14.5 1.7 %collective-permute-start.7 = (f32[32,128]{1,0:T(8,128)S(1)}, f32[32,128]{1,0:T(8,128)S(1)}, u32[]{:S(2)}, u32[]{:S(2)}) collective-permute-start(f32[32,128]{1,0:T(8,128)S(1)} %get-tuple-element.35.field_ref.image_ref), channel_id=1, source_target_pairs={{0,4},{4,8},{8,12},{12,16},{16,20},{20,24},{24,28},{28,0},{1,5},{5... | collective-permute-start | bytes 49160 | tf_op jit(solution)/shard_map/ppermute | solution.py:465
  16.2 1.2 %shard_map.90 = (f32[32,128]{1,0:T(8,128)S(1)}, f32[32,128]{1,0:T(8,128)S(1)}, f32[64,128]{1,0:T(8,128)S(1)}) custom-call(s32[2,16]{1,0:T(2,128)S(1)} %bitcast.19, f32[48,9216]{1,0:T(8,128)S(1)} %bitcast_convert_fusion.blocks_ref, f32[32,128]{1,0:T(8,128)S(1)} %get-tuple-element.35.field_ref.image_ref, s32[128,128]{1,0:T(8,128)S(1)} %get-tuple-element.27.aligned_ref.refs_0_), custom_call_target="tpu_custom_call" | custom-call | flops 1000000 | bytes 1000000 | tf_op jit(solution)/shard_map/pallas_call | solution.py:24
  17.4 3.1 %collective-permute-start.6 = (f32[32,128]{1,0:T(8,128)S(1)}, f32[32,128]{1,0:T(8,128)S(1)}, u32[]{:S(2)}, u32[]{:S(2)}) collective-permute-start(f32[32,128]{1,0:T(8,128)S(1)} %get-tuple-element.41), channel_id=1, source_target_pairs={{0,28},{4,0},{8,4},{12,8},{16,12},{20,16},{24,20},{28,24},{1,29},{... | collective-permute-start | bytes 49160 | tf_op jit(solution)/shard_map/ppermute | solution.py:465
  20.5 0.5 %collective-permute-done.7.last_ref = f32[32,128]{1,0:T(8,128)S(1)} collective-permute-done((f32[32,128]{1,0:T(8,128)S(1)}, f32[32,128]{1,0:T(8,128)S(1)}, u32[]{:S(2)}, u32[]{:S(2)}) %collective-permute-start.7) | collective-permute-done | bytes 16416 | tf_op jit(solution)/shard_map/ppermute | solution.py:465
  21.0 1.1 %shard_map.91 = (f32[32,1,128]{2,1,0:T(1,128)}, f32[64,128]{1,0:T(8,128)S(1)}) custom-call(f32[32,128]{1,0:T(8,128)S(1)} %get-tuple-element.36.product_ref, f32[64,128]{1,0:T(8,128)S(1)} %get-tuple-element.38.weights_ref.weights_west_ref, f32[64,128]{1,0:T(8,128)S(1)} %get-tuple-element.39.own_ref.west_ref, s32[64,128]{1,0:T(8,128)S(1)} %get-tuple-element.42.rows_ref, ...), custom_call_target="tpu_custom_call" | custom-call | flops 1000000 | bytes 1000000 | tf_op jit(solution)/shard_map/pallas_call | solution.py:24
  22.1 2.5 %all-to-all-start = ((f32[32,1,128]{2,1,0:T(1,128)}), f32[32,1,128]{2,1,0:T(1,128)S(1)}, u32[]{:S(2)}, u32[]{:S(2)}) async-start(f32[32,1,128]{2,1,0:T(1,128)} %get-tuple-element.45), calls=%async_computation | async-start | bytes 32768 | tf_op jit(solution)/shard_map/all_to_all | solution.py:585
  24.7 1.2 %shard_map.92.second_ref = f32[32,128]{1,0:T(8,128)S(1)} custom-call(s32[128,128]{1,0:T(8,128)S(1)} %get-tuple-element.27.aligned_ref.refs_0_, f32[32,128]{1,0:T(8,128)S(1)} %get-tuple-element.36.product_ref, f32[64,128]{1,0:T(8,128)S(1)} %get-tuple-element.37.weights_east_ref, f32[64,128]{1,0:T(8,128)S(1)} %get-tuple-element.38.weights_ref.weights_west_ref, ...), custom_call_target="tpu_custom_call" | custom-call | flops 1000000000 | bytes 1000000 | tf_op jit(solution)/shard_map/pallas_call | solution.py:24
  25.9 5.9 %all-to-all-done.sums_ref = f32[32,1,128]{2,1,0:T(1,128)S(1)} async-done(((f32[32,1,128]{2,1,0:T(1,128)}), f32[32,1,128]{2,1,0:T(1,128)S(1)}, u32[]{:S(2)}, u32[]{:S(2)}) %all-to-all-start) | async-done | bytes 16416 | tf_op jit(solution)/shard_map/all_to_all | solution.py:585
  31.7 0.8 %shard_map.93 = (f32[32,96]{1,0:T(8,128)}, f32[32,96]{1,0:T(8,128)}) custom-call(f32[32,128]{1,0:T(8,128)S(1)} %get-tuple-element.25.field_ref, f32[32,128]{1,0:T(8,128)S(1)} %get-tuple-element.35.field_ref.image_ref, f32[32,128]{1,0:T(8,128)S(1)} %shard_map.92.second_ref, f32[32,1,128]{2,1,0:T(1,128)S(1)} %all-to-all-done.sums_ref), custom_call_target="tpu_custom_call" | custom-call | flops 1000000 | bytes 1000000 | tf_op jit(solution)/shard_map/pallas_call | solution.py:24
  (6 shorter events, 0.0 us)
Async XLA Ops:
  0.6 11.3 %copy-start = (s32[1,1,2,16]{3,2,1,0:T(2,128)S(1)}, s32[1,1,2,16]{3,2,1,0:T(2,128)}, u32[]{:S(2)}) copy-start(s32[1,1,2,16]{3,2,1,0:T(2,128)} %param.9) | copy-start | bytes 388
  0.6 8.2 %collective-permute-start = (f32[4,16,128]{2,1,0:T(8,128)}, f32[4,16,128]{2,1,0:T(8,128)S(1)}, u32[]{:S(2)}, u32[]{:S(2)}) collective-permute-start(f32[4,16,128]{2,1,0:T(8,128)} %bitcast.21), channel_id=1, source_target_pairs={{0,4},{4,8},{8,12},{12,16},{16,20},{20,24},{24,28},{28,0},{1,5},{5... | collective-permute-start | bytes 98312 | tf_op jit(solution)/shard_map/ppermute | solution.py:465
  5.4 7.7 %collective-permute-start.1 = (f32[136,128]{1,0:T(8,128)S(1)}, f32[136,128]{1,0:T(8,128)S(1)}, u32[]{:S(2)}, u32[]{:S(2)}) collective-permute-start(f32[136,128]{1,0:T(8,128)S(1)} %get-tuple-element.30), channel_id=1, source_target_pairs={{4,8},{8,4},{12,16},{16,12},{20,24},{24,20},{28,0},{0,28},{5,9},{9... | collective-permute-start | bytes 208904 | tf_op jit(solution)/shard_map/ppermute | solution.py:459
  8.5 4.8 %collective-permute-start.2 = (f32[136,128]{1,0:T(8,128)S(1)}, f32[136,128]{1,0:T(8,128)S(1)}, u32[]{:S(2)}, u32[]{:S(2)}) collective-permute-start(f32[136,128]{1,0:T(8,128)S(1)} %get-tuple-element.31), channel_id=1, source_target_pairs={{0,4},{4,0},{8,12},{12,8},{16,20},{20,16},{24,28},{28,24},{1,5},{5... | collective-permute-start | bytes 208904 | tf_op jit(solution)/shard_map/ppermute | solution.py:459
  8.8 4.3 %collective-permute-start.3 = (f32[32,128]{1,0:T(8,128)S(1)}, f32[32,128]{1,0:T(8,128)S(1)}, u32[]{:S(2)}, u32[]{:S(2)}) collective-permute-start(f32[32,128]{1,0:T(8,128)S(1)} %get-tuple-element.32), channel_id=1, source_target_pairs={{0,3},{1,2},{2,1},{3,0},{4,7},{5,6},{6,5},{7,4},{8,11},{9,10},{10,... | collective-permute-start | bytes 49160 | tf_op jit(solution)/shard_map/ppermute | solution.py:470
  9.3 3.9 %collective-permute-start.4 = (f32[32,128]{1,0:T(8,128)S(1)}, f32[32,128]{1,0:T(8,128)S(1)}, u32[]{:S(2)}, u32[]{:S(2)}) collective-permute-start(f32[32,128]{1,0:T(8,128)S(1)} %get-tuple-element.33), channel_id=1, source_target_pairs={{0,2},{1,3},{2,0},{3,1},{4,6},{5,7},{6,4},{7,5},{8,10},{9,11},{10,... | collective-permute-start | bytes 49160 | tf_op jit(solution)/shard_map/ppermute | solution.py:470
  10.5 2.6 %collective-permute-start.5 = (f32[32,128]{1,0:T(8,128)S(1)}, f32[32,128]{1,0:T(8,128)S(1)}, u32[]{:S(2)}, u32[]{:S(2)}) collective-permute-start(f32[32,128]{1,0:T(8,128)S(1)} %get-tuple-element.34), channel_id=1, source_target_pairs={{0,1},{1,0},{2,3},{3,2},{4,5},{5,4},{6,7},{7,6},{8,9},{9,8},{10,11... | collective-permute-start | bytes 49160 | tf_op jit(solution)/shard_map/ppermute | solution.py:470
  14.5 6.5 %collective-permute-start.7 = (f32[32,128]{1,0:T(8,128)S(1)}, f32[32,128]{1,0:T(8,128)S(1)}, u32[]{:S(2)}, u32[]{:S(2)}) collective-permute-start(f32[32,128]{1,0:T(8,128)S(1)} %get-tuple-element.35.field_ref.image_ref), channel_id=1, source_target_pairs={{0,4},{4,8},{8,12},{12,16},{16,20},{20,24},{24,28},{28,0},{1,5},{5... | collective-permute-start | bytes 49160 | tf_op jit(solution)/shard_map/ppermute | solution.py:465
  17.4 7.2 %collective-permute-start.6 = (f32[32,128]{1,0:T(8,128)S(1)}, f32[32,128]{1,0:T(8,128)S(1)}, u32[]{:S(2)}, u32[]{:S(2)}) collective-permute-start(f32[32,128]{1,0:T(8,128)S(1)} %get-tuple-element.41), channel_id=1, source_target_pairs={{0,28},{4,0},{8,4},{12,8},{16,12},{20,16},{24,20},{28,24},{1,29},{... | collective-permute-start | bytes 49160 | tf_op jit(solution)/shard_map/ppermute | solution.py:465
  22.1 9.6 %all-to-all-start = ((f32[32,1,128]{2,1,0:T(1,128)}), f32[32,1,128]{2,1,0:T(1,128)S(1)}, u32[]{:S(2)}, u32[]{:S(2)}) async-start(f32[32,1,128]{2,1,0:T(1,128)} %get-tuple-element.45), calls=%async_computation | async-start | bytes 32768 | tf_op jit(solution)/shard_map/all_to_all | solution.py:585

commit v27 on v24

--- a/solution.py
+++ b/solution.py
@@ -183,7 +183,7 @@
     tiles = width // LANES
     segments = width // size
     groups = size // segments
-    batch = next(k for k in (4, 3, 2, 1) if groups % k == 0)
+    batch = next(k for k in (8, 4, 3, 2, 1) if groups % k == 0)
 
     def place(position):
         segment = sum(jnp.where(position >= k * size, 1, 0) for k in range(1, segments))

time: 32.7 us -> 32.7 us (level)
  no operation moved by 1% of the time
where the time goes in v27:
time: 32.7 us; the launch traced here: 32.5 us
  starting transfers between devices  15.4 us (47%)
  Pallas kernels  7.36 us (23%)
  waiting for transfers between devices  6.8 us (21%)
  other arithmetic  2.2 us (7%)
  between operations  0.73 us (2%)
    ppermute x3, starting transfers between devices, from_behind(): return lax.ppermute(value, axis, pairs)  7.85 us
    pallas_call x8, Pallas kernels, call(): pl.pallas_call(body, out_shape=outs, in_specs=[spec for _, spec in inputs...  7.36 us
    all_to_all x1, waiting for transfers between devices, on_device(): lax.all_to_all(sums, ('sub', 'blk'), split_axis=0, concat_axis=0, tiled=T...  5.88 us
    ppermute x2, starting transfers between devices, swap(): return lax.ppermute(value, 'sub', pairs)  3.12 us
    all_to_all x1, starting transfers between devices, on_device(): lax.all_to_all(sums, ('sub', 'blk'), split_axis=0, concat_axis=0, tiled=T...  2.54 us
    ppermute x3, starting transfers between devices, swap_slots(): lax.ppermute(value, 'blk', [(slot, slot ^ k) for slot in range(count)])  1.88 us
    convert_element_type x1, other arithmetic, on_device(): blocks = stiffness[0, 0].astype(F32)  1.28 us
    add x1, other arithmetic, on_device(): indices.astype(F32) + placed(field, 2 * faces)  0.92 us
  transfers between devices with their start and end apart: 9, of which 4 were waited for; matrix products, arithmetic and copies ran while one was open for 7% of the time, Pallas kernels for 17%

profile of v27, /device:TPU:0, one launch (start us, length us, event | category | flops | bytes accessed | tf_op | source)
XLA Modules:
  0.0 32.5 jit_solution(16925014473045368192)
XLA Ops:
  0.6 3.0 %collective-permute-start = (f32[4,16,128]{2,1,0:T(8,128)}, f32[4,16,128]{2,1,0:T(8,128)S(1)}, u32[]{:S(2)}, u32[]{:S(2)}) collective-permute-start(f32[4,16,128]{2,1,0:T(8,128)} %bitcast.21), channel_id=1, source_target_pairs={{0,4},{4,8},{8,12},{12,16},{16,20},{20,24},{24,28},{28,0},{1,5},{5... | collective-permute-start | bytes 98312 | tf_op jit(solution)/shard_map/ppermute | solution.py:462
  3.7 0.9 %pad_add_fusion.packed_ref = f32[232,128]{1,0:T(8,128)S(1)} fusion(f32[64,128]{1,0:T(8,128)} %bitcast.22, f32[32,96]{1,0:T(8,128)} %bitcast.23, s32[1,4]{1,0:T(1,128)} %bitcast.24, s32[1,64]{1,0:T(1,128)} %bitcast.25, s32[128,128]{1,0:T(8,128)} %bitcast.20), kind=kLoop, calls=%fused_computation.1 | loop fusion | flops 148480 | bytes 229648 | tf_op jit(solution)/shard_map/add | solution.py:493
  4.6 0.8 %shard_map.86 = (s32[128,128]{1,0:T(8,128)S(1)}, f32[32,128]{1,0:T(8,128)S(1)}, f32[8,128]{1,0:T(8,128)S(1)}, f32[64,128]{1,0:T(8,128)S(1)}, f32[64,128]{1,0:T(8...) custom-call(f32[232,128]{1,0:T(8,128)S(1)} %pad_add_fusion.packed_ref), custom_call_target="tpu_custom_call" | custom-call | flops 1000000 | bytes 1000000 | tf_op jit(solution)/shard_map/pallas_call | solution.py:23
  5.4 3.1 %collective-permute-start.1 = (f32[136,128]{1,0:T(8,128)S(1)}, f32[136,128]{1,0:T(8,128)S(1)}, u32[]{:S(2)}, u32[]{:S(2)}) collective-permute-start(f32[136,128]{1,0:T(8,128)S(1)} %get-tuple-element.30), channel_id=1, source_target_pairs={{4,8},{8,4},{12,16},{16,12},{20,24},{24,20},{28,0},{0,28},{5,9},{9... | collective-permute-start | bytes 208904 | tf_op jit(solution)/shard_map/ppermute | solution.py:456
  8.5 0.0 collective-permute-start.2
  8.5 0.3 collective-permute-done.last_ref
  8.8 0.5 %collective-permute-start.3 = (f32[32,128]{1,0:T(8,128)S(1)}, f32[32,128]{1,0:T(8,128)S(1)}, u32[]{:S(2)}, u32[]{:S(2)}) collective-permute-start(f32[32,128]{1,0:T(8,128)S(1)} %get-tuple-element.32), channel_id=1, source_target_pairs={{0,3},{1,2},{2,1},{3,0},{4,7},{5,6},{6,5},{7,4},{8,11},{9,10},{10,... | collective-permute-start | bytes 49160 | tf_op jit(solution)/shard_map/ppermute | solution.py:467
  9.3 1.3 %collective-permute-start.4 = (f32[32,128]{1,0:T(8,128)S(1)}, f32[32,128]{1,0:T(8,128)S(1)}, u32[]{:S(2)}, u32[]{:S(2)}) collective-permute-start(f32[32,128]{1,0:T(8,128)S(1)} %get-tuple-element.33), channel_id=1, source_target_pairs={{0,2},{1,3},{2,0},{3,1},{4,6},{5,7},{6,4},{7,5},{8,10},{9,11},{10,... | collective-permute-start | bytes 49160 | tf_op jit(solution)/shard_map/ppermute | solution.py:467
  10.5 0.2 collective-permute-start.5
  10.7 1.3 %bitcast_convert_fusion.blocks_ref = f32[48,9216]{1,0:T(8,128)S(1)} fusion(bf16[1,1,48,9216]{3,2,1,0:T(8,128)(2,1)} %param.8), kind=kLoop, calls=%fused_computation | loop fusion | flops 442368 | bytes 2654208 | tf_op jit(solution)/shard_map/convert_element_type | solution.py:475
  12.0 1.1 %shard_map.87.product_ref = f32[32,128]{1,0:T(8,128)S(1)} custom-call(s32[2,16]{1,0:T(2,128)S(1)} %bitcast.18, f32[48,9216]{1,0:T(8,128)S(1)} %bitcast_convert_fusion.blocks_ref, f32[32,128]{1,0:T(8,128)S(1)} %get-tuple-element.25.field_ref), custom_call_target="tpu_custom_call" | custom-call | flops 1000000 | bytes 1000000 | tf_op jit(solution)/shard_map/pallas_call | solution.py:23
  13.1 0.0 collective-permute-done.3.refs_0_
  13.1 0.0 collective-permute-done.1.from_a_ref
  13.1 0.2 collective-permute-done.2.from_b_ref
  13.3 1.2 %shard_map.89 = (f32[32,128]{1,0:T(8,128)S(1)}, f32[64,128]{1,0:T(8,128)S(1)}, f32[64,128]{1,0:T(8,128)S(1)}, f32[64,128]{1,0:T(8,128)S(1)}, s32[64,128]{1,0:T(8,128)S(1)}, /*index=5*/s32[64,128]{1,0:T(8,128)S(1)}) custom-call(f32[232,128]{1,0:T(8,128)S(1)} %pad_add_fusion.packed_ref, f32[4,16,128]{2,1,0:T(8,128)S(1)} %collective-permute-done.last_ref, ...), custom_call_target="tpu_custom_call" | custom-call | flops 1000000 | bytes 1000000 | tf_op jit(solution)/shard_map/pallas_call | solution.py:23
  14.5 1.7 %collective-permute-start.7 = (f32[32,128]{1,0:T(8,128)S(1)}, f32[32,128]{1,0:T(8,128)S(1)}, u32[]{:S(2)}, u32[]{:S(2)}) collective-permute-start(f32[32,128]{1,0:T(8,128)S(1)} %get-tuple-element.35.field_ref.image_ref), channel_id=1, source_target_pairs={{0,4},{4,8},{8,12},{12,16},{16,20},{20,24},{24,28},{28,0},{1,5},{5... | collective-permute-start | bytes 49160 | tf_op jit(solution)/shard_map/ppermute | solution.py:462
  16.2 1.2 %shard_map.90 = (f32[32,128]{1,0:T(8,128)S(1)}, f32[32,128]{1,0:T(8,128)S(1)}, f32[64,128]{1,0:T(8,128)S(1)}) custom-call(s32[2,16]{1,0:T(2,128)S(1)} %bitcast.19, f32[48,9216]{1,0:T(8,128)S(1)} %bitcast_convert_fusion.blocks_ref, f32[32,128]{1,0:T(8,128)S(1)} %get-tuple-element.35.field_ref.image_ref, s32[128,128]{1,0:T(8,128)S(1)} %get-tuple-element.27.aligned_ref.refs_0_), custom_call_target="tpu_custom_call" | custom-call | flops 1000000 | bytes 1000000 | tf_op jit(solution)/shard_map/pallas_call | solution.py:23
  17.4 3.1 %collective-permute-start.6 = (f32[32,128]{1,0:T(8,128)S(1)}, f32[32,128]{1,0:T(8,128)S(1)}, u32[]{:S(2)}, u32[]{:S(2)}) collective-permute-start(f32[32,128]{1,0:T(8,128)S(1)} %get-tuple-element.41), channel_id=1, source_target_pairs={{0,28},{4,0},{8,4},{12,8},{16,12},{20,16},{24,20},{28,24},{1,29},{... | collective-permute-start | bytes 49160 | tf_op jit(solution)/shard_map/ppermute | solution.py:462
  20.5 0.5 %collective-permute-done.7.last_ref = f32[32,128]{1,0:T(8,128)S(1)} collective-permute-done((f32[32,128]{1,0:T(8,128)S(1)}, f32[32,128]{1,0:T(8,128)S(1)}, u32[]{:S(2)}, u32[]{:S(2)}) %collective-permute-start.7) | collective-permute-done | bytes 16416 | tf_op jit(solution)/shard_map/ppermute | solution.py:462
  21.0 1.1 %shard_map.91 = (f32[32,1,128]{2,1,0:T(1,128)}, f32[64,128]{1,0:T(8,128)S(1)}) custom-call(f32[32,128]{1,0:T(8,128)S(1)} %get-tuple-element.36.product_ref, f32[64,128]{1,0:T(8,128)S(1)} %get-tuple-element.38.weights_ref.weights_west_ref, f32[64,128]{1,0:T(8,128)S(1)} %get-tuple-element.39.own_ref.west_ref, s32[64,128]{1,0:T(8,128)S(1)} %get-tuple-element.42.rows_ref, ...), custom_call_target="tpu_custom_call" | custom-call | flops 1000000 | bytes 1000000 | tf_op jit(solution)/shard_map/pallas_call | solution.py:23
  22.1 2.5 %all-to-all-start = ((f32[32,1,128]{2,1,0:T(1,128)}), f32[32,1,128]{2,1,0:T(1,128)S(1)}, u32[]{:S(2)}, u32[]{:S(2)}) async-start(f32[32,1,128]{2,1,0:T(1,128)} %get-tuple-element.45), calls=%async_computation | async-start | bytes 32768 | tf_op jit(solution)/shard_map/all_to_all | solution.py:582
  24.7 1.2 %shard_map.92.second_ref = f32[32,128]{1,0:T(8,128)S(1)} custom-call(s32[128,128]{1,0:T(8,128)S(1)} %get-tuple-element.27.aligned_ref.refs_0_, f32[32,128]{1,0:T(8,128)S(1)} %get-tuple-element.36.product_ref, f32[64,128]{1,0:T(8,128)S(1)} %get-tuple-element.37.weights_east_ref, f32[64,128]{1,0:T(8,128)S(1)} %get-tuple-element.38.weights_ref.weights_west_ref, ...), custom_call_target="tpu_custom_call" | custom-call | flops 1000000000 | bytes 1000000 | tf_op jit(solution)/shard_map/pallas_call | solution.py:23
  25.8 5.9 %all-to-all-done.sums_ref = f32[32,1,128]{2,1,0:T(1,128)S(1)} async-done(((f32[32,1,128]{2,1,0:T(1,128)}), f32[32,1,128]{2,1,0:T(1,128)S(1)}, u32[]{:S(2)}, u32[]{:S(2)}) %all-to-all-start) | async-done | bytes 16416 | tf_op jit(solution)/shard_map/all_to_all | solution.py:582
  31.7 0.8 %shard_map.93 = (f32[32,96]{1,0:T(8,128)}, f32[32,96]{1,0:T(8,128)}) custom-call(f32[32,128]{1,0:T(8,128)S(1)} %get-tuple-element.25.field_ref, f32[32,128]{1,0:T(8,128)S(1)} %get-tuple-element.35.field_ref.image_ref, f32[32,128]{1,0:T(8,128)S(1)} %shard_map.92.second_ref, f32[32,1,128]{2,1,0:T(1,128)S(1)} %all-to-all-done.sums_ref), custom_call_target="tpu_custom_call" | custom-call | flops 1000000 | bytes 1000000 | tf_op jit(solution)/shard_map/pallas_call | solution.py:23
  (6 shorter events, 0.0 us)
Async XLA Ops:
  0.6 11.3 %copy-start = (s32[1,1,2,16]{3,2,1,0:T(2,128)S(1)}, s32[1,1,2,16]{3,2,1,0:T(2,128)}, u32[]{:S(2)}) copy-start(s32[1,1,2,16]{3,2,1,0:T(2,128)} %param.9) | copy-start | bytes 388
  0.6 8.2 %collective-permute-start = (f32[4,16,128]{2,1,0:T(8,128)}, f32[4,16,128]{2,1,0:T(8,128)S(1)}, u32[]{:S(2)}, u32[]{:S(2)}) collective-permute-start(f32[4,16,128]{2,1,0:T(8,128)} %bitcast.21), channel_id=1, source_target_pairs={{0,4},{4,8},{8,12},{12,16},{16,20},{20,24},{24,28},{28,0},{1,5},{5... | collective-permute-start | bytes 98312 | tf_op jit(solution)/shard_map/ppermute | solution.py:462
  5.4 7.7 %collective-permute-start.1 = (f32[136,128]{1,0:T(8,128)S(1)}, f32[136,128]{1,0:T(8,128)S(1)}, u32[]{:S(2)}, u32[]{:S(2)}) collective-permute-start(f32[136,128]{1,0:T(8,128)S(1)} %get-tuple-element.30), channel_id=1, source_target_pairs={{4,8},{8,4},{12,16},{16,12},{20,24},{24,20},{28,0},{0,28},{5,9},{9... | collective-permute-start | bytes 208904 | tf_op jit(solution)/shard_map/ppermute | solution.py:456
  8.5 4.8 %collective-permute-start.2 = (f32[136,128]{1,0:T(8,128)S(1)}, f32[136,128]{1,0:T(8,128)S(1)}, u32[]{:S(2)}, u32[]{:S(2)}) collective-permute-start(f32[136,128]{1,0:T(8,128)S(1)} %get-tuple-element.31), channel_id=1, source_target_pairs={{0,4},{4,0},{8,12},{12,8},{16,20},{20,16},{24,28},{28,24},{1,5},{5... | collective-permute-start | bytes 208904 | tf_op jit(solution)/shard_map/ppermute | solution.py:456
  8.8 4.3 %collective-permute-start.3 = (f32[32,128]{1,0:T(8,128)S(1)}, f32[32,128]{1,0:T(8,128)S(1)}, u32[]{:S(2)}, u32[]{:S(2)}) collective-permute-start(f32[32,128]{1,0:T(8,128)S(1)} %get-tuple-element.32), channel_id=1, source_target_pairs={{0,3},{1,2},{2,1},{3,0},{4,7},{5,6},{6,5},{7,4},{8,11},{9,10},{10,... | collective-permute-start | bytes 49160 | tf_op jit(solution)/shard_map/ppermute | solution.py:467
  9.3 3.9 %collective-permute-start.4 = (f32[32,128]{1,0:T(8,128)S(1)}, f32[32,128]{1,0:T(8,128)S(1)}, u32[]{:S(2)}, u32[]{:S(2)}) collective-permute-start(f32[32,128]{1,0:T(8,128)S(1)} %get-tuple-element.33), channel_id=1, source_target_pairs={{0,2},{1,3},{2,0},{3,1},{4,6},{5,7},{6,4},{7,5},{8,10},{9,11},{10,... | collective-permute-start | bytes 49160 | tf_op jit(solution)/shard_map/ppermute | solution.py:467
  10.5 2.6 %collective-permute-start.5 = (f32[32,128]{1,0:T(8,128)S(1)}, f32[32,128]{1,0:T(8,128)S(1)}, u32[]{:S(2)}, u32[]{:S(2)}) collective-permute-start(f32[32,128]{1,0:T(8,128)S(1)} %get-tuple-element.34), channel_id=1, source_target_pairs={{0,1},{1,0},{2,3},{3,2},{4,5},{5,4},{6,7},{7,6},{8,9},{9,8},{10,11... | collective-permute-start | bytes 49160 | tf_op jit(solution)/shard_map/ppermute | solution.py:467
  14.5 6.5 %collective-permute-start.7 = (f32[32,128]{1,0:T(8,128)S(1)}, f32[32,128]{1,0:T(8,128)S(1)}, u32[]{:S(2)}, u32[]{:S(2)}) collective-permute-start(f32[32,128]{1,0:T(8,128)S(1)} %get-tuple-element.35.field_ref.image_ref), channel_id=1, source_target_pairs={{0,4},{4,8},{8,12},{12,16},{16,20},{20,24},{24,28},{28,0},{1,5},{5... | collective-permute-start | bytes 49160 | tf_op jit(solution)/shard_map/ppermute | solution.py:462
  17.4 7.2 %collective-permute-start.6 = (f32[32,128]{1,0:T(8,128)S(1)}, f32[32,128]{1,0:T(8,128)S(1)}, u32[]{:S(2)}, u32[]{:S(2)}) collective-permute-start(f32[32,128]{1,0:T(8,128)S(1)} %get-tuple-element.41), channel_id=1, source_target_pairs={{0,28},{4,0},{8,4},{12,8},{16,12},{20,16},{24,20},{28,24},{1,29},{... | collective-permute-start | bytes 49160 | tf_op jit(solution)/shard_map/ppermute | solution.py:462
  22.1 9.6 %all-to-all-start = ((f32[32,1,128]{2,1,0:T(1,128)}), f32[32,1,128]{2,1,0:T(1,128)S(1)}, u32[]{:S(2)}, u32[]{:S(2)}) async-start(f32[32,1,128]{2,1,0:T(1,128)} %get-tuple-element.45), calls=%async_computation | async-start | bytes 32768 | tf_op jit(solution)/shard_map/all_to_all | solution.py:582
